TPU v7x, 128 devices: a whole 4x4x4 slice. The times are simulated.
128 devices in a mesh: dp: 32 (over x, z, y_hi), tensor: 4 (over y_lo, core).
Axes of the slice: x: 4, y: 4 (y_hi: 2, y_lo: 2; y = y_hi * 2 + y_lo), z: 4, core: 2. Of those that a mesh axis runs over, the one named last changes fastest.
Arguments:
- tokens: bfloat16 [32768, 1536], P(('dp', 'tensor')), may hold values from -6 to 6
- norm_gains: float32 [2, 1536], P(None, ('dp', 'tensor')), may hold values from 0.25 to 1.75
- w_query: bfloat16 [1536, 1536], P('dp', 'tensor'), may hold values from -0.15625 to 0.15625
- w_keyval: bfloat16 [1536, 1536], P('dp', 'tensor'), may hold values from -0.15625 to 0.15625
- w_out: bfloat16 [1536, 1536], P('tensor', 'dp'), may hold values from -2 to 2
- w_gateup: bfloat16 [1536, 2, 4096], P('dp', None, 'tensor'), may hold values from -0.15625 to 0.15625
- w_down: bfloat16 [4096, 1536], P('tensor', 'dp'), may hold values from -0.09375 to 0.09375
- cotangent: bfloat16 [32768, 1536], P(('dp', 'tensor')), may hold values from -6 to 6
Outputs:
- result: bfloat16 [32768, 1536], P(('dp', 'tensor'))
- input_grad: bfloat16 [32768, 1536], P(('dp', 'tensor'))
- grad_query: float32 [1536, 1536], P('dp', 'tensor')
- grad_keyval: float32 [1536, 1536], P('dp', 'tensor')
- grad_out: float32 [1536, 1536], P('tensor', 'dp')
- grad_gateup: float32 [1536, 2, 4096], P('dp', None, 'tensor')
- grad_down: float32 [4096, 1536], P('tensor', 'dp')
- grad_gains: float32 [2, 1536], P(None, ('dp', 'tensor'))
All inputs are finite; a program needn't handle non-finite values.
Results may differ from a plain program's by a relative error of at most 0.02.
Values may be sent and summed in bfloat16 or wider, within the bound.
No kernel may reach another device: no remote copies, remote signals or barrier semaphores. Data moves between devices by JAX's collectives and lax.ppermute only.
A program may use at most 128 MiB of HBM per device.

v0:
```python
import jax
import jax.numpy as jnp
from jax import lax
from jax.experimental import pallas as pl
from jax.experimental.pallas import tpu as pltpu
from jax.sharding import Mesh, PartitionSpec as P

HD = 96
F32 = jnp.float32
BF16 = jnp.bfloat16
norm_eps = 1e-05
rope_base = 100000.0
LOG2E = 1.4426950408889634
SCALE = HD ** (-0.5)
MIB = 1024 * 1024

QUERY_AT, KEYVAL_AT, OUT_AT, ATTN_WIDTH = 0, 384, 768, 1152


def dot_n(left, right):
    return jnp.dot(left, right, preferred_element_type=F32)


def dot_t(left, right):
    return lax.dot_general(left, right, (((1,), (1,)), ((), ())), preferred_element_type=F32)


def dot_tn(left, right):
    return lax.dot_general(left, right, (((0,), (0,)), ((), ())), preferred_element_type=F32)


def block_at(index, size):
    return pl.ds(pl.multiple_of(index * size, size), size)


def causal_mask(scores, size):
    key_at = lax.broadcasted_iota(jnp.int32, (size, size), 0)
    query_at = lax.broadcasted_iota(jnp.int32, (size, size), 1)
    tail = jnp.where(key_at <= query_at, scores[-size:], -1e30)
    if scores.shape[0] == size:
        return tail
    return jnp.concatenate([scores[:-size], tail], 0)


def project_kernel(place, t0, t1, t2, t3, w_ref, gains_ref, cos_ref, sin_ref,
                   h_ref, qt_ref, q_ref, kt_ref, k_ref, vt_ref, v_ref):
    block = place[0]
    half = HD // 2
    gain_row = gains_ref[0:1, :]
    for step, piece in enumerate((t0, t1, t2, t3)):
        size = piece.shape[0]
        at = block_at(lax.bitwise_xor(block, step), size)
        value = piece[...].astype(F32)
        factor = lax.rsqrt(jnp.mean(value * value, -1, keepdims=True) + norm_eps)
        normed = (value * factor * gain_row).astype(BF16)
        h_ref[at, :] = normed
        cosine = cos_ref[:, at]
        sine = sin_ref[:, at]
        query = dot_n(normed, w_ref[:, QUERY_AT:KEYVAL_AT]).T
        keyval = dot_n(normed, w_ref[:, KEYVAL_AT:OUT_AT]).T

        def rotated(field):
            first, second = field[:half], field[half:]
            return jnp.concatenate(
                [first * cosine - second * sine, second * cosine + first * sine], 0
            )

        for head in range(query.shape[0] // HD):
            turned = rotated(query[head * HD : (head + 1) * HD])
            qt_ref[head, :, at] = turned.astype(BF16)
            q_ref[head, at, :] = turned.T.astype(BF16)
        for head in range(keyval.shape[0] // (2 * HD)):
            turned = rotated(keyval[2 * head * HD : (2 * head + 1) * HD])
            value_t = keyval[(2 * head + 1) * HD : (2 * head + 2) * HD]
            kt_ref[head, :, at] = turned.astype(BF16)
            k_ref[head, at, :] = turned.T.astype(BF16)
            vt_ref[head, :, at] = value_t.astype(BF16)
            v_ref[head, at, :] = value_t.T.astype(BF16)


def whole():
    return pl.BlockSpec(memory_space=pltpu.VMEM)


def scalars():
    return pl.BlockSpec(memory_space=pltpu.SMEM)


def project(place, pieces, weights, gain_rows, cosine, sine):
    length = 4 * pieces[0].shape[0]
    width = pieces[0].shape[1]
    heads = (KEYVAL_AT - QUERY_AT) // HD
    groups = (OUT_AT - KEYVAL_AT) // (2 * HD)
    shapes = [
        ((length, width), BF16),
        ((heads, HD, length), BF16), ((heads, length, HD), BF16),
        ((groups, HD, length), BF16), ((groups, length, HD), BF16),
        ((groups, HD, length), BF16), ((groups, length, HD), BF16),
    ]
    return pl.pallas_call(
        project_kernel,
        out_shape=[jax.ShapeDtypeStruct(*shape) for shape in shapes],
        in_specs=[scalars()] + [whole()] * 8,
        out_specs=[whole()] * len(shapes),
        compiler_params=pltpu.CompilerParams(vmem_limit_bytes=56 * MIB),
        cost_estimate=pl.CostEstimate(
            flops=4 * length * width * 384, bytes_accessed=16 * MIB, transcendentals=0),
        name="project",
    )(place, *pieces, weights, gain_rows, cosine, sine)


def attend_kernel(place, qt_ref, k_ref, vt_ref, w_ref,
                  attn_ref, attnt_ref, lse_ref, keep_ref, send_ref, natural):
    block = place[0]
    heads, _, length = qt_ref.shape
    group_size = heads // k_ref.shape[0]
    size = length // 4

    def one_head(head, carry):
        group = head // group_size
        for step in range(4):
            reach = (step + 1) * size
            columns = slice(step * size, reach)
            scores = causal_mask(dot_n(k_ref[group, :reach, :], qt_ref[head, :, columns]), size)
            top = jnp.max(scores, 0, keepdims=True)
            expo = jnp.exp2((scores - top) * (SCALE * LOG2E))
            total = jnp.sum(expo, 0, keepdims=True)
            probs = (expo * (1.0 / total)).astype(BF16)
            mixed = dot_n(vt_ref[group, :, :reach], probs)
            attnt_ref[head, :, columns] = mixed.astype(BF16)
            lse_ref[head, :, columns] = top * (SCALE * LOG2E) + jnp.log2(total)
        return carry

    lax.fori_loop(0, heads, one_head, 0)
    natural[...] = attnt_ref[...].reshape(heads * HD, length).T
    for step in range(4):
        at = block_at(lax.bitwise_xor(block, step), size)
        rows = natural[at, :]
        attn_ref[step * size : (step + 1) * size, :] = rows
        part = dot_t(rows, w_ref[:, OUT_AT:ATTN_WIDTH]).astype(BF16)
        if step % 2 == 0:
            keep_ref[step // 2] = part
        else:
            send_ref[step // 2] = part


def attend(place, qt, k, vt, weights):
    heads, _, length = qt.shape
    width = weights.shape[0]
    size = length // 4
    shapes = [
        ((length, heads * HD), BF16), ((heads, HD, length), BF16), ((heads, 1, length), F32),
        ((2, size, width), BF16), ((2, size, width), BF16),
    ]
    return pl.pallas_call(
        attend_kernel,
        out_shape=[jax.ShapeDtypeStruct(*shape) for shape in shapes],
        in_specs=[scalars()] + [whole()] * 4,
        out_specs=[whole()] * len(shapes),
        scratch_shapes=[pltpu.VMEM((length, heads * HD), BF16)],
        compiler_params=pltpu.CompilerParams(vmem_limit_bytes=56 * MIB),
        cost_estimate=pl.CostEstimate(
            flops=8 * 1024**3, bytes_accessed=16 * MIB, transcendentals=heads * length * length),
        name="attend",
    )(place, qt, k, vt, weights)


def attend_back_kernel(place, o0, o1, o2, o3, t0, t1, t2, t3, w_ref, qt_ref, q_ref, kt_ref, k_ref,
                       v_ref, attnt_ref, lse_ref, cos_ref, sin_ref,
                       dqkv_ref, keep_ref, send_ref, gain_ref,
                       do_ref, dot_ref, delta_ref, dk_ref, dv_ref, turned_ref):
    block = place[0]
    heads, _, length = qt_ref.shape
    groups = k_ref.shape[0]
    group_size = heads // groups
    size = length // 4
    half = HD // 2
    for step, piece in enumerate((o0, o1, o2, o3)):
        at = block_at(lax.bitwise_xor(block, step), size)
        grad = dot_n(piece[...], w_ref[:, OUT_AT:ATTN_WIDTH]).astype(BF16)
        grad_t = grad.astype(F32).T.astype(BF16)
        for head in range(heads):
            dot_ref[head, :, at] = grad_t[head * HD : (head + 1) * HD]
            do_ref[head, at, :] = grad[:, head * HD : (head + 1) * HD]
    delta_ref[...] = jnp.sum(
        attnt_ref[...].astype(F32) * dot_ref[...].astype(F32), 1, keepdims=True)
    dk_ref[...] = jnp.zeros_like(dk_ref)
    dv_ref[...] = jnp.zeros_like(dv_ref)

    def turned_back(field, cosine, sine):
        first, second = field[:half], field[half:]
        return jnp.concatenate(
            [first * cosine + second * sine, second * cosine - first * sine], 0)

    def one_head(head, carry):
        group = head // group_size
        for step in range(4):
            reach = (step + 1) * size
            columns = slice(step * size, reach)
            scores = causal_mask(dot_n(k_ref[group, :reach, :], qt_ref[head, :, columns]), size)
            soft = jnp.exp2(scores * (SCALE * LOG2E) - lse_ref[head, :, columns])
            d_probs = dot_n(v_ref[group, :reach, :], dot_ref[head, :, columns])
            d_scores = (soft * (d_probs - delta_ref[head, :, columns])).astype(BF16)
            dv_ref[group, :reach, :] += dot_n(soft.astype(BF16), do_ref[head, columns, :])
            dk_ref[group, :reach, :] += dot_n(d_scores, q_ref[head, columns, :])
            d_query = dot_n(kt_ref[group, :, :reach], d_scores) * SCALE
            turned_ref[head, :, columns] = turned_back(
                d_query, cos_ref[:, columns], sin_ref[:, columns])
        return carry

    lax.fori_loop(0, heads, one_head, 0)
    for group in range(groups):
        turned_ref[heads + 2 * group] = turned_back(
            dk_ref[group].T * SCALE, cos_ref[...], sin_ref[...])
        turned_ref[heads + 2 * group + 1] = dv_ref[group].T
    dqkv_ref[...] = turned_ref[...].reshape((heads + 2 * groups) * HD, length).T.astype(BF16)
    gain = jnp.zeros(gain_ref.shape, F32)
    for step, piece in enumerate((t0, t1, t2, t3)):
        at = block_at(lax.bitwise_xor(block, step), size)
        part = dot_t(dqkv_ref[at, :], w_ref[:, QUERY_AT:OUT_AT])
        value = piece[...].astype(F32)
        factor = lax.rsqrt(jnp.mean(value * value, -1, keepdims=True) + norm_eps)
        gain += jnp.sum(part * (value * factor), 0, keepdims=True)
        if step % 2 == 0:
            keep_ref[step // 2] = part.astype(BF16)
        else:
            send_ref[step // 2] = part.astype(BF16)
    gain_ref[...] = gain


def attend_back(place, pieces, token_pieces, weights, qt, q, kt, k, v, attnt, lse, cosine, sine):
    heads, _, length = qt.shape
    groups = k.shape[0]
    width = weights.shape[0]
    size = length // 4
    every = heads + 2 * groups
    shapes = [
        ((length, every * HD), BF16), ((2, size, width), BF16), ((2, size, width), BF16),
        ((1, width), F32),
    ]
    return pl.pallas_call(
        attend_back_kernel,
        out_shape=[jax.ShapeDtypeStruct(*shape) for shape in shapes],
        in_specs=[scalars()] + [whole()] * 18,
        out_specs=[whole()] * len(shapes),
        scratch_shapes=[
            pltpu.VMEM((heads, length, HD), BF16), pltpu.VMEM((heads, HD, length), BF16),
            pltpu.VMEM((heads, 1, length), F32),
            pltpu.VMEM((groups, length, HD), F32), pltpu.VMEM((groups, length, HD), F32),
            pltpu.VMEM((every, HD, length), F32),
        ],
        compiler_params=pltpu.CompilerParams(vmem_limit_bytes=56 * MIB),
        cost_estimate=pl.CostEstimate(
            flops=20 * 1024**3, bytes_accessed=24 * MIB, transcendentals=heads * length * length),
        name="attend_back",
    )(place, *pieces, *token_pieces, weights, qt, q, kt, k, v, attnt, lse, cosine, sine)


def feed_kernel(with_first, with_second, *refs):
    refs = list(refs)
    w_hbm = refs.pop(0)
    if with_first:
        normed_refs, grad_refs = refs[0:2], refs[2:4]
        hidden_ref, dgu_ref = refs[4:6]
        refs = refs[6:]
    else:
        hidden_ref, dgu_ref = refs[0:2]
        refs = refs[2:]
    if with_second:
        back_refs, out_refs = refs[0:2], refs[2:4]
        refs = refs[4:]
    w_ref, sem = refs
    hidden_w = hidden_ref.shape[1]
    size = hidden_ref.shape[0] // 2
    parts = [slice(i * hidden_w, (i + 1) * hidden_w) for i in range(3)]
    copies = [
        pltpu.make_async_copy(w_hbm.at[:, part], w_ref.at[:, part], sem.at[i])
        for i, part in enumerate(parts)
    ]
    for copy in copies:
        copy.start()
    for i in range(2):
        rows = slice(i * size, (i + 1) * size)
        if with_first:
            if i == 0:
                copies[0].wait()
            gate = dot_n(normed_refs[i][...], w_ref[:, parts[0]])
            if i == 0:
                copies[1].wait()
            up = dot_n(normed_refs[i][...], w_ref[:, parts[1]])
            sig = 1.0 / (1.0 + jnp.exp2(gate * (-LOG2E)))
            silu = gate * sig
            hidden = (silu * up).astype(BF16)
            hidden_ref[rows, :] = hidden
            if i == 0:
                copies[2].wait()
            d_hidden = dot_n(grad_refs[i][...], w_ref[:, parts[2]])
            d_gate = (d_hidden * up * (sig * (1.0 + gate * (1.0 - sig)))).astype(BF16)
            d_up = (d_hidden * silu).astype(BF16)
            dgu_ref[rows, :hidden_w] = d_gate
            dgu_ref[rows, hidden_w:] = d_up
        if with_second:
            if not with_first and i == 0:
                copies[0].wait()
                copies[1].wait()
            d_normed = dot_t(dgu_ref[rows, :], w_ref[:, : 2 * hidden_w])
            back_refs[i][...] = d_normed.astype(BF16)
            if not with_first and i == 0:
                copies[2].wait()
            out_refs[i][...] = dot_t(hidden_ref[rows, :], w_ref[:, parts[2]]).astype(BF16)


def feed(weights, normed_pieces, grad_pieces, first=None, with_second=True):
    width = weights.shape[0]
    hidden_w = weights.shape[1] // 3
    with_first = first is None
    size = normed_pieces[0].shape[0]
    piece = jax.ShapeDtypeStruct((size, width), BF16)
    shapes = []
    if with_first:
        shapes += [
            jax.ShapeDtypeStruct((2 * size, hidden_w), BF16),
            jax.ShapeDtypeStruct((2 * size, 2 * hidden_w), BF16),
        ]
    if with_second:
        shapes += [piece] * 4
    operands = (*normed_pieces, *grad_pieces) if with_first else first
    products = 3 * with_first + 3 * with_second
    return pl.pallas_call(
        lambda *refs: feed_kernel(with_first, with_second, *refs),
        out_shape=shapes,
        in_specs=[pl.BlockSpec(memory_space=pl.ANY)] + [whole()] * len(operands),
        out_specs=[whole()] * len(shapes),
        scratch_shapes=[
            pltpu.VMEM((width, 3 * hidden_w), BF16), pltpu.SemaphoreType.DMA((3,)),
        ],
        compiler_params=pltpu.CompilerParams(vmem_limit_bytes=56 * MIB),
        cost_estimate=pl.CostEstimate(
            flops=4 * products * size * width * hidden_w, bytes_accessed=16 * MIB,
            transcendentals=2 * size * hidden_w * with_first),
        name="feed_" + "ab"[with_second] if with_first else "feed_c",
    )(weights, *operands)


def feed_grads_kernel(h0, h1, h2, h3, g0, g1, g2, g3, dgu_a, dgu_b, hidden_a, hidden_b,
                      out_ref, left_ref):
    tile = pl.program_id(0)
    size = h0.shape[0]

    def turn(pieces):
        for i, piece in enumerate(pieces):
            left_ref[:, i * size : (i + 1) * size] = piece[...].T

    @pl.when(tile == 0)
    def _():
        turn((h0, h1, h2, h3))

    gate_up_tiles = 2 * pl.num_programs(0) // 3

    @pl.when(tile == gate_up_tiles)
    def _():
        turn((g0, g1, g2, g3))

    @pl.when(tile < gate_up_tiles)
    def _():
        right = jnp.concatenate([dgu_a[...], dgu_b[...]], 0)
        out_ref[...] = dot_n(left_ref[...], right).astype(BF16)

    @pl.when(tile >= gate_up_tiles)
    def _():
        right = jnp.concatenate([hidden_a[...], hidden_b[...]], 0)
        out_ref[...] = dot_n(left_ref[...], right).astype(BF16)


def feed_grads(normed_pieces, grad_pieces, dgu_a, dgu_b, hidden_a, hidden_b):
    size, width = normed_pieces[0].shape
    half, hidden_w = hidden_a.shape
    column = 512
    tiles = 3 * hidden_w // column
    split = 2 * tiles // 3
    whole_piece = pl.BlockSpec((size, width), lambda i: (0, 0), pipeline_mode=pl.Buffered(1))
    dgu_spec = pl.BlockSpec((half, column), lambda i: (0, jnp.minimum(i, split - 1)))
    hidden_spec = pl.BlockSpec((half, column), lambda i: (0, jnp.maximum(i - split, 0)))
    return pl.pallas_call(
        feed_grads_kernel,
        grid=(tiles,),
        out_shape=jax.ShapeDtypeStruct((width, 3 * hidden_w), BF16),
        in_specs=[whole_piece] * 8 + [dgu_spec] * 2 + [hidden_spec] * 2,
        out_specs=pl.BlockSpec((width, column), lambda i: (0, i)),
        scratch_shapes=[pltpu.VMEM((width, 4 * size), BF16)],
        compiler_params=pltpu.CompilerParams(vmem_limit_bytes=56 * MIB),
        cost_estimate=pl.CostEstimate(
            flops=12 * half * width * hidden_w, bytes_accessed=22 * MIB, transcendentals=0),
        name="feed_grads",
    )(*normed_pieces, *grad_pieces, dgu_a, dgu_b, hidden_a, hidden_b)


LATE_OUT, LATE_WIDTH = 128, 640


def late_grads_kernel(place, h_ref, o0, o1, o2, o3, dqkv_ref, attn_ref, gains_ref, *refs):
    x_refs, y_refs = refs[0:4], refs[4:8]
    left_ref, first_ref, second_ref = refs[8:]
    ix, iz = place[1], place[2]
    width = h_ref.shape[1]
    heads_w = attn_ref.shape[1]
    size = o0.shape[0]
    rows = width // 16
    left_ref[...] = h_ref[...].T
    part = dot_n(left_ref[...], dqkv_ref[...]).astype(BF16)
    first_ref[:, :heads_w] = part[:, :heads_w]
    second_ref[:, LATE_WIDTH - heads_w :] = part[:, heads_w:]
    for i, piece in enumerate((o0, o1, o2, o3)):
        left_ref[:, i * size : (i + 1) * size] = piece[...].T
    part = dot_n(left_ref[...], attn_ref[...]).astype(BF16)
    first_ref[:, heads_w : heads_w + LATE_OUT] = part[:, :LATE_OUT]
    second_ref[:, : heads_w - LATE_OUT] = part[:, LATE_OUT:]
    first_ref[:, heads_w + LATE_OUT :] = gains_ref[...].T.astype(BF16)
    for offset in range(4):
        to_x = lax.rem(ix + 4 - offset, 4)
        to_z = lax.rem(iz + 4 - offset, 4)
        for block in range(4):
            x_refs[offset][block] = first_ref[block_at(to_x * 4 + block, rows), :]
            y_refs[offset][block] = second_ref[block_at(block * 4 + to_z, rows), :]


def late_grads(place, h_first, out_pieces, d_qkv, attn, gains):
    length, width = h_first.shape
    block = jax.ShapeDtypeStruct((4, width // 16, LATE_WIDTH), BF16)
    return pl.pallas_call(
        late_grads_kernel,
        out_shape=[block] * 8,
        in_specs=[scalars()] + [whole()] * 8,
        out_specs=[whole()] * 8,
        scratch_shapes=[
            pltpu.VMEM((width, length), BF16),
            pltpu.VMEM((width, LATE_WIDTH), BF16), pltpu.VMEM((width, LATE_WIDTH), BF16),
        ],
        compiler_params=pltpu.CompilerParams(vmem_limit_bytes=56 * MIB),
        cost_estimate=pl.CostEstimate(
            flops=2 * length * width * 1152, bytes_accessed=16 * MIB, transcendentals=0),
        name="late_grads",
    )(place, h_first, *out_pieces, d_qkv, attn, gains)


def late_middle_kernel(place, *refs):
    x_in, y_in, outs = refs[0:4], refs[4:8], refs[8:]
    ix, iz = place[1], place[2]
    for inputs, at, first in ((x_in, iz, 0), (y_in, ix, 4)):
        for offset in range(4):
            to = lax.rem(at + 4 - offset, 4)
            total = inputs[0][to].astype(F32)
            for ref in inputs[1:]:
                total += ref[to].astype(F32)
            outs[first + offset][...] = total.astype(BF16)


def late_middle(place, along_x, along_z):
    _, rows, width = along_x[0].shape
    block = jax.ShapeDtypeStruct((rows, width), BF16)
    return pl.pallas_call(
        late_middle_kernel,
        out_shape=[block] * 8,
        in_specs=[scalars()] + [whole()] * 8,
        out_specs=[whole()] * 8,
        name="late_middle",
    )(place, *along_x, *along_z)


def late_last_kernel(place, *refs):
    x_in, y_in, keep_ref, send_ref = refs[0:4], refs[4:8], refs[8], refs[9]
    mine = place[3]
    rows = keep_ref.shape[0]
    for inputs, columns in ((x_in, slice(0, LATE_WIDTH)), (y_in, slice(LATE_WIDTH, 2 * LATE_WIDTH))):
        for ref, half in ((keep_ref, mine), (send_ref, 1 - mine)):
            at = block_at(half, rows)
            total = inputs[0][at, :].astype(F32)
            for other_ref in inputs[1:]:
                total += other_ref[at, :].astype(F32)
            ref[:, columns] = total.astype(ref.dtype)


def late_last(place, along_z, along_x):
    rows, width = along_x[0].shape
    return pl.pallas_call(
        late_last_kernel,
        out_shape=[
            jax.ShapeDtypeStruct((rows // 2, 2 * width), F32),
            jax.ShapeDtypeStruct((rows // 2, 2 * width), BF16),
        ],
        in_specs=[scalars()] + [whole()] * 8,
        out_specs=[whole()] * 2,
        name="late_last",
    )(place, *along_z, *along_x)


def norm_rows(values_in):
    factor = lax.rsqrt(jnp.mean(values_in * values_in, -1, keepdims=True) + norm_eps)
    return (values_in * factor, factor)


def norm_back(grad_in, normed, factor, gain_row):
    grad_normed = grad_in * gain_row
    inner = jnp.mean(grad_normed * normed, -1, keepdims=True)
    return (factor * (grad_normed - normed * inner), jnp.sum(grad_in * normed, 0))


def from_offset(v, axis, offset, size):
    return lax.ppermute(v, axis, [((i + offset) % size, i) for i in range(size)])


def other(v, axis):
    return from_offset(v, axis, 1, 2)


def pair_rows(v, axis):
    it = other(v, axis)
    flag = lax.axis_index(axis) == 0
    return jnp.concatenate([jnp.where(flag, v, it), jnp.where(flag, it, v)], 0)


def tensor_pieces(v):
    far = other(v, "yl")
    return [v, other(v, "core"), far, other(far, "core")]


def tensor_sum(own, core, chip, diagonal):
    far = chip.astype(F32) + other(diagonal, "core").astype(F32)
    near = own.astype(F32) + other(core, "core").astype(F32)
    return near + other(far.astype(BF16), "yl").astype(F32)


def from_others(v, axis):
    return [v[0]] + [from_offset(v[i], axis, i, 4) for i in range(1, 4)]


def sum_everywhere(v):
    for axis in ("core", "yl", "yh"):
        v = v + other(v, axis)
    for axis in ("z", "x"):
        v = v + from_offset(v, axis, 1, 4) + from_offset(v, axis, 3, 4) + from_offset(v, axis, 2, 4)
    return v


def gather_rows(v):
    return lax.all_gather(pair_rows(v, "yh"), ("x", "z"), axis=0, tiled=True)


def scatter_rows(v):
    two = lax.psum_scatter(v, ("x", "z"), scatter_dimension=0, tiled=True)
    rows = two.shape[0] // 2
    iyh = lax.axis_index("yh")
    keep = lax.dynamic_slice_in_dim(two, iyh * rows, rows, 0)
    send = lax.dynamic_slice_in_dim(two, (1 - iyh) * rows, rows, 0)
    return keep.astype(F32) + other(send, "yh").astype(F32)


def body(tokens, norm_gains, w_query, w_keyval, w_out, w_gateup, w_down, cotangent):
    D = tokens.shape[1]
    length = 4 * tokens.shape[0]
    hidden_w = w_down.shape[0]
    heads_w = w_query.shape[1]
    gains_w = norm_gains.shape[1]
    block = lax.axis_index("yl") * 2 + lax.axis_index("core")
    row = (lax.axis_index("x") * 4 + lax.axis_index("z")) * 2 + lax.axis_index("yh")
    gains_at = (row * 4 + block) * gains_w
    place = jnp.stack(
        [block, lax.axis_index("x"), lax.axis_index("z"), lax.axis_index("yh")]
    ).astype(jnp.int32)

    attn_w = gather_rows(jnp.concatenate([w_query, w_keyval, w_out.T], 1))
    mlp_w = gather_rows(jnp.concatenate([w_gateup[:, 0], w_gateup[:, 1], w_down.T], 1))
    token_pieces = tensor_pieces(tokens)
    gain_rows = sum_everywhere(
        lax.dynamic_update_slice(jnp.zeros((2, D), F32), norm_gains, (0, gains_at))
    )
    grad_pieces = tensor_pieces(cotangent)
    token_pieces, grad_pieces = lax.optimization_barrier((token_pieces, grad_pieces))

    positions = jnp.arange(length).astype(F32)
    freqs = rope_base ** (-(jnp.arange(HD // 2).astype(F32) * 2.0 / HD))
    angles = freqs[:, None] * positions[None, :]
    cosine, sine = jnp.cos(angles), jnp.sin(angles)

    h_first, qt, q, kt, k, vt, v = project(place, token_pieces, attn_w, gain_rows, cosine, sine)
    attn, attnt, lse, keep, send = attend(place, qt, k, vt, attn_w)
    both = keep.astype(F32) + other(send, "core").astype(F32)
    middle = tokens.astype(F32) + both[0] + other(both[1].astype(BF16), "yl").astype(F32)
    normed2, factor2 = norm_rows(middle)
    h_pieces = tensor_pieces((normed2 * gain_rows[1]).astype(BF16))

    hidden_a, dgu_a = feed(mlp_w, h_pieces[:2], grad_pieces[:2], with_second=False)
    hidden_b, dgu_b, back_chip, back_diag, out_chip, out_diag = feed(
        mlp_w, h_pieces[2:], grad_pieces[2:]
    )
    back_own, back_core, out_own, out_core = feed(
        mlp_w, h_pieces[:2], grad_pieces[:2], first=(hidden_a, dgu_a)
    )
    mlp_grads = feed_grads(h_pieces, grad_pieces, dgu_a, dgu_b, hidden_a, hidden_b)
    early = scatter_rows(mlp_grads)
    d_h2_own = tensor_sum(back_own, back_core, back_chip, back_diag)

    d_norm2, gain_two = norm_back(d_h2_own, normed2, factor2, gain_rows[1])
    d_middle = cotangent.astype(F32) + d_norm2
    out_pieces = tensor_pieces(d_middle.astype(BF16))
    out_pieces, out_parts = lax.optimization_barrier(
        (out_pieces, (out_own, out_core, out_chip, out_diag))
    )
    result = (middle + tensor_sum(*out_parts)).astype(BF16)

    d_qkv, keep, send, gain_one = attend_back(
        place, out_pieces, token_pieces, attn_w, qt, q, kt, k, v, attnt, lse, cosine, sine
    )
    gains = jnp.concatenate([gain_one, gain_two[None], jnp.zeros((126, D), F32)], 0)
    parts = late_grads(place, h_first, out_pieces, d_qkv, attn, gains)
    parts = late_middle(place, from_others(parts[:4], "x"), from_others(parts[4:], "z"))
    late_keep, late_send = late_last(
        place, from_others(parts[:4], "z"), from_others(parts[4:], "x")
    )
    late = late_keep + other(late_send, "yh").astype(F32)

    both = keep.astype(F32) + other(send, "core").astype(F32)
    d_h1_own = both[0] + other(both[1].astype(BF16), "yl").astype(F32)
    normed1, factor1 = norm_rows(tokens.astype(F32))
    d_norm1, _ = norm_back(d_h1_own, normed1, factor1, gain_rows[0])
    input_grad = (d_middle + d_norm1).astype(BF16)

    out_at = heads_w + LATE_OUT
    grad_out = jnp.concatenate([late[:, heads_w:out_at], late[:, LATE_WIDTH : LATE_WIDTH + heads_w - LATE_OUT]], 1)
    gain_sum = late[:, out_at : out_at + 2].T
    for axis in ("core", "yl"):
        gain_sum = gain_sum + other(gain_sum, axis)
    grad_gains = lax.dynamic_slice(gain_sum, (0, block * gains_w), (2, gains_w))
    return (
        result,
        input_grad,
        late[:, :heads_w],
        late[:, 2 * LATE_WIDTH - heads_w :],
        grad_out.T,
        early[:, : 2 * hidden_w].reshape(-1, 2, hidden_w),
        early[:, 2 * hidden_w :].T,
        grad_gains,
    )


def solution(mesh):
    fine = Mesh(mesh.devices.reshape(4, 4, 2, 2, 2), ("x", "z", "yh", "yl", "core"))
    dp = ("x", "z", "yh")
    tensor = ("yl", "core")
    every = dp + tensor
    weights = (P(dp, tensor), P(dp, tensor), P(tensor, dp), P(dp, None, tensor), P(tensor, dp))
    rows = P(every, None)
    gains = P(None, every)
    return jax.shard_map(
        body,
        mesh=fine,
        in_specs=(rows, gains) + weights + (rows,),
        out_specs=(rows, rows) + weights + (gains,),
        check_vma=False,
    )
```

profile of v0, /device:TPU:1, one launch (start us, length us, event | category | flops | bytes accessed | tf_op | source)
XLA Modules:
  0.0 428.5 jit_solution(6644244922539819154)
XLA Ops:
  8.1 3.8 collective-permute-start.6
  16.5 3.0 collective-permute-start.18
  19.5 5.6 %collective-permute-done.18 = bf16[48,3072]{1,0:T(8,128)(2,1)S(1)} collective-permute-done((bf16[48,3072]{1,0:T(8,128)(2,1)S(1)}, bf16[48,3072]{1,0:T(8,128)(2,1)S(1)}, u32[]{:S(2)}, u32[]{:S(2)}) %collective-permute-start.18) | collective-permute-done | bytes 294944 | tf_op jit(solution)/shard_map/ppermute | solution.py:509
  32.1 33.1 %collective-permute-done.8 = f32[2,1536]{1,0:T(2,128)S(1)} collective-permute-done((f32[2,1536]{1,0:T(2,128)S(1)}, f32[2,1536]{1,0:T(2,128)S(1)}, u32[]{:S(2)}, u32[]{:S(2)}) %collective-permute-start.8) | collective-permute-done | bytes 12320 | tf_op jit(solution)/shard_map/ppermute | solution.py:509
  65.2 3.1 collective-permute-start.9
  69.4 3.7 collective-permute-start.12
  80.3 2.8 collective-permute-start.15
  94.4 9.6 %project.1 = (bf16[1024,1536]{1,0:T(8,128)(2,1)}, bf16[4,96,1024]{2,1,0:T(8,128)(2,1)}, bf16[4,1024,96]{2,1,0:T(8,128)(2,1)}, bf16[2,96,1024]{2,1,0:T(8,128)(2,1...) custom-call(s32[4]{0:T(128)} %pad_add_fusion.place, ...), custom_call_target="tpu_custom_call" | custom-call | flops 2415919104 | bytes 16777216 | tf_op jit(solution)/shard_map/project/pallas_call | solution.py:100
  104.0 14.3 %attend.1 = (bf16[1024,384]{1,0:T(8,128)(2,1)}, bf16[4,96,1024]{2,1,0:T(8,128)(2,1)}, f32[4,1,1024]{2,1,0:T(1,128)}, bf16[2,256,1536]{2,1,0:T(8,128)(2,1)}, bf16[2,256,1536]{2,1,0:T(8,128)(2,1)}) custom-call(s32[4]{0:T(128)} %pad_add_fusion.place, bf16[4,96,1024]{2,1,0:T(8,128)(2,1)} %get-tuple-element.74.qt_ref, ...), custom_call_target="tpu_custom_call" | custom-call | flops 8589934592 | bytes 16777216 | tf_op jit(solution)/shard_map/attend/pallas_call | solution.py:155
  120.3 3.2 collective-permute-done.16
  127.0 17.6 %collective-permute-done.17 = bf16[256,1536]{1,0:T(8,128)(2,1)S(1)} collective-permute-done((bf16[256,1536]{1,0:T(8,128)(2,1)S(1)}, bf16[256,1536]{1,0:T(8,128)(2,1)S(1)}, u32[]{:S(2)}, u32[]{:S(2)}) %collective-permute-start.17) | collective-permute-done | bytes 786464 | tf_op jit(solution)/shard_map/ppermute | solution.py:509
  146.7 16.7 %collective-permute-done.21.refs_1_.h2 = bf16[256,1536]{1,0:T(8,128)(2,1)S(1)} collective-permute-done((bf16[256,1536]{1,0:T(8,128)(2,1)S(1)}, bf16[256,1536]{1,0:T(8,128)(2,1)S(1)}, u32[]{:S(2)}, u32[]{:S(2)}) %collective-permute-start.21) | collective-permute-done | bytes 786464 | tf_op jit(solution)/shard_map/ppermute | solution.py:509
  167.4 15.2 %feed_b.1 = (bf16[512,1024]{1,0:T(8,128)(2,1)}, bf16[512,2048]{1,0:T(8,128)(2,1)}, bf16[256,1536]{1,0:T(8,128)(2,1)}, bf16[256,1536]{1,0:T(8,128)(2,1)}, bf16[25...) custom-call(bf16[1536,3072]{1,0:T(8,128)(2,1)} %all-gather.5.cloned.1.call-done.refs_0_, bf16[256,1536]{1,0:T(8,128)(2,1)} %copy-done.39, ...), custom_call_target="tpu_custom_call" | custom-call | flops 9663676416 | bytes 16777216 | tf_op jit(solution)/shard_map/feed_b/pallas_call | solution.py:329
  182.6 10.8 %feed_a.1 = (bf16[512,1024]{1,0:T(8,128)(2,1)}, bf16[512,2048]{1,0:T(8,128)(2,1)}) custom-call(bf16[1536,3072]{1,0:T(8,128)(2,1)} %all-gather.5.cloned.1.call-done.refs_0_, bf16[256,1536]{1,0:T(8,128)(2,1)} %copy-done.16, bf16[256,1536]{1,0:T(8,128)(2,1)} %collective-permute-done.19.refs_2_.h1, bf16[256,1536]{1,0:T(8,128)(2,1)} %g0, bf16[256,1536]{1,0:T(8,128)(2,1)} %copy-done.34), custom_call_target="tpu_custom_call" | custom-call | flops 4831838208 | bytes 16777216 | tf_op jit(solution)/shard_map/feed_a/pallas_call | solution.py:329
  193.5 18.0 %feed_grads.1 = bf16[1536,3072]{1,0:T(8,128)(2,1)} custom-call(bf16[256,1536]{1,0:T(8,128)(2,1)} %copy-done.16, bf16[256,1536]{1,0:T(8,128)(2,1)} %collective-permute-done.19.refs_2_.h1, bf16[256,1536]{1,0:T(8,128)(2,1)} %copy-done.39, bf16[256,1536]{1,0:T(8,128)(2,1)} %collective-permute-done.22.refs_2_.h3, bf16[256,1536]{1,0:T(8,128)(2,1)} %g0, ...), custom_call_target="tpu_custom_call" | custom-call | flops 9663676416 | bytes 23068672 | tf_op jit(solution)/shard_map/feed_grads/pallas_call | solution.py:384
  213.0 11.0 %feed_c.1 = (bf16[256,1536]{1,0:T(8,128)(2,1)}, bf16[256,1536]{1,0:T(8,128)(2,1)}, bf16[256,1536]{1,0:T(8,128)(2,1)}, bf16[256,1536]{1,0:T(8,128)(2,1)}) custom-call(bf16[1536,3072]{1,0:T(8,128)(2,1)} %all-gather.5.cloned.1.call-done.refs_0_, bf16[512,1024]{1,0:T(8,128)(2,1)} %get-tuple-element.81.refs_1_.hidden_a, ...), custom_call_target="tpu_custom_call" | custom-call | flops 4831838208 | bytes 16777216 | tf_op jit(solution)/shard_map/feed_c/pallas_call | solution.py:329
  226.6 16.9 %collective-permute-done.24 = bf16[256,1536]{1,0:T(8,128)(2,1)S(1)} collective-permute-done((bf16[256,1536]{1,0:T(8,128)(2,1)S(1)}, bf16[256,1536]{1,0:T(8,128)(2,1)S(1)}, u32[]{:S(2)}, u32[]{:S(2)}) %collective-permute-start.24) | collective-permute-done | bytes 786464 | tf_op jit(solution)/shard_map/ppermute | solution.py:509
  249.0 15.4 %collective-permute-done.26.o2 = bf16[256,1536]{1,0:T(8,128)(2,1)S(1)} collective-permute-done((bf16[256,1536]{1,0:T(8,128)(2,1)S(1)}, bf16[256,1536]{1,0:T(8,128)(2,1)S(1)}, u32[]{:S(2)}, u32[]{:S(2)}) %collective-permute-start.26) | collective-permute-done | bytes 786464 | tf_op jit(solution)/shard_map/ppermute | solution.py:509
  269.1 20.0 %attend_back.1 = (bf16[1024,768]{1,0:T(8,128)(2,1)}, bf16[2,256,1536]{2,1,0:T(8,128)(2,1)}, bf16[2,256,1536]{2,1,0:T(8,128)(2,1)}, f32[1,1536]{1,0:T(1,128)}) custom-call(s32[4]{0:T(128)} %pad_add_fusion.place, bf16[256,1536]{1,0:T(8,128)(2,1)} %copy-done.12, bf16[256,1536]{1,0:T(8,128)(2,1)} %copy-done.36, bf16[256,1536]{1,0:T(8,128)(2,1)} %copy-done.35, ...), custom_call_target="tpu_custom_call" | custom-call | flops 21474836480 | bytes 25165824 | tf_op jit(solution)/shard_map/attend_back/pallas_call | solution.py:241
  290.8 10.8 %late_grads.1 = (bf16[4,96,640]{2,1,0:T(8,128)(2,1)}, bf16[4,96,640]{2,1,0:T(8,128)(2,1)}, bf16[4,96,640]{2,1,0:T(8,128)(2,1)}, bf16[4,96,640]{2,1,0:T(8,128)(2,...) custom-call(s32[4]{0:T(128)} %pad_add_fusion.place, ...), custom_call_target="tpu_custom_call" | custom-call | flops 3623878656 | bytes 16777216 | tf_op jit(solution)/shard_map/late_grads/pallas_call | solution.py:430
  307.8 17.3 %collective-permute-done.33.refs_1_ = bf16[4,96,640]{2,1,0:T(8,128)(2,1)S(1)} collective-permute-done((bf16[4,96,640]{2,1,0:T(8,128)(2,1)}, bf16[4,96,640]{2,1,0:T(8,128)(2,1)S(1)}, u32[]{:S(2)}, u32[]{:S(2)}) %collective-permute-start.33) | collective-permute-done | bytes 491552 | tf_op jit(solution)/shard_map/ppermute | solution.py:509
  325.4 3.7 collective-permute-done.35.refs_3_
  329.2 9.0 %collective-permute-done.38.refs_7_ = bf16[4,96,640]{2,1,0:T(8,128)(2,1)} collective-permute-done((bf16[4,96,640]{2,1,0:T(8,128)(2,1)}, bf16[4,96,640]{2,1,0:T(8,128)(2,1)}, u32[]{:S(2)}, u32[]{:S(2)}) %collective-permute-start.38) | collective-permute-done | bytes 491552 | tf_op jit(solution)/shard_map/ppermute | solution.py:509
  338.1 3.3 late_middle.1
  343.0 4.4 %collective-permute-start.42 = (bf16[96,640]{1,0:T(8,128)(2,1)}, bf16[96,640]{1,0:T(8,128)(2,1)S(1)}, u32[]{:S(2)}, u32[]{:S(2)}) collective-permute-start(bf16[96,640]{1,0:T(8,128)(2,1)} %get-tuple-element.125), channel_id=1, source_target_pairs={{32,0},{64,32},{96,64},{0,96},{33,1},{65,33},{97,65},{1,97},{34,2}... | collective-permute-start | bytes 368648 | tf_op jit(solution)/shard_map/ppermute | solution.py:509
  356.7 3.2 collective-permute-start.45
  359.9 4.4 %collective-permute-start.29 = (bf16[256,1536]{1,0:T(8,128)(2,1)}, bf16[256,1536]{1,0:T(8,128)(2,1)S(1)}, u32[]{:S(2)}, u32[]{:S(2)}) collective-permute-start(bf16[256,1536]{1,0:T(8,128)(2,1)} %get-tuple-element.96), channel_id=1, source_target_pairs={{1,0},{0,1},{3,2},{2,3},{5,4},{4,5},{7,6},{6,7},{9,8},{8,9},{11,10... | collective-permute-start | bytes 2359304 | tf_op jit(solution)/shard_map/ppermute | solution.py:509
  365.8 2.8 collective-permute-start.47
  377.9 12.8 %collective-permute-done.30 = bf16[256,1536]{1,0:T(8,128)(2,1)} collective-permute-done((bf16[256,1536]{1,0:T(8,128)(2,1)}, bf16[256,1536]{1,0:T(8,128)(2,1)}, u32[]{:S(2)}, u32[]{:S(2)}) %collective-permute-start.30) | collective-permute-done | bytes 786464 | tf_op jit(solution)/shard_map/ppermute | solution.py:509
  393.3 14.1 %collective-permute-done.32 = bf16[256,1536]{1,0:T(8,128)(2,1)S(1)} collective-permute-done((bf16[256,1536]{1,0:T(8,128)(2,1)}, bf16[256,1536]{1,0:T(8,128)(2,1)S(1)}, u32[]{:S(2)}, u32[]{:S(2)}) %collective-permute-start.32) | collective-permute-done | bytes 786464 | tf_op jit(solution)/shard_map/ppermute | solution.py:509
  411.1 2.8 collective-permute-start.46
  413.9 3.3 fusion.6
  (221 shorter events, 98.1 us)
Async XLA Ops:
  7.2 87.2 %all-gather.3.cloned.1.call-start = ((), (), s32[]{:S(2)}) async-start(), calls=%async_computation.1 | async-start | bytes 3760128 | tf_op jit(solution)/shard_map/all_gather | solution.py:546
  16.0 151.3 %all-gather.5.cloned.1.call-start = ((), (), s32[]{:S(2)}) async-start(), calls=%async_computation.2 | async-start | bytes 10027008 | tf_op jit(solution)/shard_map/all_gather | solution.py:546
  16.5 8.6 %collective-permute-start.18 = (bf16[48,3072]{1,0:T(8,128)(2,1)S(1)}, bf16[48,3072]{1,0:T(8,128)(2,1)S(1)}, u32[]{:S(2)}, u32[]{:S(2)}) collective-permute-start(bf16[48,3072]{1,0:T(8,128)(2,1)S(1)} %pad_maximum_fusion.1), channel_id=1, source_target_pairs={{4,0},{0,4},{5,1},{1,5},{6,2},{2,6},{7,3},{3,7},{12,8},{8,12},{13,... | collective-permute-start | bytes 884744 | tf_op jit(solution)/shard_map/ppermute | solution.py:509
  26.1 384.0 %reduce-scatter.2.cloned.1.call-start = ((), (), s32[]{:S(2)}) async-start(), calls=%async_computation.3 | async-start | bytes 10027008 | tf_op jit(solution)/shard_map/reduce_scatter | solution.py:550
  28.9 56.8 %collective-permute-start.1 = (bf16[256,1536]{1,0:T(8,128)(2,1)S(1)}, bf16[256,1536]{1,0:T(8,128)(2,1)S(1)}, u32[]{:S(2)}, u32[]{:S(2)}) collective-permute-start(bf16[256,1536]{1,0:T(8,128)(2,1)S(1)} %copy-done.3), channel_id=1, source_target_pairs={{2,0},{0,2},{3,1},{1,3},{6,4},{4,6},{7,5},{5,7},{10,8},{8,10},{11,... | collective-permute-start | bytes 2359304 | tf_op jit(solution)/shard_map/ppermute | solution.py:509
  30.3 56.8 %collective-permute-start.4 = (bf16[256,1536]{1,0:T(8,128)(2,1)S(1)}, bf16[256,1536]{1,0:T(8,128)(2,1)}, u32[]{:S(2)}, u32[]{:S(2)}) collective-permute-start(bf16[256,1536]{1,0:T(8,128)(2,1)S(1)} %copy-done.9), channel_id=1, source_target_pairs={{2,0},{0,2},{3,1},{1,3},{6,4},{4,6},{7,5},{5,7},{10,8},{8,10},{11,... | collective-permute-start | bytes 2359304 | tf_op jit(solution)/shard_map/ppermute | solution.py:509
  30.7 34.6 %collective-permute-start.8 = (f32[2,1536]{1,0:T(2,128)S(1)}, f32[2,1536]{1,0:T(2,128)S(1)}, u32[]{:S(2)}, u32[]{:S(2)}) collective-permute-start(f32[2,1536]{1,0:T(2,128)S(1)} %add.129), channel_id=1, source_target_pairs={{2,0},{0,2},{3,1},{1,3},{6,4},{4,6},{7,5},{5,7},{10,8},{8,10},{11,... | collective-permute-start | bytes 36872 | tf_op jit(solution)/shard_map/ppermute | solution.py:509
  75.8 16.7 %collective-permute-start = (bf16[256,1536]{1,0:T(8,128)(2,1)S(1)}, bf16[256,1536]{1,0:T(8,128)(2,1)S(1)}, u32[]{:S(2)}, u32[]{:S(2)}) collective-permute-start(bf16[256,1536]{1,0:T(8,128)(2,1)S(1)} %copy-done.3), channel_id=1, source_target_pairs={{1,0},{0,1},{3,2},{2,3},{5,4},{4,5},{7,6},{6,7},{9,8},{8,9},{11,10... | collective-permute-start | bytes 2359304 | tf_op jit(solution)/shard_map/ppermute | solution.py:509
  78.6 14.0 %collective-permute-start.3 = (bf16[256,1536]{1,0:T(8,128)(2,1)S(1)}, bf16[256,1536]{1,0:T(8,128)(2,1)S(1)}, u32[]{:S(2)}, u32[]{:S(2)}) collective-permute-start(bf16[256,1536]{1,0:T(8,128)(2,1)S(1)} %copy-done.9), channel_id=1, source_target_pairs={{1,0},{0,1},{3,2},{2,3},{5,4},{4,5},{7,6},{6,7},{9,8},{8,9},{11,10... | collective-permute-start | bytes 2359304 | tf_op jit(solution)/shard_map/ppermute | solution.py:509
  87.1 7.3 %collective-permute-start.5 = (bf16[256,1536]{1,0:T(8,128)(2,1)}, bf16[256,1536]{1,0:T(8,128)(2,1)}, u32[]{:S(2)}, u32[]{:S(2)}) collective-permute-start(bf16[256,1536]{1,0:T(8,128)(2,1)} %collective-permute-done.4.refs_3_.g2), channel_id=1, source_target_pairs={{1,0},{0,1},{3,2},{2,3},{5,4},{4,5},{7,6},{6,7},{9,8},{8,9},{11,10... | collective-permute-start | bytes 2359304 | tf_op jit(solution)/shard_map/ppermute | solution.py:509
  125.6 19.0 %collective-permute-start.17 = (bf16[256,1536]{1,0:T(8,128)(2,1)S(1)}, bf16[256,1536]{1,0:T(8,128)(2,1)S(1)}, u32[]{:S(2)}, u32[]{:S(2)}) collective-permute-start(bf16[256,1536]{1,0:T(8,128)(2,1)S(1)} %fusion.11), channel_id=1, source_target_pairs={{2,0},{0,2},{3,1},{1,3},{6,4},{4,6},{7,5},{5,7},{10,8},{8,10},{11,... | collective-permute-start | bytes 2359304 | tf_op jit(solution)/shard_map/ppermute | solution.py:509
  145.3 18.1 %collective-permute-start.21 = (bf16[256,1536]{1,0:T(8,128)(2,1)S(1)}, bf16[256,1536]{1,0:T(8,128)(2,1)S(1)}, u32[]{:S(2)}, u32[]{:S(2)}) collective-permute-start(bf16[256,1536]{1,0:T(8,128)(2,1)S(1)} %multiply_convert_fusion.refs_1_.h0), channel_id=1, source_target_pairs={{2,0},{0,2},{3,1},{1,3},{6,4},{4,6},{7,5},{5,7},{10,8},{8,10},{11,... | collective-permute-start | bytes 2359304 | tf_op jit(solution)/shard_map/ppermute | solution.py:509
  165.3 17.3 %collective-permute-start.19 = (bf16[256,1536]{1,0:T(8,128)(2,1)S(1)}, bf16[256,1536]{1,0:T(8,128)(2,1)}, u32[]{:S(2)}, u32[]{:S(2)}) collective-permute-start(bf16[256,1536]{1,0:T(8,128)(2,1)S(1)} %multiply_convert_fusion.refs_1_.h0), channel_id=1, source_target_pairs={{1,0},{0,1},{3,2},{2,3},{5,4},{4,5},{7,6},{6,7},{9,8},{8,9},{11,10... | collective-permute-start | bytes 2359304 | tf_op jit(solution)/shard_map/ppermute | solution.py:509
  212.6 11.6 %collective-permute-start.23 = (bf16[256,1536]{1,0:T(8,128)(2,1)S(1)}, bf16[256,1536]{1,0:T(8,128)(2,1)S(1)}, u32[]{:S(2)}, u32[]{:S(2)}) collective-permute-start(bf16[256,1536]{1,0:T(8,128)(2,1)S(1)} %copy-done.38), channel_id=1, source_target_pairs={{1,0},{0,1},{3,2},{2,3},{5,4},{4,5},{7,6},{6,7},{9,8},{8,9},{11,10... | collective-permute-start | bytes 2359304 | tf_op jit(solution)/shard_map/ppermute | solution.py:509
  224.4 19.0 %collective-permute-start.24 = (bf16[256,1536]{1,0:T(8,128)(2,1)S(1)}, bf16[256,1536]{1,0:T(8,128)(2,1)S(1)}, u32[]{:S(2)}, u32[]{:S(2)}) collective-permute-start(bf16[256,1536]{1,0:T(8,128)(2,1)S(1)} %add_convert_fusion.2), channel_id=1, source_target_pairs={{2,0},{0,2},{3,1},{1,3},{6,4},{4,6},{7,5},{5,7},{10,8},{8,10},{11,... | collective-permute-start | bytes 2359304 | tf_op jit(solution)/shard_map/ppermute | solution.py:509
  246.4 18.1 %collective-permute-start.26 = (bf16[256,1536]{1,0:T(8,128)(2,1)S(1)}, bf16[256,1536]{1,0:T(8,128)(2,1)S(1)}, u32[]{:S(2)}, u32[]{:S(2)}) collective-permute-start(bf16[256,1536]{1,0:T(8,128)(2,1)S(1)} %get-tuple-element.97.o0), channel_id=1, source_target_pairs={{2,0},{0,2},{3,1},{1,3},{6,4},{4,6},{7,5},{5,7},{10,8},{8,10},{11,... | collective-permute-start | bytes 2359304 | tf_op jit(solution)/shard_map/ppermute | solution.py:509
  247.7 18.7 %collective-permute-start.25 = (bf16[256,1536]{1,0:T(8,128)(2,1)S(1)}, bf16[256,1536]{1,0:T(8,128)(2,1)S(1)}, u32[]{:S(2)}, u32[]{:S(2)}) collective-permute-start(bf16[256,1536]{1,0:T(8,128)(2,1)S(1)} %get-tuple-element.97.o0), channel_id=1, source_target_pairs={{1,0},{0,1},{3,2},{2,3},{5,4},{4,5},{7,6},{6,7},{9,8},{8,9},{11,10... | collective-permute-start | bytes 2359304 | tf_op jit(solution)/shard_map/ppermute | solution.py:509
  301.6 23.5 %collective-permute-start.33 = (bf16[4,96,640]{2,1,0:T(8,128)(2,1)}, bf16[4,96,640]{2,1,0:T(8,128)(2,1)S(1)}, u32[]{:S(2)}, u32[]{:S(2)}) collective-permute-start(bf16[4,96,640]{2,1,0:T(8,128)(2,1)} %get-tuple-element.113), channel_id=1, source_target_pairs={{32,0},{64,32},{96,64},{0,96},{33,1},{65,33},{97,65},{1,97},{34,2}... | collective-permute-start | bytes 1474568 | tf_op jit(solution)/shard_map/ppermute | solution.py:509
  304.4 21.0 %collective-permute-start.34 = (bf16[4,96,640]{2,1,0:T(8,128)(2,1)}, bf16[4,96,640]{2,1,0:T(8,128)(2,1)S(1)}, u32[]{:S(2)}, u32[]{:S(2)}) collective-permute-start(bf16[4,96,640]{2,1,0:T(8,128)(2,1)} %get-tuple-element.114), channel_id=1, source_target_pairs={{64,0},{96,32},{0,64},{32,96},{65,1},{97,33},{1,65},{33,97},{66,2}... | collective-permute-start | bytes 1474568 | tf_op jit(solution)/shard_map/ppermute | solution.py:509
  304.4 24.8 %collective-permute-start.35 = (bf16[4,96,640]{2,1,0:T(8,128)(2,1)}, bf16[4,96,640]{2,1,0:T(8,128)(2,1)S(1)}, u32[]{:S(2)}, u32[]{:S(2)}) collective-permute-start(bf16[4,96,640]{2,1,0:T(8,128)(2,1)} %get-tuple-element.115), channel_id=1, source_target_pairs={{96,0},{0,32},{32,64},{64,96},{97,1},{1,33},{33,65},{65,97},{98,2}... | collective-permute-start | bytes 1474568 | tf_op jit(solution)/shard_map/ppermute | solution.py:509
  305.0 24.1 %collective-permute-start.36 = (bf16[4,96,640]{2,1,0:T(8,128)(2,1)}, bf16[4,96,640]{2,1,0:T(8,128)(2,1)S(1)}, u32[]{:S(2)}, u32[]{:S(2)}) collective-permute-start(bf16[4,96,640]{2,1,0:T(8,128)(2,1)} %get-tuple-element.117), channel_id=1, source_target_pairs={{8,0},{16,8},{24,16},{0,24},{9,1},{17,9},{25,17},{1,25},{10,2},{18... | collective-permute-start | bytes 1474568 | tf_op jit(solution)/shard_map/ppermute | solution.py:509
  307.8 21.3 %collective-permute-start.37 = (bf16[4,96,640]{2,1,0:T(8,128)(2,1)}, bf16[4,96,640]{2,1,0:T(8,128)(2,1)}, u32[]{:S(2)}, u32[]{:S(2)}) collective-permute-start(bf16[4,96,640]{2,1,0:T(8,128)(2,1)} %get-tuple-element.118), channel_id=1, source_target_pairs={{16,0},{24,8},{0,16},{8,24},{17,1},{25,9},{1,17},{9,25},{18,2},{26... | collective-permute-start | bytes 1474568 | tf_op jit(solution)/shard_map/ppermute | solution.py:509
  325.2 13.0 %collective-permute-start.38 = (bf16[4,96,640]{2,1,0:T(8,128)(2,1)}, bf16[4,96,640]{2,1,0:T(8,128)(2,1)}, u32[]{:S(2)}, u32[]{:S(2)}) collective-permute-start(bf16[4,96,640]{2,1,0:T(8,128)(2,1)} %get-tuple-element.119), channel_id=1, source_target_pairs={{24,0},{0,8},{8,16},{16,24},{25,1},{1,9},{9,17},{17,25},{26,2},{2,... | collective-permute-start | bytes 1474568 | tf_op jit(solution)/shard_map/ppermute | solution.py:509
  343.0 7.4 %collective-permute-start.42 = (bf16[96,640]{1,0:T(8,128)(2,1)}, bf16[96,640]{1,0:T(8,128)(2,1)S(1)}, u32[]{:S(2)}, u32[]{:S(2)}) collective-permute-start(bf16[96,640]{1,0:T(8,128)(2,1)} %get-tuple-element.125), channel_id=1, source_target_pairs={{32,0},{64,32},{96,64},{0,96},{33,1},{65,33},{97,65},{1,97},{34,2}... | collective-permute-start | bytes 368648 | tf_op jit(solution)/shard_map/ppermute | solution.py:509
  356.7 8.1 %collective-permute-start.45 = (bf16[48,1280]{1,0:T(8,128)(2,1)}, bf16[48,1280]{1,0:T(8,128)(2,1)S(1)}, u32[]{:S(2)}, u32[]{:S(2)}) collective-permute-start(bf16[48,1280]{1,0:T(8,128)(2,1)} %get-tuple-element.129), channel_id=1, source_target_pairs={{4,0},{0,4},{5,1},{1,5},{6,2},{2,6},{7,3},{3,7},{12,8},{8,12},{13,... | collective-permute-start | bytes 368648 | tf_op jit(solution)/shard_map/ppermute | solution.py:509
  359.9 11.0 %collective-permute-start.29 = (bf16[256,1536]{1,0:T(8,128)(2,1)}, bf16[256,1536]{1,0:T(8,128)(2,1)S(1)}, u32[]{:S(2)}, u32[]{:S(2)}) collective-permute-start(bf16[256,1536]{1,0:T(8,128)(2,1)} %get-tuple-element.96), channel_id=1, source_target_pairs={{1,0},{0,1},{3,2},{2,3},{5,4},{4,5},{7,6},{6,7},{9,8},{8,9},{11,10... | collective-permute-start | bytes 2359304 | tf_op jit(solution)/shard_map/ppermute | solution.py:509
  364.3 13.6 %collective-permute-start.28 = (bf16[256,1536]{1,0:T(8,128)(2,1)}, bf16[256,1536]{1,0:T(8,128)(2,1)}, u32[]{:S(2)}, u32[]{:S(2)}) collective-permute-start(bf16[256,1536]{1,0:T(8,128)(2,1)} %get-tuple-element.94), channel_id=1, source_target_pairs={{1,0},{0,1},{3,2},{2,3},{5,4},{4,5},{7,6},{6,7},{9,8},{8,9},{11,10... | collective-permute-start | bytes 2359304 | tf_op jit(solution)/shard_map/ppermute | solution.py:509
  364.3 7.9 %collective-permute-start.31 = (bf16[2,256,1536]{2,1,0:T(8,128)(2,1)}, bf16[2,256,1536]{2,1,0:T(8,128)(2,1)S(1)}, u32[]{:S(2)}, u32[]{:S(2)}) collective-permute-start(bf16[2,256,1536]{2,1,0:T(8,128)(2,1)} %get-tuple-element.107), channel_id=1, source_target_pairs={{1,0},{0,1},{3,2},{2,3},{5,4},{4,5},{7,6},{6,7},{9,8},{8,9},{11,10... | collective-permute-start | bytes 4718600 | tf_op jit(solution)/shard_map/ppermute | solution.py:509
  369.6 7.6 %collective-permute-start.48 = (f32[2,48]{0,1:T(8,128)S(1)}, f32[2,48]{0,1:T(8,128)S(1)}, u32[]{:S(2)}, u32[]{:S(2)}) collective-permute-start(f32[2,48]{0,1:T(8,128)S(1)} %fusion.14), channel_id=1, source_target_pairs={{2,0},{0,2},{3,1},{1,3},{6,4},{4,6},{7,5},{5,7},{10,8},{8,10},{11,... | collective-permute-start | bytes 1160 | tf_op jit(solution)/shard_map/ppermute | solution.py:509
  371.9 18.8 %collective-permute-start.30 = (bf16[256,1536]{1,0:T(8,128)(2,1)}, bf16[256,1536]{1,0:T(8,128)(2,1)}, u32[]{:S(2)}, u32[]{:S(2)}) collective-permute-start(bf16[256,1536]{1,0:T(8,128)(2,1)} %add_convert_fusion.1), channel_id=1, source_target_pairs={{2,0},{0,2},{3,1},{1,3},{6,4},{4,6},{7,5},{5,7},{10,8},{8,10},{11,... | collective-permute-start | bytes 2359304 | tf_op jit(solution)/shard_map/ppermute | solution.py:509
  375.4 32.0 %collective-permute-start.32 = (bf16[256,1536]{1,0:T(8,128)(2,1)}, bf16[256,1536]{1,0:T(8,128)(2,1)S(1)}, u32[]{:S(2)}, u32[]{:S(2)}) collective-permute-start(bf16[256,1536]{1,0:T(8,128)(2,1)} %fusion.12), channel_id=1, source_target_pairs={{2,0},{0,2},{3,1},{1,3},{6,4},{4,6},{7,5},{5,7},{10,8},{8,10},{11,... | collective-permute-start | bytes 2359304 | tf_op jit(solution)/shard_map/ppermute | solution.py:509
  411.1 8.6 %collective-permute-start.46 = (bf16[48,3072]{1,0:T(8,128)(2,1)S(1)}, bf16[48,3072]{1,0:T(8,128)(2,1)S(1)}, u32[]{:S(2)}, u32[]{:S(2)}) collective-permute-start(bf16[48,3072]{1,0:T(8,128)(2,1)S(1)} %constant_dynamic-slice_fusion), channel_id=1, source_target_pairs={{4,0},{0,4},{5,1},{1,5},{6,2},{2,6},{7,3},{3,7},{12,8},{8,12},{13,... | collective-permute-start | bytes 884744 | tf_op jit(solution)/shard_map/ppermute | solution.py:509
  (60 other events, 485.1 us)
Sparse Core Ops, SparseCore 0:
  16.2 52.2 all-gather.2
  70.6 75.1 all-gather.4
  211.6 87.6 reduce-scatter.1
where the time goes:
time: 436 us; the launch traced here: 429 us
  waiting for transfers between devices  184 us (42%)
  Pallas kernels  115 us (26%)
  starting transfers between devices  76.5 us (18%)
  other arithmetic  24.2 us (6%)
  between operations  14.7 us (3%)
  local copies, waits for them, and re-layouts  13.7 us (3%)
    ppermute x49, waiting for transfers between devices, from_offset(): lax.ppermute(v, axis, [((i + offset) % size, i) for i in range(size)])  184 us
    ppermute x49, starting transfers between devices, from_offset(): lax.ppermute(v, axis, [((i + offset) % size, i) for i in range(size)])  76.4 us
    pallas_call x3, Pallas kernels, feed(): pl.pallas_call(lambda *refs: feed_kernel(with_first, with_second, *refs),...  37 us
    pallas_call x1, Pallas kernels, attend_back(): pl.pallas_call(attend_back_kernel, out_shape=[jax.ShapeDtypeStruct(*shape...  20 us
    pallas_call x1, Pallas kernels, feed_grads(): pl.pallas_call(feed_grads_kernel, grid=(tiles,), out_shape=jax.ShapeDtype...  18 us
    pallas_call x1, Pallas kernels, attend(): pl.pallas_call(attend_kernel, out_shape=[jax.ShapeDtypeStruct(*shape) for...  14.3 us
    pallas_call x1, Pallas kernels, late_grads(): pl.pallas_call(late_grads_kernel, out_shape=[block] * 8, in_specs=[scalar...  10.8 us
    pallas_call x1, Pallas kernels, project(): pl.pallas_call(project_kernel, out_shape=[jax.ShapeDtypeStruct(*shape) fo...  9.6 us
  transfers between devices with their start and end apart: 52, of which 25 were waited for; matrix products, arithmetic and copies ran while one was open for 6% of the time, Pallas kernels for 20%

commit v1 on v0

v1 whole, which is shorter than its diff:
```python
import jax
import jax.numpy as jnp
from jax import lax
from jax.experimental import pallas as pl
from jax.experimental.pallas import tpu as pltpu
from jax.sharding import Mesh, PartitionSpec as P

HD = 96
F32 = jnp.float32
BF16 = jnp.bfloat16
norm_eps = 1e-05
rope_base = 100000.0
LOG2E = 1.4426950408889634
SCALE = HD ** (-0.5)
MIB = 1024 * 1024
SMALL = pl.CostEstimate(flops=1, bytes_accessed=1, transcendentals=0)

QUERY_AT, KEYVAL_AT, OUT_AT, ATTN_WIDTH = 0, 384, 768, 1152


def dot_n(left, right):
    return jnp.dot(left, right, preferred_element_type=F32)


def dot_t(left, right):
    return lax.dot_general(left, right, (((1,), (1,)), ((), ())), preferred_element_type=F32)


def dot_tn(left, right):
    return lax.dot_general(left, right, (((0,), (0,)), ((), ())), preferred_element_type=F32)


def block_at(index, size):
    return pl.ds(pl.multiple_of(index * size, size), size)


def causal_mask(scores, size):
    key_at = lax.broadcasted_iota(jnp.int32, (size, size), 0)
    query_at = lax.broadcasted_iota(jnp.int32, (size, size), 1)
    tail = jnp.where(key_at <= query_at, scores[-size:], -1e30)
    if scores.shape[0] == size:
        return tail
    return jnp.concatenate([scores[:-size], tail], 0)


class Moves:
    def __init__(self, sems):
        self.sems = sems
        self.started = []

    def start(self, source, target):
        copy = pltpu.make_async_copy(source, target, self.sems.at[len(self.started)])
        copy.start()
        self.started.append(copy)
        return copy

    def wait(self):
        for copy in self.started:
            copy.wait()


def vmem(shape, dtype=BF16):
    return pltpu.VMEM(shape, dtype)


def like(shape, dtype=BF16):
    return jax.ShapeDtypeStruct(shape, dtype)


def whole():
    return pl.BlockSpec(memory_space=pltpu.VMEM)


def apart():
    return pl.BlockSpec(memory_space=pl.ANY)


def scalars():
    return pl.BlockSpec(memory_space=pltpu.SMEM)


def kernel_call(kernel, name, place, small, large, outs, small_outs, scratch, fetches, stores, limit):
    return pl.pallas_call(
        kernel,
        out_shape=list(small_outs) + list(outs),
        in_specs=[scalars()] + [whole()] * len(small) + [apart()] * len(large),
        out_specs=[whole()] * len(small_outs) + [apart()] * len(outs),
        scratch_shapes=list(scratch)
        + [pltpu.SemaphoreType.DMA((fetches,)), pltpu.SemaphoreType.DMA((stores,))],
        compiler_params=pltpu.CompilerParams(vmem_limit_bytes=limit * MIB),
        cost_estimate=SMALL,
        name=name,
    )(place, *small, *large)


def attend_kernel(place, gains_ref, cos_ref, sin_ref, t0, t1, t2, t3, w_hbm,
                  lse_ref, h_hbm, qt_hbm, q_hbm, kt_hbm, k_hbm, v_hbm, attn_hbm, attnt_hbm,
                  o0, o1, o2, o3,
                  t_ref, w_ref, h_ref, qt_ref, q_ref, kt_ref, k_ref, vt_ref, v_ref,
                  natural, attn_ref, attnt_ref, part_ref, in_sem, out_sem):
    block = place[0]
    half = HD // 2
    size = t_ref.shape[1]
    heads, _, length = qt_ref.shape
    group_size = heads // k_ref.shape[0]
    fetch, store = Moves(in_sem), Moves(out_sem)
    pieces = (t0, t1, t2, t3)
    came = [fetch.start(pieces[0], t_ref.at[0])]
    proj = pl.ds(0, OUT_AT)
    w_came = fetch.start(w_hbm.at[:, proj], w_ref.at[:, proj])
    came += [fetch.start(pieces[i], t_ref.at[i]) for i in range(1, 4)]
    last = pl.ds(OUT_AT, ATTN_WIDTH - OUT_AT)
    o_came = fetch.start(w_hbm.at[:, last], w_ref.at[:, last])
    gain_row = gains_ref[0:1, :]
    for step in range(4):
        at = block_at(lax.bitwise_xor(block, step), size)
        came[step].wait()
        value = t_ref[step].astype(F32)
        factor = lax.rsqrt(jnp.mean(value * value, -1, keepdims=True) + norm_eps)
        normed = (value * factor * gain_row).astype(BF16)
        h_ref[at, :] = normed
        cosine = cos_ref[:, at]
        sine = sin_ref[:, at]
        if step == 0:
            w_came.wait()
        every = dot_n(normed, w_ref[:, :OUT_AT]).T
        query, keyval = every[:KEYVAL_AT], every[KEYVAL_AT:]

        def rotated(field):
            first, second = field[:half], field[half:]
            return jnp.concatenate(
                [first * cosine - second * sine, second * cosine + first * sine], 0
            )

        for head in range(query.shape[0] // HD):
            turned = rotated(query[head * HD : (head + 1) * HD])
            qt_ref[head, :, at] = turned.astype(BF16)
            q_ref[head, at, :] = turned.T.astype(BF16)
        for head in range(keyval.shape[0] // (2 * HD)):
            turned = rotated(keyval[2 * head * HD : (2 * head + 1) * HD])
            value_t = keyval[(2 * head + 1) * HD : (2 * head + 2) * HD]
            kt_ref[head, :, at] = turned.astype(BF16)
            k_ref[head, at, :] = turned.T.astype(BF16)
            vt_ref[head, :, at] = value_t.astype(BF16)
            v_ref[head, at, :] = value_t.T.astype(BF16)
    for source, target in ((h_ref, h_hbm), (qt_ref, qt_hbm), (q_ref, q_hbm), (kt_ref, kt_hbm),
                           (k_ref, k_hbm), (v_ref, v_hbm)):
        store.start(source, target)

    def one_head(head, carry):
        group = head // group_size
        for step in range(4):
            reach = (step + 1) * size
            columns = slice(step * size, reach)
            scores = causal_mask(dot_n(k_ref[group, :reach, :], qt_ref[head, :, columns]), size)
            top = jnp.max(scores, 0, keepdims=True)
            expo = jnp.exp2((scores - top) * (SCALE * LOG2E))
            total = jnp.sum(expo, 0, keepdims=True)
            probs = (expo * (1.0 / total)).astype(BF16)
            mixed = dot_n(vt_ref[group, :, :reach], probs)
            attnt_ref[head, :, columns] = mixed.astype(BF16)
            lse_ref[head, :, columns] = top * (SCALE * LOG2E) + jnp.log2(total)
        return carry

    lax.fori_loop(0, heads, one_head, 0)
    store.start(attnt_ref, attnt_hbm)
    natural[...] = attnt_ref[...].reshape(heads * HD, length).T
    o_came.wait()
    for step, out in ((1, o1), (3, o3), (2, o2), (0, o0)):
        at = block_at(lax.bitwise_xor(block, step), size)
        rows = natural[at, :]
        attn_ref[step * size : (step + 1) * size, :] = rows
        part_ref[step] = dot_t(rows, w_ref[:, OUT_AT:ATTN_WIDTH]).astype(BF16)
        store.start(part_ref.at[step], out)
    store.start(attn_ref, attn_hbm)
    store.wait()


def attend(place, pieces, weights, gain_rows, cosine, sine):
    size, width = pieces[0].shape
    length = 4 * size
    heads = (KEYVAL_AT - QUERY_AT) // HD
    groups = (OUT_AT - KEYVAL_AT) // (2 * HD)
    columns, rows = (heads, HD, length), (heads, length, HD)
    g_columns, g_rows = (groups, HD, length), (groups, length, HD)
    outs = [(length, width), columns, rows, g_columns, g_rows, g_rows,
            (length, heads * HD), columns] + [(size, width)] * 4
    scratch = [(4, size, width), (width, ATTN_WIDTH), (length, width), columns, rows,
               g_columns, g_rows, g_columns, g_rows,
               (length, heads * HD), (length, heads * HD), columns, (4, size, width)]
    return kernel_call(
        attend_kernel, "attend", place, (gain_rows, cosine, sine), (*pieces, weights),
        [like(s) for s in outs], [like((heads, 1, length), F32)], [vmem(s) for s in scratch],
        6, 12, 52)


def attend_back_kernel(place, lse_ref, cos_ref, sin_ref, gain2_ref,
                       o0, o1, o2, o3, t0, t1, t2, t3, w_hbm, h_hbm, qt_hbm, q_hbm, kt_hbm,
                       k_hbm, v_hbm, attn_hbm, attnt_hbm,
                       c0, c1, c2, c3, x0, x1, x2, x3, y0, y1, y2, y3,
                       o_ref, t_ref, w_ref, h_ref, qt_ref, q_ref, kt_ref, k_ref, v_ref,
                       attn_ref, attnt_ref,
                       do_ref, dot_ref, dqkv_ref, part_ref, first_ref, second_ref,
                       delta_ref, dk_ref, dv_ref, turned_ref, in_sem, out_sem):
    block, ix, iz = place[0], place[1], place[2]
    heads, _, length = qt_ref.shape
    groups = k_ref.shape[0]
    group_size = heads // groups
    size = length // 4
    half = HD // 2
    width = w_ref.shape[0]
    heads_w = heads * HD
    fetch, store = Moves(in_sem), Moves(out_sem)
    last = pl.ds(OUT_AT, ATTN_WIDTH - OUT_AT)
    early = [fetch.start(w_hbm.at[:, last], w_ref.at[:, last])]
    early += [
        fetch.start(piece, o_ref.at[pl.ds(i * size, size), :])
        for i, piece in enumerate((o0, o1, o2, o3))
    ]
    for source, target in ((attnt_hbm, attnt_ref), (qt_hbm, qt_ref), (q_hbm, q_ref),
                           (kt_hbm, kt_ref), (k_hbm, k_ref), (v_hbm, v_ref)):
        early.append(fetch.start(source, target))
    proj = pl.ds(0, OUT_AT)
    later = [
        fetch.start(attn_hbm, attn_ref),
        fetch.start(h_hbm, h_ref),
        fetch.start(w_hbm.at[:, proj], w_ref.at[:, proj]),
    ]
    later += [fetch.start(piece, t_ref.at[i]) for i, piece in enumerate((t0, t1, t2, t3))]
    early[0].wait()
    for step in range(4):
        at = block_at(lax.bitwise_xor(block, step), size)
        early[1 + step].wait()
        grad = dot_n(o_ref[step * size : (step + 1) * size, :], w_ref[:, OUT_AT:ATTN_WIDTH])
        grad_t = grad.T.astype(BF16)
        grad = grad.astype(BF16)
        for head in range(heads):
            dot_ref[head, :, at] = grad_t[head * HD : (head + 1) * HD]
            do_ref[head, at, :] = grad[:, head * HD : (head + 1) * HD]
    for copy in early[5:]:
        copy.wait()
    delta_ref[...] = jnp.sum(
        attnt_ref[...].astype(F32) * dot_ref[...].astype(F32), 1, keepdims=True)
    dk_ref[...] = jnp.zeros_like(dk_ref)
    dv_ref[...] = jnp.zeros_like(dv_ref)

    def turned_back(field, cosine, sine):
        first, second = field[:half], field[half:]
        return jnp.concatenate(
            [first * cosine + second * sine, second * cosine - first * sine], 0)

    def one_head(head, carry):
        group = head // group_size
        for step in range(4):
            reach = (step + 1) * size
            columns = slice(step * size, reach)
            scores = causal_mask(dot_n(k_ref[group, :reach, :], qt_ref[head, :, columns]), size)
            soft = jnp.exp2(scores * (SCALE * LOG2E) - lse_ref[head, :, columns])
            d_probs = dot_n(v_ref[group, :reach, :], dot_ref[head, :, columns])
            d_scores = (soft * (d_probs - delta_ref[head, :, columns])).astype(BF16)
            dv_ref[group, :reach, :] += dot_n(soft.astype(BF16), do_ref[head, columns, :])
            dk_ref[group, :reach, :] += dot_n(d_scores, q_ref[head, columns, :])
            d_query = dot_n(kt_ref[group, :, :reach], d_scores) * SCALE
            turned_ref[head, :, columns] = turned_back(
                d_query, cos_ref[:, columns], sin_ref[:, columns])
        return carry

    lax.fori_loop(0, heads, one_head, 0)
    for group in range(groups):
        turned_ref[heads + 2 * group] = turned_back(
            dk_ref[group].T * SCALE, cos_ref[...], sin_ref[...])
        turned_ref[heads + 2 * group + 1] = dv_ref[group].T
    dqkv_ref[...] = turned_ref[...].reshape((heads + 2 * groups) * HD, length).T.astype(BF16)
    for copy in later:
        copy.wait()

    gain = jnp.zeros((1, width), F32)
    for step, out in ((1, c1), (3, c3), (2, c2), (0, c0)):
        at = block_at(lax.bitwise_xor(block, step), size)
        part = dot_t(dqkv_ref[at, :], w_ref[:, QUERY_AT:OUT_AT])
        value = t_ref[step].astype(F32)
        factor = lax.rsqrt(jnp.mean(value * value, -1, keepdims=True) + norm_eps)
        gain += jnp.sum(part * (value * factor), 0, keepdims=True)
        part_ref[step] = part.astype(BF16)
        store.start(part_ref.at[step], out)

    rows = width // 16
    part = dot_tn(h_ref[...], dqkv_ref[...]).astype(BF16)
    first_ref[:, :heads_w] = part[:, :heads_w]
    second_ref[:, LATE_WIDTH - heads_w :] = part[:, heads_w:]
    part = dot_tn(o_ref[...], attn_ref[...]).astype(BF16)
    first_ref[:, heads_w : heads_w + LATE_OUT] = part[:, :LATE_OUT]
    second_ref[:, : heads_w - LATE_OUT] = part[:, LATE_OUT:]
    gains = jnp.concatenate([gain, gain2_ref[...], jnp.zeros((126, width), F32)], 0)
    first_ref[:, heads_w + LATE_OUT :] = gains.T.astype(BF16)
    for offset, (x_out, y_out) in enumerate(((x0, y0), (x1, y1), (x2, y2), (x3, y3))):
        to_x = lax.rem(ix + 4 - offset, 4)
        to_z = lax.rem(iz + 4 - offset, 4)
        store.start(first_ref.at[block_at(to_x, 4 * rows), :], x_out)
        for i in range(4):
            store.start(second_ref.at[block_at(i * 4 + to_z, rows), :], y_out.at[i])
    store.wait()


def attend_back(place, lse, cosine, sine, gain_two, pieces, token_pieces, weights, h_first,
                qt, q, kt, k, v, attn, attnt):
    size, width = pieces[0].shape
    heads, _, length = qt.shape
    groups = k.shape[0]
    every = heads + 2 * groups
    rows = width // 16
    outs = [(size, width)] * 4 + [(4 * rows, LATE_WIDTH)] * 4 + [(4, rows, LATE_WIDTH)] * 4
    scratch = [
        (length, width), (4, size, width), (width, ATTN_WIDTH), (length, width),
        qt.shape, q.shape, kt.shape, k.shape, v.shape, attn.shape, attnt.shape,
        (heads, length, HD), (heads, HD, length), (length, every * HD), (4, size, width),
        (width, LATE_WIDTH), (width, LATE_WIDTH),
    ]
    wide = [(heads, 1, length), (groups, length, HD), (groups, length, HD), (every, HD, length)]
    return kernel_call(
        attend_back_kernel, "attend_back", place, (lse, cosine, sine, gain_two),
        (*pieces, *token_pieces, weights, h_first, qt, q, kt, k, v, attn, attnt),
        [like(s) for s in outs], [],
        [vmem(s) for s in scratch] + [vmem(s, F32) for s in wide], 18, 24, 56)


def feed_kernel(place, h0, h1, g0, g1, w_hbm, hidden_hbm, dgu_hbm, b0, b1, r0, r1,
                w_ref, h_ref, g_ref, hidden_ref, dgu_ref, back_ref, out_ref, in_sem, out_sem):
    del place
    hidden_w = hidden_ref.shape[1]
    size = h_ref.shape[1]
    parts = [slice(i * hidden_w, (i + 1) * hidden_w) for i in range(3)]
    fetch, store = Moves(in_sem), Moves(out_sem)

    def weight(i):
        at = pl.ds(i * hidden_w, hidden_w)
        return fetch.start(w_hbm.at[:, at], w_ref.at[:, at])

    came = [fetch.start(h0, h_ref.at[0]), weight(0), weight(1), fetch.start(g0, g_ref.at[0]),
            weight(2), fetch.start(h1, h_ref.at[1]), fetch.start(g1, g_ref.at[1])]
    for i, (back, out) in enumerate(((b0, r0), (b1, r1))):
        rows = slice(i * size, (i + 1) * size)
        at = pl.ds(i * size, size)
        for copy in came[0:2] if i == 0 else came[5:7]:
            copy.wait()
        gate = dot_n(h_ref[i], w_ref[:, parts[0]])
        if i == 0:
            came[2].wait()
        up = dot_n(h_ref[i], w_ref[:, parts[1]])
        sig = 1.0 / (1.0 + jnp.exp2(gate * (-LOG2E)))
        silu = gate * sig
        hidden = (silu * up).astype(BF16)
        hidden_ref[rows, :] = hidden
        store.start(hidden_ref.at[at, :], hidden_hbm.at[at, :])
        if i == 0:
            came[3].wait()
            came[4].wait()
        d_hidden = dot_n(g_ref[i], w_ref[:, parts[2]])
        dgu_ref[rows, :hidden_w] = (
            d_hidden * up * (sig * (1.0 + gate * (1.0 - sig)))).astype(BF16)
        dgu_ref[rows, hidden_w:] = (d_hidden * silu).astype(BF16)
        store.start(dgu_ref.at[at, :], dgu_hbm.at[at, :])
        back_ref[i] = dot_t(dgu_ref[rows, :], w_ref[:, : 2 * hidden_w]).astype(BF16)
        store.start(back_ref.at[i], back)
        out_ref[i] = dot_t(hidden_ref[rows, :], w_ref[:, parts[2]]).astype(BF16)
        store.start(out_ref.at[i], out)
    store.wait()


def feed(place, weights, normed_pieces, grad_pieces):
    size, width = normed_pieces[0].shape
    hidden_w = weights.shape[1] // 3
    wide = [(2 * size, hidden_w), (2 * size, 2 * hidden_w)]
    return kernel_call(
        feed_kernel, "feed", place, (), (*normed_pieces, *grad_pieces, weights),
        [like(s) for s in wide + [(size, width)] * 4], [],
        [vmem(s) for s in [weights.shape] + [(2, size, width)] * 2 + wide + [(2, size, width)] * 2],
        7, 8, 40)


def feed_grads_kernel(place, h0, h1, h2, h3, g0, g1, g2, g3, dgu_a, dgu_b, hidden_a, hidden_b,
                      out_hbm, h_ref, g_ref, dgu_ref, hidden_ref, out_ref, in_sem, out_sem):
    del place
    size = h0.shape[0]
    half, hidden_w = hidden_a.shape
    column = 512
    fetch, store = Moves(in_sem), Moves(out_sem)

    def rows_of(pieces, ref):
        return [
            fetch.start(piece, ref.at[pl.ds(i * size, size), :]) for i, piece in enumerate(pieces)
        ]

    def tiles_of(pieces, ref):
        tiles = []
        for tile in range(ref.shape[1] // column):
            at = pl.ds(tile * column, column)
            tiles.append([
                fetch.start(piece.at[:, at], ref.at[pl.ds(i * half, half), at])
                for i, piece in enumerate(pieces)
            ])
        return tiles

    h_came = rows_of((h0, h1, h2, h3), h_ref)
    dgu_came = tiles_of((dgu_a, dgu_b), dgu_ref)
    g_came = rows_of((g0, g1, g2, g3), g_ref)
    hidden_came = tiles_of((hidden_a, hidden_b), hidden_ref)
    at = 0
    for came, left, tiles, right in (
        (h_came, h_ref, dgu_came, dgu_ref), (g_came, g_ref, hidden_came, hidden_ref)
    ):
        for copy in came:
            copy.wait()
        for tile, copies in enumerate(tiles):
            for copy in copies:
                copy.wait()
            columns = pl.ds(at, column)
            out_ref[:, columns] = dot_tn(
                left[...], right[:, tile * column : (tile + 1) * column]).astype(BF16)
            store.start(out_ref.at[:, columns], out_hbm.at[:, columns])
            at += column
    store.wait()


def feed_grads(place, normed_pieces, grad_pieces, dgu_a, dgu_b, hidden_a, hidden_b):
    size, width = normed_pieces[0].shape
    half, hidden_w = hidden_a.shape
    scratch = [(4 * size, width)] * 2 + [(2 * half, 2 * hidden_w), (2 * half, hidden_w),
                                         (width, 3 * hidden_w)]
    return kernel_call(
        feed_grads_kernel, "feed_grads", place, (),
        (*normed_pieces, *grad_pieces, dgu_a, dgu_b, hidden_a, hidden_b),
        [like((width, 3 * hidden_w))], [], [vmem(s) for s in scratch], 20, 6, 36)[0]


LATE_OUT, LATE_WIDTH = 128, 640


def late_middle_kernel(place, *refs):
    x_in, y_in, outs = refs[0:4], refs[4:8], refs[8:]
    ix, iz = place[1], place[2]
    rows = outs[0].shape[0]
    for offset in range(4):
        at = block_at(lax.rem(iz + 4 - offset, 4), rows)
        total = x_in[0][at, :].astype(F32)
        for ref in x_in[1:]:
            total += ref[at, :].astype(F32)
        outs[offset][...] = total.astype(BF16)
        to = lax.rem(ix + 4 - offset, 4)
        total = y_in[0][to].astype(F32)
        for ref in y_in[1:]:
            total += ref[to].astype(F32)
        outs[4 + offset][...] = total.astype(BF16)


def late_middle(place, along_x, along_z):
    _, rows, width = along_z[0].shape
    return pl.pallas_call(
        late_middle_kernel,
        out_shape=[like((rows, width))] * 8,
        in_specs=[scalars()] + [whole()] * 8,
        out_specs=[whole()] * 8,
        cost_estimate=SMALL,
        name="late_middle",
    )(place, *along_x, *along_z)


def late_last_kernel(place, *refs):
    x_in, y_in, keep_ref, send_ref = refs[0:4], refs[4:8], refs[8], refs[9]
    mine = place[3]
    rows = keep_ref.shape[0]
    for inputs, columns in ((x_in, slice(0, LATE_WIDTH)), (y_in, slice(LATE_WIDTH, 2 * LATE_WIDTH))):
        for ref, half in ((keep_ref, mine), (send_ref, 1 - mine)):
            at = block_at(half, rows)
            total = inputs[0][at, :].astype(F32)
            for other_ref in inputs[1:]:
                total += other_ref[at, :].astype(F32)
            ref[:, columns] = total.astype(ref.dtype)


def late_last(place, along_z, along_x):
    rows, width = along_x[0].shape
    return pl.pallas_call(
        late_last_kernel,
        out_shape=[
            jax.ShapeDtypeStruct((rows // 2, 2 * width), F32),
            jax.ShapeDtypeStruct((rows // 2, 2 * width), BF16),
        ],
        in_specs=[scalars()] + [whole()] * 8,
        out_specs=[whole()] * 2,
        cost_estimate=SMALL,
        name="late_last",
    )(place, *along_z, *along_x)


def norm_rows(values_in):
    factor = lax.rsqrt(jnp.mean(values_in * values_in, -1, keepdims=True) + norm_eps)
    return (values_in * factor, factor)


def norm_back(grad_in, normed, factor, gain_row):
    grad_normed = grad_in * gain_row
    inner = jnp.mean(grad_normed * normed, -1, keepdims=True)
    return (factor * (grad_normed - normed * inner), jnp.sum(grad_in * normed, 0))


def from_offset(v, axis, offset, size):
    return lax.ppermute(v, axis, [((i + offset) % size, i) for i in range(size)])


def other(v, axis):
    return from_offset(v, axis, 1, 2)


def pair_rows(v, axis):
    it = other(v, axis)
    flag = lax.axis_index(axis) == 0
    return jnp.concatenate([jnp.where(flag, v, it), jnp.where(flag, it, v)], 0)


def near_sum(own, core):
    return own.astype(F32) + other(core, "core").astype(F32)


def far_sum(chip, diagonal):
    return near_sum(chip, diagonal).astype(BF16)


def after(value, first):
    return lax.optimization_barrier((value, first))


def from_others(v, axis):
    return [v[0]] + [from_offset(v[i], axis, i, 4) for i in range(1, 4)]


def gather_rows(v):
    return lax.all_gather(pair_rows(v, "yh"), ("x", "z"), axis=0, tiled=True)


def scatter_rows(v):
    two = lax.psum_scatter(v, ("x", "z"), scatter_dimension=0, tiled=True)
    rows = two.shape[0] // 2
    iyh = lax.axis_index("yh")
    keep = lax.dynamic_slice_in_dim(two, iyh * rows, rows, 0)
    send = lax.dynamic_slice_in_dim(two, (1 - iyh) * rows, rows, 0)
    return keep.astype(F32) + other(send, "yh").astype(F32)


def body(tokens, norm_gains, w_query, w_keyval, w_out, w_gateup, w_down, cotangent):
    D = tokens.shape[1]
    length = 4 * tokens.shape[0]
    hidden_w = w_down.shape[0]
    heads_w = w_query.shape[1]
    gains_w = norm_gains.shape[1]
    block = lax.axis_index("yl") * 2 + lax.axis_index("core")
    row = (lax.axis_index("x") * 4 + lax.axis_index("z")) * 2 + lax.axis_index("yh")
    gains_at = (row * 4 + block) * gains_w
    place = jnp.stack(
        [block, lax.axis_index("x"), lax.axis_index("z"), lax.axis_index("yh")]
    ).astype(jnp.int32)

    attn_w = gather_rows(jnp.concatenate([w_query, w_keyval, w_out.T], 1))
    mlp_w = gather_rows(jnp.concatenate([w_gateup[:, 0], w_gateup[:, 1], w_down.T], 1))
    gain_rows = lax.dynamic_update_slice(jnp.zeros((2, D), F32), norm_gains, (0, gains_at))
    for axis in ("core", "yl", "yh"):
        gain_rows = gain_rows + other(gain_rows, axis)
    tokens, gain_rows = after(tokens, gain_rows)
    for axis in ("z", "x"):
        gain_rows = gain_rows + sum(from_offset(gain_rows, axis, i, 4) for i in (1, 3, 2))
    token_far = other(tokens, "yl")
    token_pieces = [tokens, other(tokens, "core"), token_far, other(token_far, "core")]
    cotangent, token_far = after(cotangent, token_far)
    grad_far = other(cotangent, "yl")
    grad_pieces = [cotangent, other(cotangent, "core"), grad_far, other(grad_far, "core")]
    token_pieces, grad_pieces = after(token_pieces, grad_pieces)

    positions = jnp.arange(length).astype(F32)
    freqs = rope_base ** (-(jnp.arange(HD // 2).astype(F32) * 2.0 / HD))
    angles = freqs[:, None] * positions[None, :]
    cosine, sine = jnp.cos(angles), jnp.sin(angles)

    lse, h_first, qt, q, kt, k, v, attn, attnt, *parts = attend(
        place, token_pieces, attn_w, gain_rows, cosine, sine
    )
    middle_far = far_sum(parts[2], parts[3])
    middle = (
        tokens.astype(F32) + near_sum(parts[0], parts[1]) + other(middle_far, "yl").astype(F32)
    )
    normed2, factor2 = norm_rows(middle)
    h_own = (normed2 * gain_rows[1]).astype(BF16)

    h_pieces = [h_own, other(h_own, "core")]
    h_far = other(h_own, "yl")
    hidden_a, dgu_a, back_own, back_core, out_own, out_core = feed(
        place, mlp_w, h_pieces, grad_pieces[:2]
    )
    h_far, hidden_a = after(h_far, hidden_a)
    h_pieces += [h_far, other(h_far, "core")]
    hidden_b, dgu_b, back_chip, back_diag, out_chip, out_diag = feed(
        place, mlp_w, h_pieces[2:], grad_pieces[2:]
    )
    back_near = near_sum(back_own, back_core)
    out_near = near_sum(out_own, out_core)

    back_far = far_sum(back_chip, back_diag)
    hidden_b, back_far = after(hidden_b, back_far)
    mlp_grads = feed_grads(place, h_pieces, grad_pieces, dgu_a, dgu_b, hidden_a, hidden_b)
    back_far = other(back_far, "yl").astype(F32)
    mlp_grads, back_far = after(mlp_grads, back_far)
    d_h2_own = back_near + back_far
    early = scatter_rows(mlp_grads)
    out_far = far_sum(out_chip, out_diag)

    d_norm2, gain_two = norm_back(d_h2_own, normed2, factor2, gain_rows[1])
    d_middle = cotangent.astype(F32) + d_norm2
    d_out = d_middle.astype(BF16)
    d_out_far = other(d_out, "yl")
    d_out_far, out_near = after(d_out_far, out_near)
    out_pieces = [d_out, other(d_out, "core"), d_out_far, other(d_out_far, "core")]
    out_far, out_pieces = after(out_far, out_pieces)
    out_far = other(out_far, "yl").astype(F32)

    back = attend_back(
        place, lse, cosine, sine, gain_two[None], out_pieces, token_pieces, attn_w,
        h_first, qt, q, kt, k, v, attn, attnt,
    )
    out_near, back = after(out_near, back)
    result = (middle + out_near + out_far).astype(BF16)
    parts, late_parts = back[:4], back[4:]
    late_parts, result = after(late_parts, result)
    d_far = far_sum(parts[2], parts[3])
    along_x, along_z = from_others(late_parts[:4], "x"), from_others(late_parts[4:], "z")
    along_x, d_far = after(along_x, d_far)
    middle_parts = late_middle(place, along_x, along_z)
    along_z, along_x = from_others(middle_parts[:4], "z"), from_others(middle_parts[4:], "x")
    late_keep, late_send = late_last(place, along_z, along_x)
    d_h1_own = near_sum(parts[0], parts[1]) + other(d_far, "yl").astype(F32)
    late_other, (d_h1_own, early) = after(other(late_send, "yh"), (d_h1_own, early))
    late = late_keep + late_other.astype(F32)

    normed1, factor1 = norm_rows(tokens.astype(F32))
    d_norm1, _ = norm_back(d_h1_own, normed1, factor1, gain_rows[0])
    input_grad = (d_middle + d_norm1).astype(BF16)

    out_at = heads_w + LATE_OUT
    grad_out = jnp.concatenate([late[:, heads_w:out_at], late[:, LATE_WIDTH : LATE_WIDTH + heads_w - LATE_OUT]], 1)
    gain_sum = late[:, out_at : out_at + 2].T
    for axis in ("core", "yl"):
        gain_sum = gain_sum + other(gain_sum, axis)
    grad_gains = lax.dynamic_slice(gain_sum, (0, block * gains_w), (2, gains_w))
    return (
        result,
        input_grad,
        late[:, :heads_w],
        late[:, 2 * LATE_WIDTH - heads_w :],
        grad_out.T,
        early[:, : 2 * hidden_w].reshape(-1, 2, hidden_w),
        early[:, 2 * hidden_w :].T,
        grad_gains,
    )


def solution(mesh):
    fine = Mesh(mesh.devices.reshape(4, 4, 2, 2, 2), ("x", "z", "yh", "yl", "core"))
    dp = ("x", "z", "yh")
    tensor = ("yl", "core")
    every = dp + tensor
    weights = (P(dp, tensor), P(dp, tensor), P(tensor, dp), P(dp, None, tensor), P(tensor, dp))
    rows = P(every, None)
    gains = P(None, every)
    return jax.shard_map(
        body,
        mesh=fine,
        in_specs=(rows, gains) + weights + (rows,),
        out_specs=(rows, rows) + weights + (gains,),
        check_vma=False,
    )
```

time: 436 us -> 366 us (0.84)
  waiting for transfers between devices: 184 us -> 139 us
  Pallas kernels: 115 us -> 93.6 us
    ppermute x49 -> x51, waiting for transfers between devices: 184 us -> 124 us  [from_offset(): lax.ppermute(v, axis, [((i + offset) % size, i) for i in range(size)])]
    pallas_call x9 -> x6, Pallas kernels: 113 us -> 91.5 us  [the longest x5 88.2 us: kernel_call(): pl.pallas_call(kernel, out_shape=list(small_outs) + list(outs), in_specs=...]
    all_gather x2, waiting for transfers between devices: 0.01 us -> 14.8 us  [gather_rows(): return lax.all_gather(pair_rows(v, 'yh'), ('x', 'z'), axis=0, tiled=True)]
    convert_element_type x5 -> x8, other arithmetic: 5.87 us -> 8.73 us  [the longest x4 3.02 us: far_sum(): return near_sum(chip, diagonal).astype(BF16)]
    unnamed x81 -> x111, local copies, waits for them, and re-layouts: 8.29 us -> 10.3 us
    ppermute x49 -> x51, starting transfers between devices: 76.4 us -> 74.5 us  [from_offset(): lax.ppermute(v, axis, [((i + offset) % size, i) for i in range(size)])]
  transfers between devices with their start and end apart: 52 -> 54, of which waited for: 25 -> 27; matrix products, arithmetic and copies ran while one was open for 6% -> 6% of each run, Pallas kernels for 20% -> 22%
where the time goes in v1:
time: 366 us; the launch traced here: 360 us
  waiting for transfers between devices  139 us (38%)
  Pallas kernels  93.6 us (26%)
  starting transfers between devices  74.6 us (20%)
  other arithmetic  22.9 us (6%)
  local copies, waits for them, and re-layouts  15.2 us (4%)
  between operations  14.7 us (4%)
    ppermute x51, waiting for transfers between devices, from_offset(): lax.ppermute(v, axis, [((i + offset) % size, i) for i in range(size)])  124 us
    pallas_call x5, Pallas kernels, kernel_call(): pl.pallas_call(kernel, out_shape=list(small_outs) + list(outs), in_specs=...  88.2 us
    ppermute x51, starting transfers between devices, from_offset(): lax.ppermute(v, axis, [((i + offset) % size, i) for i in range(size)])  74.5 us
    all_gather x2, waiting for transfers between devices, gather_rows(): return lax.all_gather(pair_rows(v, 'yh'), ('x', 'z'), axis=0, tiled=True)  14.8 us
    unnamed x111, local copies, waits for them, and re-layouts  10.3 us
  transfers between devices with their start and end apart: 54, of which 27 were waited for; matrix products, arithmetic and copies ran while one was open for 6% of the time, Pallas kernels for 22%

profile of v1, /device:TPU:1, one launch (start us, length us, event | category | flops | bytes accessed | tf_op | source)
XLA Modules:
  0.0 359.9 jit_solution(4270220944558983181)
XLA Ops:
  8.1 3.8 %collective-permute-start.15 = (bf16[48,1152]{1,0:T(8,128)(2,1)S(1)}, bf16[48,1152]{1,0:T(8,128)(2,1)S(1)}, u32[]{:S(2)}, u32[]{:S(2)}) collective-permute-start(bf16[48,1152]{1,0:T(8,128)(2,1)S(1)} %pad_maximum_fusion.3), channel_id=1, source_target_pairs={{4,0},{0,4},{5,1},{1,5},{6,2},{2,6},{7,3},{3,7},{12,8},{8,12},{13,... | collective-permute-start | bytes 331784 | tf_op jit(solution)/shard_map/ppermute | solution.py:508
  11.9 2.5 collective-permute-done.15
  16.5 3.0 collective-permute-start.20
  19.5 5.6 %collective-permute-done.20 = bf16[48,3072]{1,0:T(8,128)(2,1)S(1)} collective-permute-done((bf16[48,3072]{1,0:T(8,128)(2,1)S(1)}, bf16[48,3072]{1,0:T(8,128)(2,1)S(1)}, u32[]{:S(2)}, u32[]{:S(2)}) %collective-permute-start.20) | collective-permute-done | bytes 294944 | tf_op jit(solution)/shard_map/ppermute | solution.py:508
  26.5 2.4 collective-permute-start
  33.0 3.1 collective-permute-start.2
  38.6 15.9 %collective-permute-done.3.t2 = bf16[256,1536]{1,0:T(8,128)(2,1)S(1)} collective-permute-done((bf16[256,1536]{1,0:T(8,128)(2,1)}, bf16[256,1536]{1,0:T(8,128)(2,1)S(1)}, u32[]{:S(2)}, u32[]{:S(2)}) %collective-permute-start.3) | collective-permute-done | bytes 786464 | tf_op jit(solution)/shard_map/ppermute | solution.py:508
  55.7 3.8 %collective-permute-start.4 = (f32[2,1536]{1,0:T(2,128)S(1)}, f32[2,1536]{1,0:T(2,128)S(1)}, u32[]{:S(2)}, u32[]{:S(2)}) collective-permute-start(f32[2,1536]{1,0:T(2,128)S(1)} %add.137), channel_id=1, source_target_pairs={{8,0},{16,8},{24,16},{0,24},{9,1},{17,9},{25,17},{1,25},{10,2},{18... | collective-permute-start | bytes 36872 | tf_op jit(solution)/shard_map/ppermute | solution.py:508
  61.1 2.7 collective-permute-done.5
  65.6 5.6 %collective-permute-start.10 = (bf16[256,1536]{1,0:T(8,128)(2,1)}, bf16[256,1536]{1,0:T(8,128)(2,1)S(1)}, u32[]{:S(2)}, u32[]{:S(2)}) collective-permute-start(bf16[256,1536]{1,0:T(8,128)(2,1)} %t0.1), channel_id=1, source_target_pairs={{1,0},{0,1},{3,2},{2,3},{5,4},{4,5},{7,6},{6,7},{9,8},{8,9},{11,10... | collective-permute-start | bytes 2359304 | tf_op jit(solution)/shard_map/ppermute | solution.py:508
  75.2 3.6 %collective-permute-start.9 = (f32[2,1536]{1,0:T(2,128)S(1)}, f32[2,1536]{1,0:T(2,128)S(1)}, u32[]{:S(2)}, u32[]{:S(2)}) collective-permute-start(f32[2,1536]{1,0:T(2,128)S(1)} %add_add_fusion.2), channel_id=1, source_target_pairs={{64,0},{96,32},{0,64},{32,96},{65,1},{97,33},{1,65},{33,97},{66,2}... | collective-permute-start | bytes 36872 | tf_op jit(solution)/shard_map/ppermute | solution.py:508
  81.8 19.1 %attend.1 = (f32[4,1,1024]{2,1,0:T(1,128)S(1)}, bf16[1024,1536]{1,0:T(8,128)(2,1)}, bf16[4,96,1024]{2,1,0:T(8,128)(2,1)}, bf16[4,1024,96]{2,1,0:T(8,128)(2,1)}, ...) custom-call(s32[4]{0:T(128)S(1)} %pad_add_fusion.place, ...), custom_call_target="tpu_custom_call" | custom-call | flops 1 | bytes 1 | tf_op jit(solution)/shard_map/attend/pallas_call | solution.py:83
  107.2 18.1 %collective-permute-done.18 = bf16[256,1536]{1,0:T(8,128)(2,1)S(1)} collective-permute-done((bf16[256,1536]{1,0:T(8,128)(2,1)S(1)}, bf16[256,1536]{1,0:T(8,128)(2,1)S(1)}, u32[]{:S(2)}, u32[]{:S(2)}) %collective-permute-start.18) | collective-permute-done | bytes 786464 | tf_op jit(solution)/shard_map/ppermute | solution.py:508
  131.4 14.8 %all-gather.5.cloned.1.call-done.w_hbm = bf16[1536,3072]{1,0:T(8,128)(2,1)} async-done(((bf16[96,3072]{1,0:T(8,128)(2,1)}), bf16[1536,3072]{1,0:T(8,128)(2,1)}) %all-gather.5.cloned.1.call-update) | async-done | bytes 9437200 | tf_op jit(solution)/shard_map/all_gather | solution.py:538
  147.3 14.8 %feed.2 = (bf16[512,1024]{1,0:T(8,128)(2,1)S(1)}, bf16[512,2048]{1,0:T(8,128)(2,1)S(1)}, bf16[256,1536]{1,0:T(8,128)(2,1)S(1)}, bf16[256,1536]{1,0:T(8,128)(2,1)...) custom-call(s32[4]{0:T(128)S(1)} %pad_add_fusion.place, ...), custom_call_target="tpu_custom_call" | custom-call | flops 1 | bytes 1 | tf_op jit(solution)/shard_map/feed/pallas_call | solution.py:83
  168.6 15.0 %feed.3 = (bf16[512,1024]{1,0:T(8,128)(2,1)S(1)}, bf16[512,2048]{1,0:T(8,128)(2,1)S(1)}, bf16[256,1536]{1,0:T(8,128)(2,1)S(1)}, bf16[256,1536]{1,0:T(8,128)(2,1)...) custom-call(s32[4]{0:T(128)S(1)} %pad_add_fusion.place, ...), custom_call_target="tpu_custom_call" | custom-call | flops 1 | bytes 1 | tf_op jit(solution)/shard_map/feed/pallas_call | solution.py:83
  189.5 14.8 %feed_grads.1 = bf16[1536,3072]{1,0:T(8,128)(2,1)} custom-call(s32[4]{0:T(128)S(1)} %pad_add_fusion.place, bf16[256,1536]{1,0:T(8,128)(2,1)S(1)} %multiply_convert_fusion.h0, bf16[256,1536]{1,0:T(8,128)(2,1)S(1)} %copy-done.5, bf16[256,1536]{1,0:T(8,128)(2,1)} %collective-permute-done.22.h0.h2, bf16[256,1536]{1,0:T(8,128)(2,1)S(1)} %collective-permute-done.23.h1.h3, ...), custom_call_target="tpu_custom_call" | custom-call | flops 1 | bytes 1 | tf_op jit(solution)/shard_map/feed_grads/pallas_call | solution.py:83
  204.3 3.1 collective-permute-done.25
  207.4 2.5 convert_element_type.142
  214.1 2.7 multiply_reduce_fusion
  221.0 16.7 %collective-permute-done.26.o2 = bf16[256,1536]{1,0:T(8,128)(2,1)S(1)} collective-permute-done((bf16[256,1536]{1,0:T(8,128)(2,1)S(1)}, bf16[256,1536]{1,0:T(8,128)(2,1)S(1)}, u32[]{:S(2)}, u32[]{:S(2)}) %collective-permute-start.26) | collective-permute-done | bytes 786464 | tf_op jit(solution)/shard_map/ppermute | solution.py:508
  242.4 24.5 %attend_back.1 = (bf16[256,1536]{1,0:T(8,128)(2,1)}, bf16[256,1536]{1,0:T(8,128)(2,1)}, bf16[256,1536]{1,0:T(8,128)(2,1)}, bf16[256,1536]{1,0:T(8,128)(2,1)}, bf...) custom-call(s32[4]{0:T(128)} %copy-done.17, ...), custom_call_target="tpu_custom_call" | custom-call | flops 1 | bytes 1 | tf_op jit(solution)/shard_map/attend_back/pallas_call | solution.py:83
  268.9 2.4 collective-permute-start.32
  274.1 8.7 %collective-permute-done.32.refs_1_ = bf16[384,640]{1,0:T(8,128)(2,1)S(1)} collective-permute-done((bf16[384,640]{1,0:T(8,128)(2,1)S(1)}, bf16[384,640]{1,0:T(8,128)(2,1)S(1)}, u32[]{:S(2)}, u32[]{:S(2)}) %collective-permute-start.32) | collective-permute-done | bytes 491552 | tf_op jit(solution)/shard_map/ppermute | solution.py:508
  285.4 2.5 collective-permute-start.46
  288.0 18.1 %collective-permute-done.34.refs_3_ = bf16[384,640]{1,0:T(8,128)(2,1)} collective-permute-done((bf16[384,640]{1,0:T(8,128)(2,1)S(1)}, bf16[384,640]{1,0:T(8,128)(2,1)}, u32[]{:S(2)}, u32[]{:S(2)}) %collective-permute-start.34) | collective-permute-done | bytes 491552 | tf_op jit(solution)/shard_map/ppermute | solution.py:508
  307.4 3.3 late_middle.1
  317.1 2.8 collective-permute-start.43
  322.6 2.8 collective-permute-done.44.refs_7_
  331.9 7.4 %collective-permute-done.48 = bf16[48,3072]{1,0:T(8,128)(2,1)S(1)} collective-permute-done((bf16[48,3072]{1,0:T(8,128)(2,1)S(1)}, bf16[48,3072]{1,0:T(8,128)(2,1)S(1)}, u32[]{:S(2)}, u32[]{:S(2)}) %collective-permute-start.48) | collective-permute-done | bytes 294944 | tf_op jit(solution)/shard_map/ppermute | solution.py:508
  339.4 4.8 %collective-permute-start.49 = (f32[2,48]{0,1:T(8,128)S(1)}, f32[2,48]{0,1:T(8,128)S(1)}, u32[]{:S(2)}, u32[]{:S(2)}) collective-permute-start(f32[2,48]{0,1:T(8,128)S(1)} %slice_bitcast_fusion.1), channel_id=1, source_target_pairs={{1,0},{0,1},{3,2},{2,3},{5,4},{4,5},{7,6},{6,7},{9,8},{8,9},{11,10... | collective-permute-start | bytes 1160 | tf_op jit(solution)/shard_map/ppermute | solution.py:508
  346.5 2.5 fusion.6
  (250 shorter events, 92.0 us)
Async XLA Ops:
  7.2 74.6 %all-gather.3.cloned.1.call-start = ((), (), s32[]{:S(2)}) async-start(), calls=%async_computation.1 | async-start | bytes 3760128 | tf_op jit(solution)/shard_map/all_gather | solution.py:538
  16.0 130.2 %all-gather.5.cloned.1.call-start = ((), (), s32[]{:S(2)}) async-start(), calls=%async_computation.2 | async-start | bytes 10027008 | tf_op jit(solution)/shard_map/all_gather | solution.py:538
  16.5 8.6 %collective-permute-start.20 = (bf16[48,3072]{1,0:T(8,128)(2,1)S(1)}, bf16[48,3072]{1,0:T(8,128)(2,1)S(1)}, u32[]{:S(2)}, u32[]{:S(2)}) collective-permute-start(bf16[48,3072]{1,0:T(8,128)(2,1)S(1)} %pad_maximum_fusion.1), channel_id=1, source_target_pairs={{4,0},{0,4},{5,1},{1,5},{6,2},{2,6},{7,3},{3,7},{12,8},{8,12},{13,... | collective-permute-start | bytes 884744 | tf_op jit(solution)/shard_map/ppermute | solution.py:508
  26.1 303.6 %reduce-scatter.2.cloned.1.call-start = ((), (), s32[]{:S(2)}) async-start(), calls=%async_computation.3 | async-start | bytes 10027008 | tf_op jit(solution)/shard_map/reduce_scatter | solution.py:542
  37.2 17.3 %collective-permute-start.3 = (bf16[256,1536]{1,0:T(8,128)(2,1)}, bf16[256,1536]{1,0:T(8,128)(2,1)S(1)}, u32[]{:S(2)}, u32[]{:S(2)}) collective-permute-start(bf16[256,1536]{1,0:T(8,128)(2,1)} %t0.1), channel_id=1, source_target_pairs={{2,0},{0,2},{3,1},{1,3},{6,4},{4,6},{7,5},{5,7},{10,8},{8,10},{11,... | collective-permute-start | bytes 2359304 | tf_op jit(solution)/shard_map/ppermute | solution.py:508
  54.5 18.1 %collective-permute-start.13 = (bf16[256,1536]{1,0:T(8,128)(2,1)S(1)}, bf16[256,1536]{1,0:T(8,128)(2,1)S(1)}, u32[]{:S(2)}, u32[]{:S(2)}) collective-permute-start(bf16[256,1536]{1,0:T(8,128)(2,1)S(1)} %copy-done), channel_id=1, source_target_pairs={{2,0},{0,2},{3,1},{1,3},{6,4},{4,6},{7,5},{5,7},{10,8},{8,10},{11,... | collective-permute-start | bytes 2359304 | tf_op jit(solution)/shard_map/ppermute | solution.py:508
  63.9 7.5 %collective-permute-start.7 = (f32[2,1536]{1,0:T(2,128)S(1)}, f32[2,1536]{1,0:T(2,128)S(1)}, u32[]{:S(2)}, u32[]{:S(2)}) collective-permute-start(f32[2,1536]{1,0:T(2,128)S(1)} %add_add_fusion.2), channel_id=1, source_target_pairs={{32,0},{64,32},{96,64},{0,96},{33,1},{65,33},{97,65},{1,97},{34,2}... | collective-permute-start | bytes 36872 | tf_op jit(solution)/shard_map/ppermute | solution.py:508
  65.6 14.3 %collective-permute-start.10 = (bf16[256,1536]{1,0:T(8,128)(2,1)}, bf16[256,1536]{1,0:T(8,128)(2,1)S(1)}, u32[]{:S(2)}, u32[]{:S(2)}) collective-permute-start(bf16[256,1536]{1,0:T(8,128)(2,1)} %t0.1), channel_id=1, source_target_pairs={{1,0},{0,1},{3,2},{2,3},{5,4},{4,5},{7,6},{6,7},{9,8},{8,9},{11,10... | collective-permute-start | bytes 2359304 | tf_op jit(solution)/shard_map/ppermute | solution.py:508
  71.2 8.8 %collective-permute-start.12 = (bf16[256,1536]{1,0:T(8,128)(2,1)S(1)}, bf16[256,1536]{1,0:T(8,128)(2,1)S(1)}, u32[]{:S(2)}, u32[]{:S(2)}) collective-permute-start(bf16[256,1536]{1,0:T(8,128)(2,1)S(1)} %copy-done), channel_id=1, source_target_pairs={{1,0},{0,1},{3,2},{2,3},{5,4},{4,5},{7,6},{6,7},{9,8},{8,9},{11,10... | collective-permute-start | bytes 2359304 | tf_op jit(solution)/shard_map/ppermute | solution.py:508
  71.4 8.6 %collective-permute-start.11 = (bf16[256,1536]{1,0:T(8,128)(2,1)S(1)}, bf16[256,1536]{1,0:T(8,128)(2,1)S(1)}, u32[]{:S(2)}, u32[]{:S(2)}) collective-permute-start(bf16[256,1536]{1,0:T(8,128)(2,1)S(1)} %collective-permute-done.3.t2), channel_id=1, source_target_pairs={{1,0},{0,1},{3,2},{2,3},{5,4},{4,5},{7,6},{6,7},{9,8},{8,9},{11,10... | collective-permute-start | bytes 2359304 | tf_op jit(solution)/shard_map/ppermute | solution.py:508
  72.6 9.1 %collective-permute-start.14 = (bf16[256,1536]{1,0:T(8,128)(2,1)S(1)}, bf16[256,1536]{1,0:T(8,128)(2,1)S(1)}, u32[]{:S(2)}, u32[]{:S(2)}) collective-permute-start(bf16[256,1536]{1,0:T(8,128)(2,1)S(1)} %collective-permute-done.13.g0.g2), channel_id=1, source_target_pairs={{1,0},{0,1},{3,2},{2,3},{5,4},{4,5},{7,6},{6,7},{9,8},{8,9},{11,10... | collective-permute-start | bytes 2359304 | tf_op jit(solution)/shard_map/ppermute | solution.py:508
  106.4 18.9 %collective-permute-start.18 = (bf16[256,1536]{1,0:T(8,128)(2,1)S(1)}, bf16[256,1536]{1,0:T(8,128)(2,1)S(1)}, u32[]{:S(2)}, u32[]{:S(2)}) collective-permute-start(bf16[256,1536]{1,0:T(8,128)(2,1)S(1)} %add_convert_fusion.4), channel_id=1, source_target_pairs={{2,0},{0,2},{3,1},{1,3},{6,4},{4,6},{7,5},{5,7},{10,8},{8,10},{11,... | collective-permute-start | bytes 2359304 | tf_op jit(solution)/shard_map/ppermute | solution.py:508
  128.6 37.1 %collective-permute-start.22 = (bf16[256,1536]{1,0:T(8,128)(2,1)S(1)}, bf16[256,1536]{1,0:T(8,128)(2,1)}, u32[]{:S(2)}, u32[]{:S(2)}) collective-permute-start(bf16[256,1536]{1,0:T(8,128)(2,1)S(1)} %multiply_convert_fusion.h0), channel_id=1, source_target_pairs={{2,0},{0,2},{3,1},{1,3},{6,4},{4,6},{7,5},{5,7},{10,8},{8,10},{11,... | collective-permute-start | bytes 2359304 | tf_op jit(solution)/shard_map/ppermute | solution.py:508
  188.0 19.5 %collective-permute-start.25 = (bf16[256,1536]{1,0:T(8,128)(2,1)}, bf16[256,1536]{1,0:T(8,128)(2,1)}, u32[]{:S(2)}, u32[]{:S(2)}) collective-permute-start(bf16[256,1536]{1,0:T(8,128)(2,1)} %add_convert_fusion.3), channel_id=1, source_target_pairs={{2,0},{0,2},{3,1},{1,3},{6,4},{4,6},{7,5},{5,7},{10,8},{8,10},{11,... | collective-permute-start | bytes 2359304 | tf_op jit(solution)/shard_map/ppermute | solution.py:508
  212.2 8.4 %collective-permute-start.27 = (bf16[256,1536]{1,0:T(8,128)(2,1)S(1)}, bf16[256,1536]{1,0:T(8,128)(2,1)S(1)}, u32[]{:S(2)}, u32[]{:S(2)}) collective-permute-start(bf16[256,1536]{1,0:T(8,128)(2,1)S(1)} %copy-done.22), channel_id=1, source_target_pairs={{1,0},{0,1},{3,2},{2,3},{5,4},{4,5},{7,6},{6,7},{9,8},{8,9},{11,10... | collective-permute-start | bytes 2359304 | tf_op jit(solution)/shard_map/ppermute | solution.py:508
  218.8 18.9 %collective-permute-start.26 = (bf16[256,1536]{1,0:T(8,128)(2,1)S(1)}, bf16[256,1536]{1,0:T(8,128)(2,1)S(1)}, u32[]{:S(2)}, u32[]{:S(2)}) collective-permute-start(bf16[256,1536]{1,0:T(8,128)(2,1)S(1)} %get-tuple-element.144.o0), channel_id=1, source_target_pairs={{2,0},{0,2},{3,1},{1,3},{6,4},{4,6},{7,5},{5,7},{10,8},{8,10},{11,... | collective-permute-start | bytes 2359304 | tf_op jit(solution)/shard_map/ppermute | solution.py:508
  220.0 18.8 %collective-permute-start.28 = (bf16[256,1536]{1,0:T(8,128)(2,1)S(1)}, bf16[256,1536]{1,0:T(8,128)(2,1)S(1)}, u32[]{:S(2)}, u32[]{:S(2)}) collective-permute-start(bf16[256,1536]{1,0:T(8,128)(2,1)S(1)} %copy-done.20), channel_id=1, source_target_pairs={{1,0},{0,1},{3,2},{2,3},{5,4},{4,5},{7,6},{6,7},{9,8},{8,9},{11,10... | collective-permute-start | bytes 2359304 | tf_op jit(solution)/shard_map/ppermute | solution.py:508
  220.9 18.1 %collective-permute-start.29 = (bf16[256,1536]{1,0:T(8,128)(2,1)S(1)}, bf16[256,1536]{1,0:T(8,128)(2,1)S(1)}, u32[]{:S(2)}, u32[]{:S(2)}) collective-permute-start(bf16[256,1536]{1,0:T(8,128)(2,1)S(1)} %get-tuple-element.144.o0), channel_id=1, source_target_pairs={{1,0},{0,1},{3,2},{2,3},{5,4},{4,5},{7,6},{6,7},{9,8},{8,9},{11,10... | collective-permute-start | bytes 2359304 | tf_op jit(solution)/shard_map/ppermute | solution.py:508
  240.6 27.0 %collective-permute-start.31 = (bf16[256,1536]{1,0:T(8,128)(2,1)S(1)}, bf16[256,1536]{1,0:T(8,128)(2,1)S(1)}, u32[]{:S(2)}, u32[]{:S(2)}) collective-permute-start(bf16[256,1536]{1,0:T(8,128)(2,1)S(1)} %add_convert_fusion.2), channel_id=1, source_target_pairs={{2,0},{0,2},{3,1},{1,3},{6,4},{4,6},{7,5},{5,7},{10,8},{8,10},{11,... | collective-permute-start | bytes 2359304 | tf_op jit(solution)/shard_map/ppermute | solution.py:508
  268.9 13.9 %collective-permute-start.32 = (bf16[384,640]{1,0:T(8,128)(2,1)S(1)}, bf16[384,640]{1,0:T(8,128)(2,1)S(1)}, u32[]{:S(2)}, u32[]{:S(2)}) collective-permute-start(bf16[384,640]{1,0:T(8,128)(2,1)S(1)} %copy-done.54), channel_id=1, source_target_pairs={{32,0},{64,32},{96,64},{0,96},{33,1},{65,33},{97,65},{1,97},{34,2}... | collective-permute-start | bytes 1474568 | tf_op jit(solution)/shard_map/ppermute | solution.py:508
  271.3 14.2 %collective-permute-start.33 = (bf16[384,640]{1,0:T(8,128)(2,1)S(1)}, bf16[384,640]{1,0:T(8,128)(2,1)S(1)}, u32[]{:S(2)}, u32[]{:S(2)}) collective-permute-start(bf16[384,640]{1,0:T(8,128)(2,1)S(1)} %copy-done.53), channel_id=1, source_target_pairs={{64,0},{96,32},{0,64},{32,96},{65,1},{97,33},{1,65},{33,97},{66,2}... | collective-permute-start | bytes 1474568 | tf_op jit(solution)/shard_map/ppermute | solution.py:508
  271.8 34.2 %collective-permute-start.34 = (bf16[384,640]{1,0:T(8,128)(2,1)S(1)}, bf16[384,640]{1,0:T(8,128)(2,1)}, u32[]{:S(2)}, u32[]{:S(2)}) collective-permute-start(bf16[384,640]{1,0:T(8,128)(2,1)S(1)} %copy-done.52), channel_id=1, source_target_pairs={{96,0},{0,32},{32,64},{64,96},{97,1},{1,33},{33,65},{65,97},{98,2}... | collective-permute-start | bytes 1474568 | tf_op jit(solution)/shard_map/ppermute | solution.py:508
  272.4 33.9 %collective-permute-start.36 = (bf16[4,96,640]{2,1,0:T(8,128)(2,1)S(1)}, bf16[4,96,640]{2,1,0:T(8,128)(2,1)}, u32[]{:S(2)}, u32[]{:S(2)}) collective-permute-start(bf16[4,96,640]{2,1,0:T(8,128)(2,1)S(1)} %copy-done.51), channel_id=1, source_target_pairs={{8,0},{16,8},{24,16},{0,24},{9,1},{17,9},{25,17},{1,25},{10,2},{18... | collective-permute-start | bytes 1474568 | tf_op jit(solution)/shard_map/ppermute | solution.py:508
  273.3 33.0 %collective-permute-start.37 = (bf16[4,96,640]{2,1,0:T(8,128)(2,1)S(1)}, bf16[4,96,640]{2,1,0:T(8,128)(2,1)}, u32[]{:S(2)}, u32[]{:S(2)}) collective-permute-start(bf16[4,96,640]{2,1,0:T(8,128)(2,1)S(1)} %copy-done.50), channel_id=1, source_target_pairs={{16,0},{24,8},{0,16},{8,24},{17,1},{25,9},{1,17},{9,25},{18,2},{26... | collective-permute-start | bytes 1474568 | tf_op jit(solution)/shard_map/ppermute | solution.py:508
  282.8 24.6 %collective-permute-start.38 = (bf16[4,96,640]{2,1,0:T(8,128)(2,1)S(1)}, bf16[4,96,640]{2,1,0:T(8,128)(2,1)}, u32[]{:S(2)}, u32[]{:S(2)}) collective-permute-start(bf16[4,96,640]{2,1,0:T(8,128)(2,1)S(1)} %copy-done.49), channel_id=1, source_target_pairs={{24,0},{0,8},{8,16},{16,24},{25,1},{1,9},{9,17},{17,25},{26,2},{2,... | collective-permute-start | bytes 1474568 | tf_op jit(solution)/shard_map/ppermute | solution.py:508
  285.4 46.1 %collective-permute-start.46 = (bf16[256,1536]{1,0:T(8,128)(2,1)}, bf16[256,1536]{1,0:T(8,128)(2,1)S(1)}, u32[]{:S(2)}, u32[]{:S(2)}) collective-permute-start(bf16[256,1536]{1,0:T(8,128)(2,1)} %get-tuple-element.203), channel_id=1, source_target_pairs={{1,0},{0,1},{3,2},{2,3},{5,4},{4,5},{7,6},{6,7},{9,8},{8,9},{11,10... | collective-permute-start | bytes 2359304 | tf_op jit(solution)/shard_map/ppermute | solution.py:508
  306.1 25.5 %collective-permute-start.47 = (bf16[256,1536]{1,0:T(8,128)(2,1)S(1)}, bf16[256,1536]{1,0:T(8,128)(2,1)S(1)}, u32[]{:S(2)}, u32[]{:S(2)}) collective-permute-start(bf16[256,1536]{1,0:T(8,128)(2,1)S(1)} %add_convert_fusion), channel_id=1, source_target_pairs={{2,0},{0,2},{3,1},{1,3},{6,4},{4,6},{7,5},{5,7},{10,8},{8,10},{11,... | collective-permute-start | bytes 2359304 | tf_op jit(solution)/shard_map/ppermute | solution.py:508
  312.0 7.9 %collective-permute-start.41 = (bf16[96,640]{1,0:T(8,128)(2,1)}, bf16[96,640]{1,0:T(8,128)(2,1)S(1)}, u32[]{:S(2)}, u32[]{:S(2)}) collective-permute-start(bf16[96,640]{1,0:T(8,128)(2,1)} %get-tuple-element.196), channel_id=1, source_target_pairs={{24,0},{0,8},{8,16},{16,24},{25,1},{1,9},{9,17},{17,25},{26,2},{2,... | collective-permute-start | bytes 368648 | tf_op jit(solution)/shard_map/ppermute | solution.py:508
  315.0 6.4 %collective-permute-start.42 = (bf16[96,640]{1,0:T(8,128)(2,1)}, bf16[96,640]{1,0:T(8,128)(2,1)}, u32[]{:S(2)}, u32[]{:S(2)}) collective-permute-start(bf16[96,640]{1,0:T(8,128)(2,1)} %get-tuple-element.198), channel_id=1, source_target_pairs={{32,0},{64,32},{96,64},{0,96},{33,1},{65,33},{97,65},{1,97},{34,2}... | collective-permute-start | bytes 368648 | tf_op jit(solution)/shard_map/ppermute | solution.py:508
  327.5 11.8 %collective-permute-start.45 = (bf16[48,1280]{1,0:T(8,128)(2,1)}, bf16[48,1280]{1,0:T(8,128)(2,1)S(1)}, u32[]{:S(2)}, u32[]{:S(2)}) collective-permute-start(bf16[48,1280]{1,0:T(8,128)(2,1)} %get-tuple-element.201), channel_id=1, source_target_pairs={{4,0},{0,4},{5,1},{1,5},{6,2},{2,6},{7,3},{3,7},{12,8},{8,12},{13,... | collective-permute-start | bytes 368648 | tf_op jit(solution)/shard_map/ppermute | solution.py:508
  330.7 8.6 %collective-permute-start.48 = (bf16[48,3072]{1,0:T(8,128)(2,1)S(1)}, bf16[48,3072]{1,0:T(8,128)(2,1)S(1)}, u32[]{:S(2)}, u32[]{:S(2)}) collective-permute-start(bf16[48,3072]{1,0:T(8,128)(2,1)S(1)} %constant_dynamic-slice_fusion), channel_id=1, source_target_pairs={{4,0},{0,4},{5,1},{1,5},{6,2},{2,6},{7,3},{3,7},{12,8},{8,12},{13,... | collective-permute-start | bytes 884744 | tf_op jit(solution)/shard_map/ppermute | solution.py:508
  339.4 10.2 %collective-permute-start.49 = (f32[2,48]{0,1:T(8,128)S(1)}, f32[2,48]{0,1:T(8,128)S(1)}, u32[]{:S(2)}, u32[]{:S(2)}) collective-permute-start(f32[2,48]{0,1:T(8,128)S(1)} %slice_bitcast_fusion.1), channel_id=1, source_target_pairs={{1,0},{0,1},{3,2},{2,3},{5,4},{4,5},{7,6},{6,7},{9,8},{8,9},{11,10... | collective-permute-start | bytes 1160 | tf_op jit(solution)/shard_map/ppermute | solution.py:508
  (77 other events, 755.1 us)
Sparse Core Ops, SparseCore 0:
  16.2 52.5 all-gather.2
  70.9 75.2 all-gather.4
  210.0 97.1 reduce-scatter.1

commit v2 on v1

--- a/solution.py
+++ b/solution.py
@@ -15,7 +15,10 @@
 MIB = 1024 * 1024
 SMALL = pl.CostEstimate(flops=1, bytes_accessed=1, transcendentals=0)
 
-QUERY_AT, KEYVAL_AT, OUT_AT, ATTN_WIDTH = 0, 384, 768, 1152
+GAIN_AT, OUT_AT, QUERY_AT, KEYVAL_AT, REST_AT, ATTN_WIDTH = 0, 128, 256, 640, 1024, 1280
+HALF_WIDTH = ATTN_WIDTH // 2
+OUT_CUT = QUERY_AT - OUT_AT
+LIMIT = 60
 
 
 def dot_n(left, right):
@@ -79,52 +82,65 @@
     return pl.BlockSpec(memory_space=pltpu.SMEM)
 
 
-def kernel_call(kernel, name, place, small, large, outs, small_outs, scratch, fetches, stores, limit):
+def kernel_call(kernel, name, place, small, large, outs, small_outs, scratch, *copies):
     return pl.pallas_call(
         kernel,
         out_shape=list(small_outs) + list(outs),
         in_specs=[scalars()] + [whole()] * len(small) + [apart()] * len(large),
         out_specs=[whole()] * len(small_outs) + [apart()] * len(outs),
         scratch_shapes=list(scratch)
-        + [pltpu.SemaphoreType.DMA((fetches,)), pltpu.SemaphoreType.DMA((stores,))],
-        compiler_params=pltpu.CompilerParams(vmem_limit_bytes=limit * MIB),
+        + [pltpu.SemaphoreType.DMA((count,)) for count in copies],
+        compiler_params=pltpu.CompilerParams(vmem_limit_bytes=LIMIT * MIB),
         cost_estimate=SMALL,
         name=name,
     )(place, *small, *large)
 
 
-def attend_kernel(place, gains_ref, cos_ref, sin_ref, t0, t1, t2, t3, w_hbm,
-                  lse_ref, h_hbm, qt_hbm, q_hbm, kt_hbm, k_hbm, v_hbm, attn_hbm, attnt_hbm,
+def probs_at(step, size):
+    return step * (step + 1) // 2 * size, (step + 1) * size
+
+
+def attend_kernel(place, cos_ref, sin_ref, t0, t1, t2, t3, a0, a1, a2, a3, b0, b1, b2, b3,
+                  gains_ref, w_hbm, h_hbm, q_hbm, kt_hbm, v_hbm, attn_hbm, attnt_hbm, probs_hbm,
                   o0, o1, o2, o3,
                   t_ref, w_ref, h_ref, qt_ref, q_ref, kt_ref, k_ref, vt_ref, v_ref,
-                  natural, attn_ref, attnt_ref, part_ref, in_sem, out_sem):
-    block = place[0]
+                  natural, attn_ref, attnt_ref, probs_ref, part_ref, in_sem, out_sem, probs_sem):
+    block, ix, iz = place[0], place[1], place[2]
     half = HD // 2
     size = t_ref.shape[1]
     heads, _, length = qt_ref.shape
     group_size = heads // k_ref.shape[0]
+    rows = a0.shape[1]
     fetch, store = Moves(in_sem), Moves(out_sem)
-    pieces = (t0, t1, t2, t3)
-    came = [fetch.start(pieces[0], t_ref.at[0])]
-    proj = pl.ds(0, OUT_AT)
-    w_came = fetch.start(w_hbm.at[:, proj], w_ref.at[:, proj])
-    came += [fetch.start(pieces[i], t_ref.at[i]) for i in range(1, 4)]
-    last = pl.ds(OUT_AT, ATTN_WIDTH - OUT_AT)
-    o_came = fetch.start(w_hbm.at[:, last], w_ref.at[:, last])
-    gain_row = gains_ref[0:1, :]
+    came = []
+    for far, (along_x, along_z) in enumerate(zip((a0, a1, a2, a3), (b0, b1, b2, b3))):
+        for near in range(4):
+            at_a = lax.rem(ix + far, 4) * 4 + lax.rem(iz + near, 4)
+            at_b = lax.rem(ix + near, 4) * 4 + lax.rem(iz + far, 4)
+            came.append(fetch.start(
+                along_x.at[near], w_ref.at[block_at(at_a, rows), pl.ds(0, HALF_WIDTH)]))
+            came.append(fetch.start(
+                along_z.at[near], w_ref.at[block_at(at_b, rows), pl.ds(HALF_WIDTH, HALF_WIDTH)]))
+    tokens_came = [
+        fetch.start(piece, t_ref.at[i]) for i, piece in enumerate((t0, t1, t2, t3))
+    ]
+    for copy in came:
+        copy.wait()
+    store.start(w_ref, w_hbm)
+    gains = w_ref[:, GAIN_AT:OUT_AT].astype(F32).T
+    gain_row = gains[0:1] + gains[2:3]
+    gains_ref[...] = gains[0:2] + gains[2:4]
     for step in range(4):
         at = block_at(lax.bitwise_xor(block, step), size)
-        came[step].wait()
+        tokens_came[step].wait()
         value = t_ref[step].astype(F32)
         factor = lax.rsqrt(jnp.mean(value * value, -1, keepdims=True) + norm_eps)
         normed = (value * factor * gain_row).astype(BF16)
         h_ref[at, :] = normed
         cosine = cos_ref[:, at]
         sine = sin_ref[:, at]
-        if step == 0:
-            w_came.wait()
-        every = dot_n(normed, w_ref[:, :OUT_AT]).T
-        query, keyval = every[:KEYVAL_AT], every[KEYVAL_AT:]
+        every = dot_n(normed, w_ref[:, QUERY_AT:REST_AT]).T
+        query, keyval = every[: KEYVAL_AT - QUERY_AT], every[KEYVAL_AT - QUERY_AT :]
 
         def rotated(field):
             first, second = field[:half], field[half:]
@@ -143,95 +159,105 @@
             k_ref[head, at, :] = turned.T.astype(BF16)
             vt_ref[head, :, at] = value_t.astype(BF16)
             v_ref[head, at, :] = value_t.T.astype(BF16)
-    for source, target in ((h_ref, h_hbm), (qt_ref, qt_hbm), (q_ref, q_hbm), (kt_ref, kt_hbm),
-                           (k_ref, k_hbm), (v_ref, v_hbm)):
+    for source, target in ((h_ref, h_hbm), (q_ref, q_hbm), (kt_ref, kt_hbm), (v_ref, v_hbm)):
         store.start(source, target)
+
+    def probs_copy(head):
+        return pltpu.make_async_copy(probs_ref.at[head], probs_hbm.at[head], probs_sem.at[head])
 
     def one_head(head, carry):
         group = head // group_size
         for step in range(4):
-            reach = (step + 1) * size
+            first, reach = probs_at(step, size)
             columns = slice(step * size, reach)
             scores = causal_mask(dot_n(k_ref[group, :reach, :], qt_ref[head, :, columns]), size)
             top = jnp.max(scores, 0, keepdims=True)
             expo = jnp.exp2((scores - top) * (SCALE * LOG2E))
             total = jnp.sum(expo, 0, keepdims=True)
             probs = (expo * (1.0 / total)).astype(BF16)
+            probs_ref[head, first : first + reach, :] = probs
             mixed = dot_n(vt_ref[group, :, :reach], probs)
             attnt_ref[head, :, columns] = mixed.astype(BF16)
-            lse_ref[head, :, columns] = top * (SCALE * LOG2E) + jnp.log2(total)
+        probs_copy(head).start()
         return carry
 
     lax.fori_loop(0, heads, one_head, 0)
     store.start(attnt_ref, attnt_hbm)
     natural[...] = attnt_ref[...].reshape(heads * HD, length).T
-    o_came.wait()
     for step, out in ((1, o1), (3, o3), (2, o2), (0, o0)):
         at = block_at(lax.bitwise_xor(block, step), size)
-        rows = natural[at, :]
-        attn_ref[step * size : (step + 1) * size, :] = rows
-        part_ref[step] = dot_t(rows, w_ref[:, OUT_AT:ATTN_WIDTH]).astype(BF16)
+        attn = natural[at, :]
+        attn_ref[step * size : (step + 1) * size, :] = attn
+        part = dot_t(attn[:, :OUT_CUT], w_ref[:, OUT_AT:QUERY_AT])
+        part += dot_t(attn[:, OUT_CUT:], w_ref[:, REST_AT:])
+        part_ref[step] = part.astype(BF16)
         store.start(part_ref.at[step], out)
     store.start(attn_ref, attn_hbm)
     store.wait()
-
-
-def attend(place, pieces, weights, gain_rows, cosine, sine):
-    size, width = pieces[0].shape
-    length = 4 * size
+    for head in range(heads):
+        probs_copy(head).wait()
+
+
+def attend(place, pieces, along_x, along_z, cosine, sine):
+    width = pieces[0].shape[1]
+    length = cosine.shape[1]
+    size = length // 4
     heads = (KEYVAL_AT - QUERY_AT) // HD
-    groups = (OUT_AT - KEYVAL_AT) // (2 * HD)
+    groups = (REST_AT - KEYVAL_AT) // (2 * HD)
     columns, rows = (heads, HD, length), (heads, length, HD)
     g_columns, g_rows = (groups, HD, length), (groups, length, HD)
-    outs = [(length, width), columns, rows, g_columns, g_rows, g_rows,
-            (length, heads * HD), columns] + [(size, width)] * 4
+    probs = (heads, sum(probs_at(3, size)), size)
+    outs = [(width, ATTN_WIDTH), (length, width), rows, g_columns, g_rows,
+            (length, heads * HD), columns, probs] + [(size, width)] * 4
     scratch = [(4, size, width), (width, ATTN_WIDTH), (length, width), columns, rows,
                g_columns, g_rows, g_columns, g_rows,
-               (length, heads * HD), (length, heads * HD), columns, (4, size, width)]
+               (length, heads * HD), (length, heads * HD), columns, probs, (4, size, width)]
     return kernel_call(
-        attend_kernel, "attend", place, (gain_rows, cosine, sine), (*pieces, weights),
-        [like(s) for s in outs], [like((heads, 1, length), F32)], [vmem(s) for s in scratch],
-        6, 12, 52)
-
-
-def attend_back_kernel(place, lse_ref, cos_ref, sin_ref, gain2_ref,
-                       o0, o1, o2, o3, t0, t1, t2, t3, w_hbm, h_hbm, qt_hbm, q_hbm, kt_hbm,
-                       k_hbm, v_hbm, attn_hbm, attnt_hbm,
+        attend_kernel, "attend", place, (cosine, sine), (*pieces, *along_x, *along_z),
+        [like(s) for s in outs], [like((2, width), F32)], [vmem(s) for s in scratch],
+        36, 11, heads)
+
+
+def attend_back_kernel(place, cos_ref, sin_ref, gain2_ref,
+                       o0, o1, o2, o3, t0, t1, t2, t3, w_hbm, h_hbm, q_hbm, kt_hbm,
+                       v_hbm, attn_hbm, attnt_hbm, probs_hbm,
                        c0, c1, c2, c3, x0, x1, x2, x3, y0, y1, y2, y3,
-                       o_ref, t_ref, w_ref, h_ref, qt_ref, q_ref, kt_ref, k_ref, v_ref,
-                       attn_ref, attnt_ref,
+                       o_ref, t_ref, w_ref, h_ref, q_ref, kt_ref, v_ref,
+                       attn_ref, attnt_ref, probs_ref,
                        do_ref, dot_ref, dqkv_ref, part_ref, first_ref, second_ref,
-                       delta_ref, dk_ref, dv_ref, turned_ref, in_sem, out_sem):
+                       delta_ref, dk_ref, dv_ref, turned_ref, in_sem, out_sem, probs_sem):
     block, ix, iz = place[0], place[1], place[2]
-    heads, _, length = qt_ref.shape
-    groups = k_ref.shape[0]
+    heads, length, _ = q_ref.shape
+    groups = v_ref.shape[0]
     group_size = heads // groups
     size = length // 4
     half = HD // 2
     width = w_ref.shape[0]
     heads_w = heads * HD
     fetch, store = Moves(in_sem), Moves(out_sem)
-    last = pl.ds(OUT_AT, ATTN_WIDTH - OUT_AT)
-    early = [fetch.start(w_hbm.at[:, last], w_ref.at[:, last])]
+    early = [fetch.start(w_hbm, w_ref)]
     early += [
         fetch.start(piece, o_ref.at[pl.ds(i * size, size), :])
         for i, piece in enumerate((o0, o1, o2, o3))
     ]
-    for source, target in ((attnt_hbm, attnt_ref), (qt_hbm, qt_ref), (q_hbm, q_ref),
-                           (kt_hbm, kt_ref), (k_hbm, k_ref), (v_hbm, v_ref)):
+    for source, target in ((attnt_hbm, attnt_ref), (v_hbm, v_ref), (q_hbm, q_ref),
+                           (kt_hbm, kt_ref)):
         early.append(fetch.start(source, target))
-    proj = pl.ds(0, OUT_AT)
-    later = [
-        fetch.start(attn_hbm, attn_ref),
-        fetch.start(h_hbm, h_ref),
-        fetch.start(w_hbm.at[:, proj], w_ref.at[:, proj]),
-    ]
+
+    def probs_copy(head):
+        return pltpu.make_async_copy(probs_hbm.at[head], probs_ref.at[head], probs_sem.at[head])
+
+    for head in range(heads):
+        probs_copy(head).start()
+    later = [fetch.start(attn_hbm, attn_ref), fetch.start(h_hbm, h_ref)]
     later += [fetch.start(piece, t_ref.at[i]) for i, piece in enumerate((t0, t1, t2, t3))]
     early[0].wait()
     for step in range(4):
         at = block_at(lax.bitwise_xor(block, step), size)
         early[1 + step].wait()
-        grad = dot_n(o_ref[step * size : (step + 1) * size, :], w_ref[:, OUT_AT:ATTN_WIDTH])
+        grad_in = o_ref[step * size : (step + 1) * size, :]
+        grad = jnp.concatenate(
+            [dot_n(grad_in, w_ref[:, OUT_AT:QUERY_AT]), dot_n(grad_in, w_ref[:, REST_AT:])], 1)
         grad_t = grad.T.astype(BF16)
         grad = grad.astype(BF16)
         for head in range(heads):
@@ -251,14 +277,14 @@
 
     def one_head(head, carry):
         group = head // group_size
+        probs_copy(head).wait()
         for step in range(4):
-            reach = (step + 1) * size
+            first, reach = probs_at(step, size)
             columns = slice(step * size, reach)
-            scores = causal_mask(dot_n(k_ref[group, :reach, :], qt_ref[head, :, columns]), size)
-            soft = jnp.exp2(scores * (SCALE * LOG2E) - lse_ref[head, :, columns])
+            probs = probs_ref[head, first : first + reach, :]
             d_probs = dot_n(v_ref[group, :reach, :], dot_ref[head, :, columns])
-            d_scores = (soft * (d_probs - delta_ref[head, :, columns])).astype(BF16)
-            dv_ref[group, :reach, :] += dot_n(soft.astype(BF16), do_ref[head, columns, :])
+            d_scores = (probs.astype(F32) * (d_probs - delta_ref[head, :, columns])).astype(BF16)
+            dv_ref[group, :reach, :] += dot_n(probs, do_ref[head, columns, :])
             dk_ref[group, :reach, :] += dot_n(d_scores, q_ref[head, columns, :])
             d_query = dot_n(kt_ref[group, :, :reach], d_scores) * SCALE
             turned_ref[head, :, columns] = turned_back(
@@ -277,7 +303,7 @@
     gain = jnp.zeros((1, width), F32)
     for step, out in ((1, c1), (3, c3), (2, c2), (0, c0)):
         at = block_at(lax.bitwise_xor(block, step), size)
-        part = dot_t(dqkv_ref[at, :], w_ref[:, QUERY_AT:OUT_AT])
+        part = dot_t(dqkv_ref[at, :], w_ref[:, QUERY_AT:REST_AT])
         value = t_ref[step].astype(F32)
         factor = lax.rsqrt(jnp.mean(value * value, -1, keepdims=True) + norm_eps)
         gain += jnp.sum(part * (value * factor), 0, keepdims=True)
@@ -302,26 +328,26 @@
     store.wait()
 
 
-def attend_back(place, lse, cosine, sine, gain_two, pieces, token_pieces, weights, h_first,
-                qt, q, kt, k, v, attn, attnt):
+def attend_back(place, cosine, sine, gain_two, pieces, token_pieces, weights, h_first,
+                q, kt, v, attn, attnt, probs):
     size, width = pieces[0].shape
-    heads, _, length = qt.shape
-    groups = k.shape[0]
+    heads, length, _ = q.shape
+    groups = v.shape[0]
     every = heads + 2 * groups
     rows = width // 16
     outs = [(size, width)] * 4 + [(4 * rows, LATE_WIDTH)] * 4 + [(4, rows, LATE_WIDTH)] * 4
     scratch = [
         (length, width), (4, size, width), (width, ATTN_WIDTH), (length, width),
-        qt.shape, q.shape, kt.shape, k.shape, v.shape, attn.shape, attnt.shape,
+        q.shape, kt.shape, v.shape, attn.shape, attnt.shape, probs.shape,
         (heads, length, HD), (heads, HD, length), (length, every * HD), (4, size, width),
         (width, LATE_WIDTH), (width, LATE_WIDTH),
     ]
     wide = [(heads, 1, length), (groups, length, HD), (groups, length, HD), (every, HD, length)]
     return kernel_call(
-        attend_back_kernel, "attend_back", place, (lse, cosine, sine, gain_two),
-        (*pieces, *token_pieces, weights, h_first, qt, q, kt, k, v, attn, attnt),
+        attend_back_kernel, "attend_back", place, (cosine, sine, gain_two),
+        (*pieces, *token_pieces, weights, h_first, q, kt, v, attn, attnt, probs),
         [like(s) for s in outs], [],
-        [vmem(s) for s in scratch] + [vmem(s, F32) for s in wide], 18, 24, 56)
+        [vmem(s) for s in scratch] + [vmem(s, F32) for s in wide], 15, 24, heads)
 
 
 def feed_kernel(place, h0, h1, g0, g1, w_hbm, hidden_hbm, dgu_hbm, b0, b1, r0, r1,
@@ -375,7 +401,7 @@
         feed_kernel, "feed", place, (), (*normed_pieces, *grad_pieces, weights),
         [like(s) for s in wide + [(size, width)] * 4], [],
         [vmem(s) for s in [weights.shape] + [(2, size, width)] * 2 + wide + [(2, size, width)] * 2],
-        7, 8, 40)
+        7, 8)
 
 
 def feed_grads_kernel(place, h0, h1, h2, h3, g0, g1, g2, g3, dgu_a, dgu_b, hidden_a, hidden_b,
@@ -430,7 +456,7 @@
     return kernel_call(
         feed_grads_kernel, "feed_grads", place, (),
         (*normed_pieces, *grad_pieces, dgu_a, dgu_b, hidden_a, hidden_b),
-        [like((width, 3 * hidden_w))], [], [vmem(s) for s in scratch], 20, 6, 36)[0]
+        [like((width, 3 * hidden_w))], [], [vmem(s) for s in scratch], 20, 6)[0]
 
 
 LATE_OUT, LATE_WIDTH = 128, 640
@@ -530,8 +556,16 @@
     return lax.optimization_barrier((value, first))
 
 
-def from_others(v, axis):
-    return [v[0]] + [from_offset(v[i], axis, i, 4) for i in range(1, 4)]
+def from_both(along_first, first_axis, along_second, second_axis):
+    near = [
+        from_offset(part[i], axis, i, 4)
+        for i in (1, 3)
+        for part, axis in ((along_first, first_axis), (along_second, second_axis))
+    ]
+    opposite, near = after((along_first[2], along_second[2]), near)
+    first = [along_first[0], near[0], from_offset(opposite[0], first_axis, 2, 4), near[2]]
+    second = [along_second[0], near[1], from_offset(opposite[1], second_axis, 2, 4), near[3]]
+    return first, second
 
 
 def gather_rows(v):
@@ -554,35 +588,58 @@
     heads_w = w_query.shape[1]
     gains_w = norm_gains.shape[1]
     block = lax.axis_index("yl") * 2 + lax.axis_index("core")
-    row = (lax.axis_index("x") * 4 + lax.axis_index("z")) * 2 + lax.axis_index("yh")
-    gains_at = (row * 4 + block) * gains_w
     place = jnp.stack(
         [block, lax.axis_index("x"), lax.axis_index("z"), lax.axis_index("yh")]
     ).astype(jnp.int32)
 
-    attn_w = gather_rows(jnp.concatenate([w_query, w_keyval, w_out.T], 1))
-    mlp_w = gather_rows(jnp.concatenate([w_gateup[:, 0], w_gateup[:, 1], w_down.T], 1))
-    gain_rows = lax.dynamic_update_slice(jnp.zeros((2, D), F32), norm_gains, (0, gains_at))
+    mlp_own = jnp.concatenate([w_gateup[:, 0], w_gateup[:, 1], w_down.T], 1)
+    mlp_w = gather_rows(mlp_own)
+
+    out_t = w_out.T
+    attn_own = jnp.concatenate(
+        [
+            jnp.zeros((out_t.shape[0], OUT_AT), BF16),
+            out_t[:, :OUT_CUT],
+            w_query,
+            w_keyval,
+            out_t[:, OUT_CUT:],
+        ],
+        1,
+    )
+    near = other(tokens, "core")
+    attn_pair = pair_rows(attn_own, "yh")
+
+    pair_w = 8 * gains_w
+    gain_at = (lax.axis_index("yh") * 4 + block) * gains_w
+    gain_part = lax.dynamic_update_slice(jnp.zeros((2, pair_w), F32), norm_gains, (0, gain_at))
     for axis in ("core", "yl", "yh"):
-        gain_rows = gain_rows + other(gain_rows, axis)
-    tokens, gain_rows = after(tokens, gain_rows)
-    for axis in ("z", "x"):
-        gain_rows = gain_rows + sum(from_offset(gain_rows, axis, i, 4) for i in (1, 3, 2))
-    token_far = other(tokens, "yl")
-    token_pieces = [tokens, other(tokens, "core"), token_far, other(token_far, "core")]
-    cotangent, token_far = after(cotangent, token_far)
+        gain_part = gain_part + other(gain_part, axis)
+    gain_part = gain_part.T
+    gain_high = gain_part.astype(BF16)
+    gain_low = (gain_part - gain_high.astype(F32)).astype(BF16)
+    first, second = attn_pair[:, :HALF_WIDTH], attn_pair[:, HALF_WIDTH:]
+    first += jnp.pad(gain_high, ((0, 0), (0, HALF_WIDTH - 2)))
+    first += jnp.pad(gain_low, ((0, 0), (2, HALF_WIDTH - 4)))
+
+    tokens, (first, near) = after(tokens, (first, near))
+    far = other(tokens, "yl")
+    along_z, along_x = from_both([first] * 4, "z", [second] * 4, "x")
+    along_z, along_x, far = lax.optimization_barrier((jnp.stack(along_z), jnp.stack(along_x), far))
+    token_pieces = [tokens, near, far, other(far, "core")]
+    cotangent, far = after(cotangent, far)
     grad_far = other(cotangent, "yl")
-    grad_pieces = [cotangent, other(cotangent, "core"), grad_far, other(grad_far, "core")]
-    token_pieces, grad_pieces = after(token_pieces, grad_pieces)
+    along_x, along_z = from_both([along_z] * 4, "x", [along_x] * 4, "z")
 
     positions = jnp.arange(length).astype(F32)
     freqs = rope_base ** (-(jnp.arange(HD // 2).astype(F32) * 2.0 / HD))
     angles = freqs[:, None] * positions[None, :]
     cosine, sine = jnp.cos(angles), jnp.sin(angles)
 
-    lse, h_first, qt, q, kt, k, v, attn, attnt, *parts = attend(
-        place, token_pieces, attn_w, gain_rows, cosine, sine
+    gain_rows, attn_w, h_first, q, kt, v, attn, attnt, probs, *parts = attend(
+        place, token_pieces, along_x, along_z, cosine, sine
     )
+    grad_far, parts = after(grad_far, parts)
+    grad_pieces = [cotangent, other(cotangent, "core"), grad_far, other(grad_far, "core")]
     middle_far = far_sum(parts[2], parts[3])
     middle = (
         tokens.astype(F32) + near_sum(parts[0], parts[1]) + other(middle_far, "yl").astype(F32)
@@ -606,9 +663,8 @@
     back_far = far_sum(back_chip, back_diag)
     hidden_b, back_far = after(hidden_b, back_far)
     mlp_grads = feed_grads(place, h_pieces, grad_pieces, dgu_a, dgu_b, hidden_a, hidden_b)
-    back_far = other(back_far, "yl").astype(F32)
-    mlp_grads, back_far = after(mlp_grads, back_far)
-    d_h2_own = back_near + back_far
+    mlp_grads, back_far = after(mlp_grads, other(back_far, "yl"))
+    d_h2_own = back_near + back_far.astype(F32)
     early = scatter_rows(mlp_grads)
     out_far = far_sum(out_chip, out_diag)
 
@@ -619,21 +675,21 @@
     d_out_far, out_near = after(d_out_far, out_near)
     out_pieces = [d_out, other(d_out, "core"), d_out_far, other(d_out_far, "core")]
     out_far, out_pieces = after(out_far, out_pieces)
-    out_far = other(out_far, "yl").astype(F32)
+    out_far = other(out_far, "yl")
 
     back = attend_back(
-        place, lse, cosine, sine, gain_two[None], out_pieces, token_pieces, attn_w,
-        h_first, qt, q, kt, k, v, attn, attnt,
+        place, cosine, sine, gain_two[None], out_pieces, token_pieces, attn_w,
+        h_first, q, kt, v, attn, attnt, probs,
     )
     out_near, back = after(out_near, back)
-    result = (middle + out_near + out_far).astype(BF16)
+    result = (middle + out_near + out_far.astype(F32)).astype(BF16)
     parts, late_parts = back[:4], back[4:]
     late_parts, result = after(late_parts, result)
     d_far = far_sum(parts[2], parts[3])
-    along_x, along_z = from_others(late_parts[:4], "x"), from_others(late_parts[4:], "z")
+    along_x, along_z = from_both(late_parts[:4], "x", late_parts[4:], "z")
     along_x, d_far = after(along_x, d_far)
     middle_parts = late_middle(place, along_x, along_z)
-    along_z, along_x = from_others(middle_parts[:4], "z"), from_others(middle_parts[4:], "x")
+    along_z, along_x = from_both(middle_parts[:4], "z", middle_parts[4:], "x")
     late_keep, late_send = late_last(place, along_z, along_x)
     d_h1_own = near_sum(parts[0], parts[1]) + other(d_far, "yl").astype(F32)
     late_other, (d_h1_own, early) = after(other(late_send, "yh"), (d_h1_own, early))

time: 366 us -> 378 us (1.033)
  waiting for transfers between devices: 139 us -> 161 us
  local copies, waits for them, and re-layouts: 15.2 us -> 9.14 us
    ppermute x51 -> x57, waiting for transfers between devices: 124 us -> 161 us  [from_offset(): lax.ppermute(v, axis, [((i + offset) % size, i) for i in range(size)])]
    all_gather x2 -> x1, waiting for transfers between devices: 14.8 us -> 0.01 us  [gather_rows(): return lax.all_gather(pair_rows(v, 'yh'), ('x', 'z'), axis=0, tiled=True)]
    unnamed x111 -> x96, local copies, waits for them, and re-layouts: 10.3 us -> 3.3 us
    ppermute x51 -> x57, starting transfers between devices: 74.5 us -> 71.7 us  [from_offset(): lax.ppermute(v, axis, [((i + offset) % size, i) for i in range(size)])]
  transfers between devices with their start and end apart: 54 -> 59, of which waited for: 27 -> 35; matrix products, arithmetic and copies ran while one was open for 6% -> 5% of each run, Pallas kernels for 22% -> 22%
where the time goes in v2:
time: 378 us; the launch traced here: 372 us
  waiting for transfers between devices  161 us (43%)
  Pallas kernels  95.7 us (25%)
  starting transfers between devices  71.7 us (19%)
  other arithmetic  19.8 us (5%)
  between operations  14.8 us (4%)
  local copies, waits for them, and re-layouts  9.14 us (2%)
    ppermute x57, waiting for transfers between devices, from_offset(): lax.ppermute(v, axis, [((i + offset) % size, i) for i in range(size)])  161 us
    pallas_call x5, Pallas kernels, kernel_call(): pl.pallas_call(kernel, out_shape=list(small_outs) + list(outs), in_specs=...  90.2 us
    ppermute x57, starting transfers between devices, from_offset(): lax.ppermute(v, axis, [((i + offset) % size, i) for i in range(size)])  71.7 us
  transfers between devices with their start and end apart: 59, of which 35 were waited for; matrix products, arithmetic and copies ran while one was open for 5% of the time, Pallas kernels for 22%

profile of v2, /device:TPU:1, one launch (start us, length us, event | category | flops | bytes accessed | tf_op | source)
XLA Modules:
  0.0 371.9 jit_solution(6318312362280382623)
XLA Ops:
  9.6 3.8 %collective-permute-start.25 = (bf16[48,3072]{1,0:T(8,128)(2,1)S(1)}, bf16[48,3072]{1,0:T(8,128)(2,1)S(1)}, u32[]{:S(2)}, u32[]{:S(2)}) collective-permute-start(bf16[48,3072]{1,0:T(8,128)(2,1)S(1)} %pad_maximum_fusion.3), channel_id=1, source_target_pairs={{4,0},{0,4},{5,1},{1,5},{6,2},{2,6},{7,3},{3,7},{12,8},{8,12},{13,... | collective-permute-start | bytes 884744 | tf_op jit(solution)/shard_map/ppermute | solution.py:534
  13.5 6.5 %collective-permute-done.25 = bf16[48,3072]{1,0:T(8,128)(2,1)S(1)} collective-permute-done((bf16[48,3072]{1,0:T(8,128)(2,1)S(1)}, bf16[48,3072]{1,0:T(8,128)(2,1)S(1)}, u32[]{:S(2)}, u32[]{:S(2)}) %collective-permute-start.25) | collective-permute-done | bytes 294944 | tf_op jit(solution)/shard_map/ppermute | solution.py:534
  27.0 3.0 collective-permute-start.3
  32.2 3.1 collective-permute-done
  36.4 2.5 collective-permute-start.6
  38.8 3.8 %collective-permute-start.5 = (bf16[96,640]{1,0:T(8,128)(2,1)S(1)}, bf16[96,640]{1,0:T(8,128)(2,1)S(1)}, u32[]{:S(2)}, u32[]{:S(2)}) collective-permute-start(bf16[96,640]{1,0:T(8,128)(2,1)S(1)} %get-tuple-element.136), channel_id=1, source_target_pairs={{8,0},{16,8},{24,16},{0,24},{9,1},{17,9},{25,17},{1,25},{10,2},{18... | collective-permute-start | bytes 368648 | tf_op jit(solution)/shard_map/ppermute | solution.py:534
  46.4 4.0 %collective-permute-done.7 = bf16[96,640]{1,0:T(8,128)(2,1)S(1)} collective-permute-done((bf16[96,640]{1,0:T(8,128)(2,1)S(1)}, bf16[96,640]{1,0:T(8,128)(2,1)S(1)}, u32[]{:S(2)}, u32[]{:S(2)}) %collective-permute-start.7) | collective-permute-done | bytes 122912 | tf_op jit(solution)/shard_map/ppermute | solution.py:534
  51.8 3.8 %collective-permute-done.10 = bf16[96,640]{1,0:T(8,128)(2,1)S(1)} collective-permute-done((bf16[96,640]{1,0:T(8,128)(2,1)S(1)}, bf16[96,640]{1,0:T(8,128)(2,1)S(1)}, u32[]{:S(2)}, u32[]{:S(2)}) %collective-permute-start.10) | collective-permute-done | bytes 122912 | tf_op jit(solution)/shard_map/ppermute | solution.py:534
  60.8 5.8 %collective-permute-start.13 = (bf16[256,1536]{1,0:T(8,128)(2,1)S(1)}, bf16[256,1536]{1,0:T(8,128)(2,1)S(1)}, u32[]{:S(2)}, u32[]{:S(2)}) collective-permute-start(bf16[256,1536]{1,0:T(8,128)(2,1)S(1)} %collective-permute-done.11.t2), channel_id=1, source_target_pairs={{1,0},{0,1},{3,2},{2,3},{5,4},{4,5},{7,6},{6,7},{9,8},{8,9},{11,10... | collective-permute-start | bytes 2359304 | tf_op jit(solution)/shard_map/ppermute | solution.py:534
  66.6 11.6 %collective-permute-done.14.a1 = bf16[4,96,640]{2,1,0:T(8,128)(2,1)} collective-permute-done((bf16[4,96,640]{2,1,0:T(8,128)(2,1)}, bf16[4,96,640]{2,1,0:T(8,128)(2,1)}, u32[]{:S(2)}, u32[]{:S(2)}) %collective-permute-start.14) | collective-permute-done | bytes 491552 | tf_op jit(solution)/shard_map/ppermute | solution.py:534
  80.3 2.4 collective-permute-done.16.a3
  85.6 19.9 %collective-permute-done.18.a2 = bf16[4,96,640]{2,1,0:T(8,128)(2,1)} collective-permute-done((bf16[4,96,640]{2,1,0:T(8,128)(2,1)}, bf16[4,96,640]{2,1,0:T(8,128)(2,1)}, u32[]{:S(2)}, u32[]{:S(2)}) %collective-permute-start.18) | collective-permute-done | bytes 491552 | tf_op jit(solution)/shard_map/ppermute | solution.py:534
  106.4 21.3 %attend.1 = (f32[2,1536]{1,0:T(2,128)}, bf16[1536,1280]{1,0:T(8,128)(2,1)}, bf16[1024,1536]{1,0:T(8,128)(2,1)}, bf16[4,1024,96]{2,1,0:T(8,128)(2,1)}, bf16[2,96,...) custom-call(s32[4]{0:T(128)} %pad_add_fusion.place, ...), custom_call_target="tpu_custom_call" | custom-call | flops 1 | bytes 1 | tf_op jit(solution)/shard_map/attend/pallas_call | solution.py:86
  127.8 8.2 %collective-permute-start.21 = (bf16[256,1536]{1,0:T(8,128)(2,1)}, bf16[256,1536]{1,0:T(8,128)(2,1)S(1)}, u32[]{:S(2)}, u32[]{:S(2)}) collective-permute-start(bf16[256,1536]{1,0:T(8,128)(2,1)} %get-tuple-element.160), channel_id=1, source_target_pairs={{1,0},{0,1},{3,2},{2,3},{5,4},{4,5},{7,6},{6,7},{9,8},{8,9},{11,10... | collective-permute-start | bytes 2359304 | tf_op jit(solution)/shard_map/ppermute | solution.py:534
  141.0 17.3 %collective-permute-done.22 = bf16[256,1536]{1,0:T(8,128)(2,1)S(1)} collective-permute-done((bf16[256,1536]{1,0:T(8,128)(2,1)S(1)}, bf16[256,1536]{1,0:T(8,128)(2,1)S(1)}, u32[]{:S(2)}, u32[]{:S(2)}) %collective-permute-start.22) | collective-permute-done | bytes 786464 | tf_op jit(solution)/shard_map/ppermute | solution.py:534
  162.9 14.7 %feed.2 = (bf16[512,1024]{1,0:T(8,128)(2,1)}, bf16[512,2048]{1,0:T(8,128)(2,1)}, bf16[256,1536]{1,0:T(8,128)(2,1)}, bf16[256,1536]{1,0:T(8,128)(2,1)}, bf16[256,...) custom-call(s32[4]{0:T(128)} %pad_add_fusion.place, bf16[256,1536]{1,0:T(8,128)(2,1)} %copy-done.5, ...), custom_call_target="tpu_custom_call" | custom-call | flops 1 | bytes 1 | tf_op jit(solution)/shard_map/feed/pallas_call | solution.py:86
  183.7 14.7 %feed.3 = (bf16[512,1024]{1,0:T(8,128)(2,1)}, bf16[512,2048]{1,0:T(8,128)(2,1)}, bf16[256,1536]{1,0:T(8,128)(2,1)}, bf16[256,1536]{1,0:T(8,128)(2,1)}, bf16[256,...) custom-call(s32[4]{0:T(128)} %pad_add_fusion.place, bf16[256,1536]{1,0:T(8,128)(2,1)} %collective-permute-done.27.h0.h2, ...), custom_call_target="tpu_custom_call" | custom-call | flops 1 | bytes 1 | tf_op jit(solution)/shard_map/feed/pallas_call | solution.py:86
  201.0 2.2 add_convert_fusion.3
  204.4 15.4 %feed_grads.1 = bf16[1536,3072]{1,0:T(8,128)(2,1)} custom-call(s32[4]{0:T(128)} %pad_add_fusion.place, bf16[256,1536]{1,0:T(8,128)(2,1)} %copy-done.5, bf16[256,1536]{1,0:T(8,128)(2,1)} %collective-permute-done.23.h1, bf16[256,1536]{1,0:T(8,128)(2,1)} %collective-permute-done.27.h0.h2, bf16[256,1536]{1,0:T(8,128)(2,1)} %copy-done.9, bf16[256,1536]{1,0:T(8,128)(2,1)} %g0.1, ...), custom_call_target="tpu_custom_call" | custom-call | flops 1 | bytes 1 | tf_op jit(solution)/shard_map/feed_grads/pallas_call | solution.py:86
  219.8 2.8 collective-permute-done.31
  231.0 16.9 %collective-permute-done.32.o2 = bf16[256,1536]{1,0:T(8,128)(2,1)S(1)} collective-permute-done((bf16[256,1536]{1,0:T(8,128)(2,1)S(1)}, bf16[256,1536]{1,0:T(8,128)(2,1)S(1)}, u32[]{:S(2)}, u32[]{:S(2)}) %collective-permute-start.32) | collective-permute-done | bytes 786464 | tf_op jit(solution)/shard_map/ppermute | solution.py:534
  252.4 24.1 %attend_back.1 = (bf16[256,1536]{1,0:T(8,128)(2,1)}, bf16[256,1536]{1,0:T(8,128)(2,1)}, bf16[256,1536]{1,0:T(8,128)(2,1)}, bf16[256,1536]{1,0:T(8,128)(2,1)}, bf...) custom-call(s32[4]{0:T(128)} %pad_add_fusion.place, ...), custom_call_target="tpu_custom_call" | custom-call | flops 1 | bytes 1 | tf_op jit(solution)/shard_map/attend_back/pallas_call | solution.py:86
  276.9 2.7 add_convert_fusion.1
  279.6 2.7 collective-permute-start.38
  284.7 10.3 %collective-permute-done.38.refs_1_ = bf16[384,640]{1,0:T(8,128)(2,1)S(1)} collective-permute-done((bf16[384,640]{1,0:T(8,128)(2,1)S(1)}, bf16[384,640]{1,0:T(8,128)(2,1)S(1)}, u32[]{:S(2)}, u32[]{:S(2)}) %collective-permute-start.38) | collective-permute-done | bytes 491552 | tf_op jit(solution)/shard_map/ppermute | solution.py:534
  299.9 17.3 %collective-permute-done.42.refs_2_ = bf16[384,640]{1,0:T(8,128)(2,1)S(1)} collective-permute-done((bf16[384,640]{1,0:T(8,128)(2,1)S(1)}, bf16[384,640]{1,0:T(8,128)(2,1)S(1)}, u32[]{:S(2)}, u32[]{:S(2)}) %collective-permute-start.42) | collective-permute-done | bytes 491552 | tf_op jit(solution)/shard_map/ppermute | solution.py:534
  319.2 3.4 late_middle.1
  328.0 3.3 collective-permute-done.46.refs_5_
  334.5 4.2 %collective-permute-done.49.refs_2_ = bf16[96,640]{1,0:T(8,128)(2,1)} collective-permute-done((bf16[96,640]{1,0:T(8,128)(2,1)}, bf16[96,640]{1,0:T(8,128)(2,1)}, u32[]{:S(2)}, u32[]{:S(2)}) %collective-permute-start.49) | collective-permute-done | bytes 122912 | tf_op jit(solution)/shard_map/ppermute | solution.py:534
  342.0 2.7 collective-permute-start.51
  346.3 8.6 %collective-permute-done.54 = bf16[48,3072]{1,0:T(8,128)(2,1)S(1)} collective-permute-done((bf16[48,3072]{1,0:T(8,128)(2,1)S(1)}, bf16[48,3072]{1,0:T(8,128)(2,1)S(1)}, u32[]{:S(2)}, u32[]{:S(2)}) %collective-permute-start.54) | collective-permute-done | bytes 294944 | tf_op jit(solution)/shard_map/ppermute | solution.py:534
  355.1 3.2 collective-permute-start.55
  (244 shorter events, 91.1 us)
Async XLA Ops:
  7.2 155.7 %all-gather.2.cloned.1.call-start = ((), (), s32[]{:S(2)}) async-start(), calls=%async_computation.1 | async-start | bytes 10027008 | tf_op jit(solution)/shard_map/all_gather | solution.py:572
  9.6 10.3 %collective-permute-start.25 = (bf16[48,3072]{1,0:T(8,128)(2,1)S(1)}, bf16[48,3072]{1,0:T(8,128)(2,1)S(1)}, u32[]{:S(2)}, u32[]{:S(2)}) collective-permute-start(bf16[48,3072]{1,0:T(8,128)(2,1)S(1)} %pad_maximum_fusion.3), channel_id=1, source_target_pairs={{4,0},{0,4},{5,1},{1,5},{6,2},{2,6},{7,3},{3,7},{12,8},{8,12},{13,... | collective-permute-start | bytes 884744 | tf_op jit(solution)/shard_map/ppermute | solution.py:534
  21.0 323.7 %reduce-scatter.2.cloned.1.call-start = ((), (), s32[]{:S(2)}) async-start(), calls=%async_computation.2 | async-start | bytes 10027008 | tf_op jit(solution)/shard_map/reduce_scatter | solution.py:576
  35.4 22.5 %collective-permute-start.11 = (bf16[256,1536]{1,0:T(8,128)(2,1)S(1)}, bf16[256,1536]{1,0:T(8,128)(2,1)S(1)}, u32[]{:S(2)}, u32[]{:S(2)}) collective-permute-start(bf16[256,1536]{1,0:T(8,128)(2,1)S(1)} %copy-done), channel_id=1, source_target_pairs={{2,0},{0,2},{3,1},{1,3},{6,4},{4,6},{7,5},{5,7},{10,8},{8,10},{11,... | collective-permute-start | bytes 2359304 | tf_op jit(solution)/shard_map/ppermute | solution.py:534
  57.9 20.3 %collective-permute-start.14 = (bf16[4,96,640]{2,1,0:T(8,128)(2,1)}, bf16[4,96,640]{2,1,0:T(8,128)(2,1)}, u32[]{:S(2)}, u32[]{:S(2)}) collective-permute-start(bf16[4,96,640]{2,1,0:T(8,128)(2,1)} %pad_maximum_fusion.1.a0), channel_id=1, source_target_pairs={{32,0},{64,32},{96,64},{0,96},{33,1},{65,33},{97,65},{1,97},{34,2}... | collective-permute-start | bytes 1474568 | tf_op jit(solution)/shard_map/ppermute | solution.py:534
  58.9 21.4 %collective-permute-start.15 = (bf16[4,96,640]{2,1,0:T(8,128)(2,1)}, bf16[4,96,640]{2,1,0:T(8,128)(2,1)}, u32[]{:S(2)}, u32[]{:S(2)}) collective-permute-start(bf16[4,96,640]{2,1,0:T(8,128)(2,1)} %pad_maximum_fusion.2.b0), channel_id=1, source_target_pairs={{8,0},{16,8},{24,16},{0,24},{9,1},{17,9},{25,17},{1,25},{10,2},{18... | collective-permute-start | bytes 1474568 | tf_op jit(solution)/shard_map/ppermute | solution.py:534
  59.9 22.9 %collective-permute-start.16 = (bf16[4,96,640]{2,1,0:T(8,128)(2,1)}, bf16[4,96,640]{2,1,0:T(8,128)(2,1)}, u32[]{:S(2)}, u32[]{:S(2)}) collective-permute-start(bf16[4,96,640]{2,1,0:T(8,128)(2,1)} %pad_maximum_fusion.1.a0), channel_id=1, source_target_pairs={{96,0},{0,32},{32,64},{64,96},{97,1},{1,33},{33,65},{65,97},{98,2}... | collective-permute-start | bytes 1474568 | tf_op jit(solution)/shard_map/ppermute | solution.py:534
  59.9 22.9 %collective-permute-start.17 = (bf16[4,96,640]{2,1,0:T(8,128)(2,1)}, bf16[4,96,640]{2,1,0:T(8,128)(2,1)}, u32[]{:S(2)}, u32[]{:S(2)}) collective-permute-start(bf16[4,96,640]{2,1,0:T(8,128)(2,1)} %pad_maximum_fusion.2.b0), channel_id=1, source_target_pairs={{24,0},{0,8},{8,16},{16,24},{25,1},{1,9},{9,17},{17,25},{26,2},{2,... | collective-permute-start | bytes 1474568 | tf_op jit(solution)/shard_map/ppermute | solution.py:534
  60.8 24.8 %collective-permute-start.13 = (bf16[256,1536]{1,0:T(8,128)(2,1)S(1)}, bf16[256,1536]{1,0:T(8,128)(2,1)S(1)}, u32[]{:S(2)}, u32[]{:S(2)}) collective-permute-start(bf16[256,1536]{1,0:T(8,128)(2,1)S(1)} %collective-permute-done.11.t2), channel_id=1, source_target_pairs={{1,0},{0,1},{3,2},{2,3},{5,4},{4,5},{7,6},{6,7},{9,8},{8,9},{11,10... | collective-permute-start | bytes 2359304 | tf_op jit(solution)/shard_map/ppermute | solution.py:534
  78.2 49.6 %collective-permute-start.12 = (bf16[256,1536]{1,0:T(8,128)(2,1)S(1)}, bf16[256,1536]{1,0:T(8,128)(2,1)}, u32[]{:S(2)}, u32[]{:S(2)}) collective-permute-start(bf16[256,1536]{1,0:T(8,128)(2,1)S(1)} %copy-done.3), channel_id=1, source_target_pairs={{2,0},{0,2},{3,1},{1,3},{6,4},{4,6},{7,5},{5,7},{10,8},{8,10},{11,... | collective-permute-start | bytes 2359304 | tf_op jit(solution)/shard_map/ppermute | solution.py:534
  82.8 22.8 %collective-permute-start.18 = (bf16[4,96,640]{2,1,0:T(8,128)(2,1)}, bf16[4,96,640]{2,1,0:T(8,128)(2,1)}, u32[]{:S(2)}, u32[]{:S(2)}) collective-permute-start(bf16[4,96,640]{2,1,0:T(8,128)(2,1)} %pad_maximum_fusion.1.a0), channel_id=1, source_target_pairs={{64,0},{96,32},{0,64},{32,96},{65,1},{97,33},{1,65},{33,97},{66,2}... | collective-permute-start | bytes 1474568 | tf_op jit(solution)/shard_map/ppermute | solution.py:534
  83.3 23.1 %collective-permute-start.19 = (bf16[4,96,640]{2,1,0:T(8,128)(2,1)}, bf16[4,96,640]{2,1,0:T(8,128)(2,1)}, u32[]{:S(2)}, u32[]{:S(2)}) collective-permute-start(bf16[4,96,640]{2,1,0:T(8,128)(2,1)} %pad_maximum_fusion.2.b0), channel_id=1, source_target_pairs={{16,0},{24,8},{0,16},{8,24},{17,1},{25,9},{1,17},{9,25},{18,2},{26... | collective-permute-start | bytes 1474568 | tf_op jit(solution)/shard_map/ppermute | solution.py:534
  127.8 10.3 %collective-permute-start.21 = (bf16[256,1536]{1,0:T(8,128)(2,1)}, bf16[256,1536]{1,0:T(8,128)(2,1)S(1)}, u32[]{:S(2)}, u32[]{:S(2)}) collective-permute-start(bf16[256,1536]{1,0:T(8,128)(2,1)} %get-tuple-element.160), channel_id=1, source_target_pairs={{1,0},{0,1},{3,2},{2,3},{5,4},{4,5},{7,6},{6,7},{9,8},{8,9},{11,10... | collective-permute-start | bytes 2359304 | tf_op jit(solution)/shard_map/ppermute | solution.py:534
  139.4 18.8 %collective-permute-start.22 = (bf16[256,1536]{1,0:T(8,128)(2,1)S(1)}, bf16[256,1536]{1,0:T(8,128)(2,1)S(1)}, u32[]{:S(2)}, u32[]{:S(2)}) collective-permute-start(bf16[256,1536]{1,0:T(8,128)(2,1)S(1)} %add_convert_fusion.4), channel_id=1, source_target_pairs={{2,0},{0,2},{3,1},{1,3},{6,4},{4,6},{7,5},{5,7},{10,8},{8,10},{11,... | collective-permute-start | bytes 2359304 | tf_op jit(solution)/shard_map/ppermute | solution.py:534
  140.3 21.7 %collective-permute-start.24 = (bf16[256,1536]{1,0:T(8,128)(2,1)S(1)}, bf16[256,1536]{1,0:T(8,128)(2,1)S(1)}, u32[]{:S(2)}, u32[]{:S(2)}) collective-permute-start(bf16[256,1536]{1,0:T(8,128)(2,1)S(1)} %copy-done.3), channel_id=1, source_target_pairs={{1,0},{0,1},{3,2},{2,3},{5,4},{4,5},{7,6},{6,7},{9,8},{8,9},{11,10... | collective-permute-start | bytes 2359304 | tf_op jit(solution)/shard_map/ppermute | solution.py:534
  160.4 19.2 %collective-permute-start.27 = (bf16[256,1536]{1,0:T(8,128)(2,1)S(1)}, bf16[256,1536]{1,0:T(8,128)(2,1)}, u32[]{:S(2)}, u32[]{:S(2)}) collective-permute-start(bf16[256,1536]{1,0:T(8,128)(2,1)S(1)} %multiply_convert_fusion.h0), channel_id=1, source_target_pairs={{2,0},{0,2},{3,1},{1,3},{6,4},{4,6},{7,5},{5,7},{10,8},{8,10},{11,... | collective-permute-start | bytes 2359304 | tf_op jit(solution)/shard_map/ppermute | solution.py:534
  161.2 19.4 %collective-permute-start.29 = (bf16[256,1536]{1,0:T(8,128)(2,1)}, bf16[256,1536]{1,0:T(8,128)(2,1)}, u32[]{:S(2)}, u32[]{:S(2)}) collective-permute-start(bf16[256,1536]{1,0:T(8,128)(2,1)} %collective-permute-done.12.g0.g2), channel_id=1, source_target_pairs={{1,0},{0,1},{3,2},{2,3},{5,4},{4,5},{7,6},{6,7},{9,8},{8,9},{11,10... | collective-permute-start | bytes 2359304 | tf_op jit(solution)/shard_map/ppermute | solution.py:534
  203.2 19.3 %collective-permute-start.31 = (bf16[256,1536]{1,0:T(8,128)(2,1)}, bf16[256,1536]{1,0:T(8,128)(2,1)S(1)}, u32[]{:S(2)}, u32[]{:S(2)}) collective-permute-start(bf16[256,1536]{1,0:T(8,128)(2,1)} %add_convert_fusion.3), channel_id=1, source_target_pairs={{2,0},{0,2},{3,1},{1,3},{6,4},{4,6},{7,5},{5,7},{10,8},{8,10},{11,... | collective-permute-start | bytes 2359304 | tf_op jit(solution)/shard_map/ppermute | solution.py:534
  229.0 18.9 %collective-permute-start.32 = (bf16[256,1536]{1,0:T(8,128)(2,1)S(1)}, bf16[256,1536]{1,0:T(8,128)(2,1)S(1)}, u32[]{:S(2)}, u32[]{:S(2)}) collective-permute-start(bf16[256,1536]{1,0:T(8,128)(2,1)S(1)} %get-tuple-element.182.o0), channel_id=1, source_target_pairs={{2,0},{0,2},{3,1},{1,3},{6,4},{4,6},{7,5},{5,7},{10,8},{8,10},{11,... | collective-permute-start | bytes 2359304 | tf_op jit(solution)/shard_map/ppermute | solution.py:534
  229.8 19.2 %collective-permute-start.34 = (bf16[256,1536]{1,0:T(8,128)(2,1)S(1)}, bf16[256,1536]{1,0:T(8,128)(2,1)S(1)}, u32[]{:S(2)}, u32[]{:S(2)}) collective-permute-start(bf16[256,1536]{1,0:T(8,128)(2,1)S(1)} %copy-done.38), channel_id=1, source_target_pairs={{1,0},{0,1},{3,2},{2,3},{5,4},{4,5},{7,6},{6,7},{9,8},{8,9},{11,10... | collective-permute-start | bytes 2359304 | tf_op jit(solution)/shard_map/ppermute | solution.py:534
  230.7 19.3 %collective-permute-start.35 = (bf16[256,1536]{1,0:T(8,128)(2,1)S(1)}, bf16[256,1536]{1,0:T(8,128)(2,1)S(1)}, u32[]{:S(2)}, u32[]{:S(2)}) collective-permute-start(bf16[256,1536]{1,0:T(8,128)(2,1)S(1)} %get-tuple-element.182.o0), channel_id=1, source_target_pairs={{1,0},{0,1},{3,2},{2,3},{5,4},{4,5},{7,6},{6,7},{9,8},{8,9},{11,10... | collective-permute-start | bytes 2359304 | tf_op jit(solution)/shard_map/ppermute | solution.py:534
  250.9 26.0 %collective-permute-start.37 = (bf16[256,1536]{1,0:T(8,128)(2,1)}, bf16[256,1536]{1,0:T(8,128)(2,1)}, u32[]{:S(2)}, u32[]{:S(2)}) collective-permute-start(bf16[256,1536]{1,0:T(8,128)(2,1)} %add_convert_fusion.2), channel_id=1, source_target_pairs={{2,0},{0,2},{3,1},{1,3},{6,4},{4,6},{7,5},{5,7},{10,8},{8,10},{11,... | collective-permute-start | bytes 2359304 | tf_op jit(solution)/shard_map/ppermute | solution.py:534
  276.6 23.1 %collective-permute-start.43 = (bf16[256,1536]{1,0:T(8,128)(2,1)}, bf16[256,1536]{1,0:T(8,128)(2,1)S(1)}, u32[]{:S(2)}, u32[]{:S(2)}) collective-permute-start(bf16[256,1536]{1,0:T(8,128)(2,1)} %get-tuple-element.228), channel_id=1, source_target_pairs={{1,0},{0,1},{3,2},{2,3},{5,4},{4,5},{7,6},{6,7},{9,8},{8,9},{11,10... | collective-permute-start | bytes 2359304 | tf_op jit(solution)/shard_map/ppermute | solution.py:534
  279.6 15.3 %collective-permute-start.38 = (bf16[384,640]{1,0:T(8,128)(2,1)S(1)}, bf16[384,640]{1,0:T(8,128)(2,1)S(1)}, u32[]{:S(2)}, u32[]{:S(2)}) collective-permute-start(bf16[384,640]{1,0:T(8,128)(2,1)S(1)} %copy-done.44), channel_id=1, source_target_pairs={{32,0},{64,32},{96,64},{0,96},{33,1},{65,33},{97,65},{1,97},{34,2}... | collective-permute-start | bytes 1474568 | tf_op jit(solution)/shard_map/ppermute | solution.py:534
  282.2 12.7 %collective-permute-start.39 = (bf16[4,96,640]{2,1,0:T(8,128)(2,1)S(1)}, bf16[4,96,640]{2,1,0:T(8,128)(2,1)S(1)}, u32[]{:S(2)}, u32[]{:S(2)}) collective-permute-start(bf16[4,96,640]{2,1,0:T(8,128)(2,1)S(1)} %copy-done.43), channel_id=1, source_target_pairs={{8,0},{16,8},{24,16},{0,24},{9,1},{17,9},{25,17},{1,25},{10,2},{18... | collective-permute-start | bytes 1474568 | tf_op jit(solution)/shard_map/ppermute | solution.py:534
  282.3 13.2 %collective-permute-start.40 = (bf16[384,640]{1,0:T(8,128)(2,1)S(1)}, bf16[384,640]{1,0:T(8,128)(2,1)S(1)}, u32[]{:S(2)}, u32[]{:S(2)}) collective-permute-start(bf16[384,640]{1,0:T(8,128)(2,1)S(1)} %copy-done.42), channel_id=1, source_target_pairs={{96,0},{0,32},{32,64},{64,96},{97,1},{1,33},{33,65},{65,97},{98,2}... | collective-permute-start | bytes 1474568 | tf_op jit(solution)/shard_map/ppermute | solution.py:534
  283.3 14.0 %collective-permute-start.41 = (bf16[4,96,640]{2,1,0:T(8,128)(2,1)S(1)}, bf16[4,96,640]{2,1,0:T(8,128)(2,1)S(1)}, u32[]{:S(2)}, u32[]{:S(2)}) collective-permute-start(bf16[4,96,640]{2,1,0:T(8,128)(2,1)S(1)} %copy-done.41), channel_id=1, source_target_pairs={{24,0},{0,8},{8,16},{16,24},{25,1},{1,9},{9,17},{17,25},{26,2},{2,... | collective-permute-start | bytes 1474568 | tf_op jit(solution)/shard_map/ppermute | solution.py:534
  297.3 19.9 %collective-permute-start.42 = (bf16[384,640]{1,0:T(8,128)(2,1)S(1)}, bf16[384,640]{1,0:T(8,128)(2,1)S(1)}, u32[]{:S(2)}, u32[]{:S(2)}) collective-permute-start(bf16[384,640]{1,0:T(8,128)(2,1)S(1)} %copy-done.40), channel_id=1, source_target_pairs={{64,0},{96,32},{0,64},{32,96},{65,1},{97,33},{1,65},{33,97},{66,2}... | collective-permute-start | bytes 1474568 | tf_op jit(solution)/shard_map/ppermute | solution.py:534
  299.1 20.1 %collective-permute-start.44 = (bf16[4,96,640]{2,1,0:T(8,128)(2,1)S(1)}, bf16[4,96,640]{2,1,0:T(8,128)(2,1)}, u32[]{:S(2)}, u32[]{:S(2)}) collective-permute-start(bf16[4,96,640]{2,1,0:T(8,128)(2,1)S(1)} %copy-done.39), channel_id=1, source_target_pairs={{16,0},{24,8},{0,16},{8,24},{17,1},{25,9},{1,17},{9,25},{18,2},{26... | collective-permute-start | bytes 1474568 | tf_op jit(solution)/shard_map/ppermute | solution.py:534
  324.2 21.8 %collective-permute-start.52 = (bf16[256,1536]{1,0:T(8,128)(2,1)}, bf16[256,1536]{1,0:T(8,128)(2,1)S(1)}, u32[]{:S(2)}, u32[]{:S(2)}) collective-permute-start(bf16[256,1536]{1,0:T(8,128)(2,1)} %get-tuple-element.253), channel_id=1, source_target_pairs={{1,0},{0,1},{3,2},{2,3},{5,4},{4,5},{7,6},{6,7},{9,8},{8,9},{11,10... | collective-permute-start | bytes 2359304 | tf_op jit(solution)/shard_map/ppermute | solution.py:534
  325.3 20.8 %collective-permute-start.53 = (bf16[256,1536]{1,0:T(8,128)(2,1)S(1)}, bf16[256,1536]{1,0:T(8,128)(2,1)S(1)}, u32[]{:S(2)}, u32[]{:S(2)}) collective-permute-start(bf16[256,1536]{1,0:T(8,128)(2,1)S(1)} %add_convert_fusion), channel_id=1, source_target_pairs={{2,0},{0,2},{3,1},{1,3},{6,4},{4,6},{7,5},{5,7},{10,8},{8,10},{11,... | collective-permute-start | bytes 2359304 | tf_op jit(solution)/shard_map/ppermute | solution.py:534
  342.0 13.0 %collective-permute-start.51 = (bf16[48,1280]{1,0:T(8,128)(2,1)}, bf16[48,1280]{1,0:T(8,128)(2,1)S(1)}, u32[]{:S(2)}, u32[]{:S(2)}) collective-permute-start(bf16[48,1280]{1,0:T(8,128)(2,1)} %get-tuple-element.251), channel_id=1, source_target_pairs={{4,0},{0,4},{5,1},{1,5},{6,2},{2,6},{7,3},{3,7},{12,8},{8,12},{13,... | collective-permute-start | bytes 368648 | tf_op jit(solution)/shard_map/ppermute | solution.py:534
  (72 other events, 789.9 us)
Sparse Core Ops, SparseCore 0:
  21.1 101.7 all-gather.1
  222.7 98.0 reduce-scatter.1

commit v3 on v2

--- a/solution.py
+++ b/solution.py
@@ -540,8 +540,14 @@
 
 def pair_rows(v, axis):
     it = other(v, axis)
-    flag = lax.axis_index(axis) == 0
-    return jnp.concatenate([jnp.where(flag, v, it), jnp.where(flag, it, v)], 0)
+    mine = jnp.arange(2)[:, None, None] == lax.axis_index(axis)
+    return jnp.where(mine, v[None], it[None]).reshape(2 * v.shape[0], v.shape[1])
+
+
+def side_by_side(parts, width):
+    return sum(
+        jnp.pad(part, ((0, 0), (at, width - at - part.shape[1]))) for at, part in parts
+    )
 
 
 def near_sum(own, core):
@@ -556,20 +562,20 @@
     return lax.optimization_barrier((value, first))
 
 
-def from_both(along_first, first_axis, along_second, second_axis):
+def from_both(along_first, first_axis, along_second, second_axis, large):
     near = [
         from_offset(part[i], axis, i, 4)
         for i in (1, 3)
         for part, axis in ((along_first, first_axis), (along_second, second_axis))
     ]
-    opposite, near = after((along_first[2], along_second[2]), near)
-    first = [along_first[0], near[0], from_offset(opposite[0], first_axis, 2, 4), near[2]]
-    second = [along_second[0], near[1], from_offset(opposite[1], second_axis, 2, 4), near[3]]
+    opposite = along_first[2], along_second[2]
+    if large:
+        opposite, near = after(opposite, near)
+    far = [from_offset(opposite[0], first_axis, 2, 4), from_offset(opposite[1], second_axis, 2, 4)]
+    near, far = after(near, far)
+    first = [along_first[0], near[0], far[0], near[2]]
+    second = [along_second[0], near[1], far[1], near[3]]
     return first, second
-
-
-def gather_rows(v):
-    return lax.all_gather(pair_rows(v, "yh"), ("x", "z"), axis=0, tiled=True)
 
 
 def scatter_rows(v):
@@ -592,22 +598,21 @@
         [block, lax.axis_index("x"), lax.axis_index("z"), lax.axis_index("yh")]
     ).astype(jnp.int32)
 
-    mlp_own = jnp.concatenate([w_gateup[:, 0], w_gateup[:, 1], w_down.T], 1)
-    mlp_w = gather_rows(mlp_own)
-
     out_t = w_out.T
-    attn_own = jnp.concatenate(
+    attn_own = side_by_side(
         [
-            jnp.zeros((out_t.shape[0], OUT_AT), BF16),
-            out_t[:, :OUT_CUT],
-            w_query,
-            w_keyval,
-            out_t[:, OUT_CUT:],
+            (OUT_AT, out_t[:, :OUT_CUT]),
+            (QUERY_AT, w_query),
+            (KEYVAL_AT, w_keyval),
+            (REST_AT, out_t[:, OUT_CUT:]),
         ],
-        1,
+        ATTN_WIDTH,
     )
     near = other(tokens, "core")
     attn_pair = pair_rows(attn_own, "yh")
+    mlp_own, attn_pair = after((w_gateup[:, 0], w_gateup[:, 1], w_down.T), attn_pair)
+    mlp_own = [(i * hidden_w, part) for i, part in enumerate(mlp_own)]
+    mlp_pair = pair_rows(side_by_side(mlp_own, 3 * hidden_w), "yh")
 
     pair_w = 8 * gains_w
     gain_at = (lax.axis_index("yh") * 4 + block) * gains_w
@@ -618,17 +623,19 @@
     gain_high = gain_part.astype(BF16)
     gain_low = (gain_part - gain_high.astype(F32)).astype(BF16)
     first, second = attn_pair[:, :HALF_WIDTH], attn_pair[:, HALF_WIDTH:]
-    first += jnp.pad(gain_high, ((0, 0), (0, HALF_WIDTH - 2)))
-    first += jnp.pad(gain_low, ((0, 0), (2, HALF_WIDTH - 4)))
+    first += side_by_side([(0, gain_high), (2, gain_low)], HALF_WIDTH)
 
     tokens, (first, near) = after(tokens, (first, near))
     far = other(tokens, "yl")
-    along_z, along_x = from_both([first] * 4, "z", [second] * 4, "x")
-    along_z, along_x, far = lax.optimization_barrier((jnp.stack(along_z), jnp.stack(along_x), far))
+    along_z, along_x = from_both([first] * 4, "z", [second] * 4, "x", False)
+    along_z, along_x, far, mlp_pair = lax.optimization_barrier(
+        (jnp.stack(along_z), jnp.stack(along_x), far, mlp_pair)
+    )
+    mlp_w = lax.all_gather(mlp_pair, ("x", "z"), axis=0, tiled=True)
     token_pieces = [tokens, near, far, other(far, "core")]
     cotangent, far = after(cotangent, far)
     grad_far = other(cotangent, "yl")
-    along_x, along_z = from_both([along_z] * 4, "x", [along_x] * 4, "z")
+    along_x, along_z = from_both([along_z] * 4, "x", [along_x] * 4, "z", True)
 
     positions = jnp.arange(length).astype(F32)
     freqs = rope_base ** (-(jnp.arange(HD // 2).astype(F32) * 2.0 / HD))
@@ -684,16 +691,15 @@
     out_near, back = after(out_near, back)
     result = (middle + out_near + out_far.astype(F32)).astype(BF16)
     parts, late_parts = back[:4], back[4:]
-    late_parts, result = after(late_parts, result)
-    d_far = far_sum(parts[2], parts[3])
-    along_x, along_z = from_both(late_parts[:4], "x", late_parts[4:], "z")
-    along_x, d_far = after(along_x, d_far)
+    d_far = other(far_sum(parts[2], parts[3]), "yl")
+    along_x, along_z = from_both(late_parts[:4], "x", late_parts[4:], "z", True)
+    along_x, (d_far, result) = after(along_x, (d_far, result))
     middle_parts = late_middle(place, along_x, along_z)
-    along_z, along_x = from_both(middle_parts[:4], "z", middle_parts[4:], "x")
+    along_z, along_x = from_both(middle_parts[:4], "z", middle_parts[4:], "x", False)
+    d_h1_own = near_sum(parts[0], parts[1]) + d_far.astype(F32)
+    along_z, (d_h1_own, early) = after(along_z, (d_h1_own, early))
     late_keep, late_send = late_last(place, along_z, along_x)
-    d_h1_own = near_sum(parts[0], parts[1]) + other(d_far, "yl").astype(F32)
-    late_other, (d_h1_own, early) = after(other(late_send, "yh"), (d_h1_own, early))
-    late = late_keep + late_other.astype(F32)
+    late = late_keep + other(late_send, "yh").astype(F32)
 
     normed1, factor1 = norm_rows(tokens.astype(F32))
     d_norm1, _ = norm_back(d_h1_own, normed1, factor1, gain_rows[0])

time: 378 us -> 354 us (0.937)
  the two profiles are of different devices: /device:TPU:1 before, /device:TPU:2 now
where the time goes in v3:
time: 354 us; the launch traced here: 348 us
  waiting for transfers between devices  127 us (36%)
  Pallas kernels  95.4 us (27%)
  starting transfers between devices  69.2 us (20%)
  other arithmetic  26.1 us (7%)
  between operations  14.9 us (4%)
  local copies, waits for them, and re-layouts  14.8 us (4%)
    ppermute x57, waiting for transfers between devices, from_offset(): lax.ppermute(v, axis, [((i + offset) % size, i) for i in range(size)])  127 us
    pallas_call x5, Pallas kernels, kernel_call(): pl.pallas_call(kernel, out_shape=list(small_outs) + list(outs), in_specs=...  89.9 us
    ppermute x57, starting transfers between devices, from_offset(): lax.ppermute(v, axis, [((i + offset) % size, i) for i in range(size)])  69.1 us
    unnamed x78, local copies, waits for them, and re-layouts  7.37 us
  transfers between devices with their start and end apart: 59, of which 26 were waited for; matrix products, arithmetic and copies ran while one was open for 9% of the time, Pallas kernels for 23%

profile of v3, /device:TPU:2, one launch (start us, length us, event | category | flops | bytes accessed | tf_op | source)
XLA Modules:
  0.0 347.7 jit_solution(17952328445177063971)
XLA Ops:
  10.6 3.3 collective-permute-start
  16.5 3.4 collective-permute-done.2
  21.4 4.1 %collective-permute-done.3 = f32[2,96]{0,1:T(8,128)S(1)} collective-permute-done((f32[2,96]{0,1:T(8,128)S(1)}, f32[2,96]{0,1:T(8,128)S(1)}, u32[]{:S(2)}, u32[]{:S(2)}) %collective-permute-start.3) | collective-permute-done | bytes 800 | tf_op jit(solution)/shard_map/ppermute | solution.py:534
  34.9 4.0 %collective-permute-start.5 = (bf16[96,640]{1,0:T(8,128)(2,1)S(1)}, bf16[96,640]{1,0:T(8,128)(2,1)}, u32[]{:S(2)}, u32[]{:S(2)}) collective-permute-start(bf16[96,640]{1,0:T(8,128)(2,1)S(1)} %get-tuple-element.147), channel_id=1, source_target_pairs={{8,0},{16,8},{24,16},{0,24},{9,1},{17,9},{25,17},{1,25},{10,2},{18... | collective-permute-start | bytes 368648 | tf_op jit(solution)/shard_map/ppermute | solution.py:534
  39.0 11.4 %collective-permute-done.12 = bf16[48,3072]{1,0:T(8,128)(2,1)S(1)} collective-permute-done((bf16[48,3072]{1,0:T(8,128)(2,1)S(1)}, bf16[48,3072]{1,0:T(8,128)(2,1)S(1)}, u32[]{:S(2)}, u32[]{:S(2)}) %collective-permute-start.12) | collective-permute-done | bytes 294944 | tf_op jit(solution)/shard_map/ppermute | solution.py:534
  50.4 3.9 %collective-permute-start.9 = (bf16[96,640]{1,0:T(8,128)(2,1)S(1)}, bf16[96,640]{1,0:T(8,128)(2,1)}, u32[]{:S(2)}, u32[]{:S(2)}) collective-permute-start(bf16[96,640]{1,0:T(8,128)(2,1)S(1)} %get-tuple-element.147), channel_id=1, source_target_pairs={{16,0},{24,8},{0,16},{8,24},{17,1},{25,9},{1,17},{9,25},{18,2},{26... | collective-permute-start | bytes 368648 | tf_op jit(solution)/shard_map/ppermute | solution.py:534
  61.8 3.7 %collective-permute-start.16 = (bf16[4,96,640]{2,1,0:T(8,128)(2,1)}, bf16[4,96,640]{2,1,0:T(8,128)(2,1)S(1)}, u32[]{:S(2)}, u32[]{:S(2)}) collective-permute-start(bf16[4,96,640]{2,1,0:T(8,128)(2,1)} %pad_maximum_fusion.1.b0), channel_id=1, source_target_pairs={{8,0},{16,8},{24,16},{0,24},{9,1},{17,9},{25,17},{1,25},{10,2},{18... | collective-permute-start | bytes 1474568 | tf_op jit(solution)/shard_map/ppermute | solution.py:534
  66.9 4.1 %collective-permute-done.15.a1 = bf16[4,96,640]{2,1,0:T(8,128)(2,1)S(1)} collective-permute-done((bf16[4,96,640]{2,1,0:T(8,128)(2,1)}, bf16[4,96,640]{2,1,0:T(8,128)(2,1)S(1)}, u32[]{:S(2)}, u32[]{:S(2)}) %collective-permute-start.15) | collective-permute-done | bytes 491552 | tf_op jit(solution)/shard_map/ppermute | solution.py:534
  72.3 7.2 %collective-permute-done.17.a3 = bf16[4,96,640]{2,1,0:T(8,128)(2,1)} collective-permute-done((bf16[4,96,640]{2,1,0:T(8,128)(2,1)}, bf16[4,96,640]{2,1,0:T(8,128)(2,1)}, u32[]{:S(2)}, u32[]{:S(2)}) %collective-permute-start.17) | collective-permute-done | bytes 491552 | tf_op jit(solution)/shard_map/ppermute | solution.py:534
  79.5 6.6 %collective-permute-start.19 = (bf16[4,96,640]{2,1,0:T(8,128)(2,1)}, bf16[4,96,640]{2,1,0:T(8,128)(2,1)}, u32[]{:S(2)}, u32[]{:S(2)}) collective-permute-start(bf16[4,96,640]{2,1,0:T(8,128)(2,1)} %pad_maximum_fusion.a0), channel_id=1, source_target_pairs={{64,0},{96,32},{0,64},{32,96},{65,1},{97,33},{1,65},{33,97},{66,2}... | collective-permute-start | bytes 1474568 | tf_op jit(solution)/shard_map/ppermute | solution.py:534
  88.5 7.5 %collective-permute-done.19.a2 = bf16[4,96,640]{2,1,0:T(8,128)(2,1)} collective-permute-done((bf16[4,96,640]{2,1,0:T(8,128)(2,1)}, bf16[4,96,640]{2,1,0:T(8,128)(2,1)}, u32[]{:S(2)}, u32[]{:S(2)}) %collective-permute-start.19) | collective-permute-done | bytes 491552 | tf_op jit(solution)/shard_map/ppermute | solution.py:534
  98.0 21.1 %attend.1 = (f32[2,1536]{1,0:T(2,128)}, bf16[1536,1280]{1,0:T(8,128)(2,1)}, bf16[1024,1536]{1,0:T(8,128)(2,1)}, bf16[4,1024,96]{2,1,0:T(8,128)(2,1)}, bf16[2,96,...) custom-call(s32[4]{0:T(128)} %pad_add_fusion.2.place, ...), custom_call_target="tpu_custom_call" | custom-call | flops 1 | bytes 1 | tf_op jit(solution)/shard_map/attend/pallas_call | solution.py:86
  124.7 18.1 %collective-permute-done.23 = bf16[256,1536]{1,0:T(8,128)(2,1)S(1)} collective-permute-done((bf16[256,1536]{1,0:T(8,128)(2,1)S(1)}, bf16[256,1536]{1,0:T(8,128)(2,1)S(1)}, u32[]{:S(2)}, u32[]{:S(2)}) %collective-permute-start.23) | collective-permute-done | bytes 786464 | tf_op jit(solution)/shard_map/ppermute | solution.py:534
  146.7 14.7 %feed.2 = (bf16[512,1024]{1,0:T(8,128)(2,1)}, bf16[512,2048]{1,0:T(8,128)(2,1)}, bf16[256,1536]{1,0:T(8,128)(2,1)}, bf16[256,1536]{1,0:T(8,128)(2,1)}, bf16[256,...) custom-call(s32[4]{0:T(128)} %pad_add_fusion.2.place, bf16[256,1536]{1,0:T(8,128)(2,1)} %copy-done.5, ...), custom_call_target="tpu_custom_call" | custom-call | flops 1 | bytes 1 | tf_op jit(solution)/shard_map/feed/pallas_call | solution.py:86
  161.4 2.4 collective-permute-done.27.h0.h2
  164.0 2.5 collective-permute-done.28.h1.h3
  167.4 14.7 %feed.3 = (bf16[512,1024]{1,0:T(8,128)(2,1)}, bf16[512,2048]{1,0:T(8,128)(2,1)}, bf16[256,1536]{1,0:T(8,128)(2,1)}, bf16[256,1536]{1,0:T(8,128)(2,1)}, bf16[256,...) custom-call(s32[4]{0:T(128)} %pad_add_fusion.2.place, bf16[256,1536]{1,0:T(8,128)(2,1)} %collective-permute-done.27.h0.h2, ...), custom_call_target="tpu_custom_call" | custom-call | flops 1 | bytes 1 | tf_op jit(solution)/shard_map/feed/pallas_call | solution.py:86
  182.4 2.4 collective-permute-done.30
  188.8 15.4 %feed_grads.1 = bf16[1536,3072]{1,0:T(8,128)(2,1)} custom-call(s32[4]{0:T(128)} %pad_add_fusion.2.place, bf16[256,1536]{1,0:T(8,128)(2,1)} %copy-done.5, bf16[256,1536]{1,0:T(8,128)(2,1)} %collective-permute-done.24.h1, bf16[256,1536]{1,0:T(8,128)(2,1)} %collective-permute-done.27.h0.h2, bf16[256,1536]{1,0:T(8,128)(2,1)} %copy-done.8, bf16[256,1536]{1,0:T(8,128)(2,1)} %g0.1, ...), custom_call_target="tpu_custom_call" | custom-call | flops 1 | bytes 1 | tf_op jit(solution)/shard_map/feed_grads/pallas_call | solution.py:86
  204.2 3.0 collective-permute-done.31
  215.0 17.3 %collective-permute-done.32.o2 = bf16[256,1536]{1,0:T(8,128)(2,1)S(1)} collective-permute-done((bf16[256,1536]{1,0:T(8,128)(2,1)S(1)}, bf16[256,1536]{1,0:T(8,128)(2,1)S(1)}, u32[]{:S(2)}, u32[]{:S(2)}) %collective-permute-start.32) | collective-permute-done | bytes 786464 | tf_op jit(solution)/shard_map/ppermute | solution.py:534
  236.0 24.0 %attend_back.1 = (bf16[256,1536]{1,0:T(8,128)(2,1)}, bf16[256,1536]{1,0:T(8,128)(2,1)}, bf16[256,1536]{1,0:T(8,128)(2,1)}, bf16[256,1536]{1,0:T(8,128)(2,1)}, bf...) custom-call(s32[4]{0:T(128)} %pad_add_fusion.2.place, ...), custom_call_target="tpu_custom_call" | custom-call | flops 1 | bytes 1 | tf_op jit(solution)/shard_map/attend_back/pallas_call | solution.py:86
  267.8 9.1 %collective-permute-done.37.refs_1_ = bf16[384,640]{1,0:T(8,128)(2,1)S(1)} collective-permute-done((bf16[384,640]{1,0:T(8,128)(2,1)}, bf16[384,640]{1,0:T(8,128)(2,1)S(1)}, u32[]{:S(2)}, u32[]{:S(2)}) %collective-permute-start.37) | collective-permute-done | bytes 491552 | tf_op jit(solution)/shard_map/ppermute | solution.py:534
  282.9 2.4 add_convert_fusion
  285.3 16.4 %collective-permute-done.41.refs_2_ = bf16[384,640]{1,0:T(8,128)(2,1)} collective-permute-done((bf16[384,640]{1,0:T(8,128)(2,1)S(1)}, bf16[384,640]{1,0:T(8,128)(2,1)}, u32[]{:S(2)}, u32[]{:S(2)}) %collective-permute-start.41) | collective-permute-done | bytes 491552 | tf_op jit(solution)/shard_map/ppermute | solution.py:534
  302.7 3.3 late_middle.1
  312.8 3.1 collective-permute-start.51
  315.9 3.0 collective-permute-start.53
  322.0 2.6 collective-permute-done.53
  326.8 3.0 collective-permute-start.54
  331.4 2.8 fusion.6
  337.5 2.5 collective-permute-done.56
  (230 shorter events, 89.8 us)
Async XLA Ops:
  7.2 139.5 %all-gather.2.cloned.1.call-start = ((), (), s32[]{:S(2)}) async-start(), calls=%async_computation.1 | async-start | bytes 10027008 | tf_op jit(solution)/shard_map/all_gather | solution.py:634
  10.6 15.0 %collective-permute-start = (bf16[48,1280]{1,0:T(8,128)(2,1)S(1)}, bf16[48,1280]{1,0:T(8,128)(2,1)S(1)}, u32[]{:S(2)}, u32[]{:S(2)}) collective-permute-start(bf16[48,1280]{1,0:T(8,128)(2,1)S(1)} %pad_add_fusion.1), channel_id=1, source_target_pairs={{4,0},{0,4},{5,1},{1,5},{6,2},{2,6},{7,3},{3,7},{12,8},{8,12},{13,... | collective-permute-start | bytes 368648 | tf_op jit(solution)/shard_map/ppermute | solution.py:534
  13.9 11.9 %collective-permute-start.4 = (bf16[256,1536]{1,0:T(8,128)(2,1)}, bf16[256,1536]{1,0:T(8,128)(2,1)S(1)}, u32[]{:S(2)}, u32[]{:S(2)}) collective-permute-start(bf16[256,1536]{1,0:T(8,128)(2,1)} %t0.1), channel_id=1, source_target_pairs={{1,0},{0,1},{3,2},{2,3},{5,4},{4,5},{7,6},{6,7},{9,8},{8,9},{11,10... | collective-permute-start | bytes 2359304 | tf_op jit(solution)/shard_map/ppermute | solution.py:534
  25.8 35.3 %collective-permute-start.11 = (bf16[256,1536]{1,0:T(8,128)(2,1)S(1)}, bf16[256,1536]{1,0:T(8,128)(2,1)S(1)}, u32[]{:S(2)}, u32[]{:S(2)}) collective-permute-start(bf16[256,1536]{1,0:T(8,128)(2,1)S(1)} %copy-done), channel_id=1, source_target_pairs={{2,0},{0,2},{3,1},{1,3},{6,4},{4,6},{7,5},{5,7},{10,8},{8,10},{11,... | collective-permute-start | bytes 2359304 | tf_op jit(solution)/shard_map/ppermute | solution.py:534
  26.7 23.7 %collective-permute-start.12 = (bf16[48,3072]{1,0:T(8,128)(2,1)S(1)}, bf16[48,3072]{1,0:T(8,128)(2,1)S(1)}, u32[]{:S(2)}, u32[]{:S(2)}) collective-permute-start(bf16[48,3072]{1,0:T(8,128)(2,1)S(1)} %pad_add_fusion), channel_id=1, source_target_pairs={{4,0},{0,4},{5,1},{1,5},{6,2},{2,6},{7,3},{3,7},{12,8},{8,12},{13,... | collective-permute-start | bytes 884744 | tf_op jit(solution)/shard_map/ppermute | solution.py:534
  32.0 23.3 %collective-permute-start.8 = (bf16[96,640]{1,0:T(8,128)(2,1)S(1)}, bf16[96,640]{1,0:T(8,128)(2,1)}, u32[]{:S(2)}, u32[]{:S(2)}) collective-permute-start(bf16[96,640]{1,0:T(8,128)(2,1)S(1)} %get-tuple-element.312), channel_id=1, source_target_pairs={{96,0},{0,32},{32,64},{64,96},{97,1},{1,33},{33,65},{65,97},{98,2}... | collective-permute-start | bytes 368648 | tf_op jit(solution)/shard_map/ppermute | solution.py:534
  34.9 20.4 %collective-permute-start.5 = (bf16[96,640]{1,0:T(8,128)(2,1)S(1)}, bf16[96,640]{1,0:T(8,128)(2,1)}, u32[]{:S(2)}, u32[]{:S(2)}) collective-permute-start(bf16[96,640]{1,0:T(8,128)(2,1)S(1)} %get-tuple-element.147), channel_id=1, source_target_pairs={{8,0},{16,8},{24,16},{0,24},{9,1},{17,9},{25,17},{1,25},{10,2},{18... | collective-permute-start | bytes 368648 | tf_op jit(solution)/shard_map/ppermute | solution.py:534
  39.0 16.3 %collective-permute-start.7 = (bf16[96,640]{1,0:T(8,128)(2,1)S(1)}, bf16[96,640]{1,0:T(8,128)(2,1)}, u32[]{:S(2)}, u32[]{:S(2)}) collective-permute-start(bf16[96,640]{1,0:T(8,128)(2,1)S(1)} %get-tuple-element.147), channel_id=1, source_target_pairs={{24,0},{0,8},{8,16},{16,24},{25,1},{1,9},{9,17},{17,25},{26,2},{2,... | collective-permute-start | bytes 368648 | tf_op jit(solution)/shard_map/ppermute | solution.py:534
  61.1 249.0 %reduce-scatter.2.cloned.1.call-start = ((), (), s32[]{:S(2)}) async-start(), calls=%async_computation.2 | async-start | bytes 10027008 | tf_op jit(solution)/shard_map/reduce_scatter | solution.py:582
  65.4 14.1 %collective-permute-start.17 = (bf16[4,96,640]{2,1,0:T(8,128)(2,1)}, bf16[4,96,640]{2,1,0:T(8,128)(2,1)}, u32[]{:S(2)}, u32[]{:S(2)}) collective-permute-start(bf16[4,96,640]{2,1,0:T(8,128)(2,1)} %pad_maximum_fusion.a0), channel_id=1, source_target_pairs={{96,0},{0,32},{32,64},{64,96},{97,1},{1,33},{33,65},{65,97},{98,2}... | collective-permute-start | bytes 1474568 | tf_op jit(solution)/shard_map/ppermute | solution.py:534
  66.9 12.6 %collective-permute-start.18 = (bf16[4,96,640]{2,1,0:T(8,128)(2,1)}, bf16[4,96,640]{2,1,0:T(8,128)(2,1)}, u32[]{:S(2)}, u32[]{:S(2)}) collective-permute-start(bf16[4,96,640]{2,1,0:T(8,128)(2,1)} %pad_maximum_fusion.1.b0), channel_id=1, source_target_pairs={{24,0},{0,8},{8,16},{16,24},{25,1},{1,9},{9,17},{17,25},{26,2},{2,... | collective-permute-start | bytes 1474568 | tf_op jit(solution)/shard_map/ppermute | solution.py:534
  66.9 30.2 %collective-permute-start.14 = (bf16[256,1536]{1,0:T(8,128)(2,1)S(1)}, bf16[256,1536]{1,0:T(8,128)(2,1)S(1)}, u32[]{:S(2)}, u32[]{:S(2)}) collective-permute-start(bf16[256,1536]{1,0:T(8,128)(2,1)S(1)} %collective-permute-done.11.t2), channel_id=1, source_target_pairs={{1,0},{0,1},{3,2},{2,3},{5,4},{4,5},{7,6},{6,7},{9,8},{8,9},{11,10... | collective-permute-start | bytes 2359304 | tf_op jit(solution)/shard_map/ppermute | solution.py:534
  71.1 48.2 %collective-permute-start.13 = (bf16[256,1536]{1,0:T(8,128)(2,1)S(1)}, bf16[256,1536]{1,0:T(8,128)(2,1)}, u32[]{:S(2)}, u32[]{:S(2)}) collective-permute-start(bf16[256,1536]{1,0:T(8,128)(2,1)S(1)} %copy-done.3), channel_id=1, source_target_pairs={{2,0},{0,2},{3,1},{1,3},{6,4},{4,6},{7,5},{5,7},{10,8},{8,10},{11,... | collective-permute-start | bytes 2359304 | tf_op jit(solution)/shard_map/ppermute | solution.py:534
  79.5 16.4 %collective-permute-start.19 = (bf16[4,96,640]{2,1,0:T(8,128)(2,1)}, bf16[4,96,640]{2,1,0:T(8,128)(2,1)}, u32[]{:S(2)}, u32[]{:S(2)}) collective-permute-start(bf16[4,96,640]{2,1,0:T(8,128)(2,1)} %pad_maximum_fusion.a0), channel_id=1, source_target_pairs={{64,0},{96,32},{0,64},{32,96},{65,1},{97,33},{1,65},{33,97},{66,2}... | collective-permute-start | bytes 1474568 | tf_op jit(solution)/shard_map/ppermute | solution.py:534
  123.2 19.7 %collective-permute-start.23 = (bf16[256,1536]{1,0:T(8,128)(2,1)S(1)}, bf16[256,1536]{1,0:T(8,128)(2,1)S(1)}, u32[]{:S(2)}, u32[]{:S(2)}) collective-permute-start(bf16[256,1536]{1,0:T(8,128)(2,1)S(1)} %add_convert_fusion.4), channel_id=1, source_target_pairs={{2,0},{0,2},{3,1},{1,3},{6,4},{4,6},{7,5},{5,7},{10,8},{8,10},{11,... | collective-permute-start | bytes 2359304 | tf_op jit(solution)/shard_map/ppermute | solution.py:534
  124.7 21.2 %collective-permute-start.25 = (bf16[256,1536]{1,0:T(8,128)(2,1)S(1)}, bf16[256,1536]{1,0:T(8,128)(2,1)S(1)}, u32[]{:S(2)}, u32[]{:S(2)}) collective-permute-start(bf16[256,1536]{1,0:T(8,128)(2,1)S(1)} %copy-done.3), channel_id=1, source_target_pairs={{1,0},{0,1},{3,2},{2,3},{5,4},{4,5},{7,6},{6,7},{9,8},{8,9},{11,10... | collective-permute-start | bytes 2359304 | tf_op jit(solution)/shard_map/ppermute | solution.py:534
  143.8 20.1 %collective-permute-start.27 = (bf16[256,1536]{1,0:T(8,128)(2,1)S(1)}, bf16[256,1536]{1,0:T(8,128)(2,1)}, u32[]{:S(2)}, u32[]{:S(2)}) collective-permute-start(bf16[256,1536]{1,0:T(8,128)(2,1)S(1)} %multiply_convert_fusion.h0), channel_id=1, source_target_pairs={{2,0},{0,2},{3,1},{1,3},{6,4},{4,6},{7,5},{5,7},{10,8},{8,10},{11,... | collective-permute-start | bytes 2359304 | tf_op jit(solution)/shard_map/ppermute | solution.py:534
  145.3 18.7 %collective-permute-start.29 = (bf16[256,1536]{1,0:T(8,128)(2,1)}, bf16[256,1536]{1,0:T(8,128)(2,1)}, u32[]{:S(2)}, u32[]{:S(2)}) collective-permute-start(bf16[256,1536]{1,0:T(8,128)(2,1)} %collective-permute-done.13.g0.g2), channel_id=1, source_target_pairs={{1,0},{0,1},{3,2},{2,3},{5,4},{4,5},{7,6},{6,7},{9,8},{8,9},{11,10... | collective-permute-start | bytes 2359304 | tf_op jit(solution)/shard_map/ppermute | solution.py:534
  187.0 20.2 %collective-permute-start.31 = (bf16[256,1536]{1,0:T(8,128)(2,1)}, bf16[256,1536]{1,0:T(8,128)(2,1)S(1)}, u32[]{:S(2)}, u32[]{:S(2)}) collective-permute-start(bf16[256,1536]{1,0:T(8,128)(2,1)} %add_convert_fusion.3), channel_id=1, source_target_pairs={{2,0},{0,2},{3,1},{1,3},{6,4},{4,6},{7,5},{5,7},{10,8},{8,10},{11,... | collective-permute-start | bytes 2359304 | tf_op jit(solution)/shard_map/ppermute | solution.py:534
  212.7 19.6 %collective-permute-start.32 = (bf16[256,1536]{1,0:T(8,128)(2,1)S(1)}, bf16[256,1536]{1,0:T(8,128)(2,1)S(1)}, u32[]{:S(2)}, u32[]{:S(2)}) collective-permute-start(bf16[256,1536]{1,0:T(8,128)(2,1)S(1)} %get-tuple-element.205.o0), channel_id=1, source_target_pairs={{2,0},{0,2},{3,1},{1,3},{6,4},{4,6},{7,5},{5,7},{10,8},{8,10},{11,... | collective-permute-start | bytes 2359304 | tf_op jit(solution)/shard_map/ppermute | solution.py:534
  214.2 18.2 %collective-permute-start.34 = (bf16[256,1536]{1,0:T(8,128)(2,1)S(1)}, bf16[256,1536]{1,0:T(8,128)(2,1)S(1)}, u32[]{:S(2)}, u32[]{:S(2)}) collective-permute-start(bf16[256,1536]{1,0:T(8,128)(2,1)S(1)} %copy-done.35), channel_id=1, source_target_pairs={{1,0},{0,1},{3,2},{2,3},{5,4},{4,5},{7,6},{6,7},{9,8},{8,9},{11,10... | collective-permute-start | bytes 2359304 | tf_op jit(solution)/shard_map/ppermute | solution.py:534
  214.4 19.8 %collective-permute-start.35 = (bf16[256,1536]{1,0:T(8,128)(2,1)S(1)}, bf16[256,1536]{1,0:T(8,128)(2,1)S(1)}, u32[]{:S(2)}, u32[]{:S(2)}) collective-permute-start(bf16[256,1536]{1,0:T(8,128)(2,1)S(1)} %get-tuple-element.205.o0), channel_id=1, source_target_pairs={{1,0},{0,1},{3,2},{2,3},{5,4},{4,5},{7,6},{6,7},{9,8},{8,9},{11,10... | collective-permute-start | bytes 2359304 | tf_op jit(solution)/shard_map/ppermute | solution.py:534
  260.7 22.2 %collective-permute-start.45 = (bf16[256,1536]{1,0:T(8,128)(2,1)}, bf16[256,1536]{1,0:T(8,128)(2,1)}, u32[]{:S(2)}, u32[]{:S(2)}) collective-permute-start(bf16[256,1536]{1,0:T(8,128)(2,1)} %add_convert_fusion.2), channel_id=1, source_target_pairs={{2,0},{0,2},{3,1},{1,3},{6,4},{4,6},{7,5},{5,7},{10,8},{8,10},{11,... | collective-permute-start | bytes 2359304 | tf_op jit(solution)/shard_map/ppermute | solution.py:534
  262.2 14.7 %collective-permute-start.37 = (bf16[384,640]{1,0:T(8,128)(2,1)}, bf16[384,640]{1,0:T(8,128)(2,1)S(1)}, u32[]{:S(2)}, u32[]{:S(2)}) collective-permute-start(bf16[384,640]{1,0:T(8,128)(2,1)} %get-tuple-element.232), channel_id=1, source_target_pairs={{32,0},{64,32},{96,64},{0,96},{33,1},{65,33},{97,65},{1,97},{34,2}... | collective-permute-start | bytes 1474568 | tf_op jit(solution)/shard_map/ppermute | solution.py:534
  262.7 15.1 %collective-permute-start.38 = (bf16[4,96,640]{2,1,0:T(8,128)(2,1)}, bf16[4,96,640]{2,1,0:T(8,128)(2,1)}, u32[]{:S(2)}, u32[]{:S(2)}) collective-permute-start(bf16[4,96,640]{2,1,0:T(8,128)(2,1)} %get-tuple-element.233), channel_id=1, source_target_pairs={{8,0},{16,8},{24,16},{0,24},{9,1},{17,9},{25,17},{1,25},{10,2},{18... | collective-permute-start | bytes 1474568 | tf_op jit(solution)/shard_map/ppermute | solution.py:534
  263.9 14.0 %collective-permute-start.39 = (bf16[384,640]{1,0:T(8,128)(2,1)}, bf16[384,640]{1,0:T(8,128)(2,1)}, u32[]{:S(2)}, u32[]{:S(2)}) collective-permute-start(bf16[384,640]{1,0:T(8,128)(2,1)} %get-tuple-element.234), channel_id=1, source_target_pairs={{96,0},{0,32},{32,64},{64,96},{97,1},{1,33},{33,65},{65,97},{98,2}... | collective-permute-start | bytes 1474568 | tf_op jit(solution)/shard_map/ppermute | solution.py:534
  265.3 14.0 %collective-permute-start.40 = (bf16[4,96,640]{2,1,0:T(8,128)(2,1)}, bf16[4,96,640]{2,1,0:T(8,128)(2,1)}, u32[]{:S(2)}, u32[]{:S(2)}) collective-permute-start(bf16[4,96,640]{2,1,0:T(8,128)(2,1)} %get-tuple-element.235), channel_id=1, source_target_pairs={{24,0},{0,8},{8,16},{16,24},{25,1},{1,9},{9,17},{17,25},{26,2},{2,... | collective-permute-start | bytes 1474568 | tf_op jit(solution)/shard_map/ppermute | solution.py:534
  276.9 25.8 %collective-permute-start.44 = (bf16[256,1536]{1,0:T(8,128)(2,1)S(1)}, bf16[256,1536]{1,0:T(8,128)(2,1)}, u32[]{:S(2)}, u32[]{:S(2)}) collective-permute-start(bf16[256,1536]{1,0:T(8,128)(2,1)S(1)} %add_convert_fusion.1), channel_id=1, source_target_pairs={{2,0},{0,2},{3,1},{1,3},{6,4},{4,6},{7,5},{5,7},{10,8},{8,10},{11,... | collective-permute-start | bytes 2359304 | tf_op jit(solution)/shard_map/ppermute | solution.py:534
  277.8 33.3 %collective-permute-start.52 = (bf16[256,1536]{1,0:T(8,128)(2,1)}, bf16[256,1536]{1,0:T(8,128)(2,1)}, u32[]{:S(2)}, u32[]{:S(2)}) collective-permute-start(bf16[256,1536]{1,0:T(8,128)(2,1)} %get-tuple-element.269), channel_id=1, source_target_pairs={{1,0},{0,1},{3,2},{2,3},{5,4},{4,5},{7,6},{6,7},{9,8},{8,9},{11,10... | collective-permute-start | bytes 2359304 | tf_op jit(solution)/shard_map/ppermute | solution.py:534
  279.4 22.3 %collective-permute-start.41 = (bf16[384,640]{1,0:T(8,128)(2,1)S(1)}, bf16[384,640]{1,0:T(8,128)(2,1)}, u32[]{:S(2)}, u32[]{:S(2)}) collective-permute-start(bf16[384,640]{1,0:T(8,128)(2,1)S(1)} %copy-done.37), channel_id=1, source_target_pairs={{64,0},{96,32},{0,64},{32,96},{65,1},{97,33},{1,65},{33,97},{66,2}... | collective-permute-start | bytes 1474568 | tf_op jit(solution)/shard_map/ppermute | solution.py:534
  281.6 21.1 %collective-permute-start.42 = (bf16[4,96,640]{2,1,0:T(8,128)(2,1)S(1)}, bf16[4,96,640]{2,1,0:T(8,128)(2,1)}, u32[]{:S(2)}, u32[]{:S(2)}) collective-permute-start(bf16[4,96,640]{2,1,0:T(8,128)(2,1)S(1)} %copy-done.36), channel_id=1, source_target_pairs={{16,0},{24,8},{0,16},{8,24},{17,1},{25,9},{1,17},{9,25},{18,2},{26... | collective-permute-start | bytes 1474568 | tf_op jit(solution)/shard_map/ppermute | solution.py:534
  309.4 11.3 %collective-permute-start.49 = (bf16[96,640]{1,0:T(8,128)(2,1)}, bf16[96,640]{1,0:T(8,128)(2,1)S(1)}, u32[]{:S(2)}, u32[]{:S(2)}) collective-permute-start(bf16[96,640]{1,0:T(8,128)(2,1)} %get-tuple-element.262), channel_id=1, source_target_pairs={{96,0},{0,32},{32,64},{64,96},{97,1},{1,33},{33,65},{65,97},{98,2}... | collective-permute-start | bytes 368648 | tf_op jit(solution)/shard_map/ppermute | solution.py:534
  (65 other events, 583.7 us)
Sparse Core Ops, SparseCore 0:
  61.2 84.9 all-gather.1
  207.3 93.7 reduce-scatter.1

commit v4 on v3

--- a/solution.py
+++ b/solution.py
@@ -218,13 +218,12 @@
         36, 11, heads)
 
 
-def attend_back_kernel(place, cos_ref, sin_ref, gain2_ref,
-                       o0, o1, o2, o3, t0, t1, t2, t3, w_hbm, h_hbm, q_hbm, kt_hbm,
-                       v_hbm, attn_hbm, attnt_hbm, probs_hbm,
-                       c0, c1, c2, c3, x0, x1, x2, x3, y0, y1, y2, y3,
-                       o_ref, t_ref, w_ref, h_ref, q_ref, kt_ref, v_ref,
-                       attn_ref, attnt_ref, probs_ref,
-                       do_ref, dot_ref, dqkv_ref, part_ref, first_ref, second_ref,
+def attend_back_kernel(place, cos_ref, sin_ref,
+                       o0, o1, o2, o3, w_hbm, h_hbm, q_hbm, kt_hbm, v_hbm, attn_hbm, attnt_hbm,
+                       probs_hbm,
+                       dqkv_hbm, x0, x1, x2, x3, y0, y1, y2, y3,
+                       o_ref, w_ref, h_ref, q_ref, kt_ref, v_ref, attn_ref, attnt_ref, probs_ref,
+                       do_ref, dot_ref, dqkv_ref, first_ref, second_ref,
                        delta_ref, dk_ref, dv_ref, turned_ref, in_sem, out_sem, probs_sem):
     block, ix, iz = place[0], place[1], place[2]
     heads, length, _ = q_ref.shape
@@ -235,40 +234,44 @@
     width = w_ref.shape[0]
     heads_w = heads * HD
     fetch, store = Moves(in_sem), Moves(out_sem)
-    early = [fetch.start(w_hbm, w_ref)]
+    rest_w = ATTN_WIDTH - REST_AT
+    early = [
+        fetch.start(w_hbm.at[:, pl.ds(OUT_AT, OUT_CUT)], w_ref.at[:, pl.ds(0, OUT_CUT)]),
+        fetch.start(w_hbm.at[:, pl.ds(REST_AT, rest_w)], w_ref.at[:, pl.ds(OUT_CUT, rest_w)]),
+    ]
     early += [
         fetch.start(piece, o_ref.at[pl.ds(i * size, size), :])
         for i, piece in enumerate((o0, o1, o2, o3))
     ]
-    for source, target in ((attnt_hbm, attnt_ref), (v_hbm, v_ref), (q_hbm, q_ref),
-                           (kt_hbm, kt_ref)):
-        early.append(fetch.start(source, target))
 
     def probs_copy(head):
         return pltpu.make_async_copy(probs_hbm.at[head], probs_ref.at[head], probs_sem.at[head])
 
+    middle = [
+        fetch.start(source, target)
+        for source, target in ((attnt_hbm, attnt_ref), (v_hbm, v_ref), (q_hbm, q_ref),
+                               (kt_hbm, kt_ref))
+    ]
     for head in range(heads):
         probs_copy(head).start()
     later = [fetch.start(attn_hbm, attn_ref), fetch.start(h_hbm, h_ref)]
-    later += [fetch.start(piece, t_ref.at[i]) for i, piece in enumerate((t0, t1, t2, t3))]
-    early[0].wait()
+    dk_ref[...] = jnp.zeros_like(dk_ref)
+    dv_ref[...] = jnp.zeros_like(dv_ref)
+    for copy in early[:2]:
+        copy.wait()
     for step in range(4):
         at = block_at(lax.bitwise_xor(block, step), size)
-        early[1 + step].wait()
-        grad_in = o_ref[step * size : (step + 1) * size, :]
-        grad = jnp.concatenate(
-            [dot_n(grad_in, w_ref[:, OUT_AT:QUERY_AT]), dot_n(grad_in, w_ref[:, REST_AT:])], 1)
+        early[2 + step].wait()
+        grad = dot_n(o_ref[step * size : (step + 1) * size, :], w_ref[...])
         grad_t = grad.T.astype(BF16)
         grad = grad.astype(BF16)
         for head in range(heads):
             dot_ref[head, :, at] = grad_t[head * HD : (head + 1) * HD]
             do_ref[head, at, :] = grad[:, head * HD : (head + 1) * HD]
-    for copy in early[5:]:
+    for copy in middle:
         copy.wait()
     delta_ref[...] = jnp.sum(
         attnt_ref[...].astype(F32) * dot_ref[...].astype(F32), 1, keepdims=True)
-    dk_ref[...] = jnp.zeros_like(dk_ref)
-    dv_ref[...] = jnp.zeros_like(dv_ref)
 
     def turned_back(field, cosine, sine):
         first, second = field[:half], field[half:]
@@ -297,28 +300,17 @@
             dk_ref[group].T * SCALE, cos_ref[...], sin_ref[...])
         turned_ref[heads + 2 * group + 1] = dv_ref[group].T
     dqkv_ref[...] = turned_ref[...].reshape((heads + 2 * groups) * HD, length).T.astype(BF16)
+    store.start(dqkv_ref, dqkv_hbm)
     for copy in later:
         copy.wait()
-
-    gain = jnp.zeros((1, width), F32)
-    for step, out in ((1, c1), (3, c3), (2, c2), (0, c0)):
-        at = block_at(lax.bitwise_xor(block, step), size)
-        part = dot_t(dqkv_ref[at, :], w_ref[:, QUERY_AT:REST_AT])
-        value = t_ref[step].astype(F32)
-        factor = lax.rsqrt(jnp.mean(value * value, -1, keepdims=True) + norm_eps)
-        gain += jnp.sum(part * (value * factor), 0, keepdims=True)
-        part_ref[step] = part.astype(BF16)
-        store.start(part_ref.at[step], out)
 
     rows = width // 16
     part = dot_tn(h_ref[...], dqkv_ref[...]).astype(BF16)
     first_ref[:, :heads_w] = part[:, :heads_w]
     second_ref[:, LATE_WIDTH - heads_w :] = part[:, heads_w:]
     part = dot_tn(o_ref[...], attn_ref[...]).astype(BF16)
-    first_ref[:, heads_w : heads_w + LATE_OUT] = part[:, :LATE_OUT]
+    first_ref[:, heads_w:] = part[:, :LATE_OUT]
     second_ref[:, : heads_w - LATE_OUT] = part[:, LATE_OUT:]
-    gains = jnp.concatenate([gain, gain2_ref[...], jnp.zeros((126, width), F32)], 0)
-    first_ref[:, heads_w + LATE_OUT :] = gains.T.astype(BF16)
     for offset, (x_out, y_out) in enumerate(((x0, y0), (x1, y1), (x2, y2), (x3, y3))):
         to_x = lax.rem(ix + 4 - offset, 4)
         to_z = lax.rem(iz + 4 - offset, 4)
@@ -328,26 +320,50 @@
     store.wait()
 
 
-def attend_back(place, cosine, sine, gain_two, pieces, token_pieces, weights, h_first,
-                q, kt, v, attn, attnt, probs):
+def attend_back(place, cosine, sine, pieces, weights, h_first, q, kt, v, attn, attnt, probs):
     size, width = pieces[0].shape
     heads, length, _ = q.shape
     groups = v.shape[0]
     every = heads + 2 * groups
     rows = width // 16
-    outs = [(size, width)] * 4 + [(4 * rows, LATE_WIDTH)] * 4 + [(4, rows, LATE_WIDTH)] * 4
+    outs = [(length, every * HD)] + [(4 * rows, LATE_WIDTH)] * 4 + [(4, rows, LATE_WIDTH)] * 4
     scratch = [
-        (length, width), (4, size, width), (width, ATTN_WIDTH), (length, width),
+        (length, width), (width, heads * HD), (length, width),
         q.shape, kt.shape, v.shape, attn.shape, attnt.shape, probs.shape,
-        (heads, length, HD), (heads, HD, length), (length, every * HD), (4, size, width),
+        (heads, length, HD), (heads, HD, length), (length, every * HD),
         (width, LATE_WIDTH), (width, LATE_WIDTH),
     ]
     wide = [(heads, 1, length), (groups, length, HD), (groups, length, HD), (every, HD, length)]
     return kernel_call(
-        attend_back_kernel, "attend_back", place, (cosine, sine, gain_two),
-        (*pieces, *token_pieces, weights, h_first, q, kt, v, attn, attnt, probs),
+        attend_back_kernel, "attend_back", place, (cosine, sine),
+        (*pieces, weights, h_first, q, kt, v, attn, attnt, probs),
         [like(s) for s in outs], [],
-        [vmem(s) for s in scratch] + [vmem(s, F32) for s in wide], 15, 24, heads)
+        [vmem(s) for s in scratch] + [vmem(s, F32) for s in wide], 12, 21, heads)
+
+
+def project_back_kernel(place, dqkv_hbm, w_hbm, c0, c1, c2, c3,
+                        dqkv_ref, w_ref, part_ref, in_sem, out_sem):
+    block = place[0]
+    size = part_ref.shape[1]
+    fetch, store = Moves(in_sem), Moves(out_sem)
+    fetch.start(w_hbm.at[:, pl.ds(QUERY_AT, REST_AT - QUERY_AT)], w_ref)
+    fetch.start(dqkv_hbm, dqkv_ref)
+    fetch.wait()
+    for step, out in ((3, c3), (2, c2), (1, c1), (0, c0)):
+        at = block_at(lax.bitwise_xor(block, step), size)
+        part_ref[step] = dot_t(dqkv_ref[at, :], w_ref[...]).astype(BF16)
+        store.start(part_ref.at[step], out)
+    store.wait()
+
+
+def project_back(place, d_qkv, weights):
+    length, every_w = d_qkv.shape
+    width = weights.shape[0]
+    size = length // 4
+    return kernel_call(
+        project_back_kernel, "project_back", place, (), (d_qkv, weights),
+        [like((size, width))] * 4, [],
+        [vmem(s) for s in (d_qkv.shape, (width, every_w), (4, size, width))], 2, 4)
 
 
 def feed_kernel(place, h0, h1, g0, g1, w_hbm, hidden_hbm, dgu_hbm, b0, b1, r0, r1,
@@ -459,7 +475,7 @@
         [like((width, 3 * hidden_w))], [], [vmem(s) for s in scratch], 20, 6)[0]
 
 
-LATE_OUT, LATE_WIDTH = 128, 640
+LATE_OUT, LATE_WIDTH = 192, 576
 
 
 def late_middle_kernel(place, *refs):
@@ -527,7 +543,7 @@
 def norm_back(grad_in, normed, factor, gain_row):
     grad_normed = grad_in * gain_row
     inner = jnp.mean(grad_normed * normed, -1, keepdims=True)
-    return (factor * (grad_normed - normed * inner), jnp.sum(grad_in * normed, 0))
+    return factor * (grad_normed - normed * inner)
 
 
 def from_offset(v, axis, offset, size):
@@ -562,7 +578,7 @@
     return lax.optimization_barrier((value, first))
 
 
-def from_both(along_first, first_axis, along_second, second_axis, large):
+def from_both(along_first, first_axis, along_second, second_axis, large, beside=()):
     near = [
         from_offset(part[i], axis, i, 4)
         for i in (1, 3)
@@ -570,12 +586,12 @@
     ]
     opposite = along_first[2], along_second[2]
     if large:
-        opposite, near = after(opposite, near)
+        opposite, (near, beside) = after(opposite, (near, beside))
     far = [from_offset(opposite[0], first_axis, 2, 4), from_offset(opposite[1], second_axis, 2, 4)]
     near, far = after(near, far)
     first = [along_first[0], near[0], far[0], near[2]]
     second = [along_second[0], near[1], far[1], near[3]]
-    return first, second
+    return first, second, beside
 
 
 def scatter_rows(v):
@@ -608,9 +624,8 @@
         ],
         ATTN_WIDTH,
     )
-    near = other(tokens, "core")
     attn_pair = pair_rows(attn_own, "yh")
-    mlp_own, attn_pair = after((w_gateup[:, 0], w_gateup[:, 1], w_down.T), attn_pair)
+    mlp_own = (w_gateup[:, 0], w_gateup[:, 1], w_down.T)
     mlp_own = [(i * hidden_w, part) for i, part in enumerate(mlp_own)]
     mlp_pair = pair_rows(side_by_side(mlp_own, 3 * hidden_w), "yh")
 
@@ -620,22 +635,24 @@
     for axis in ("core", "yl", "yh"):
         gain_part = gain_part + other(gain_part, axis)
     gain_part = gain_part.T
-    gain_high = gain_part.astype(BF16)
-    gain_low = (gain_part - gain_high.astype(F32)).astype(BF16)
+    gain_high = lax.reduce_precision(gain_part, 8, 7)
+    gain_low = (gain_part - gain_high).astype(BF16)
+    gain_high = gain_high.astype(BF16)
     first, second = attn_pair[:, :HALF_WIDTH], attn_pair[:, HALF_WIDTH:]
     first += side_by_side([(0, gain_high), (2, gain_low)], HALF_WIDTH)
 
-    tokens, (first, near) = after(tokens, (first, near))
-    far = other(tokens, "yl")
-    along_z, along_x = from_both([first] * 4, "z", [second] * 4, "x", False)
-    along_z, along_x, far, mlp_pair = lax.optimization_barrier(
-        (jnp.stack(along_z), jnp.stack(along_x), far, mlp_pair)
+    first, mlp_pair = after(first, mlp_pair)
+    along_z, along_x, _ = from_both([first] * 4, "z", [second] * 4, "x", False)
+    along_z, along_x, mlp_pair, tokens = lax.optimization_barrier(
+        (jnp.stack(along_z), jnp.stack(along_x), mlp_pair, tokens)
     )
     mlp_w = lax.all_gather(mlp_pair, ("x", "z"), axis=0, tiled=True)
-    token_pieces = [tokens, near, far, other(far, "core")]
+    along_x, along_z, far = from_both(
+        [along_z] * 4, "x", [along_x] * 4, "z", True, other(tokens, "yl")
+    )
+    token_pieces = [tokens, other(tokens, "core"), far, other(far, "core")]
     cotangent, far = after(cotangent, far)
     grad_far = other(cotangent, "yl")
-    along_x, along_z = from_both([along_z] * 4, "x", [along_x] * 4, "z", True)
 
     positions = jnp.arange(length).astype(F32)
     freqs = rope_base ** (-(jnp.arange(HD // 2).astype(F32) * 2.0 / HD))
@@ -675,7 +692,7 @@
     early = scatter_rows(mlp_grads)
     out_far = far_sum(out_chip, out_diag)
 
-    d_norm2, gain_two = norm_back(d_h2_own, normed2, factor2, gain_rows[1])
+    d_norm2 = norm_back(d_h2_own, normed2, factor2, gain_rows[1])
     d_middle = cotangent.astype(F32) + d_norm2
     d_out = d_middle.astype(BF16)
     d_out_far = other(d_out, "yl")
@@ -685,39 +702,48 @@
     out_far = other(out_far, "yl")
 
     back = attend_back(
-        place, cosine, sine, gain_two[None], out_pieces, token_pieces, attn_w,
-        h_first, q, kt, v, attn, attnt, probs,
-    )
-    out_near, back = after(out_near, back)
+        place, cosine, sine, out_pieces, attn_w, h_first, q, kt, v, attn, attnt, probs
+    )
+    d_qkv, *late_parts = back
+    d_qkv, out_far = after(d_qkv, out_far)
+    along_x, along_z, parts = from_both(
+        late_parts[:4], "x", late_parts[4:], "z", True, project_back(place, d_qkv, attn_w)
+    )
+    d_far = other(far_sum(parts[2], parts[3]), "yl")
     result = (middle + out_near + out_far.astype(F32)).astype(BF16)
-    parts, late_parts = back[:4], back[4:]
-    d_far = other(far_sum(parts[2], parts[3]), "yl")
-    along_x, along_z = from_both(late_parts[:4], "x", late_parts[4:], "z", True)
-    along_x, (d_far, result) = after(along_x, (d_far, result))
+    along_x, result = after(along_x, result)
     middle_parts = late_middle(place, along_x, along_z)
-    along_z, along_x = from_both(middle_parts[:4], "z", middle_parts[4:], "x", False)
+    along_z, along_x, _ = from_both(middle_parts[:4], "z", middle_parts[4:], "x", False)
     d_h1_own = near_sum(parts[0], parts[1]) + d_far.astype(F32)
     along_z, (d_h1_own, early) = after(along_z, (d_h1_own, early))
     late_keep, late_send = late_last(place, along_z, along_x)
     late = late_keep + other(late_send, "yh").astype(F32)
 
     normed1, factor1 = norm_rows(tokens.astype(F32))
-    d_norm1, _ = norm_back(d_h1_own, normed1, factor1, gain_rows[0])
+    d_norm1 = norm_back(d_h1_own, normed1, factor1, gain_rows[0])
     input_grad = (d_middle + d_norm1).astype(BF16)
 
-    out_at = heads_w + LATE_OUT
-    grad_out = jnp.concatenate([late[:, heads_w:out_at], late[:, LATE_WIDTH : LATE_WIDTH + heads_w - LATE_OUT]], 1)
-    gain_sum = late[:, out_at : out_at + 2].T
+    grad_query = late[:, :heads_w]
+    grad_keyval = late[:, 2 * LATE_WIDTH - heads_w :]
+    grad_out = late[:, heads_w : 2 * LATE_WIDTH - heads_w].T
+    grad_gateup = early[:, : 2 * hidden_w].reshape(-1, 2, hidden_w)
+
+    gain_sum = jnp.stack(
+        [
+            jnp.sum(grad_query * w_query.astype(F32) + grad_keyval * w_keyval.astype(F32), 1),
+            jnp.sum(grad_gateup * w_gateup.astype(F32), (1, 2)),
+        ]
+    )
     for axis in ("core", "yl"):
         gain_sum = gain_sum + other(gain_sum, axis)
-    grad_gains = lax.dynamic_slice(gain_sum, (0, block * gains_w), (2, gains_w))
+    grad_gains = lax.dynamic_slice(gain_sum, (0, block * gains_w), (2, gains_w)) / norm_gains
     return (
         result,
         input_grad,
-        late[:, :heads_w],
-        late[:, 2 * LATE_WIDTH - heads_w :],
-        grad_out.T,
-        early[:, : 2 * hidden_w].reshape(-1, 2, hidden_w),
+        grad_query,
+        grad_keyval,
+        grad_out,
+        grad_gateup,
         early[:, 2 * hidden_w :].T,
         grad_gains,
     )

time: 354 us -> 351 us (level)
  the two profiles are of different devices: /device:TPU:2 before, /device:TPU:1 now
where the time goes in v4:
time: 351 us; the launch traced here: 345 us
  waiting for transfers between devices  115 us (33%)
  Pallas kernels  97.5 us (28%)
  starting transfers between devices  79.3 us (23%)
  other arithmetic  27.1 us (8%)
  between operations  15.1 us (4%)
  local copies, waits for them, and re-layouts  11.2 us (3%)
    ppermute x57, waiting for transfers between devices, from_offset(): lax.ppermute(v, axis, [((i + offset) % size, i) for i in range(size)])  115 us
    pallas_call x6, Pallas kernels, kernel_call(): pl.pallas_call(kernel, out_shape=list(small_outs) + list(outs), in_specs=...  92.1 us
    ppermute x57, starting transfers between devices, from_offset(): lax.ppermute(v, axis, [((i + offset) % size, i) for i in range(size)])  79.3 us
  transfers between devices with their start and end apart: 59, of which 28 were waited for; matrix products, arithmetic and copies ran while one was open for 8% of the time, Pallas kernels for 23%

profile of v4, /device:TPU:1, one launch (start us, length us, event | category | flops | bytes accessed | tf_op | source)
XLA Modules:
  0.0 345.2 jit_solution(54038822032526470)
XLA Ops:
  11.9 3.1 collective-permute-start
  21.7 6.0 %collective-permute-done.3 = f32[2,96]{0,1:T(8,128)S(1)} collective-permute-done((f32[2,96]{0,1:T(8,128)S(1)}, f32[2,96]{0,1:T(8,128)S(1)}, u32[]{:S(2)}, u32[]{:S(2)}) %collective-permute-start.3) | collective-permute-done | bytes 800 | tf_op jit(solution)/shard_map/ppermute | solution.py:550
  28.0 2.8 collective-permute-start.10
  33.3 3.8 %collective-permute-start.5 = (bf16[96,640]{1,0:T(8,128)(2,1)S(1)}, bf16[96,640]{1,0:T(8,128)(2,1)S(1)}, u32[]{:S(2)}, u32[]{:S(2)}) collective-permute-start(bf16[96,640]{1,0:T(8,128)(2,1)S(1)} %get-tuple-element.135), channel_id=1, source_target_pairs={{8,0},{16,8},{24,16},{0,24},{9,1},{17,9},{25,17},{1,25},{10,2},{18... | collective-permute-start | bytes 368648 | tf_op jit(solution)/shard_map/ppermute | solution.py:550
  38.9 4.4 %collective-permute-done.7 = bf16[96,640]{1,0:T(8,128)(2,1)S(1)} collective-permute-done((bf16[96,640]{1,0:T(8,128)(2,1)S(1)}, bf16[96,640]{1,0:T(8,128)(2,1)S(1)}, u32[]{:S(2)}, u32[]{:S(2)}) %collective-permute-start.7) | collective-permute-done | bytes 122912 | tf_op jit(solution)/shard_map/ppermute | solution.py:550
  48.6 5.0 %collective-permute-done.11.a1 = bf16[4,96,640]{2,1,0:T(8,128)(2,1)S(1)} collective-permute-done((bf16[4,96,640]{2,1,0:T(8,128)(2,1)S(1)}, bf16[4,96,640]{2,1,0:T(8,128)(2,1)S(1)}, u32[]{:S(2)}, u32[]{:S(2)}) %collective-permute-start.11) | collective-permute-done | bytes 491552 | tf_op jit(solution)/shard_map/ppermute | solution.py:550
  53.6 7.7 %collective-permute-start.17 = (bf16[256,1536]{1,0:T(8,128)(2,1)S(1)}, bf16[256,1536]{1,0:T(8,128)(2,1)}, u32[]{:S(2)}, u32[]{:S(2)}) collective-permute-start(bf16[256,1536]{1,0:T(8,128)(2,1)S(1)} %copy-done), channel_id=1, source_target_pairs={{1,0},{0,1},{3,2},{2,3},{5,4},{4,5},{7,6},{6,7},{9,8},{8,9},{11,10... | collective-permute-start | bytes 2359304 | tf_op jit(solution)/shard_map/ppermute | solution.py:550
  61.3 8.9 %collective-permute-start.18 = (bf16[256,1536]{1,0:T(8,128)(2,1)}, bf16[256,1536]{1,0:T(8,128)(2,1)}, u32[]{:S(2)}, u32[]{:S(2)}) collective-permute-start(bf16[256,1536]{1,0:T(8,128)(2,1)} %collective-permute-done.15.t2), channel_id=1, source_target_pairs={{1,0},{0,1},{3,2},{2,3},{5,4},{4,5},{7,6},{6,7},{9,8},{8,9},{11,10... | collective-permute-start | bytes 2359304 | tf_op jit(solution)/shard_map/ppermute | solution.py:550
  72.8 11.8 %collective-permute-done.19.a2 = bf16[4,96,640]{2,1,0:T(8,128)(2,1)} collective-permute-done((bf16[4,96,640]{2,1,0:T(8,128)(2,1)S(1)}, bf16[4,96,640]{2,1,0:T(8,128)(2,1)}, u32[]{:S(2)}, u32[]{:S(2)}) %collective-permute-start.19) | collective-permute-done | bytes 491552 | tf_op jit(solution)/shard_map/ppermute | solution.py:550
  84.7 21.1 %attend.1 = (f32[2,1536]{1,0:T(2,128)}, bf16[1536,1280]{1,0:T(8,128)(2,1)}, bf16[1024,1536]{1,0:T(8,128)(2,1)}, bf16[4,1024,96]{2,1,0:T(8,128)(2,1)}, bf16[2,96,...) custom-call(s32[4]{0:T(128)} %pad_add_fusion.2.place, ...), custom_call_target="tpu_custom_call" | custom-call | flops 1 | bytes 1 | tf_op jit(solution)/shard_map/attend/pallas_call | solution.py:86
  112.7 16.8 %collective-permute-done.23 = bf16[256,1536]{1,0:T(8,128)(2,1)S(1)} collective-permute-done((bf16[256,1536]{1,0:T(8,128)(2,1)S(1)}, bf16[256,1536]{1,0:T(8,128)(2,1)S(1)}, u32[]{:S(2)}, u32[]{:S(2)}) %collective-permute-start.23) | collective-permute-done | bytes 786464 | tf_op jit(solution)/shard_map/ppermute | solution.py:550
  135.1 14.8 %feed.2 = (bf16[512,1024]{1,0:T(8,128)(2,1)}, bf16[512,2048]{1,0:T(8,128)(2,1)}, bf16[256,1536]{1,0:T(8,128)(2,1)}, bf16[256,1536]{1,0:T(8,128)(2,1)}, bf16[256,...) custom-call(s32[4]{0:T(128)} %pad_add_fusion.2.place, bf16[256,1536]{1,0:T(8,128)(2,1)} %multiply_convert_fusion.h0, ...), custom_call_target="tpu_custom_call" | custom-call | flops 1 | bytes 1 | tf_op jit(solution)/shard_map/feed/pallas_call | solution.py:86
  153.0 2.1 collective-permute-done.27.h1.h3
  156.0 14.8 %feed.3 = (bf16[512,1024]{1,0:T(8,128)(2,1)}, bf16[512,2048]{1,0:T(8,128)(2,1)}, bf16[256,1536]{1,0:T(8,128)(2,1)}, bf16[256,1536]{1,0:T(8,128)(2,1)}, bf16[256,...) custom-call(s32[4]{0:T(128)} %pad_add_fusion.2.place, bf16[256,1536]{1,0:T(8,128)(2,1)} %collective-permute-done.24.h0.h2, ...), custom_call_target="tpu_custom_call" | custom-call | flops 1 | bytes 1 | tf_op jit(solution)/shard_map/feed/pallas_call | solution.py:86
  171.2 2.1 collective-permute-done.31
  173.3 2.2 add_convert_fusion.2
  177.1 15.4 %feed_grads.1 = bf16[1536,3072]{1,0:T(8,128)(2,1)} custom-call(s32[4]{0:T(128)} %pad_add_fusion.2.place, bf16[256,1536]{1,0:T(8,128)(2,1)} %multiply_convert_fusion.h0, bf16[256,1536]{1,0:T(8,128)(2,1)} %collective-permute-done.25.h1, bf16[256,1536]{1,0:T(8,128)(2,1)} %collective-permute-done.24.h0.h2, bf16[256,1536]{1,0:T(8,128)(2,1)} %copy-done.8, ...), custom_call_target="tpu_custom_call" | custom-call | flops 1 | bytes 1 | tf_op jit(solution)/shard_map/feed_grads/pallas_call | solution.py:86
  192.5 2.3 collective-permute-done.32
  200.1 3.1 fusion.11
  206.7 15.3 %collective-permute-done.34.o2 = bf16[256,1536]{1,0:T(8,128)(2,1)S(1)} collective-permute-done((bf16[256,1536]{1,0:T(8,128)(2,1)S(1)}, bf16[256,1536]{1,0:T(8,128)(2,1)S(1)}, u32[]{:S(2)}, u32[]{:S(2)}) %collective-permute-start.34) | collective-permute-done | bytes 786464 | tf_op jit(solution)/shard_map/ppermute | solution.py:550
  226.7 19.7 %attend_back.1 = (bf16[1024,768]{1,0:T(8,128)(2,1)}, bf16[384,576]{1,0:T(8,128)(2,1)}, bf16[384,576]{1,0:T(8,128)(2,1)}, bf16[384,576]{1,0:T(8,128)(2,1)}, bf16[...) custom-call(s32[4]{0:T(128)} %pad_add_fusion.2.place, ...), custom_call_target="tpu_custom_call" | custom-call | flops 1 | bytes 1 | tf_op jit(solution)/shard_map/attend_back/pallas_call | solution.py:86
  246.4 2.7 collective-permute-start.37
  251.7 6.4 %project_back.1 = (bf16[256,1536]{1,0:T(8,128)(2,1)}, bf16[256,1536]{1,0:T(8,128)(2,1)}, bf16[256,1536]{1,0:T(8,128)(2,1)}, bf16[256,1536]{1,0:T(8,128)(2,1)}) custom-call(s32[4]{0:T(128)} %pad_add_fusion.2.place, bf16[1024,768]{1,0:T(8,128)(2,1)} %get-tuple-element.210.dqkv_hbm, bf16[1536,1280]{1,0:T(8,128)(2,1)} %get-tuple-element.193.w_hbm), custom_call_target="tpu_custom_call" | custom-call | flops 1 | bytes 1 | tf_op jit(solution)/shard_map/project_back/pallas_call | solution.py:86
  258.1 5.4 %collective-permute-done.37.refs_1_ = bf16[384,576]{1,0:T(8,128)(2,1)S(1)} collective-permute-done((bf16[384,576]{1,0:T(8,128)(2,1)}, bf16[384,576]{1,0:T(8,128)(2,1)S(1)}, u32[]{:S(2)}, u32[]{:S(2)}) %collective-permute-start.37) | collective-permute-done | bytes 442400 | tf_op jit(solution)/shard_map/ppermute | solution.py:550
  269.9 2.2 add_convert_fusion
  274.3 16.6 %collective-permute-done.42.refs_2_ = bf16[384,576]{1,0:T(8,128)(2,1)S(1)} collective-permute-done((bf16[384,576]{1,0:T(8,128)(2,1)}, bf16[384,576]{1,0:T(8,128)(2,1)S(1)}, u32[]{:S(2)}, u32[]{:S(2)}) %collective-permute-start.42) | collective-permute-done | bytes 442400 | tf_op jit(solution)/shard_map/ppermute | solution.py:550
  292.4 3.3 late_middle.1
  306.0 3.2 collective-permute-done.49.refs_6_
  312.2 5.1 %collective-permute-done.53 = bf16[48,3072]{1,0:T(8,128)(2,1)S(1)} collective-permute-done((bf16[48,3072]{1,0:T(8,128)(2,1)S(1)}, bf16[48,3072]{1,0:T(8,128)(2,1)S(1)}, u32[]{:S(2)}, u32[]{:S(2)}) %collective-permute-start.53) | collective-permute-done | bytes 294944 | tf_op jit(solution)/shard_map/ppermute | solution.py:550
  317.4 2.1 late_last.1
  322.1 2.8 collective-permute-done.54
  326.7 6.7 %collective-permute-start.55 = (f32[2,48]{1,0:T(2,128)S(1)}, f32[2,48]{1,0:T(2,128)S(1)}, u32[]{:S(2)}, u32[]{:S(2)}) collective-permute-start(f32[2,48]{1,0:T(2,128)S(1)} %pad_maximum_fusion.2), channel_id=1, source_target_pairs={{1,0},{0,1},{3,2},{2,3},{5,4},{4,5},{7,6},{6,7},{9,8},{8,9},{11,10... | collective-permute-start | bytes 1160 | tf_op jit(solution)/shard_map/ppermute | solution.py:550
  (231 shorter events, 90.4 us)
Async XLA Ops:
  7.2 127.9 %all-gather.2.cloned.1.call-start = ((), (), s32[]{:S(2)}) async-start(), calls=%async_computation.1 | async-start | bytes 10027008 | tf_op jit(solution)/shard_map/all_gather | solution.py:649
  11.9 15.9 %collective-permute-start = (bf16[48,1280]{1,0:T(8,128)(2,1)S(1)}, bf16[48,1280]{1,0:T(8,128)(2,1)S(1)}, u32[]{:S(2)}, u32[]{:S(2)}) collective-permute-start(bf16[48,1280]{1,0:T(8,128)(2,1)S(1)} %pad_add_fusion.1), channel_id=1, source_target_pairs={{4,0},{0,4},{5,1},{1,5},{6,2},{2,6},{7,3},{3,7},{12,8},{8,12},{13,... | collective-permute-start | bytes 368648 | tf_op jit(solution)/shard_map/ppermute | solution.py:550
  17.2 15.1 %collective-permute-start.4 = (bf16[48,3072]{1,0:T(8,128)(2,1)S(1)}, bf16[48,3072]{1,0:T(8,128)(2,1)S(1)}, u32[]{:S(2)}, u32[]{:S(2)}) collective-permute-start(bf16[48,3072]{1,0:T(8,128)(2,1)S(1)} %pad_add_fusion), channel_id=1, source_target_pairs={{4,0},{0,4},{5,1},{1,5},{6,2},{2,6},{7,3},{3,7},{12,8},{8,12},{13,... | collective-permute-start | bytes 884744 | tf_op jit(solution)/shard_map/ppermute | solution.py:550
  28.0 9.0 %collective-permute-start.10 = (bf16[96,640]{1,0:T(8,128)(2,1)S(1)}, bf16[96,640]{1,0:T(8,128)(2,1)S(1)}, u32[]{:S(2)}, u32[]{:S(2)}) collective-permute-start(bf16[96,640]{1,0:T(8,128)(2,1)S(1)} %get-tuple-element.273), channel_id=1, source_target_pairs={{64,0},{96,32},{0,64},{32,96},{65,1},{97,33},{1,65},{33,97},{66,2}... | collective-permute-start | bytes 368648 | tf_op jit(solution)/shard_map/ppermute | solution.py:550
  43.5 265.6 %reduce-scatter.2.cloned.1.call-start = ((), (), s32[]{:S(2)}) async-start(), calls=%async_computation.2 | async-start | bytes 10027008 | tf_op jit(solution)/shard_map/reduce_scatter | solution.py:598
  43.6 17.7 %collective-permute-start.15 = (bf16[256,1536]{1,0:T(8,128)(2,1)S(1)}, bf16[256,1536]{1,0:T(8,128)(2,1)}, u32[]{:S(2)}, u32[]{:S(2)}) collective-permute-start(bf16[256,1536]{1,0:T(8,128)(2,1)S(1)} %copy-done), channel_id=1, source_target_pairs={{2,0},{0,2},{3,1},{1,3},{6,4},{4,6},{7,5},{5,7},{10,8},{8,10},{11,... | collective-permute-start | bytes 2359304 | tf_op jit(solution)/shard_map/ppermute | solution.py:550
  46.8 14.4 %collective-permute-start.12 = (bf16[4,96,640]{2,1,0:T(8,128)(2,1)S(1)}, bf16[4,96,640]{2,1,0:T(8,128)(2,1)S(1)}, u32[]{:S(2)}, u32[]{:S(2)}) collective-permute-start(bf16[4,96,640]{2,1,0:T(8,128)(2,1)S(1)} %pad_maximum_fusion.1.b0), channel_id=1, source_target_pairs={{8,0},{16,8},{24,16},{0,24},{9,1},{17,9},{25,17},{1,25},{10,2},{18... | collective-permute-start | bytes 1474568 | tf_op jit(solution)/shard_map/ppermute | solution.py:550
  48.6 12.7 %collective-permute-start.13 = (bf16[4,96,640]{2,1,0:T(8,128)(2,1)S(1)}, bf16[4,96,640]{2,1,0:T(8,128)(2,1)S(1)}, u32[]{:S(2)}, u32[]{:S(2)}) collective-permute-start(bf16[4,96,640]{2,1,0:T(8,128)(2,1)S(1)} %pad_maximum_fusion.a0), channel_id=1, source_target_pairs={{96,0},{0,32},{32,64},{64,96},{97,1},{1,33},{33,65},{65,97},{98,2}... | collective-permute-start | bytes 1474568 | tf_op jit(solution)/shard_map/ppermute | solution.py:550
  48.6 12.7 %collective-permute-start.14 = (bf16[4,96,640]{2,1,0:T(8,128)(2,1)S(1)}, bf16[4,96,640]{2,1,0:T(8,128)(2,1)S(1)}, u32[]{:S(2)}, u32[]{:S(2)}) collective-permute-start(bf16[4,96,640]{2,1,0:T(8,128)(2,1)S(1)} %pad_maximum_fusion.1.b0), channel_id=1, source_target_pairs={{24,0},{0,8},{8,16},{16,24},{25,1},{1,9},{9,17},{17,25},{26,2},{2,... | collective-permute-start | bytes 1474568 | tf_op jit(solution)/shard_map/ppermute | solution.py:550
  53.6 31.1 %collective-permute-start.17 = (bf16[256,1536]{1,0:T(8,128)(2,1)S(1)}, bf16[256,1536]{1,0:T(8,128)(2,1)}, u32[]{:S(2)}, u32[]{:S(2)}) collective-permute-start(bf16[256,1536]{1,0:T(8,128)(2,1)S(1)} %copy-done), channel_id=1, source_target_pairs={{1,0},{0,1},{3,2},{2,3},{5,4},{4,5},{7,6},{6,7},{9,8},{8,9},{11,10... | collective-permute-start | bytes 2359304 | tf_op jit(solution)/shard_map/ppermute | solution.py:550
  61.3 23.3 %collective-permute-start.18 = (bf16[256,1536]{1,0:T(8,128)(2,1)}, bf16[256,1536]{1,0:T(8,128)(2,1)}, u32[]{:S(2)}, u32[]{:S(2)}) collective-permute-start(bf16[256,1536]{1,0:T(8,128)(2,1)} %collective-permute-done.15.t2), channel_id=1, source_target_pairs={{1,0},{0,1},{3,2},{2,3},{5,4},{4,5},{7,6},{6,7},{9,8},{8,9},{11,10... | collective-permute-start | bytes 2359304 | tf_op jit(solution)/shard_map/ppermute | solution.py:550
  70.2 35.5 %collective-permute-start.16 = (bf16[256,1536]{1,0:T(8,128)(2,1)S(1)}, bf16[256,1536]{1,0:T(8,128)(2,1)}, u32[]{:S(2)}, u32[]{:S(2)}) collective-permute-start(bf16[256,1536]{1,0:T(8,128)(2,1)S(1)} %copy-done.2), channel_id=1, source_target_pairs={{2,0},{0,2},{3,1},{1,3},{6,4},{4,6},{7,5},{5,7},{10,8},{8,10},{11,... | collective-permute-start | bytes 2359304 | tf_op jit(solution)/shard_map/ppermute | solution.py:550
  70.2 14.4 %collective-permute-start.19 = (bf16[4,96,640]{2,1,0:T(8,128)(2,1)S(1)}, bf16[4,96,640]{2,1,0:T(8,128)(2,1)}, u32[]{:S(2)}, u32[]{:S(2)}) collective-permute-start(bf16[4,96,640]{2,1,0:T(8,128)(2,1)S(1)} %pad_maximum_fusion.a0), channel_id=1, source_target_pairs={{64,0},{96,32},{0,64},{32,96},{65,1},{97,33},{1,65},{33,97},{66,2}... | collective-permute-start | bytes 1474568 | tf_op jit(solution)/shard_map/ppermute | solution.py:550
  70.4 14.3 %collective-permute-start.20 = (bf16[4,96,640]{2,1,0:T(8,128)(2,1)S(1)}, bf16[4,96,640]{2,1,0:T(8,128)(2,1)}, u32[]{:S(2)}, u32[]{:S(2)}) collective-permute-start(bf16[4,96,640]{2,1,0:T(8,128)(2,1)S(1)} %pad_maximum_fusion.1.b0), channel_id=1, source_target_pairs={{16,0},{24,8},{0,16},{8,24},{17,1},{25,9},{1,17},{9,25},{18,2},{26... | collective-permute-start | bytes 1474568 | tf_op jit(solution)/shard_map/ppermute | solution.py:550
  110.5 18.9 %collective-permute-start.23 = (bf16[256,1536]{1,0:T(8,128)(2,1)S(1)}, bf16[256,1536]{1,0:T(8,128)(2,1)S(1)}, u32[]{:S(2)}, u32[]{:S(2)}) collective-permute-start(bf16[256,1536]{1,0:T(8,128)(2,1)S(1)} %add_convert_fusion.4), channel_id=1, source_target_pairs={{2,0},{0,2},{3,1},{1,3},{6,4},{4,6},{7,5},{5,7},{10,8},{8,10},{11,... | collective-permute-start | bytes 2359304 | tf_op jit(solution)/shard_map/ppermute | solution.py:550
  112.0 22.2 %collective-permute-start.26 = (bf16[256,1536]{1,0:T(8,128)(2,1)S(1)}, bf16[256,1536]{1,0:T(8,128)(2,1)S(1)}, u32[]{:S(2)}, u32[]{:S(2)}) collective-permute-start(bf16[256,1536]{1,0:T(8,128)(2,1)S(1)} %copy-done.2), channel_id=1, source_target_pairs={{1,0},{0,1},{3,2},{2,3},{5,4},{4,5},{7,6},{6,7},{9,8},{8,9},{11,10... | collective-permute-start | bytes 2359304 | tf_op jit(solution)/shard_map/ppermute | solution.py:550
  132.3 19.5 %collective-permute-start.24 = (bf16[256,1536]{1,0:T(8,128)(2,1)}, bf16[256,1536]{1,0:T(8,128)(2,1)}, u32[]{:S(2)}, u32[]{:S(2)}) collective-permute-start(bf16[256,1536]{1,0:T(8,128)(2,1)} %multiply_convert_fusion.h0), channel_id=1, source_target_pairs={{2,0},{0,2},{3,1},{1,3},{6,4},{4,6},{7,5},{5,7},{10,8},{8,10},{11,... | collective-permute-start | bytes 2359304 | tf_op jit(solution)/shard_map/ppermute | solution.py:550
  133.7 19.3 %collective-permute-start.28 = (bf16[256,1536]{1,0:T(8,128)(2,1)}, bf16[256,1536]{1,0:T(8,128)(2,1)}, u32[]{:S(2)}, u32[]{:S(2)}) collective-permute-start(bf16[256,1536]{1,0:T(8,128)(2,1)} %collective-permute-done.16.g0.g2), channel_id=1, source_target_pairs={{1,0},{0,1},{3,2},{2,3},{5,4},{4,5},{7,6},{6,7},{9,8},{8,9},{11,10... | collective-permute-start | bytes 2359304 | tf_op jit(solution)/shard_map/ppermute | solution.py:550
  175.5 19.2 %collective-permute-start.32 = (bf16[256,1536]{1,0:T(8,128)(2,1)}, bf16[256,1536]{1,0:T(8,128)(2,1)}, u32[]{:S(2)}, u32[]{:S(2)}) collective-permute-start(bf16[256,1536]{1,0:T(8,128)(2,1)} %add_convert_fusion.2), channel_id=1, source_target_pairs={{2,0},{0,2},{3,1},{1,3},{6,4},{4,6},{7,5},{5,7},{10,8},{8,10},{11,... | collective-permute-start | bytes 2359304 | tf_op jit(solution)/shard_map/ppermute | solution.py:550
  196.1 9.1 %collective-permute-start.35 = (bf16[256,1536]{1,0:T(8,128)(2,1)}, bf16[256,1536]{1,0:T(8,128)(2,1)S(1)}, u32[]{:S(2)}, u32[]{:S(2)}) collective-permute-start(bf16[256,1536]{1,0:T(8,128)(2,1)} %get-tuple-element.187), channel_id=1, source_target_pairs={{1,0},{0,1},{3,2},{2,3},{5,4},{4,5},{7,6},{6,7},{9,8},{8,9},{11,10... | collective-permute-start | bytes 2359304 | tf_op jit(solution)/shard_map/ppermute | solution.py:550
  203.2 18.9 %collective-permute-start.34 = (bf16[256,1536]{1,0:T(8,128)(2,1)S(1)}, bf16[256,1536]{1,0:T(8,128)(2,1)S(1)}, u32[]{:S(2)}, u32[]{:S(2)}) collective-permute-start(bf16[256,1536]{1,0:T(8,128)(2,1)S(1)} %get-tuple-element.189.o0), channel_id=1, source_target_pairs={{2,0},{0,2},{3,1},{1,3},{6,4},{4,6},{7,5},{5,7},{10,8},{8,10},{11,... | collective-permute-start | bytes 2359304 | tf_op jit(solution)/shard_map/ppermute | solution.py:550
  204.6 18.8 %collective-permute-start.29 = (bf16[256,1536]{1,0:T(8,128)(2,1)S(1)}, bf16[256,1536]{1,0:T(8,128)(2,1)S(1)}, u32[]{:S(2)}, u32[]{:S(2)}) collective-permute-start(bf16[256,1536]{1,0:T(8,128)(2,1)S(1)} %copy-done.39), channel_id=1, source_target_pairs={{1,0},{0,1},{3,2},{2,3},{5,4},{4,5},{7,6},{6,7},{9,8},{8,9},{11,10... | collective-permute-start | bytes 2359304 | tf_op jit(solution)/shard_map/ppermute | solution.py:550
  206.7 17.7 %collective-permute-start.33 = (bf16[256,1536]{1,0:T(8,128)(2,1)S(1)}, bf16[256,1536]{1,0:T(8,128)(2,1)S(1)}, u32[]{:S(2)}, u32[]{:S(2)}) collective-permute-start(bf16[256,1536]{1,0:T(8,128)(2,1)S(1)} %get-tuple-element.189.o0), channel_id=1, source_target_pairs={{1,0},{0,1},{3,2},{2,3},{5,4},{4,5},{7,6},{6,7},{9,8},{8,9},{11,10... | collective-permute-start | bytes 2359304 | tf_op jit(solution)/shard_map/ppermute | solution.py:550
  225.3 26.4 %collective-permute-start.41 = (bf16[256,1536]{1,0:T(8,128)(2,1)}, bf16[256,1536]{1,0:T(8,128)(2,1)S(1)}, u32[]{:S(2)}, u32[]{:S(2)}) collective-permute-start(bf16[256,1536]{1,0:T(8,128)(2,1)} %add_convert_fusion.3), channel_id=1, source_target_pairs={{2,0},{0,2},{3,1},{1,3},{6,4},{4,6},{7,5},{5,7},{10,8},{8,10},{11,... | collective-permute-start | bytes 2359304 | tf_op jit(solution)/shard_map/ppermute | solution.py:550
  246.4 17.1 %collective-permute-start.37 = (bf16[384,576]{1,0:T(8,128)(2,1)}, bf16[384,576]{1,0:T(8,128)(2,1)S(1)}, u32[]{:S(2)}, u32[]{:S(2)}) collective-permute-start(bf16[384,576]{1,0:T(8,128)(2,1)} %get-tuple-element.204), channel_id=1, source_target_pairs={{32,0},{64,32},{96,64},{0,96},{33,1},{65,33},{97,65},{1,97},{34,2}... | collective-permute-start | bytes 1327112 | tf_op jit(solution)/shard_map/ppermute | solution.py:550
  249.2 14.4 %collective-permute-start.38 = (bf16[4,96,576]{2,1,0:T(8,128)(2,1)}, bf16[4,96,576]{2,1,0:T(8,128)(2,1)}, u32[]{:S(2)}, u32[]{:S(2)}) collective-permute-start(bf16[4,96,576]{2,1,0:T(8,128)(2,1)} %get-tuple-element.205), channel_id=1, source_target_pairs={{8,0},{16,8},{24,16},{0,24},{9,1},{17,9},{25,17},{1,25},{10,2},{18... | collective-permute-start | bytes 1327112 | tf_op jit(solution)/shard_map/ppermute | solution.py:550
  249.2 14.8 %collective-permute-start.39 = (bf16[384,576]{1,0:T(8,128)(2,1)}, bf16[384,576]{1,0:T(8,128)(2,1)}, u32[]{:S(2)}, u32[]{:S(2)}) collective-permute-start(bf16[384,576]{1,0:T(8,128)(2,1)} %get-tuple-element.206), channel_id=1, source_target_pairs={{96,0},{0,32},{32,64},{64,96},{97,1},{1,33},{33,65},{65,97},{98,2}... | collective-permute-start | bytes 1327112 | tf_op jit(solution)/shard_map/ppermute | solution.py:550
  250.1 15.1 %collective-permute-start.40 = (bf16[4,96,576]{2,1,0:T(8,128)(2,1)}, bf16[4,96,576]{2,1,0:T(8,128)(2,1)}, u32[]{:S(2)}, u32[]{:S(2)}) collective-permute-start(bf16[4,96,576]{2,1,0:T(8,128)(2,1)} %get-tuple-element.207), channel_id=1, source_target_pairs={{24,0},{0,8},{8,16},{16,24},{25,1},{1,9},{9,17},{17,25},{26,2},{2,... | collective-permute-start | bytes 1327112 | tf_op jit(solution)/shard_map/ppermute | solution.py:550
  266.7 43.5 %collective-permute-start.50 = (bf16[256,1536]{1,0:T(8,128)(2,1)}, bf16[256,1536]{1,0:T(8,128)(2,1)}, u32[]{:S(2)}, u32[]{:S(2)}) collective-permute-start(bf16[256,1536]{1,0:T(8,128)(2,1)} %get-tuple-element.246), channel_id=1, source_target_pairs={{1,0},{0,1},{3,2},{2,3},{5,4},{4,5},{7,6},{6,7},{9,8},{8,9},{11,10... | collective-permute-start | bytes 2359304 | tf_op jit(solution)/shard_map/ppermute | solution.py:550
  266.7 24.1 %collective-permute-start.42 = (bf16[384,576]{1,0:T(8,128)(2,1)}, bf16[384,576]{1,0:T(8,128)(2,1)S(1)}, u32[]{:S(2)}, u32[]{:S(2)}) collective-permute-start(bf16[384,576]{1,0:T(8,128)(2,1)} %get-tuple-element.219), channel_id=1, source_target_pairs={{64,0},{96,32},{0,64},{32,96},{65,1},{97,33},{1,65},{33,97},{66,2}... | collective-permute-start | bytes 1327112 | tf_op jit(solution)/shard_map/ppermute | solution.py:550
  268.3 23.3 %collective-permute-start.43 = (bf16[4,96,576]{2,1,0:T(8,128)(2,1)}, bf16[4,96,576]{2,1,0:T(8,128)(2,1)S(1)}, u32[]{:S(2)}, u32[]{:S(2)}) collective-permute-start(bf16[4,96,576]{2,1,0:T(8,128)(2,1)} %get-tuple-element.220), channel_id=1, source_target_pairs={{16,0},{24,8},{0,16},{8,24},{17,1},{25,9},{1,17},{9,25},{18,2},{26... | collective-permute-start | bytes 1327112 | tf_op jit(solution)/shard_map/ppermute | solution.py:550
  272.1 38.1 %collective-permute-start.52 = (bf16[256,1536]{1,0:T(8,128)(2,1)}, bf16[256,1536]{1,0:T(8,128)(2,1)}, u32[]{:S(2)}, u32[]{:S(2)}) collective-permute-start(bf16[256,1536]{1,0:T(8,128)(2,1)} %add_convert_fusion), channel_id=1, source_target_pairs={{2,0},{0,2},{3,1},{1,3},{6,4},{4,6},{7,5},{5,7},{10,8},{8,10},{11,... | collective-permute-start | bytes 2359304 | tf_op jit(solution)/shard_map/ppermute | solution.py:550
  (67 other events, 552.6 us)
Sparse Core Ops, SparseCore 0:
  43.6 88.6 all-gather.1
  194.9 96.5 reduce-scatter.1

commit v5 on v4

--- a/solution.py
+++ b/solution.py
@@ -18,7 +18,7 @@
 GAIN_AT, OUT_AT, QUERY_AT, KEYVAL_AT, REST_AT, ATTN_WIDTH = 0, 128, 256, 640, 1024, 1280
 HALF_WIDTH = ATTN_WIDTH // 2
 OUT_CUT = QUERY_AT - OUT_AT
-LIMIT = 60
+LIMIT = 39
 
 
 def dot_n(left, right):
@@ -33,13 +33,17 @@
     return lax.dot_general(left, right, (((0,), (0,)), ((), ())), preferred_element_type=F32)
 
 
+def dot_tt(left, right):
+    return lax.dot_general(left, right, (((0,), (1,)), ((), ())), preferred_element_type=F32)
+
+
 def block_at(index, size):
     return pl.ds(pl.multiple_of(index * size, size), size)
 
 
 def causal_mask(scores, size):
-    key_at = lax.broadcasted_iota(jnp.int32, (size, size), 0)
-    query_at = lax.broadcasted_iota(jnp.int32, (size, size), 1)
+    key_at = lax.broadcasted_iota(jnp.int32, (size, scores.shape[1]), 0)
+    query_at = lax.broadcasted_iota(jnp.int32, (size, scores.shape[1]), 1) % size
     tail = jnp.where(key_at <= query_at, scores[-size:], -1e30)
     if scores.shape[0] == size:
         return tail
@@ -100,16 +104,20 @@
     return step * (step + 1) // 2 * size, (step + 1) * size
 
 
+def head_rows(head):
+    return slice(head * HD, (head + 1) * HD)
+
+
 def attend_kernel(place, cos_ref, sin_ref, t0, t1, t2, t3, a0, a1, a2, a3, b0, b1, b2, b3,
-                  gains_ref, w_hbm, h_hbm, q_hbm, kt_hbm, v_hbm, attn_hbm, attnt_hbm, probs_hbm,
+                  gains_ref, w_hbm, h_hbm, qt_hbm, kt_hbm, vt_hbm, attn_hbm, probs_hbm,
                   o0, o1, o2, o3,
-                  t_ref, w_ref, h_ref, qt_ref, q_ref, kt_ref, k_ref, vt_ref, v_ref,
-                  natural, attn_ref, attnt_ref, probs_ref, part_ref, in_sem, out_sem, probs_sem):
+                  t_ref, w_ref, h_ref, qt_ref, kt_ref, vt_ref, attn_ref, probs_ref, part_ref, k_ref,
+                  in_sem, out_sem, probs_sem):
     block, ix, iz = place[0], place[1], place[2]
     half = HD // 2
     size = t_ref.shape[1]
-    heads, _, length = qt_ref.shape
-    group_size = heads // k_ref.shape[0]
+    heads = qt_ref.shape[0]
+    group_size = heads // kt_ref.shape[0]
     rows = a0.shape[1]
     fetch, store = Moves(in_sem), Moves(out_sem)
     came = []
@@ -148,86 +156,73 @@
                 [first * cosine - second * sine, second * cosine + first * sine], 0
             )
 
-        for head in range(query.shape[0] // HD):
-            turned = rotated(query[head * HD : (head + 1) * HD])
-            qt_ref[head, :, at] = turned.astype(BF16)
-            q_ref[head, at, :] = turned.T.astype(BF16)
-        for head in range(keyval.shape[0] // (2 * HD)):
-            turned = rotated(keyval[2 * head * HD : (2 * head + 1) * HD])
-            value_t = keyval[(2 * head + 1) * HD : (2 * head + 2) * HD]
-            kt_ref[head, :, at] = turned.astype(BF16)
-            k_ref[head, at, :] = turned.T.astype(BF16)
-            vt_ref[head, :, at] = value_t.astype(BF16)
-            v_ref[head, at, :] = value_t.T.astype(BF16)
-    for source, target in ((h_ref, h_hbm), (q_ref, q_hbm), (kt_ref, kt_hbm), (v_ref, v_hbm)):
+        for head in range(heads):
+            qt_ref[head, :, at] = rotated(query[head_rows(head)]).astype(BF16)
+        for group in range(heads // group_size):
+            key = rotated(keyval[head_rows(2 * group)])
+            kt_ref[group, :, at] = key.astype(BF16)
+            k_ref[group, at, :] = key.T.astype(BF16)
+            vt_ref[group, :, at] = keyval[head_rows(2 * group + 1)].astype(BF16)
+    for source, target in ((h_ref, h_hbm), (qt_ref, qt_hbm), (kt_ref, kt_hbm), (vt_ref, vt_hbm)):
         store.start(source, target)
 
-    def probs_copy(head):
-        return pltpu.make_async_copy(probs_ref.at[head], probs_hbm.at[head], probs_sem.at[head])
-
-    def one_head(head, carry):
-        group = head // group_size
+    def probs_copy(group):
+        return pltpu.make_async_copy(
+            probs_ref.at[group], probs_hbm.at[group], probs_sem.at[group])
+
+    for group in range(heads // group_size):
+        members = range(group * group_size, (group + 1) * group_size)
         for step in range(4):
             first, reach = probs_at(step, size)
             columns = slice(step * size, reach)
-            scores = causal_mask(dot_n(k_ref[group, :reach, :], qt_ref[head, :, columns]), size)
+            query = jnp.concatenate([qt_ref[head, :, columns] for head in members], 1)
+            scores = causal_mask(dot_n(k_ref[group, :reach, :], query), size)
             top = jnp.max(scores, 0, keepdims=True)
             expo = jnp.exp2((scores - top) * (SCALE * LOG2E))
             total = jnp.sum(expo, 0, keepdims=True)
             probs = (expo * (1.0 / total)).astype(BF16)
-            probs_ref[head, first : first + reach, :] = probs
-            mixed = dot_n(vt_ref[group, :, :reach], probs)
-            attnt_ref[head, :, columns] = mixed.astype(BF16)
-        probs_copy(head).start()
-        return carry
-
-    lax.fori_loop(0, heads, one_head, 0)
-    store.start(attnt_ref, attnt_hbm)
-    natural[...] = attnt_ref[...].reshape(heads * HD, length).T
+            probs_ref[group, first : first + reach, :] = probs
+            mixed = dot_n(vt_ref[group, :, :reach], probs).astype(BF16)
+            for i, head in enumerate(members):
+                attn_ref[head_rows(head), columns] = mixed[:, i * size : (i + 1) * size]
+        probs_copy(group).start()
+    store.start(attn_ref, attn_hbm)
     for step, out in ((1, o1), (3, o3), (2, o2), (0, o0)):
         at = block_at(lax.bitwise_xor(block, step), size)
-        attn = natural[at, :]
-        attn_ref[step * size : (step + 1) * size, :] = attn
-        part = dot_t(attn[:, :OUT_CUT], w_ref[:, OUT_AT:QUERY_AT])
-        part += dot_t(attn[:, OUT_CUT:], w_ref[:, REST_AT:])
+        part = dot_tt(attn_ref[:OUT_CUT, at], w_ref[:, OUT_AT:QUERY_AT])
+        part += dot_tt(attn_ref[OUT_CUT:, at], w_ref[:, REST_AT:])
         part_ref[step] = part.astype(BF16)
         store.start(part_ref.at[step], out)
-    store.start(attn_ref, attn_hbm)
     store.wait()
-    for head in range(heads):
-        probs_copy(head).wait()
+    for group in range(heads // group_size):
+        probs_copy(group).wait()
 
 
 def attend(place, pieces, along_x, along_z, cosine, sine):
-    width = pieces[0].shape[1]
-    length = cosine.shape[1]
-    size = length // 4
+    size, width = pieces[0].shape
+    length = 4 * size
     heads = (KEYVAL_AT - QUERY_AT) // HD
     groups = (REST_AT - KEYVAL_AT) // (2 * HD)
-    columns, rows = (heads, HD, length), (heads, length, HD)
-    g_columns, g_rows = (groups, HD, length), (groups, length, HD)
-    probs = (heads, sum(probs_at(3, size)), size)
-    outs = [(width, ATTN_WIDTH), (length, width), rows, g_columns, g_rows,
-            (length, heads * HD), columns, probs] + [(size, width)] * 4
-    scratch = [(4, size, width), (width, ATTN_WIDTH), (length, width), columns, rows,
-               g_columns, g_rows, g_columns, g_rows,
-               (length, heads * HD), (length, heads * HD), columns, probs, (4, size, width)]
+    columns, g_columns = (heads, HD, length), (groups, HD, length)
+    probs = (groups, sum(probs_at(3, size)), heads // groups * size)
+    kept = [(width, ATTN_WIDTH), (length, width), columns, g_columns, g_columns,
+            (heads * HD, length), probs]
     return kernel_call(
         attend_kernel, "attend", place, (cosine, sine), (*pieces, *along_x, *along_z),
-        [like(s) for s in outs], [like((2, width), F32)], [vmem(s) for s in scratch],
-        36, 11, heads)
+        [like(s) for s in kept + [(size, width)] * 4], [like((2, width), F32)],
+        [vmem(s) for s in [(4, size, width)] + kept + [(4, size, width), (groups, length, HD)]],
+        36, 10, groups)
 
 
 def attend_back_kernel(place, cos_ref, sin_ref,
-                       o0, o1, o2, o3, w_hbm, h_hbm, q_hbm, kt_hbm, v_hbm, attn_hbm, attnt_hbm,
-                       probs_hbm,
+                       o0, o1, o2, o3, w_hbm, h_hbm, qt_hbm, kt_hbm, vt_hbm, attn_hbm, probs_hbm,
                        dqkv_hbm, x0, x1, x2, x3, y0, y1, y2, y3,
-                       o_ref, w_ref, h_ref, q_ref, kt_ref, v_ref, attn_ref, attnt_ref, probs_ref,
-                       do_ref, dot_ref, dqkv_ref, first_ref, second_ref,
-                       delta_ref, dk_ref, dv_ref, turned_ref, in_sem, out_sem, probs_sem):
+                       o_ref, w_ref, h_ref, qt_ref, kt_ref, vt_ref, attn_ref, probs_ref,
+                       do_ref, dqkv_ref, first_ref, second_ref, v_ref, delta_ref, dk_ref, dv_ref,
+                       in_sem, out_sem, probs_sem):
     block, ix, iz = place[0], place[1], place[2]
-    heads, length, _ = q_ref.shape
-    groups = v_ref.shape[0]
+    heads, _, length = qt_ref.shape
+    groups = kt_ref.shape[0]
     group_size = heads // groups
     size = length // 4
     half = HD // 2
@@ -240,75 +235,72 @@
         fetch.start(w_hbm.at[:, pl.ds(REST_AT, rest_w)], w_ref.at[:, pl.ds(OUT_CUT, rest_w)]),
     ]
     early += [
-        fetch.start(piece, o_ref.at[pl.ds(i * size, size), :])
+        fetch.start(piece, o_ref.at[block_at(lax.bitwise_xor(block, i), size), :])
         for i, piece in enumerate((o0, o1, o2, o3))
     ]
-
-    def probs_copy(head):
-        return pltpu.make_async_copy(probs_hbm.at[head], probs_ref.at[head], probs_sem.at[head])
-
     middle = [
         fetch.start(source, target)
-        for source, target in ((attnt_hbm, attnt_ref), (v_hbm, v_ref), (q_hbm, q_ref),
+        for source, target in ((attn_hbm, attn_ref), (vt_hbm, vt_ref), (qt_hbm, qt_ref),
                                (kt_hbm, kt_ref))
     ]
-    for head in range(heads):
-        probs_copy(head).start()
-    later = [fetch.start(attn_hbm, attn_ref), fetch.start(h_hbm, h_ref)]
-    dk_ref[...] = jnp.zeros_like(dk_ref)
-    dv_ref[...] = jnp.zeros_like(dv_ref)
-    for copy in early[:2]:
+
+    def probs_copy(group):
+        return pltpu.make_async_copy(
+            probs_hbm.at[group], probs_ref.at[group], probs_sem.at[group])
+
+    for group in range(groups):
+        probs_copy(group).start()
+    h_came = fetch.start(h_hbm, h_ref)
+    for copy in early:
         copy.wait()
-    for step in range(4):
-        at = block_at(lax.bitwise_xor(block, step), size)
-        early[2 + step].wait()
-        grad = dot_n(o_ref[step * size : (step + 1) * size, :], w_ref[...])
-        grad_t = grad.T.astype(BF16)
-        grad = grad.astype(BF16)
-        for head in range(heads):
-            dot_ref[head, :, at] = grad_t[head * HD : (head + 1) * HD]
-            do_ref[head, at, :] = grad[:, head * HD : (head + 1) * HD]
+    do_ref[...] = dot_tt(w_ref[...], o_ref[...]).astype(BF16)
     for copy in middle:
         copy.wait()
-    delta_ref[...] = jnp.sum(
-        attnt_ref[...].astype(F32) * dot_ref[...].astype(F32), 1, keepdims=True)
+    for group in range(groups):
+        v_ref[group] = vt_ref[group].astype(F32).T.astype(BF16)
+    for head in range(heads):
+        rows = head_rows(head)
+        delta_ref[head] = jnp.sum(
+            attn_ref[rows, :].astype(F32) * do_ref[rows, :].astype(F32), 0, keepdims=True)
 
     def turned_back(field, cosine, sine):
         first, second = field[:half], field[half:]
         return jnp.concatenate(
-            [first * cosine + second * sine, second * cosine - first * sine], 0)
-
-    def one_head(head, carry):
-        group = head // group_size
-        probs_copy(head).wait()
+            [first * cosine + second * sine, second * cosine - first * sine], 0).astype(BF16)
+
+    for group in range(groups):
+        members = range(group * group_size, (group + 1) * group_size)
+        probs_copy(group).wait()
         for step in range(4):
             first, reach = probs_at(step, size)
             columns = slice(step * size, reach)
-            probs = probs_ref[head, first : first + reach, :]
-            d_probs = dot_n(v_ref[group, :reach, :], dot_ref[head, :, columns])
-            d_scores = (probs.astype(F32) * (d_probs - delta_ref[head, :, columns])).astype(BF16)
-            dv_ref[group, :reach, :] += dot_n(probs, do_ref[head, columns, :])
-            dk_ref[group, :reach, :] += dot_n(d_scores, q_ref[head, columns, :])
+            probs = probs_ref[group, first : first + reach, :]
+            query = jnp.concatenate([qt_ref[head, :, columns] for head in members], 1)
+            d_out = jnp.concatenate([do_ref[head_rows(head), columns] for head in members], 1)
+            delta = jnp.concatenate([delta_ref[head, :, columns] for head in members], 1)
+            d_probs = dot_n(v_ref[group, :reach, :], d_out)
+            d_scores = (probs.astype(F32) * (d_probs - delta)).astype(BF16)
+            for ref, left, right in ((dv_ref, d_out, probs), (dk_ref, query, d_scores)):
+                change = dot_t(left, right)
+                if step > 0:
+                    ref[group, :, : step * size] += change[:, : step * size]
+                ref[group, :, columns] = change[:, columns]
             d_query = dot_n(kt_ref[group, :, :reach], d_scores) * SCALE
-            turned_ref[head, :, columns] = turned_back(
-                d_query, cos_ref[:, columns], sin_ref[:, columns])
-        return carry
-
-    lax.fori_loop(0, heads, one_head, 0)
-    for group in range(groups):
-        turned_ref[heads + 2 * group] = turned_back(
-            dk_ref[group].T * SCALE, cos_ref[...], sin_ref[...])
-        turned_ref[heads + 2 * group + 1] = dv_ref[group].T
-    dqkv_ref[...] = turned_ref[...].reshape((heads + 2 * groups) * HD, length).T.astype(BF16)
+            for i, head in enumerate(members):
+                dqkv_ref[head_rows(head), columns] = turned_back(
+                    d_query[:, i * size : (i + 1) * size],
+                    cos_ref[:, columns], sin_ref[:, columns])
+        dqkv_ref[head_rows(heads + 2 * group), :] = turned_back(
+            dk_ref[group] * SCALE, cos_ref[...], sin_ref[...])
+        dqkv_ref[head_rows(heads + 2 * group + 1), :] = dv_ref[group].astype(BF16)
     store.start(dqkv_ref, dqkv_hbm)
-    for copy in later:
-        copy.wait()
+    h_came.wait()
 
     rows = width // 16
-    part = dot_tn(h_ref[...], dqkv_ref[...]).astype(BF16)
+    part = dot_tt(h_ref[...], dqkv_ref[...]).astype(BF16)
     first_ref[:, :heads_w] = part[:, :heads_w]
     second_ref[:, LATE_WIDTH - heads_w :] = part[:, heads_w:]
-    part = dot_tn(o_ref[...], attn_ref[...]).astype(BF16)
+    part = dot_tt(o_ref[...], attn_ref[...]).astype(BF16)
     first_ref[:, heads_w:] = part[:, :LATE_OUT]
     second_ref[:, : heads_w - LATE_OUT] = part[:, LATE_OUT:]
     for offset, (x_out, y_out) in enumerate(((x0, y0), (x1, y1), (x2, y2), (x3, y3))):
@@ -320,25 +312,25 @@
     store.wait()
 
 
-def attend_back(place, cosine, sine, pieces, weights, h_first, q, kt, v, attn, attnt, probs):
-    size, width = pieces[0].shape
-    heads, length, _ = q.shape
-    groups = v.shape[0]
-    every = heads + 2 * groups
+def attend_back(place, cosine, sine, pieces, weights, h_first, qt, kt, vt, attn, probs):
+    width = weights.shape[0]
+    heads, _, length = qt.shape
+    groups = kt.shape[0]
+    every_w = (heads + 2 * groups) * HD
     rows = width // 16
-    outs = [(length, every * HD)] + [(4 * rows, LATE_WIDTH)] * 4 + [(4, rows, LATE_WIDTH)] * 4
+    outs = [(every_w, length)] + [(4 * rows, LATE_WIDTH)] * 4 + [(4, rows, LATE_WIDTH)] * 4
     scratch = [
         (length, width), (width, heads * HD), (length, width),
-        q.shape, kt.shape, v.shape, attn.shape, attnt.shape, probs.shape,
-        (heads, length, HD), (heads, HD, length), (length, every * HD),
-        (width, LATE_WIDTH), (width, LATE_WIDTH),
+        qt.shape, kt.shape, vt.shape, attn.shape, probs.shape,
+        attn.shape, (every_w, length), (width, LATE_WIDTH), (width, LATE_WIDTH),
+        (groups, length, HD),
     ]
-    wide = [(heads, 1, length), (groups, length, HD), (groups, length, HD), (every, HD, length)]
+    wide = [(heads, 1, length), kt.shape, kt.shape]
     return kernel_call(
         attend_back_kernel, "attend_back", place, (cosine, sine),
-        (*pieces, weights, h_first, q, kt, v, attn, attnt, probs),
+        (*pieces, weights, h_first, qt, kt, vt, attn, probs),
         [like(s) for s in outs], [],
-        [vmem(s) for s in scratch] + [vmem(s, F32) for s in wide], 12, 21, heads)
+        [vmem(s) for s in scratch] + [vmem(s, F32) for s in wide], 11, 21, groups)
 
 
 def project_back_kernel(place, dqkv_hbm, w_hbm, c0, c1, c2, c3,
@@ -351,13 +343,13 @@
     fetch.wait()
     for step, out in ((3, c3), (2, c2), (1, c1), (0, c0)):
         at = block_at(lax.bitwise_xor(block, step), size)
-        part_ref[step] = dot_t(dqkv_ref[at, :], w_ref[...]).astype(BF16)
+        part_ref[step] = dot_tt(dqkv_ref[:, at], w_ref[...]).astype(BF16)
         store.start(part_ref.at[step], out)
     store.wait()
 
 
 def project_back(place, d_qkv, weights):
-    length, every_w = d_qkv.shape
+    every_w, length = d_qkv.shape
     width = weights.shape[0]
     size = length // 4
     return kernel_call(
@@ -578,6 +570,15 @@
     return lax.optimization_barrier((value, first))
 
 
+def from_ring(v, axis, offsets):
+    return [from_offset(v, axis, i, 4) for i in offsets]
+
+
+def stack_ring(v, received, offsets):
+    parts = dict(zip(offsets, received))
+    return jnp.stack([v] + [parts[i] for i in (1, 2, 3)])
+
+
 def from_both(along_first, first_axis, along_second, second_axis, large, beside=()):
     near = [
         from_offset(part[i], axis, i, 4)
@@ -594,13 +595,12 @@
     return first, second, beside
 
 
-def scatter_rows(v):
-    two = lax.psum_scatter(v, ("x", "z"), scatter_dimension=0, tiled=True)
-    rows = two.shape[0] // 2
-    iyh = lax.axis_index("yh")
-    keep = lax.dynamic_slice_in_dim(two, iyh * rows, rows, 0)
-    send = lax.dynamic_slice_in_dim(two, (1 - iyh) * rows, rows, 0)
-    return keep.astype(F32) + other(send, "yh").astype(F32)
+def pair_sum(v, axis):
+    rows = v.shape[0] // 2
+    me = lax.axis_index(axis)
+    keep = lax.dynamic_slice_in_dim(v, me * rows, rows, 0)
+    send = lax.dynamic_slice_in_dim(v, (1 - me) * rows, rows, 0)
+    return keep.astype(F32) + other(send, axis).astype(F32)
 
 
 def body(tokens, norm_gains, w_query, w_keyval, w_out, w_gateup, w_down, cotangent):
@@ -641,16 +641,27 @@
     first, second = attn_pair[:, :HALF_WIDTH], attn_pair[:, HALF_WIDTH:]
     first += side_by_side([(0, gain_high), (2, gain_low)], HALF_WIDTH)
 
-    first, mlp_pair = after(first, mlp_pair)
-    along_z, along_x, _ = from_both([first] * 4, "z", [second] * 4, "x", False)
-    along_z, along_x, mlp_pair, tokens = lax.optimization_barrier(
-        (jnp.stack(along_z), jnp.stack(along_x), mlp_pair, tokens)
-    )
+    second_x = from_ring(second, "x", (1, 3, 2))
+    second_x, first, mlp_pair, tokens = lax.optimization_barrier(
+        (second_x, first, mlp_pair, tokens))
+    second_own = stack_ring(second, second_x, (1, 3, 2))
+    first_z = from_ring(first, "z", (1, 3, 2))
+    second_near = from_ring(second_own, "z", (1, 3))
+    far = other(tokens, "yl")
+    first_z, second_near, mlp_pair, tokens = lax.optimization_barrier(
+        (first_z, second_near, mlp_pair, tokens))
     mlp_w = lax.all_gather(mlp_pair, ("x", "z"), axis=0, tiled=True)
-    along_x, along_z, far = from_both(
-        [along_z] * 4, "x", [along_x] * 4, "z", True, other(tokens, "yl")
-    )
-    token_pieces = [tokens, other(tokens, "core"), far, other(far, "core")]
+    first_own = stack_ring(first, first_z, (1, 3, 2))
+    first_near = from_ring(first_own, "x", (1, 3))
+    second_far = from_ring(second_own, "z", (2,))
+    near = other(tokens, "core")
+    first_near, second_far, far, near = lax.optimization_barrier(
+        (first_near, second_far, far, near))
+    first_own, first_near = after(first_own, first_near)
+    first_far = from_ring(first_own, "x", (2,))
+    along_x = [first_own, first_near[0], first_far[0], first_near[1]]
+    along_z = [second_own, second_near[0], second_far[0], second_near[1]]
+    token_pieces = [tokens, near, far, other(far, "core")]
     cotangent, far = after(cotangent, far)
     grad_far = other(cotangent, "yl")
 
@@ -659,7 +670,7 @@
     angles = freqs[:, None] * positions[None, :]
     cosine, sine = jnp.cos(angles), jnp.sin(angles)
 
-    gain_rows, attn_w, h_first, q, kt, v, attn, attnt, probs, *parts = attend(
+    gain_rows, attn_w, h_first, qt, kt, vt, attn, probs, *parts = attend(
         place, token_pieces, along_x, along_z, cosine, sine
     )
     grad_far, parts = after(grad_far, parts)
@@ -689,7 +700,7 @@
     mlp_grads = feed_grads(place, h_pieces, grad_pieces, dgu_a, dgu_b, hidden_a, hidden_b)
     mlp_grads, back_far = after(mlp_grads, other(back_far, "yl"))
     d_h2_own = back_near + back_far.astype(F32)
-    early = scatter_rows(mlp_grads)
+    early = lax.psum_scatter(mlp_grads, ("x", "z"), scatter_dimension=0, tiled=True)
     out_far = far_sum(out_chip, out_diag)
 
     d_norm2 = norm_back(d_h2_own, normed2, factor2, gain_rows[1])
@@ -702,7 +713,7 @@
     out_far = other(out_far, "yl")
 
     back = attend_back(
-        place, cosine, sine, out_pieces, attn_w, h_first, q, kt, v, attn, attnt, probs
+        place, cosine, sine, out_pieces, attn_w, h_first, qt, kt, vt, attn, probs
     )
     d_qkv, *late_parts = back
     d_qkv, out_far = after(d_qkv, out_far)
@@ -713,7 +724,10 @@
     result = (middle + out_near + out_far.astype(F32)).astype(BF16)
     along_x, result = after(along_x, result)
     middle_parts = late_middle(place, along_x, along_z)
-    along_z, along_x, _ = from_both(middle_parts[:4], "z", middle_parts[4:], "x", False)
+    along_z, along_x, early = from_both(
+        middle_parts[:4], "z", middle_parts[4:], "x", True, early
+    )
+    early = pair_sum(early, "yh")
     d_h1_own = near_sum(parts[0], parts[1]) + d_far.astype(F32)
     along_z, (d_h1_own, early) = after(along_z, (d_h1_own, early))
     late_keep, late_send = late_last(place, along_z, along_x)
@@ -734,8 +748,10 @@
             jnp.sum(grad_gateup * w_gateup.astype(F32), (1, 2)),
         ]
     )
-    for axis in ("core", "yl"):
-        gain_sum = gain_sum + other(gain_sum, axis)
+    gain_sum = gain_sum + sum(
+        lax.ppermute(gain_sum, ("yl", "core"), [(i ^ step, i) for i in range(4)])
+        for step in (1, 2, 3)
+    )
     grad_gains = lax.dynamic_slice(gain_sum, (0, block * gains_w), (2, gains_w)) / norm_gains
     return (
         result,

time: 351 us -> 383 us (1.091)
  waiting for transfers between devices: 115 us -> 147 us
  local copies, waits for them, and re-layouts: 11.2 us -> 30.8 us
  other arithmetic: 27.1 us -> 19.1 us
  Pallas kernels: 97.5 us -> 90 us
  starting transfers between devices: 79.3 us -> 74 us
    ppermute x57 -> x55, waiting for transfers between devices: 115 us -> 146 us  [from_offset(): lax.ppermute(v, axis, [((i + offset) % size, i) for i in range(size)])]
    unnamed x81 -> x135, local copies, waits for them, and re-layouts: 4.95 us -> 24 us
    ppermute x57 -> x55, starting transfers between devices: 79.3 us -> 64.7 us  [from_offset(): lax.ppermute(v, axis, [((i + offset) % size, i) for i in range(size)])]
    ppermute x0 -> x3, starting transfers between devices: none -> 9.2 us  [body(): lax.ppermute(gain_sum, ('yl', 'core'), [(i ^ step, i) for i in range(4)])]
    pallas_call x6, Pallas kernels: 92.1 us -> 84.5 us  [kernel_call(): pl.pallas_call(kernel, out_shape=list(small_outs) + list(outs), in_specs=...]
    convert_element_type x4, other arithmetic: 6.81 us -> 1.64 us  [far_sum(): return near_sum(chip, diagonal).astype(BF16)]
  transfers between devices with their start and end apart: 59 -> 60, of which waited for: 28 -> 31; matrix products, arithmetic and copies ran while one was open for 8% -> 6% of each run, Pallas kernels for 23% -> 19%
where the time goes in v5:
time: 383 us; the launch traced here: 376 us
  waiting for transfers between devices  147 us (38%)
  Pallas kernels  90 us (23%)
  starting transfers between devices  74 us (19%)
  local copies, waits for them, and re-layouts  30.8 us (8%)
  other arithmetic  19.1 us (5%)
  between operations  14.9 us (4%)
    ppermute x55, waiting for transfers between devices, from_offset(): lax.ppermute(v, axis, [((i + offset) % size, i) for i in range(size)])  146 us
    pallas_call x6, Pallas kernels, kernel_call(): pl.pallas_call(kernel, out_shape=list(small_outs) + list(outs), in_specs=...  84.5 us
    ppermute x55, starting transfers between devices, from_offset(): lax.ppermute(v, axis, [((i + offset) % size, i) for i in range(size)])  64.7 us
    unnamed x135, local copies, waits for them, and re-layouts  24 us
    ppermute x3, starting transfers between devices, body(): lax.ppermute(gain_sum, ('yl', 'core'), [(i ^ step, i) for i in range(4)])  9.2 us
  transfers between devices with their start and end apart: 60, of which 31 were waited for; matrix products, arithmetic and copies ran while one was open for 6% of the time, Pallas kernels for 19%

profile of v5, /device:TPU:1, one launch (start us, length us, event | category | flops | bytes accessed | tf_op | source)
XLA Modules:
  0.0 375.8 jit_solution(6693555009012972543)
XLA Ops:
  11.9 3.1 collective-permute-start
  21.7 6.0 %collective-permute-done.6 = f32[2,96]{0,1:T(8,128)S(1)} collective-permute-done((f32[2,96]{0,1:T(8,128)S(1)}, f32[2,96]{0,1:T(8,128)S(1)}, u32[]{:S(2)}, u32[]{:S(2)}) %collective-permute-start.6) | collective-permute-done | bytes 800 | tf_op jit(solution)/shard_map/ppermute | solution.py:542
  28.0 2.5 collective-permute-start.1
  33.3 4.3 %collective-permute-done.2 = bf16[96,640]{1,0:T(8,128)(2,1)S(1)} collective-permute-done((bf16[96,640]{1,0:T(8,128)(2,1)S(1)}, bf16[96,640]{1,0:T(8,128)(2,1)S(1)}, u32[]{:S(2)}, u32[]{:S(2)}) %collective-permute-start.2) | collective-permute-done | bytes 122912 | tf_op jit(solution)/shard_map/ppermute | solution.py:542
  37.6 3.8 %collective-permute-start.11 = (bf16[4,96,640]{2,1,0:T(8,128)(2,1)S(1)}, bf16[4,96,640]{2,1,0:T(8,128)(2,1)S(1)}, u32[]{:S(2)}, u32[]{:S(2)}) collective-permute-start(bf16[4,96,640]{2,1,0:T(8,128)(2,1)S(1)} %pad_maximum_fusion.b0), channel_id=1, source_target_pairs={{8,0},{16,8},{24,16},{0,24},{9,1},{17,9},{25,17},{1,25},{10,2},{18... | collective-permute-start | bytes 1474568 | tf_op jit(solution)/shard_map/ppermute | solution.py:542
  44.7 8.8 %collective-permute-done.10 = bf16[96,640]{1,0:T(8,128)(2,1)S(1)} collective-permute-done((bf16[96,640]{1,0:T(8,128)(2,1)S(1)}, bf16[96,640]{1,0:T(8,128)(2,1)S(1)}, u32[]{:S(2)}, u32[]{:S(2)}) %collective-permute-start.10) | collective-permute-done | bytes 122912 | tf_op jit(solution)/shard_map/ppermute | solution.py:542
  59.3 5.4 %collective-permute-start.17 = (bf16[256,1536]{1,0:T(8,128)(2,1)S(1)}, bf16[256,1536]{1,0:T(8,128)(2,1)S(1)}, u32[]{:S(2)}, u32[]{:S(2)}) collective-permute-start(bf16[256,1536]{1,0:T(8,128)(2,1)S(1)} %copy-done.1), channel_id=1, source_target_pairs={{1,0},{0,1},{3,2},{2,3},{5,4},{4,5},{7,6},{6,7},{9,8},{8,9},{11,10... | collective-permute-start | bytes 2359304 | tf_op jit(solution)/shard_map/ppermute | solution.py:542
  67.1 16.6 %collective-permute-done.15.b2 = bf16[4,96,640]{2,1,0:T(8,128)(2,1)S(1)} collective-permute-done((bf16[4,96,640]{2,1,0:T(8,128)(2,1)S(1)}, bf16[4,96,640]{2,1,0:T(8,128)(2,1)S(1)}, u32[]{:S(2)}, u32[]{:S(2)}) %collective-permute-start.15) | collective-permute-done | bytes 491552 | tf_op jit(solution)/shard_map/ppermute | solution.py:542
  89.2 2.4 collective-permute-start.19
  92.5 17.7 %collective-permute-done.20.a2 = bf16[4,96,640]{2,1,0:T(8,128)(2,1)} collective-permute-done((bf16[4,96,640]{2,1,0:T(8,128)(2,1)}, bf16[4,96,640]{2,1,0:T(8,128)(2,1)}, u32[]{:S(2)}, u32[]{:S(2)}) %collective-permute-start.20) | collective-permute-done | bytes 491552 | tf_op jit(solution)/shard_map/ppermute | solution.py:542
  116.6 16.5 %attend.1 = (f32[2,1536]{1,0:T(2,128)S(1)}, bf16[1536,1280]{1,0:T(8,128)(2,1)}, bf16[1024,1536]{1,0:T(8,128)(2,1)}, bf16[4,96,1024]{2,1,0:T(8,128)(2,1)S(1)}, bf...) custom-call(s32[4]{0:T(128)S(1)} %pad_add_fusion.2.place, ...), custom_call_target="tpu_custom_call" | custom-call | flops 1 | bytes 1 | tf_op jit(solution)/shard_map/attend/pallas_call | solution.py:90
  140.4 16.3 %collective-permute-done.23 = bf16[256,1536]{1,0:T(8,128)(2,1)S(1)} collective-permute-done((bf16[256,1536]{1,0:T(8,128)(2,1)S(1)}, bf16[256,1536]{1,0:T(8,128)(2,1)S(1)}, u32[]{:S(2)}, u32[]{:S(2)}) %collective-permute-start.23) | collective-permute-done | bytes 786464 | tf_op jit(solution)/shard_map/ppermute | solution.py:542
  166.1 15.6 %feed.2 = (bf16[512,1024]{1,0:T(8,128)(2,1)S(1)}, bf16[512,2048]{1,0:T(8,128)(2,1)S(1)}, bf16[256,1536]{1,0:T(8,128)(2,1)S(1)}, bf16[256,1536]{1,0:T(8,128)(2,1)...) custom-call(s32[4]{0:T(128)S(1)} %pad_add_fusion.2.place, bf16[256,1536]{1,0:T(8,128)(2,1)S(1)} %multiply_convert_fusion.h0, ...), custom_call_target="tpu_custom_call" | custom-call | flops 1 | bytes 1 | tf_op jit(solution)/shard_map/feed/pallas_call | solution.py:90
  185.0 2.3 collective-permute-done.27.h1.h3
  187.3 14.9 %feed.3 = (bf16[512,1024]{1,0:T(8,128)(2,1)S(1)}, bf16[512,2048]{1,0:T(8,128)(2,1)S(1)}, bf16[256,1536]{1,0:T(8,128)(2,1)S(1)}, bf16[256,1536]{1,0:T(8,128)(2,1)...) custom-call(s32[4]{0:T(128)S(1)} %pad_add_fusion.2.place, ...), custom_call_target="tpu_custom_call" | custom-call | flops 1 | bytes 1 | tf_op jit(solution)/shard_map/feed/pallas_call | solution.py:90
  208.2 14.7 %feed_grads.1 = bf16[1536,3072]{1,0:T(8,128)(2,1)} custom-call(s32[4]{0:T(128)S(1)} %pad_add_fusion.2.place, bf16[256,1536]{1,0:T(8,128)(2,1)S(1)} %multiply_convert_fusion.h0, bf16[256,1536]{1,0:T(8,128)(2,1)S(1)} %copy-done.8, bf16[256,1536]{1,0:T(8,128)(2,1)} %collective-permute-done.24.h0.h2, bf16[256,1536]{1,0:T(8,128)(2,1)S(1)} %collective-permute-done.27.h1.h3, ...), custom_call_target="tpu_custom_call" | custom-call | flops 1 | bytes 1 | tf_op jit(solution)/shard_map/feed_grads/pallas_call | solution.py:90
  222.8 4.0 %collective-permute-done.32 = bf16[256,1536]{1,0:T(8,128)(2,1)} collective-permute-done((bf16[256,1536]{1,0:T(8,128)(2,1)}, bf16[256,1536]{1,0:T(8,128)(2,1)}, u32[]{:S(2)}, u32[]{:S(2)}) %collective-permute-start.32) | collective-permute-done | bytes 786464 | tf_op jit(solution)/shard_map/ppermute | solution.py:542
  230.0 2.3 multiply_reduce_fusion
  232.3 3.1 fusion.10
  237.3 16.9 %collective-permute-done.34.o2 = bf16[256,1536]{1,0:T(8,128)(2,1)S(1)} collective-permute-done((bf16[256,1536]{1,0:T(8,128)(2,1)S(1)}, bf16[256,1536]{1,0:T(8,128)(2,1)S(1)}, u32[]{:S(2)}, u32[]{:S(2)}) %collective-permute-start.34) | collective-permute-done | bytes 786464 | tf_op jit(solution)/shard_map/ppermute | solution.py:542
  258.0 18.4 %attend_back.1 = (bf16[768,1024]{1,0:T(8,128)(2,1)S(1)}, bf16[384,576]{1,0:T(8,128)(2,1)S(1)}, bf16[384,576]{1,0:T(8,128)(2,1)S(1)}, bf16[384,576]{1,0:T(8,128)(...) custom-call(s32[4]{0:T(128)S(1)} %pad_add_fusion.2.place, ...), custom_call_target="tpu_custom_call" | custom-call | flops 1 | bytes 1 | tf_op jit(solution)/shard_map/attend_back/pallas_call | solution.py:90
  279.8 4.4 %project_back.1 = (bf16[256,1536]{1,0:T(8,128)(2,1)S(1)}, bf16[256,1536]{1,0:T(8,128)(2,1)S(1)}, bf16[256,1536]{1,0:T(8,128)(2,1)S(1)}, bf16[256,1536]{1,0:T(8,128)(2,1)S(1)}) custom-call(s32[4]{0:T(128)S(1)} %pad_add_fusion.2.place, bf16[768,1024]{1,0:T(8,128)(2,1)S(1)} %get-tuple-element.207.dqkv_hbm, bf16[1536,1280]{1,0:T(8,128)(2,1)S(1)} %copy-done), custom_call_target="tpu_custom_call" | custom-call | flops 1 | bytes 1 | tf_op jit(solution)/shard_map/project_back/pallas_call | solution.py:90
  284.2 11.6 %collective-permute-done.37.refs_1_ = bf16[384,576]{1,0:T(8,128)(2,1)S(1)} collective-permute-done((bf16[384,576]{1,0:T(8,128)(2,1)S(1)}, bf16[384,576]{1,0:T(8,128)(2,1)S(1)}, u32[]{:S(2)}, u32[]{:S(2)}) %collective-permute-start.37) | collective-permute-done | bytes 442400 | tf_op jit(solution)/shard_map/ppermute | solution.py:542
  305.2 12.1 %collective-permute-done.42.refs_2_ = bf16[384,576]{1,0:T(8,128)(2,1)S(1)} collective-permute-done((bf16[384,576]{1,0:T(8,128)(2,1)S(1)}, bf16[384,576]{1,0:T(8,128)(2,1)S(1)}, u32[]{:S(2)}, u32[]{:S(2)}) %collective-permute-start.42) | collective-permute-done | bytes 442400 | tf_op jit(solution)/shard_map/ppermute | solution.py:542
  319.8 3.4 late_middle.1
  323.2 3.8 collective-permute-start.44
  332.1 2.3 collective-permute-done.47.refs_7_
  335.4 3.8 %collective-permute-start.53 = (bf16[48,3072]{1,0:T(8,128)(2,1)S(1)}, bf16[48,3072]{1,0:T(8,128)(2,1)S(1)}, u32[]{:S(2)}, u32[]{:S(2)}) collective-permute-start(bf16[48,3072]{1,0:T(8,128)(2,1)S(1)} %constant_dynamic-slice_fusion), channel_id=1, source_target_pairs={{4,0},{0,4},{5,1},{1,5},{6,2},{2,6},{7,3},{3,7},{12,8},{8,12},{13,... | collective-permute-start | bytes 884744 | tf_op jit(solution)/shard_map/ppermute | solution.py:542
  339.2 3.7 collective-permute-start.48
  345.6 2.8 collective-permute-done.49.refs_6_
  349.1 2.2 late_last.1
  357.4 7.5 %collective-permute-start.55 = (f32[2,48]{1,0:T(2,128)S(1)}, f32[2,48]{1,0:T(2,128)S(1)}, u32[]{:S(2)}, u32[]{:S(2)}) collective-permute-start(f32[2,48]{1,0:T(2,128)S(1)} %pad_maximum_fusion.2), channel_id=1, source_target_pairs={{1,0},{0,1},{3,2},{2,3},{5,4},{4,5},{7,6},{6,7},{9,8},{8,9},{11,10... | collective-permute-start | bytes 1160 | tf_op jit(solution)/shard_map/ppermute | solution.py:752
  (286 shorter events, 107.9 us)
Async XLA Ops:
  7.2 156.7 %all-gather.2.cloned.1.call-start = ((), (), s32[]{:S(2)}) async-start(), calls=%async_computation.1 | async-start | bytes 10027008 | tf_op jit(solution)/shard_map/all_gather | solution.py:653
  11.9 15.9 %collective-permute-start = (bf16[48,1280]{1,0:T(8,128)(2,1)S(1)}, bf16[48,1280]{1,0:T(8,128)(2,1)S(1)}, u32[]{:S(2)}, u32[]{:S(2)}) collective-permute-start(bf16[48,1280]{1,0:T(8,128)(2,1)S(1)} %pad_add_fusion.1), channel_id=1, source_target_pairs={{4,0},{0,4},{5,1},{1,5},{6,2},{2,6},{7,3},{3,7},{12,8},{8,12},{13,... | collective-permute-start | bytes 368648 | tf_op jit(solution)/shard_map/ppermute | solution.py:542
  17.2 15.1 %collective-permute-start.7 = (bf16[48,3072]{1,0:T(8,128)(2,1)S(1)}, bf16[48,3072]{1,0:T(8,128)(2,1)S(1)}, u32[]{:S(2)}, u32[]{:S(2)}) collective-permute-start(bf16[48,3072]{1,0:T(8,128)(2,1)S(1)} %pad_add_fusion), channel_id=1, source_target_pairs={{4,0},{0,4},{5,1},{1,5},{6,2},{2,6},{7,3},{3,7},{12,8},{8,12},{13,... | collective-permute-start | bytes 884744 | tf_op jit(solution)/shard_map/ppermute | solution.py:542
  37.6 18.8 %collective-permute-start.11 = (bf16[4,96,640]{2,1,0:T(8,128)(2,1)S(1)}, bf16[4,96,640]{2,1,0:T(8,128)(2,1)S(1)}, u32[]{:S(2)}, u32[]{:S(2)}) collective-permute-start(bf16[4,96,640]{2,1,0:T(8,128)(2,1)S(1)} %pad_maximum_fusion.b0), channel_id=1, source_target_pairs={{8,0},{16,8},{24,16},{0,24},{9,1},{17,9},{25,17},{1,25},{10,2},{18... | collective-permute-start | bytes 1474568 | tf_op jit(solution)/shard_map/ppermute | solution.py:542
  41.5 15.8 %collective-permute-start.12 = (bf16[4,96,640]{2,1,0:T(8,128)(2,1)S(1)}, bf16[4,96,640]{2,1,0:T(8,128)(2,1)S(1)}, u32[]{:S(2)}, u32[]{:S(2)}) collective-permute-start(bf16[4,96,640]{2,1,0:T(8,128)(2,1)S(1)} %pad_maximum_fusion.b0), channel_id=1, source_target_pairs={{24,0},{0,8},{8,16},{16,24},{25,1},{1,9},{9,17},{17,25},{26,2},{2,... | collective-permute-start | bytes 1474568 | tf_op jit(solution)/shard_map/ppermute | solution.py:542
  58.1 276.3 %reduce-scatter.2.cloned.1.call-start = ((), (), s32[]{:S(2)}) async-start(), calls=%async_computation.2 | async-start | bytes 10027008 | tf_op jit(solution)/shard_map/reduce_scatter | solution.py:703
  58.2 26.3 %collective-permute-start.16 = (bf16[256,1536]{1,0:T(8,128)(2,1)S(1)}, bf16[256,1536]{1,0:T(8,128)(2,1)}, u32[]{:S(2)}, u32[]{:S(2)}) collective-permute-start(bf16[256,1536]{1,0:T(8,128)(2,1)S(1)} %copy-done.1), channel_id=1, source_target_pairs={{2,0},{0,2},{3,1},{1,3},{6,4},{4,6},{7,5},{5,7},{10,8},{8,10},{11,... | collective-permute-start | bytes 2359304 | tf_op jit(solution)/shard_map/ppermute | solution.py:542
  59.3 29.0 %collective-permute-start.17 = (bf16[256,1536]{1,0:T(8,128)(2,1)S(1)}, bf16[256,1536]{1,0:T(8,128)(2,1)S(1)}, u32[]{:S(2)}, u32[]{:S(2)}) collective-permute-start(bf16[256,1536]{1,0:T(8,128)(2,1)S(1)} %copy-done.1), channel_id=1, source_target_pairs={{1,0},{0,1},{3,2},{2,3},{5,4},{4,5},{7,6},{6,7},{9,8},{8,9},{11,10... | collective-permute-start | bytes 2359304 | tf_op jit(solution)/shard_map/ppermute | solution.py:542
  64.7 19.0 %collective-permute-start.15 = (bf16[4,96,640]{2,1,0:T(8,128)(2,1)S(1)}, bf16[4,96,640]{2,1,0:T(8,128)(2,1)S(1)}, u32[]{:S(2)}, u32[]{:S(2)}) collective-permute-start(bf16[4,96,640]{2,1,0:T(8,128)(2,1)S(1)} %pad_maximum_fusion.b0), channel_id=1, source_target_pairs={{16,0},{24,8},{0,16},{8,24},{17,1},{25,9},{1,17},{9,25},{18,2},{26... | collective-permute-start | bytes 1474568 | tf_op jit(solution)/shard_map/ppermute | solution.py:542
  65.6 19.2 %collective-permute-start.13 = (bf16[4,96,640]{2,1,0:T(8,128)(2,1)}, bf16[4,96,640]{2,1,0:T(8,128)(2,1)S(1)}, u32[]{:S(2)}, u32[]{:S(2)}) collective-permute-start(bf16[4,96,640]{2,1,0:T(8,128)(2,1)} %pad_maximum_fusion.1.a0), channel_id=1, source_target_pairs={{32,0},{64,32},{96,64},{0,96},{33,1},{65,33},{97,65},{1,97},{34,2}... | collective-permute-start | bytes 1474568 | tf_op jit(solution)/shard_map/ppermute | solution.py:542
  66.6 20.9 %collective-permute-start.14 = (bf16[4,96,640]{2,1,0:T(8,128)(2,1)}, bf16[4,96,640]{2,1,0:T(8,128)(2,1)S(1)}, u32[]{:S(2)}, u32[]{:S(2)}) collective-permute-start(bf16[4,96,640]{2,1,0:T(8,128)(2,1)} %pad_maximum_fusion.1.a0), channel_id=1, source_target_pairs={{96,0},{0,32},{32,64},{64,96},{97,1},{1,33},{33,65},{65,97},{98,2}... | collective-permute-start | bytes 1474568 | tf_op jit(solution)/shard_map/ppermute | solution.py:542
  89.2 21.0 %collective-permute-start.19 = (bf16[256,1536]{1,0:T(8,128)(2,1)}, bf16[256,1536]{1,0:T(8,128)(2,1)}, u32[]{:S(2)}, u32[]{:S(2)}) collective-permute-start(bf16[256,1536]{1,0:T(8,128)(2,1)} %collective-permute-done.16.t2), channel_id=1, source_target_pairs={{1,0},{0,1},{3,2},{2,3},{5,4},{4,5},{7,6},{6,7},{9,8},{8,9},{11,10... | collective-permute-start | bytes 2359304 | tf_op jit(solution)/shard_map/ppermute | solution.py:542
  91.6 41.5 %collective-permute-start.18 = (bf16[256,1536]{1,0:T(8,128)(2,1)S(1)}, bf16[256,1536]{1,0:T(8,128)(2,1)S(1)}, u32[]{:S(2)}, u32[]{:S(2)}) collective-permute-start(bf16[256,1536]{1,0:T(8,128)(2,1)S(1)} %copy-done.2), channel_id=1, source_target_pairs={{2,0},{0,2},{3,1},{1,3},{6,4},{4,6},{7,5},{5,7},{10,8},{8,10},{11,... | collective-permute-start | bytes 2359304 | tf_op jit(solution)/shard_map/ppermute | solution.py:542
  91.6 18.6 %collective-permute-start.20 = (bf16[4,96,640]{2,1,0:T(8,128)(2,1)}, bf16[4,96,640]{2,1,0:T(8,128)(2,1)}, u32[]{:S(2)}, u32[]{:S(2)}) collective-permute-start(bf16[4,96,640]{2,1,0:T(8,128)(2,1)} %pad_maximum_fusion.1.a0), channel_id=1, source_target_pairs={{64,0},{96,32},{0,64},{32,96},{65,1},{97,33},{1,65},{33,97},{66,2}... | collective-permute-start | bytes 1474568 | tf_op jit(solution)/shard_map/ppermute | solution.py:542
  137.1 19.6 %collective-permute-start.23 = (bf16[256,1536]{1,0:T(8,128)(2,1)S(1)}, bf16[256,1536]{1,0:T(8,128)(2,1)S(1)}, u32[]{:S(2)}, u32[]{:S(2)}) collective-permute-start(bf16[256,1536]{1,0:T(8,128)(2,1)S(1)} %add_convert_fusion.4), channel_id=1, source_target_pairs={{2,0},{0,2},{3,1},{1,3},{6,4},{4,6},{7,5},{5,7},{10,8},{8,10},{11,... | collective-permute-start | bytes 2359304 | tf_op jit(solution)/shard_map/ppermute | solution.py:542
  139.1 23.0 %collective-permute-start.26 = (bf16[256,1536]{1,0:T(8,128)(2,1)S(1)}, bf16[256,1536]{1,0:T(8,128)(2,1)S(1)}, u32[]{:S(2)}, u32[]{:S(2)}) collective-permute-start(bf16[256,1536]{1,0:T(8,128)(2,1)S(1)} %copy-done.2), channel_id=1, source_target_pairs={{1,0},{0,1},{3,2},{2,3},{5,4},{4,5},{7,6},{6,7},{9,8},{8,9},{11,10... | collective-permute-start | bytes 2359304 | tf_op jit(solution)/shard_map/ppermute | solution.py:542
  160.2 24.2 %collective-permute-start.24 = (bf16[256,1536]{1,0:T(8,128)(2,1)S(1)}, bf16[256,1536]{1,0:T(8,128)(2,1)}, u32[]{:S(2)}, u32[]{:S(2)}) collective-permute-start(bf16[256,1536]{1,0:T(8,128)(2,1)S(1)} %multiply_convert_fusion.h0), channel_id=1, source_target_pairs={{2,0},{0,2},{3,1},{1,3},{6,4},{4,6},{7,5},{5,7},{10,8},{8,10},{11,... | collective-permute-start | bytes 2359304 | tf_op jit(solution)/shard_map/ppermute | solution.py:542
  161.7 23.3 %collective-permute-start.28 = (bf16[256,1536]{1,0:T(8,128)(2,1)S(1)}, bf16[256,1536]{1,0:T(8,128)(2,1)}, u32[]{:S(2)}, u32[]{:S(2)}) collective-permute-start(bf16[256,1536]{1,0:T(8,128)(2,1)S(1)} %collective-permute-done.18.g0.g2), channel_id=1, source_target_pairs={{1,0},{0,1},{3,2},{2,3},{5,4},{4,5},{7,6},{6,7},{9,8},{8,9},{11,10... | collective-permute-start | bytes 2359304 | tf_op jit(solution)/shard_map/ppermute | solution.py:542
  207.4 19.5 %collective-permute-start.32 = (bf16[256,1536]{1,0:T(8,128)(2,1)}, bf16[256,1536]{1,0:T(8,128)(2,1)}, u32[]{:S(2)}, u32[]{:S(2)}) collective-permute-start(bf16[256,1536]{1,0:T(8,128)(2,1)} %add_convert_fusion.2), channel_id=1, source_target_pairs={{2,0},{0,2},{3,1},{1,3},{6,4},{4,6},{7,5},{5,7},{10,8},{8,10},{11,... | collective-permute-start | bytes 2359304 | tf_op jit(solution)/shard_map/ppermute | solution.py:542
  235.4 18.8 %collective-permute-start.34 = (bf16[256,1536]{1,0:T(8,128)(2,1)S(1)}, bf16[256,1536]{1,0:T(8,128)(2,1)S(1)}, u32[]{:S(2)}, u32[]{:S(2)}) collective-permute-start(bf16[256,1536]{1,0:T(8,128)(2,1)S(1)} %get-tuple-element.187.o0), channel_id=1, source_target_pairs={{2,0},{0,2},{3,1},{1,3},{6,4},{4,6},{7,5},{5,7},{10,8},{8,10},{11,... | collective-permute-start | bytes 2359304 | tf_op jit(solution)/shard_map/ppermute | solution.py:542
  236.1 19.3 %collective-permute-start.29 = (bf16[256,1536]{1,0:T(8,128)(2,1)S(1)}, bf16[256,1536]{1,0:T(8,128)(2,1)S(1)}, u32[]{:S(2)}, u32[]{:S(2)}) collective-permute-start(bf16[256,1536]{1,0:T(8,128)(2,1)S(1)} %copy-done.40), channel_id=1, source_target_pairs={{1,0},{0,1},{3,2},{2,3},{5,4},{4,5},{7,6},{6,7},{9,8},{8,9},{11,10... | collective-permute-start | bytes 2359304 | tf_op jit(solution)/shard_map/ppermute | solution.py:542
  237.2 18.4 %collective-permute-start.33 = (bf16[256,1536]{1,0:T(8,128)(2,1)S(1)}, bf16[256,1536]{1,0:T(8,128)(2,1)S(1)}, u32[]{:S(2)}, u32[]{:S(2)}) collective-permute-start(bf16[256,1536]{1,0:T(8,128)(2,1)S(1)} %get-tuple-element.187.o0), channel_id=1, source_target_pairs={{1,0},{0,1},{3,2},{2,3},{5,4},{4,5},{7,6},{6,7},{9,8},{8,9},{11,10... | collective-permute-start | bytes 2359304 | tf_op jit(solution)/shard_map/ppermute | solution.py:542
  257.3 22.5 %collective-permute-start.41 = (bf16[256,1536]{1,0:T(8,128)(2,1)S(1)}, bf16[256,1536]{1,0:T(8,128)(2,1)S(1)}, u32[]{:S(2)}, u32[]{:S(2)}) collective-permute-start(bf16[256,1536]{1,0:T(8,128)(2,1)S(1)} %add_convert_fusion.3), channel_id=1, source_target_pairs={{2,0},{0,2},{3,1},{1,3},{6,4},{4,6},{7,5},{5,7},{10,8},{8,10},{11,... | collective-permute-start | bytes 2359304 | tf_op jit(solution)/shard_map/ppermute | solution.py:542
  276.4 19.4 %collective-permute-start.37 = (bf16[384,576]{1,0:T(8,128)(2,1)S(1)}, bf16[384,576]{1,0:T(8,128)(2,1)S(1)}, u32[]{:S(2)}, u32[]{:S(2)}) collective-permute-start(bf16[384,576]{1,0:T(8,128)(2,1)S(1)} %get-tuple-element.201), channel_id=1, source_target_pairs={{32,0},{64,32},{96,64},{0,96},{33,1},{65,33},{97,65},{1,97},{34,2}... | collective-permute-start | bytes 1327112 | tf_op jit(solution)/shard_map/ppermute | solution.py:542
  276.5 19.3 %collective-permute-start.38 = (bf16[4,96,576]{2,1,0:T(8,128)(2,1)S(1)}, bf16[4,96,576]{2,1,0:T(8,128)(2,1)S(1)}, u32[]{:S(2)}, u32[]{:S(2)}) collective-permute-start(bf16[4,96,576]{2,1,0:T(8,128)(2,1)S(1)} %get-tuple-element.202), channel_id=1, source_target_pairs={{8,0},{16,8},{24,16},{0,24},{9,1},{17,9},{25,17},{1,25},{10,2},{18... | collective-permute-start | bytes 1327112 | tf_op jit(solution)/shard_map/ppermute | solution.py:542
  277.0 20.1 %collective-permute-start.39 = (bf16[384,576]{1,0:T(8,128)(2,1)S(1)}, bf16[384,576]{1,0:T(8,128)(2,1)S(1)}, u32[]{:S(2)}, u32[]{:S(2)}) collective-permute-start(bf16[384,576]{1,0:T(8,128)(2,1)S(1)} %get-tuple-element.203), channel_id=1, source_target_pairs={{96,0},{0,32},{32,64},{64,96},{97,1},{1,33},{33,65},{65,97},{98,2}... | collective-permute-start | bytes 1327112 | tf_op jit(solution)/shard_map/ppermute | solution.py:542
  278.4 19.6 %collective-permute-start.40 = (bf16[4,96,576]{2,1,0:T(8,128)(2,1)S(1)}, bf16[4,96,576]{2,1,0:T(8,128)(2,1)S(1)}, u32[]{:S(2)}, u32[]{:S(2)}) collective-permute-start(bf16[4,96,576]{2,1,0:T(8,128)(2,1)S(1)} %get-tuple-element.204), channel_id=1, source_target_pairs={{24,0},{0,8},{8,16},{16,24},{25,1},{1,9},{9,17},{17,25},{26,2},{2,... | collective-permute-start | bytes 1327112 | tf_op jit(solution)/shard_map/ppermute | solution.py:542
  299.2 18.1 %collective-permute-start.42 = (bf16[384,576]{1,0:T(8,128)(2,1)S(1)}, bf16[384,576]{1,0:T(8,128)(2,1)S(1)}, u32[]{:S(2)}, u32[]{:S(2)}) collective-permute-start(bf16[384,576]{1,0:T(8,128)(2,1)S(1)} %get-tuple-element.216), channel_id=1, source_target_pairs={{64,0},{96,32},{0,64},{32,96},{65,1},{97,33},{1,65},{33,97},{66,2}... | collective-permute-start | bytes 1327112 | tf_op jit(solution)/shard_map/ppermute | solution.py:542
  300.4 18.6 %collective-permute-start.43 = (bf16[4,96,576]{2,1,0:T(8,128)(2,1)S(1)}, bf16[4,96,576]{2,1,0:T(8,128)(2,1)S(1)}, u32[]{:S(2)}, u32[]{:S(2)}) collective-permute-start(bf16[4,96,576]{2,1,0:T(8,128)(2,1)S(1)} %get-tuple-element.217), channel_id=1, source_target_pairs={{16,0},{24,8},{0,16},{8,24},{17,1},{25,9},{1,17},{9,25},{18,2},{26... | collective-permute-start | bytes 1327112 | tf_op jit(solution)/shard_map/ppermute | solution.py:542
  301.8 41.0 %collective-permute-start.50 = (bf16[256,1536]{1,0:T(8,128)(2,1)S(1)}, bf16[256,1536]{1,0:T(8,128)(2,1)}, u32[]{:S(2)}, u32[]{:S(2)}) collective-permute-start(bf16[256,1536]{1,0:T(8,128)(2,1)S(1)} %get-tuple-element.250), channel_id=1, source_target_pairs={{1,0},{0,1},{3,2},{2,3},{5,4},{4,5},{7,6},{6,7},{9,8},{8,9},{11,10... | collective-permute-start | bytes 2359304 | tf_op jit(solution)/shard_map/ppermute | solution.py:542
  302.6 40.3 %collective-permute-start.52 = (bf16[256,1536]{1,0:T(8,128)(2,1)S(1)}, bf16[256,1536]{1,0:T(8,128)(2,1)}, u32[]{:S(2)}, u32[]{:S(2)}) collective-permute-start(bf16[256,1536]{1,0:T(8,128)(2,1)S(1)} %add_convert_fusion), channel_id=1, source_target_pairs={{2,0},{0,2},{3,1},{1,3},{6,4},{4,6},{7,5},{5,7},{10,8},{8,10},{11,... | collective-permute-start | bytes 2359304 | tf_op jit(solution)/shard_map/ppermute | solution.py:542
  335.4 13.0 %collective-permute-start.53 = (bf16[48,3072]{1,0:T(8,128)(2,1)S(1)}, bf16[48,3072]{1,0:T(8,128)(2,1)S(1)}, u32[]{:S(2)}, u32[]{:S(2)}) collective-permute-start(bf16[48,3072]{1,0:T(8,128)(2,1)S(1)} %constant_dynamic-slice_fusion), channel_id=1, source_target_pairs={{4,0},{0,4},{5,1},{1,5},{6,2},{2,6},{7,3},{3,7},{12,8},{8,12},{13,... | collective-permute-start | bytes 884744 | tf_op jit(solution)/shard_map/ppermute | solution.py:542
  (95 other events, 886.1 us)
Sparse Core Ops, SparseCore 0:
  58.2 86.6 all-gather.1
  227.0 99.7 reduce-scatter.1

commit v6 on v5

--- a/solution.py
+++ b/solution.py
@@ -18,7 +18,7 @@
 GAIN_AT, OUT_AT, QUERY_AT, KEYVAL_AT, REST_AT, ATTN_WIDTH = 0, 128, 256, 640, 1024, 1280
 HALF_WIDTH = ATTN_WIDTH // 2
 OUT_CUT = QUERY_AT - OUT_AT
-LIMIT = 39
+LIMIT = 60
 
 
 def dot_n(left, right):
@@ -494,6 +494,7 @@
         out_shape=[like((rows, width))] * 8,
         in_specs=[scalars()] + [whole()] * 8,
         out_specs=[whole()] * 8,
+        compiler_params=pltpu.CompilerParams(vmem_limit_bytes=16 * MIB),
         cost_estimate=SMALL,
         name="late_middle",
     )(place, *along_x, *along_z)
@@ -522,6 +523,7 @@
         ],
         in_specs=[scalars()] + [whole()] * 8,
         out_specs=[whole()] * 2,
+        compiler_params=pltpu.CompilerParams(vmem_limit_bytes=16 * MIB),
         cost_estimate=SMALL,
         name="late_last",
     )(place, *along_z, *along_x)
@@ -568,15 +570,6 @@
 
 def after(value, first):
     return lax.optimization_barrier((value, first))
-
-
-def from_ring(v, axis, offsets):
-    return [from_offset(v, axis, i, 4) for i in offsets]
-
-
-def stack_ring(v, received, offsets):
-    parts = dict(zip(offsets, received))
-    return jnp.stack([v] + [parts[i] for i in (1, 2, 3)])
 
 
 def from_both(along_first, first_axis, along_second, second_axis, large, beside=()):
@@ -625,15 +618,14 @@
         ATTN_WIDTH,
     )
     attn_pair = pair_rows(attn_own, "yh")
-    mlp_own = (w_gateup[:, 0], w_gateup[:, 1], w_down.T)
-    mlp_own = [(i * hidden_w, part) for i, part in enumerate(mlp_own)]
-    mlp_pair = pair_rows(side_by_side(mlp_own, 3 * hidden_w), "yh")
-
     pair_w = 8 * gains_w
     gain_at = (lax.axis_index("yh") * 4 + block) * gains_w
     gain_part = lax.dynamic_update_slice(jnp.zeros((2, pair_w), F32), norm_gains, (0, gain_at))
     for axis in ("core", "yl", "yh"):
         gain_part = gain_part + other(gain_part, axis)
+    mlp_own, gain_part = after((w_gateup[:, 0], w_gateup[:, 1], w_down.T), gain_part)
+    mlp_own = [(i * hidden_w, part) for i, part in enumerate(mlp_own)]
+    mlp_pair = pair_rows(side_by_side(mlp_own, 3 * hidden_w), "yh")
     gain_part = gain_part.T
     gain_high = lax.reduce_precision(gain_part, 8, 7)
     gain_low = (gain_part - gain_high).astype(BF16)
@@ -641,27 +633,15 @@
     first, second = attn_pair[:, :HALF_WIDTH], attn_pair[:, HALF_WIDTH:]
     first += side_by_side([(0, gain_high), (2, gain_low)], HALF_WIDTH)
 
-    second_x = from_ring(second, "x", (1, 3, 2))
-    second_x, first, mlp_pair, tokens = lax.optimization_barrier(
-        (second_x, first, mlp_pair, tokens))
-    second_own = stack_ring(second, second_x, (1, 3, 2))
-    first_z = from_ring(first, "z", (1, 3, 2))
-    second_near = from_ring(second_own, "z", (1, 3))
-    far = other(tokens, "yl")
-    first_z, second_near, mlp_pair, tokens = lax.optimization_barrier(
-        (first_z, second_near, mlp_pair, tokens))
+    along_z, along_x, _ = from_both([first] * 4, "z", [second] * 4, "x", False)
+    along_z, along_x, mlp_pair, tokens = lax.optimization_barrier(
+        (jnp.stack(along_z), jnp.stack(along_x), mlp_pair, tokens)
+    )
     mlp_w = lax.all_gather(mlp_pair, ("x", "z"), axis=0, tiled=True)
-    first_own = stack_ring(first, first_z, (1, 3, 2))
-    first_near = from_ring(first_own, "x", (1, 3))
-    second_far = from_ring(second_own, "z", (2,))
-    near = other(tokens, "core")
-    first_near, second_far, far, near = lax.optimization_barrier(
-        (first_near, second_far, far, near))
-    first_own, first_near = after(first_own, first_near)
-    first_far = from_ring(first_own, "x", (2,))
-    along_x = [first_own, first_near[0], first_far[0], first_near[1]]
-    along_z = [second_own, second_near[0], second_far[0], second_near[1]]
-    token_pieces = [tokens, near, far, other(far, "core")]
+    along_x, along_z, far = from_both(
+        [along_z] * 4, "x", [along_x] * 4, "z", True, other(tokens, "yl")
+    )
+    token_pieces = [tokens, other(tokens, "core"), far, other(far, "core")]
     cotangent, far = after(cotangent, far)
     grad_far = other(cotangent, "yl")
 
@@ -696,7 +676,7 @@
     out_near = near_sum(out_own, out_core)
 
     back_far = far_sum(back_chip, back_diag)
-    hidden_b, back_far = after(hidden_b, back_far)
+    hidden_b, (back_far, back_near) = after(hidden_b, (back_far, back_near))
     mlp_grads = feed_grads(place, h_pieces, grad_pieces, dgu_a, dgu_b, hidden_a, hidden_b)
     mlp_grads, back_far = after(mlp_grads, other(back_far, "yl"))
     d_h2_own = back_near + back_far.astype(F32)

time: 383 us -> 339 us (0.89)
  waiting for transfers between devices: 147 us -> 101 us
  local copies, waits for them, and re-layouts: 30.8 us -> 11.6 us
  starting transfers between devices: 74 us -> 88.9 us
  other arithmetic: 19.1 us -> 27.7 us
    ppermute x55, waiting for transfers between devices: 146 us -> 101 us  [from_offset(): lax.ppermute(v, axis, [((i + offset) % size, i) for i in range(size)])]
    unnamed x135 -> x77, local copies, waits for them, and re-layouts: 24 us -> 4.46 us
    ppermute x55, starting transfers between devices: 64.7 us -> 80.7 us  [from_offset(): lax.ppermute(v, axis, [((i + offset) % size, i) for i in range(size)])]
    convert_element_type x4, other arithmetic: 1.64 us -> 5.71 us  [far_sum(): return near_sum(chip, diagonal).astype(BF16)]
  transfers between devices with their start and end apart: 60 -> 60, of which waited for: 31 -> 26; matrix products, arithmetic and copies ran while one was open for 6% -> 9% of each run, Pallas kernels for 19% -> 26%
where the time goes in v6:
time: 339 us; the launch traced here: 333 us
  waiting for transfers between devices  101 us (30%)
  starting transfers between devices  88.9 us (26%)
  Pallas kernels  88.1 us (26%)
  other arithmetic  27.7 us (8%)
  between operations  15.1 us (4%)
  local copies, waits for them, and re-layouts  11.6 us (3%)
    ppermute x55, waiting for transfers between devices, from_offset(): lax.ppermute(v, axis, [((i + offset) % size, i) for i in range(size)])  101 us
    pallas_call x6, Pallas kernels, kernel_call(): pl.pallas_call(kernel, out_shape=list(small_outs) + list(outs), in_specs=...  86.4 us
    ppermute x55, starting transfers between devices, from_offset(): lax.ppermute(v, axis, [((i + offset) % size, i) for i in range(size)])  80.7 us
    ppermute x3, starting transfers between devices, body(): lax.ppermute(gain_sum, ('yl', 'core'), [(i ^ step, i) for i in range(4)])  8.07 us
  transfers between devices with their start and end apart: 60, of which 26 were waited for; matrix products, arithmetic and copies ran while one was open for 9% of the time, Pallas kernels for 26%

profile of v6, /device:TPU:1, one launch (start us, length us, event | category | flops | bytes accessed | tf_op | source)
XLA Modules:
  0.0 332.5 jit_solution(3402105346106067339)
XLA Ops:
  12.0 3.1 collective-permute-start
  17.2 2.5 collective-permute-done.2
  21.8 2.4 collective-permute-done.3
  24.4 3.8 %collective-permute-start.4 = (bf16[96,640]{1,0:T(8,128)(2,1)S(1)}, bf16[96,640]{1,0:T(8,128)(2,1)S(1)}, u32[]{:S(2)}, u32[]{:S(2)}) collective-permute-start(bf16[96,640]{1,0:T(8,128)(2,1)S(1)} %get-tuple-element.292), channel_id=1, source_target_pairs={{8,0},{16,8},{24,16},{0,24},{9,1},{17,9},{25,17},{1,25},{10,2},{18... | collective-permute-start | bytes 368648 | tf_op jit(solution)/shard_map/ppermute | solution.py:544
  28.2 2.5 collective-permute-start.5
  37.7 3.5 %collective-permute-done.10 = bf16[48,3072]{1,0:T(8,128)(2,1)S(1)} collective-permute-done((bf16[48,3072]{1,0:T(8,128)(2,1)S(1)}, bf16[48,3072]{1,0:T(8,128)(2,1)S(1)}, u32[]{:S(2)}, u32[]{:S(2)}) %collective-permute-start.10) | collective-permute-done | bytes 294944 | tf_op jit(solution)/shard_map/ppermute | solution.py:544
  45.5 2.4 collective-permute-start.12
  47.9 3.7 %collective-permute-done.11.a1 = bf16[4,96,640]{2,1,0:T(8,128)(2,1)S(1)} collective-permute-done((bf16[4,96,640]{2,1,0:T(8,128)(2,1)S(1)}, bf16[4,96,640]{2,1,0:T(8,128)(2,1)S(1)}, u32[]{:S(2)}, u32[]{:S(2)}) %collective-permute-start.11) | collective-permute-done | bytes 491552 | tf_op jit(solution)/shard_map/ppermute | solution.py:544
  51.7 6.8 %collective-permute-start.17 = (bf16[256,1536]{1,0:T(8,128)(2,1)S(1)}, bf16[256,1536]{1,0:T(8,128)(2,1)}, u32[]{:S(2)}, u32[]{:S(2)}) collective-permute-start(bf16[256,1536]{1,0:T(8,128)(2,1)S(1)} %copy-done.3), channel_id=1, source_target_pairs={{1,0},{0,1},{3,2},{2,3},{5,4},{4,5},{7,6},{6,7},{9,8},{8,9},{11,10... | collective-permute-start | bytes 2359304 | tf_op jit(solution)/shard_map/ppermute | solution.py:544
  58.6 16.1 %collective-permute-start.18 = (bf16[256,1536]{1,0:T(8,128)(2,1)}, bf16[256,1536]{1,0:T(8,128)(2,1)}, u32[]{:S(2)}, u32[]{:S(2)}) collective-permute-start(bf16[256,1536]{1,0:T(8,128)(2,1)} %collective-permute-done.15.t2), channel_id=1, source_target_pairs={{1,0},{0,1},{3,2},{2,3},{5,4},{4,5},{7,6},{6,7},{9,8},{8,9},{11,10... | collective-permute-start | bytes 2359304 | tf_op jit(solution)/shard_map/ppermute | solution.py:544
  77.1 11.9 %collective-permute-done.19.a2 = bf16[4,96,640]{2,1,0:T(8,128)(2,1)} collective-permute-done((bf16[4,96,640]{2,1,0:T(8,128)(2,1)S(1)}, bf16[4,96,640]{2,1,0:T(8,128)(2,1)}, u32[]{:S(2)}, u32[]{:S(2)}) %collective-permute-start.19) | collective-permute-done | bytes 491552 | tf_op jit(solution)/shard_map/ppermute | solution.py:544
  89.0 17.9 %attend.1 = (f32[2,1536]{1,0:T(2,128)}, bf16[1536,1280]{1,0:T(8,128)(2,1)}, bf16[1024,1536]{1,0:T(8,128)(2,1)}, bf16[4,96,1024]{2,1,0:T(8,128)(2,1)}, bf16[2,96,...) custom-call(s32[4]{0:T(128)} %pad_add_fusion.2.place, ...), custom_call_target="tpu_custom_call" | custom-call | flops 1 | bytes 1 | tf_op jit(solution)/shard_map/attend/pallas_call | solution.py:90
  114.4 16.7 %collective-permute-done.23 = bf16[256,1536]{1,0:T(8,128)(2,1)S(1)} collective-permute-done((bf16[256,1536]{1,0:T(8,128)(2,1)S(1)}, bf16[256,1536]{1,0:T(8,128)(2,1)S(1)}, u32[]{:S(2)}, u32[]{:S(2)}) %collective-permute-start.23) | collective-permute-done | bytes 786464 | tf_op jit(solution)/shard_map/ppermute | solution.py:544
  135.9 14.7 %feed.2 = (bf16[512,1024]{1,0:T(8,128)(2,1)}, bf16[512,2048]{1,0:T(8,128)(2,1)}, bf16[256,1536]{1,0:T(8,128)(2,1)}, bf16[256,1536]{1,0:T(8,128)(2,1)}, bf16[256,...) custom-call(s32[4]{0:T(128)} %pad_add_fusion.2.place, bf16[256,1536]{1,0:T(8,128)(2,1)} %copy-done.8, ...), custom_call_target="tpu_custom_call" | custom-call | flops 1 | bytes 1 | tf_op jit(solution)/shard_map/feed/pallas_call | solution.py:90
  156.3 14.8 %feed.3 = (bf16[512,1024]{1,0:T(8,128)(2,1)}, bf16[512,2048]{1,0:T(8,128)(2,1)}, bf16[256,1536]{1,0:T(8,128)(2,1)}, bf16[256,1536]{1,0:T(8,128)(2,1)}, bf16[256,...) custom-call(s32[4]{0:T(128)} %pad_add_fusion.2.place, bf16[256,1536]{1,0:T(8,128)(2,1)} %collective-permute-done.24.h0.h2, ...), custom_call_target="tpu_custom_call" | custom-call | flops 1 | bytes 1 | tf_op jit(solution)/shard_map/feed/pallas_call | solution.py:90
  176.8 15.3 %feed_grads.1 = bf16[1536,3072]{1,0:T(8,128)(2,1)} custom-call(s32[4]{0:T(128)} %pad_add_fusion.2.place, bf16[256,1536]{1,0:T(8,128)(2,1)} %copy-done.8, bf16[256,1536]{1,0:T(8,128)(2,1)} %collective-permute-done.25.h1, bf16[256,1536]{1,0:T(8,128)(2,1)} %collective-permute-done.24.h0.h2, bf16[256,1536]{1,0:T(8,128)(2,1)} %copy-done.12, ...), custom_call_target="tpu_custom_call" | custom-call | flops 1 | bytes 1 | tf_op jit(solution)/shard_map/feed_grads/pallas_call | solution.py:90
  192.1 2.5 collective-permute-done.32
  197.3 3.0 fusion.10
  203.7 15.7 %collective-permute-done.34.o2 = bf16[256,1536]{1,0:T(8,128)(2,1)S(1)} collective-permute-done((bf16[256,1536]{1,0:T(8,128)(2,1)S(1)}, bf16[256,1536]{1,0:T(8,128)(2,1)S(1)}, u32[]{:S(2)}, u32[]{:S(2)}) %collective-permute-start.34) | collective-permute-done | bytes 786464 | tf_op jit(solution)/shard_map/ppermute | solution.py:544
  224.6 17.2 %attend_back.1 = (bf16[768,1024]{1,0:T(8,128)(2,1)}, bf16[384,576]{1,0:T(8,128)(2,1)}, bf16[384,576]{1,0:T(8,128)(2,1)}, bf16[384,576]{1,0:T(8,128)(2,1)}, bf16[...) custom-call(s32[4]{0:T(128)} %pad_add_fusion.2.place, ...), custom_call_target="tpu_custom_call" | custom-call | flops 1 | bytes 1 | tf_op jit(solution)/shard_map/attend_back/pallas_call | solution.py:90
  241.8 3.3 collective-permute-start.37
  246.8 6.5 %project_back.1 = (bf16[256,1536]{1,0:T(8,128)(2,1)}, bf16[256,1536]{1,0:T(8,128)(2,1)}, bf16[256,1536]{1,0:T(8,128)(2,1)}, bf16[256,1536]{1,0:T(8,128)(2,1)}) custom-call(s32[4]{0:T(128)} %pad_add_fusion.2.place, bf16[768,1024]{1,0:T(8,128)(2,1)} %get-tuple-element.221.dqkv_hbm, bf16[1536,1280]{1,0:T(8,128)(2,1)} %get-tuple-element.205.w_hbm), custom_call_target="tpu_custom_call" | custom-call | flops 1 | bytes 1 | tf_op jit(solution)/shard_map/project_back/pallas_call | solution.py:90
  253.3 8.0 %collective-permute-done.37.refs_1_ = bf16[384,576]{1,0:T(8,128)(2,1)S(1)} collective-permute-done((bf16[384,576]{1,0:T(8,128)(2,1)}, bf16[384,576]{1,0:T(8,128)(2,1)S(1)}, u32[]{:S(2)}, u32[]{:S(2)}) %collective-permute-start.37) | collective-permute-done | bytes 442400 | tf_op jit(solution)/shard_map/ppermute | solution.py:544
  263.7 2.1 collective-permute-start.42
  267.4 2.2 add_convert_fusion
  270.5 2.4 add_convert_fusion.1
  272.9 11.0 %collective-permute-done.42.refs_2_ = bf16[384,576]{1,0:T(8,128)(2,1)S(1)} collective-permute-done((bf16[384,576]{1,0:T(8,128)(2,1)}, bf16[384,576]{1,0:T(8,128)(2,1)S(1)}, u32[]{:S(2)}, u32[]{:S(2)}) %collective-permute-start.42) | collective-permute-done | bytes 442400 | tf_op jit(solution)/shard_map/ppermute | solution.py:544
  283.9 3.1 collective-permute-done.43.refs_6_
  289.6 2.3 collective-permute-done.44.refs_1_
  293.3 3.6 %collective-permute-done.47.refs_7_ = bf16[96,576]{1,0:T(8,128)(2,1)S(1)} collective-permute-done((bf16[96,576]{1,0:T(8,128)(2,1)S(1)}, bf16[96,576]{1,0:T(8,128)(2,1)S(1)}, u32[]{:S(2)}, u32[]{:S(2)}) %collective-permute-start.47) | collective-permute-done | bytes 110624 | tf_op jit(solution)/shard_map/ppermute | solution.py:544
  306.0 3.0 collective-permute-start.54
  314.5 6.3 %collective-permute-start.55 = (f32[2,48]{1,0:T(2,128)S(1)}, f32[2,48]{1,0:T(2,128)S(1)}, u32[]{:S(2)}, u32[]{:S(2)}) collective-permute-start(f32[2,48]{1,0:T(2,128)S(1)} %pad_maximum_fusion.2), channel_id=1, source_target_pairs={{1,0},{0,1},{3,2},{2,3},{5,4},{4,5},{7,6},{6,7},{9,8},{8,9},{11,10... | collective-permute-start | bytes 1160 | tf_op jit(solution)/shard_map/ppermute | solution.py:732
  (230 shorter events, 87.2 us)
Async XLA Ops:
  7.2 128.7 %all-gather.2.cloned.1.call-start = ((), (), s32[]{:S(2)}) async-start(), calls=%async_computation.1 | async-start | bytes 10027008 | tf_op jit(solution)/shard_map/all_gather | solution.py:640
  8.2 8.2 %collective-permute-start.1 = (f32[2,96]{0,1:T(8,128)S(1)}, f32[2,96]{0,1:T(8,128)S(1)}, u32[]{:S(2)}, u32[]{:S(2)}) collective-permute-start(f32[2,96]{0,1:T(8,128)S(1)} %dynamic_update_slice.5), channel_id=1, source_target_pairs={{1,0},{0,1},{3,2},{2,3},{5,4},{4,5},{7,6},{6,7},{9,8},{8,9},{11,10... | collective-permute-start | bytes 2312 | tf_op jit(solution)/shard_map/ppermute | solution.py:544
  12.0 12.2 %collective-permute-start = (bf16[48,1280]{1,0:T(8,128)(2,1)S(1)}, bf16[48,1280]{1,0:T(8,128)(2,1)S(1)}, u32[]{:S(2)}, u32[]{:S(2)}) collective-permute-start(bf16[48,1280]{1,0:T(8,128)(2,1)S(1)} %pad_add_fusion.1), channel_id=1, source_target_pairs={{4,0},{0,4},{5,1},{1,5},{6,2},{2,6},{7,3},{3,7},{12,8},{8,12},{13,... | collective-permute-start | bytes 368648 | tf_op jit(solution)/shard_map/ppermute | solution.py:544
  42.2 254.6 %reduce-scatter.2.cloned.1.call-start = ((), (), s32[]{:S(2)}) async-start(), calls=%async_computation.2 | async-start | bytes 10027008 | tf_op jit(solution)/shard_map/reduce_scatter | solution.py:683
  42.3 16.3 %collective-permute-start.15 = (bf16[256,1536]{1,0:T(8,128)(2,1)S(1)}, bf16[256,1536]{1,0:T(8,128)(2,1)}, u32[]{:S(2)}, u32[]{:S(2)}) collective-permute-start(bf16[256,1536]{1,0:T(8,128)(2,1)S(1)} %copy-done.3), channel_id=1, source_target_pairs={{2,0},{0,2},{3,1},{1,3},{6,4},{4,6},{7,5},{5,7},{10,8},{8,10},{11,... | collective-permute-start | bytes 2359304 | tf_op jit(solution)/shard_map/ppermute | solution.py:544
  45.5 13.0 %collective-permute-start.12 = (bf16[4,96,640]{2,1,0:T(8,128)(2,1)S(1)}, bf16[4,96,640]{2,1,0:T(8,128)(2,1)S(1)}, u32[]{:S(2)}, u32[]{:S(2)}) collective-permute-start(bf16[4,96,640]{2,1,0:T(8,128)(2,1)S(1)} %pad_maximum_fusion.1.b0), channel_id=1, source_target_pairs={{8,0},{16,8},{24,16},{0,24},{9,1},{17,9},{25,17},{1,25},{10,2},{18... | collective-permute-start | bytes 1474568 | tf_op jit(solution)/shard_map/ppermute | solution.py:544
  47.9 10.6 %collective-permute-start.13 = (bf16[4,96,640]{2,1,0:T(8,128)(2,1)S(1)}, bf16[4,96,640]{2,1,0:T(8,128)(2,1)S(1)}, u32[]{:S(2)}, u32[]{:S(2)}) collective-permute-start(bf16[4,96,640]{2,1,0:T(8,128)(2,1)S(1)} %pad_maximum_fusion.a0), channel_id=1, source_target_pairs={{96,0},{0,32},{32,64},{64,96},{97,1},{1,33},{33,65},{65,97},{98,2}... | collective-permute-start | bytes 1474568 | tf_op jit(solution)/shard_map/ppermute | solution.py:544
  47.9 10.6 %collective-permute-start.14 = (bf16[4,96,640]{2,1,0:T(8,128)(2,1)S(1)}, bf16[4,96,640]{2,1,0:T(8,128)(2,1)S(1)}, u32[]{:S(2)}, u32[]{:S(2)}) collective-permute-start(bf16[4,96,640]{2,1,0:T(8,128)(2,1)S(1)} %pad_maximum_fusion.1.b0), channel_id=1, source_target_pairs={{24,0},{0,8},{8,16},{16,24},{25,1},{1,9},{9,17},{17,25},{26,2},{2,... | collective-permute-start | bytes 1474568 | tf_op jit(solution)/shard_map/ppermute | solution.py:544
  51.7 37.3 %collective-permute-start.17 = (bf16[256,1536]{1,0:T(8,128)(2,1)S(1)}, bf16[256,1536]{1,0:T(8,128)(2,1)}, u32[]{:S(2)}, u32[]{:S(2)}) collective-permute-start(bf16[256,1536]{1,0:T(8,128)(2,1)S(1)} %copy-done.3), channel_id=1, source_target_pairs={{1,0},{0,1},{3,2},{2,3},{5,4},{4,5},{7,6},{6,7},{9,8},{8,9},{11,10... | collective-permute-start | bytes 2359304 | tf_op jit(solution)/shard_map/ppermute | solution.py:544
  58.6 30.4 %collective-permute-start.18 = (bf16[256,1536]{1,0:T(8,128)(2,1)}, bf16[256,1536]{1,0:T(8,128)(2,1)}, u32[]{:S(2)}, u32[]{:S(2)}) collective-permute-start(bf16[256,1536]{1,0:T(8,128)(2,1)} %collective-permute-done.15.t2), channel_id=1, source_target_pairs={{1,0},{0,1},{3,2},{2,3},{5,4},{4,5},{7,6},{6,7},{9,8},{8,9},{11,10... | collective-permute-start | bytes 2359304 | tf_op jit(solution)/shard_map/ppermute | solution.py:544
  74.6 32.4 %collective-permute-start.16 = (bf16[256,1536]{1,0:T(8,128)(2,1)S(1)}, bf16[256,1536]{1,0:T(8,128)(2,1)}, u32[]{:S(2)}, u32[]{:S(2)}) collective-permute-start(bf16[256,1536]{1,0:T(8,128)(2,1)S(1)} %copy-done.6), channel_id=1, source_target_pairs={{2,0},{0,2},{3,1},{1,3},{6,4},{4,6},{7,5},{5,7},{10,8},{8,10},{11,... | collective-permute-start | bytes 2359304 | tf_op jit(solution)/shard_map/ppermute | solution.py:544
  74.6 14.4 %collective-permute-start.19 = (bf16[4,96,640]{2,1,0:T(8,128)(2,1)S(1)}, bf16[4,96,640]{2,1,0:T(8,128)(2,1)}, u32[]{:S(2)}, u32[]{:S(2)}) collective-permute-start(bf16[4,96,640]{2,1,0:T(8,128)(2,1)S(1)} %pad_maximum_fusion.a0), channel_id=1, source_target_pairs={{64,0},{96,32},{0,64},{32,96},{65,1},{97,33},{1,65},{33,97},{66,2}... | collective-permute-start | bytes 1474568 | tf_op jit(solution)/shard_map/ppermute | solution.py:544
  74.7 14.3 %collective-permute-start.20 = (bf16[4,96,640]{2,1,0:T(8,128)(2,1)S(1)}, bf16[4,96,640]{2,1,0:T(8,128)(2,1)}, u32[]{:S(2)}, u32[]{:S(2)}) collective-permute-start(bf16[4,96,640]{2,1,0:T(8,128)(2,1)S(1)} %pad_maximum_fusion.1.b0), channel_id=1, source_target_pairs={{16,0},{24,8},{0,16},{8,24},{17,1},{25,9},{1,17},{9,25},{18,2},{26... | collective-permute-start | bytes 1474568 | tf_op jit(solution)/shard_map/ppermute | solution.py:544
  112.2 19.0 %collective-permute-start.23 = (bf16[256,1536]{1,0:T(8,128)(2,1)S(1)}, bf16[256,1536]{1,0:T(8,128)(2,1)S(1)}, u32[]{:S(2)}, u32[]{:S(2)}) collective-permute-start(bf16[256,1536]{1,0:T(8,128)(2,1)S(1)} %add_convert_fusion.4), channel_id=1, source_target_pairs={{2,0},{0,2},{3,1},{1,3},{6,4},{4,6},{7,5},{5,7},{10,8},{8,10},{11,... | collective-permute-start | bytes 2359304 | tf_op jit(solution)/shard_map/ppermute | solution.py:544
  113.7 21.3 %collective-permute-start.26 = (bf16[256,1536]{1,0:T(8,128)(2,1)S(1)}, bf16[256,1536]{1,0:T(8,128)(2,1)S(1)}, u32[]{:S(2)}, u32[]{:S(2)}) collective-permute-start(bf16[256,1536]{1,0:T(8,128)(2,1)S(1)} %copy-done.6), channel_id=1, source_target_pairs={{1,0},{0,1},{3,2},{2,3},{5,4},{4,5},{7,6},{6,7},{9,8},{8,9},{11,10... | collective-permute-start | bytes 2359304 | tf_op jit(solution)/shard_map/ppermute | solution.py:544
  133.2 19.2 %collective-permute-start.24 = (bf16[256,1536]{1,0:T(8,128)(2,1)S(1)}, bf16[256,1536]{1,0:T(8,128)(2,1)}, u32[]{:S(2)}, u32[]{:S(2)}) collective-permute-start(bf16[256,1536]{1,0:T(8,128)(2,1)S(1)} %multiply_convert_fusion.h0), channel_id=1, source_target_pairs={{2,0},{0,2},{3,1},{1,3},{6,4},{4,6},{7,5},{5,7},{10,8},{8,10},{11,... | collective-permute-start | bytes 2359304 | tf_op jit(solution)/shard_map/ppermute | solution.py:544
  134.6 19.0 %collective-permute-start.28 = (bf16[256,1536]{1,0:T(8,128)(2,1)}, bf16[256,1536]{1,0:T(8,128)(2,1)}, u32[]{:S(2)}, u32[]{:S(2)}) collective-permute-start(bf16[256,1536]{1,0:T(8,128)(2,1)} %collective-permute-done.16.g0.g2), channel_id=1, source_target_pairs={{1,0},{0,1},{3,2},{2,3},{5,4},{4,5},{7,6},{6,7},{9,8},{8,9},{11,10... | collective-permute-start | bytes 2359304 | tf_op jit(solution)/shard_map/ppermute | solution.py:544
  153.2 18.3 %collective-permute-start.31 = (bf16[256,1536]{1,0:T(8,128)(2,1)}, bf16[256,1536]{1,0:T(8,128)(2,1)S(1)}, u32[]{:S(2)}, u32[]{:S(2)}) collective-permute-start(bf16[256,1536]{1,0:T(8,128)(2,1)} %get-tuple-element.190), channel_id=1, source_target_pairs={{1,0},{0,1},{3,2},{2,3},{5,4},{4,5},{7,6},{6,7},{9,8},{8,9},{11,10... | collective-permute-start | bytes 2359304 | tf_op jit(solution)/shard_map/ppermute | solution.py:544
  175.1 19.5 %collective-permute-start.32 = (bf16[256,1536]{1,0:T(8,128)(2,1)}, bf16[256,1536]{1,0:T(8,128)(2,1)}, u32[]{:S(2)}, u32[]{:S(2)}) collective-permute-start(bf16[256,1536]{1,0:T(8,128)(2,1)} %add_convert_fusion.2), channel_id=1, source_target_pairs={{2,0},{0,2},{3,1},{1,3},{6,4},{4,6},{7,5},{5,7},{10,8},{8,10},{11,... | collective-permute-start | bytes 2359304 | tf_op jit(solution)/shard_map/ppermute | solution.py:544
  200.2 19.1 %collective-permute-start.34 = (bf16[256,1536]{1,0:T(8,128)(2,1)S(1)}, bf16[256,1536]{1,0:T(8,128)(2,1)S(1)}, u32[]{:S(2)}, u32[]{:S(2)}) collective-permute-start(bf16[256,1536]{1,0:T(8,128)(2,1)S(1)} %get-tuple-element.201.o0), channel_id=1, source_target_pairs={{2,0},{0,2},{3,1},{1,3},{6,4},{4,6},{7,5},{5,7},{10,8},{8,10},{11,... | collective-permute-start | bytes 2359304 | tf_op jit(solution)/shard_map/ppermute | solution.py:544
  201.7 18.5 %collective-permute-start.29 = (bf16[256,1536]{1,0:T(8,128)(2,1)S(1)}, bf16[256,1536]{1,0:T(8,128)(2,1)S(1)}, u32[]{:S(2)}, u32[]{:S(2)}) collective-permute-start(bf16[256,1536]{1,0:T(8,128)(2,1)S(1)} %copy-done.37), channel_id=1, source_target_pairs={{1,0},{0,1},{3,2},{2,3},{5,4},{4,5},{7,6},{6,7},{9,8},{8,9},{11,10... | collective-permute-start | bytes 2359304 | tf_op jit(solution)/shard_map/ppermute | solution.py:544
  203.5 17.8 %collective-permute-start.33 = (bf16[256,1536]{1,0:T(8,128)(2,1)S(1)}, bf16[256,1536]{1,0:T(8,128)(2,1)S(1)}, u32[]{:S(2)}, u32[]{:S(2)}) collective-permute-start(bf16[256,1536]{1,0:T(8,128)(2,1)S(1)} %get-tuple-element.201.o0), channel_id=1, source_target_pairs={{1,0},{0,1},{3,2},{2,3},{5,4},{4,5},{7,6},{6,7},{9,8},{8,9},{11,10... | collective-permute-start | bytes 2359304 | tf_op jit(solution)/shard_map/ppermute | solution.py:544
  223.0 23.8 %collective-permute-start.41 = (bf16[256,1536]{1,0:T(8,128)(2,1)}, bf16[256,1536]{1,0:T(8,128)(2,1)}, u32[]{:S(2)}, u32[]{:S(2)}) collective-permute-start(bf16[256,1536]{1,0:T(8,128)(2,1)} %add_convert_fusion.3), channel_id=1, source_target_pairs={{2,0},{0,2},{3,1},{1,3},{6,4},{4,6},{7,5},{5,7},{10,8},{8,10},{11,... | collective-permute-start | bytes 2359304 | tf_op jit(solution)/shard_map/ppermute | solution.py:544
  241.8 19.5 %collective-permute-start.37 = (bf16[384,576]{1,0:T(8,128)(2,1)}, bf16[384,576]{1,0:T(8,128)(2,1)S(1)}, u32[]{:S(2)}, u32[]{:S(2)}) collective-permute-start(bf16[384,576]{1,0:T(8,128)(2,1)} %get-tuple-element.215), channel_id=1, source_target_pairs={{32,0},{64,32},{96,64},{0,96},{33,1},{65,33},{97,65},{1,97},{34,2}... | collective-permute-start | bytes 1327112 | tf_op jit(solution)/shard_map/ppermute | solution.py:544
  245.1 16.4 %collective-permute-start.38 = (bf16[4,96,576]{2,1,0:T(8,128)(2,1)}, bf16[4,96,576]{2,1,0:T(8,128)(2,1)S(1)}, u32[]{:S(2)}, u32[]{:S(2)}) collective-permute-start(bf16[4,96,576]{2,1,0:T(8,128)(2,1)} %get-tuple-element.216), channel_id=1, source_target_pairs={{8,0},{16,8},{24,16},{0,24},{9,1},{17,9},{25,17},{1,25},{10,2},{18... | collective-permute-start | bytes 1327112 | tf_op jit(solution)/shard_map/ppermute | solution.py:544
  245.1 17.7 %collective-permute-start.39 = (bf16[384,576]{1,0:T(8,128)(2,1)}, bf16[384,576]{1,0:T(8,128)(2,1)S(1)}, u32[]{:S(2)}, u32[]{:S(2)}) collective-permute-start(bf16[384,576]{1,0:T(8,128)(2,1)} %get-tuple-element.217), channel_id=1, source_target_pairs={{96,0},{0,32},{32,64},{64,96},{97,1},{1,33},{33,65},{65,97},{98,2}... | collective-permute-start | bytes 1327112 | tf_op jit(solution)/shard_map/ppermute | solution.py:544
  245.1 17.7 %collective-permute-start.40 = (bf16[4,96,576]{2,1,0:T(8,128)(2,1)}, bf16[4,96,576]{2,1,0:T(8,128)(2,1)S(1)}, u32[]{:S(2)}, u32[]{:S(2)}) collective-permute-start(bf16[4,96,576]{2,1,0:T(8,128)(2,1)} %get-tuple-element.218), channel_id=1, source_target_pairs={{24,0},{0,8},{8,16},{16,24},{25,1},{1,9},{9,17},{17,25},{26,2},{2,... | collective-permute-start | bytes 1327112 | tf_op jit(solution)/shard_map/ppermute | solution.py:544
  263.7 20.1 %collective-permute-start.42 = (bf16[384,576]{1,0:T(8,128)(2,1)}, bf16[384,576]{1,0:T(8,128)(2,1)S(1)}, u32[]{:S(2)}, u32[]{:S(2)}) collective-permute-start(bf16[384,576]{1,0:T(8,128)(2,1)} %get-tuple-element.230), channel_id=1, source_target_pairs={{64,0},{96,32},{0,64},{32,96},{65,1},{97,33},{1,65},{33,97},{66,2}... | collective-permute-start | bytes 1327112 | tf_op jit(solution)/shard_map/ppermute | solution.py:544
  265.8 21.2 %collective-permute-start.43 = (bf16[4,96,576]{2,1,0:T(8,128)(2,1)}, bf16[4,96,576]{2,1,0:T(8,128)(2,1)S(1)}, u32[]{:S(2)}, u32[]{:S(2)}) collective-permute-start(bf16[4,96,576]{2,1,0:T(8,128)(2,1)} %get-tuple-element.231), channel_id=1, source_target_pairs={{16,0},{24,8},{0,16},{8,24},{17,1},{25,9},{1,17},{9,25},{18,2},{26... | collective-permute-start | bytes 1327112 | tf_op jit(solution)/shard_map/ppermute | solution.py:544
  266.8 33.5 %collective-permute-start.50 = (bf16[256,1536]{1,0:T(8,128)(2,1)}, bf16[256,1536]{1,0:T(8,128)(2,1)}, u32[]{:S(2)}, u32[]{:S(2)}) collective-permute-start(bf16[256,1536]{1,0:T(8,128)(2,1)} %get-tuple-element.264), channel_id=1, source_target_pairs={{1,0},{0,1},{3,2},{2,3},{5,4},{4,5},{7,6},{6,7},{9,8},{8,9},{11,10... | collective-permute-start | bytes 2359304 | tf_op jit(solution)/shard_map/ppermute | solution.py:544
  269.6 30.7 %collective-permute-start.52 = (bf16[256,1536]{1,0:T(8,128)(2,1)}, bf16[256,1536]{1,0:T(8,128)(2,1)}, u32[]{:S(2)}, u32[]{:S(2)}) collective-permute-start(bf16[256,1536]{1,0:T(8,128)(2,1)} %add_convert_fusion), channel_id=1, source_target_pairs={{2,0},{0,2},{3,1},{1,3},{6,4},{4,6},{7,5},{5,7},{10,8},{8,10},{11,... | collective-permute-start | bytes 2359304 | tf_op jit(solution)/shard_map/ppermute | solution.py:544
  314.5 9.7 %collective-permute-start.55 = (f32[2,48]{1,0:T(2,128)S(1)}, f32[2,48]{1,0:T(2,128)S(1)}, u32[]{:S(2)}, u32[]{:S(2)}) collective-permute-start(f32[2,48]{1,0:T(2,128)S(1)} %pad_maximum_fusion.2), channel_id=1, source_target_pairs={{1,0},{0,1},{3,2},{2,3},{5,4},{4,5},{7,6},{6,7},{9,8},{8,9},{11,10... | collective-permute-start | bytes 1160 | tf_op jit(solution)/shard_map/ppermute | solution.py:732
  (66 other events, 594.6 us)
Sparse Core Ops, SparseCore 0:
  42.3 91.7 all-gather.1
  194.8 96.5 reduce-scatter.1

commit v7 on v6

--- a/solution.py
+++ b/solution.py
@@ -15,9 +15,7 @@
 MIB = 1024 * 1024
 SMALL = pl.CostEstimate(flops=1, bytes_accessed=1, transcendentals=0)
 
-GAIN_AT, OUT_AT, QUERY_AT, KEYVAL_AT, REST_AT, ATTN_WIDTH = 0, 128, 256, 640, 1024, 1280
-HALF_WIDTH = ATTN_WIDTH // 2
-OUT_CUT = QUERY_AT - OUT_AT
+GAIN_AT, QUERY_AT, KEYVAL_AT, OUT_AT, ATTN_WIDTH = 0, 128, 512, 896, 1280
 LIMIT = 60
 
 
@@ -108,34 +106,23 @@
     return slice(head * HD, (head + 1) * HD)
 
 
-def attend_kernel(place, cos_ref, sin_ref, t0, t1, t2, t3, a0, a1, a2, a3, b0, b1, b2, b3,
-                  gains_ref, w_hbm, h_hbm, qt_hbm, kt_hbm, vt_hbm, attn_hbm, probs_hbm,
-                  o0, o1, o2, o3,
-                  t_ref, w_ref, h_ref, qt_ref, kt_ref, vt_ref, attn_ref, probs_ref, part_ref, k_ref,
+def attend_kernel(place, cos_ref, sin_ref, t0, t1, t2, t3, w_hbm, gains_ref, h_hbm, qt_hbm, kt_hbm, vt_hbm, attn_hbm, probs_hbm,
+                  o0, o1, o2, o3, t_ref, w_ref, h_ref, qt_ref, kt_ref, vt_ref, attn_ref, probs_ref, part_ref, k_ref,
                   in_sem, out_sem, probs_sem):
-    block, ix, iz = place[0], place[1], place[2]
+    block = place[0]
     half = HD // 2
     size = t_ref.shape[1]
     heads = qt_ref.shape[0]
     group_size = heads // kt_ref.shape[0]
-    rows = a0.shape[1]
     fetch, store = Moves(in_sem), Moves(out_sem)
-    came = []
-    for far, (along_x, along_z) in enumerate(zip((a0, a1, a2, a3), (b0, b1, b2, b3))):
-        for near in range(4):
-            at_a = lax.rem(ix + far, 4) * 4 + lax.rem(iz + near, 4)
-            at_b = lax.rem(ix + near, 4) * 4 + lax.rem(iz + far, 4)
-            came.append(fetch.start(
-                along_x.at[near], w_ref.at[block_at(at_a, rows), pl.ds(0, HALF_WIDTH)]))
-            came.append(fetch.start(
-                along_z.at[near], w_ref.at[block_at(at_b, rows), pl.ds(HALF_WIDTH, HALF_WIDTH)]))
+    parts = pl.ds(0, OUT_AT), pl.ds(OUT_AT, ATTN_WIDTH - OUT_AT)
+    w_came = [fetch.start(w_hbm.at[:, parts[0]], w_ref.at[:, parts[0]])]
     tokens_came = [
         fetch.start(piece, t_ref.at[i]) for i, piece in enumerate((t0, t1, t2, t3))
     ]
-    for copy in came:
-        copy.wait()
-    store.start(w_ref, w_hbm)
-    gains = w_ref[:, GAIN_AT:OUT_AT].astype(F32).T
+    w_came.append(fetch.start(w_hbm.at[:, parts[1]], w_ref.at[:, parts[1]]))
+    w_came[0].wait()
+    gains = w_ref[:, GAIN_AT:QUERY_AT].astype(F32).T
     gain_row = gains[0:1] + gains[2:3]
     gains_ref[...] = gains[0:2] + gains[2:4]
     for step in range(4):
@@ -147,7 +134,7 @@
         h_ref[at, :] = normed
         cosine = cos_ref[:, at]
         sine = sin_ref[:, at]
-        every = dot_n(normed, w_ref[:, QUERY_AT:REST_AT]).T
+        every = dot_n(normed, w_ref[:, QUERY_AT:OUT_AT]).T
         query, keyval = every[: KEYVAL_AT - QUERY_AT], every[KEYVAL_AT - QUERY_AT :]
 
         def rotated(field):
@@ -187,31 +174,30 @@
                 attn_ref[head_rows(head), columns] = mixed[:, i * size : (i + 1) * size]
         probs_copy(group).start()
     store.start(attn_ref, attn_hbm)
+    w_came[1].wait()
     for step, out in ((1, o1), (3, o3), (2, o2), (0, o0)):
         at = block_at(lax.bitwise_xor(block, step), size)
-        part = dot_tt(attn_ref[:OUT_CUT, at], w_ref[:, OUT_AT:QUERY_AT])
-        part += dot_tt(attn_ref[OUT_CUT:, at], w_ref[:, REST_AT:])
-        part_ref[step] = part.astype(BF16)
+        part_ref[step] = dot_tt(attn_ref[:, at], w_ref[:, OUT_AT:]).astype(BF16)
         store.start(part_ref.at[step], out)
     store.wait()
     for group in range(heads // group_size):
         probs_copy(group).wait()
 
 
-def attend(place, pieces, along_x, along_z, cosine, sine):
+def attend(place, pieces, weights, cosine, sine):
     size, width = pieces[0].shape
     length = 4 * size
     heads = (KEYVAL_AT - QUERY_AT) // HD
-    groups = (REST_AT - KEYVAL_AT) // (2 * HD)
+    groups = (OUT_AT - KEYVAL_AT) // (2 * HD)
     columns, g_columns = (heads, HD, length), (groups, HD, length)
     probs = (groups, sum(probs_at(3, size)), heads // groups * size)
-    kept = [(width, ATTN_WIDTH), (length, width), columns, g_columns, g_columns,
-            (heads * HD, length), probs]
+    kept = [(length, width), columns, g_columns, g_columns, (heads * HD, length), probs]
     return kernel_call(
-        attend_kernel, "attend", place, (cosine, sine), (*pieces, *along_x, *along_z),
+        attend_kernel, "attend", place, (cosine, sine), (*pieces, weights),
         [like(s) for s in kept + [(size, width)] * 4], [like((2, width), F32)],
-        [vmem(s) for s in [(4, size, width)] + kept + [(4, size, width), (groups, length, HD)]],
-        36, 10, groups)
+        [vmem(s) for s in [(4, size, width), weights.shape] + kept
+         + [(4, size, width), (groups, length, HD)]],
+        6, 9, groups)
 
 
 def attend_back_kernel(place, cos_ref, sin_ref,
@@ -229,11 +215,7 @@
     width = w_ref.shape[0]
     heads_w = heads * HD
     fetch, store = Moves(in_sem), Moves(out_sem)
-    rest_w = ATTN_WIDTH - REST_AT
-    early = [
-        fetch.start(w_hbm.at[:, pl.ds(OUT_AT, OUT_CUT)], w_ref.at[:, pl.ds(0, OUT_CUT)]),
-        fetch.start(w_hbm.at[:, pl.ds(REST_AT, rest_w)], w_ref.at[:, pl.ds(OUT_CUT, rest_w)]),
-    ]
+    early = [fetch.start(w_hbm.at[:, pl.ds(OUT_AT, ATTN_WIDTH - OUT_AT)], w_ref)]
     early += [
         fetch.start(piece, o_ref.at[block_at(lax.bitwise_xor(block, i), size), :])
         for i, piece in enumerate((o0, o1, o2, o3))
@@ -330,7 +312,7 @@
         attend_back_kernel, "attend_back", place, (cosine, sine),
         (*pieces, weights, h_first, qt, kt, vt, attn, probs),
         [like(s) for s in outs], [],
-        [vmem(s) for s in scratch] + [vmem(s, F32) for s in wide], 11, 21, groups)
+        [vmem(s) for s in scratch] + [vmem(s, F32) for s in wide], 10, 21, groups)
 
 
 def project_back_kernel(place, dqkv_hbm, w_hbm, c0, c1, c2, c3,
@@ -338,7 +320,7 @@
     block = place[0]
     size = part_ref.shape[1]
     fetch, store = Moves(in_sem), Moves(out_sem)
-    fetch.start(w_hbm.at[:, pl.ds(QUERY_AT, REST_AT - QUERY_AT)], w_ref)
+    fetch.start(w_hbm.at[:, pl.ds(QUERY_AT, OUT_AT - QUERY_AT)], w_ref)
     fetch.start(dqkv_hbm, dqkv_ref)
     fetch.wait()
     for step, out in ((3, c3), (2, c2), (1, c1), (0, c0)):
@@ -358,58 +340,76 @@
         [vmem(s) for s in (d_qkv.shape, (width, every_w), (4, size, width))], 2, 4)
 
 
-def feed_kernel(place, h0, h1, g0, g1, w_hbm, hidden_hbm, dgu_hbm, b0, b1, r0, r1,
+def feed_kernel(place, h0, h1, g0, g1, a0, a1, a2, a3, b0, b1, b2, b3,
+                hidden_hbm, dgu_hbm, back0, back1, out0, out1,
                 w_ref, h_ref, g_ref, hidden_ref, dgu_ref, back_ref, out_ref, in_sem, out_sem):
-    del place
+    ix, iz = place[1], place[2]
     hidden_w = hidden_ref.shape[1]
     size = h_ref.shape[1]
+    _, rows, half = a0.shape
     parts = [slice(i * hidden_w, (i + 1) * hidden_w) for i in range(3)]
     fetch, store = Moves(in_sem), Moves(out_sem)
 
-    def weight(i):
-        at = pl.ds(i * hidden_w, hidden_w)
-        return fetch.start(w_hbm.at[:, at], w_ref.at[:, at])
-
-    came = [fetch.start(h0, h_ref.at[0]), weight(0), weight(1), fetch.start(g0, g_ref.at[0]),
-            weight(2), fetch.start(h1, h_ref.at[1]), fetch.start(g1, g_ref.at[1])]
-    for i, (back, out) in enumerate(((b0, r0), (b1, r1))):
-        rows = slice(i * size, (i + 1) * size)
+    def weights(first, width):
+        copies = []
+        for far in range(4):
+            for near in range(4):
+                if first < half:
+                    at = lax.rem(ix + far, 4) * 4 + lax.rem(iz + near, 4)
+                    source = (a0, a1, a2, a3)[far].at[near, :, pl.ds(first, width)]
+                else:
+                    at = lax.rem(ix + near, 4) * 4 + lax.rem(iz + far, 4)
+                    source = (b0, b1, b2, b3)[far].at[near, :, pl.ds(first - half, width)]
+                copies.append(
+                    fetch.start(source, w_ref.at[block_at(at, rows), pl.ds(first, width)]))
+        return copies
+
+    came = [[fetch.start(h0, h_ref.at[0])] + weights(0, hidden_w)]
+    came.append(weights(hidden_w, half - hidden_w) + weights(half, 2 * hidden_w - half))
+    came.append([fetch.start(g0, g_ref.at[0])] + weights(2 * hidden_w, hidden_w))
+    came.append([fetch.start(h1, h_ref.at[1]), fetch.start(g1, g_ref.at[1])])
+
+    def wait(group):
+        for copy in came[group]:
+            copy.wait()
+
+    for i, (back, out) in enumerate(((back0, out0), (back1, out1))):
         at = pl.ds(i * size, size)
-        for copy in came[0:2] if i == 0 else came[5:7]:
-            copy.wait()
+        rows_at = slice(i * size, (i + 1) * size)
+        wait(3 if i else 0)
         gate = dot_n(h_ref[i], w_ref[:, parts[0]])
         if i == 0:
-            came[2].wait()
+            wait(1)
         up = dot_n(h_ref[i], w_ref[:, parts[1]])
         sig = 1.0 / (1.0 + jnp.exp2(gate * (-LOG2E)))
         silu = gate * sig
         hidden = (silu * up).astype(BF16)
-        hidden_ref[rows, :] = hidden
+        hidden_ref[rows_at, :] = hidden
         store.start(hidden_ref.at[at, :], hidden_hbm.at[at, :])
         if i == 0:
-            came[3].wait()
-            came[4].wait()
+            wait(2)
         d_hidden = dot_n(g_ref[i], w_ref[:, parts[2]])
-        dgu_ref[rows, :hidden_w] = (
+        dgu_ref[rows_at, :hidden_w] = (
             d_hidden * up * (sig * (1.0 + gate * (1.0 - sig)))).astype(BF16)
-        dgu_ref[rows, hidden_w:] = (d_hidden * silu).astype(BF16)
+        dgu_ref[rows_at, hidden_w:] = (d_hidden * silu).astype(BF16)
         store.start(dgu_ref.at[at, :], dgu_hbm.at[at, :])
-        back_ref[i] = dot_t(dgu_ref[rows, :], w_ref[:, : 2 * hidden_w]).astype(BF16)
+        back_ref[i] = dot_t(dgu_ref[rows_at, :], w_ref[:, : 2 * hidden_w]).astype(BF16)
         store.start(back_ref.at[i], back)
-        out_ref[i] = dot_t(hidden_ref[rows, :], w_ref[:, parts[2]]).astype(BF16)
+        out_ref[i] = dot_t(hidden_ref[rows_at, :], w_ref[:, parts[2]]).astype(BF16)
         store.start(out_ref.at[i], out)
     store.wait()
 
 
-def feed(place, weights, normed_pieces, grad_pieces):
+def feed(place, along_x, along_z, normed_pieces, grad_pieces):
     size, width = normed_pieces[0].shape
-    hidden_w = weights.shape[1] // 3
+    hidden_w = 2 * along_x[0].shape[2] // 3
     wide = [(2 * size, hidden_w), (2 * size, 2 * hidden_w)]
     return kernel_call(
-        feed_kernel, "feed", place, (), (*normed_pieces, *grad_pieces, weights),
+        feed_kernel, "feed", place, (), (*normed_pieces, *grad_pieces, *along_x, *along_z),
         [like(s) for s in wide + [(size, width)] * 4], [],
-        [vmem(s) for s in [weights.shape] + [(2, size, width)] * 2 + wide + [(2, size, width)] * 2],
-        7, 8)
+        [vmem(s) for s in [(width, 3 * hidden_w)] + [(2, size, width)] * 2 + wide
+         + [(2, size, width)] * 2],
+        68, 8)
 
 
 def feed_grads_kernel(place, h0, h1, h2, h3, g0, g1, g2, g3, dgu_a, dgu_b, hidden_a, hidden_b,
@@ -607,37 +607,33 @@
         [block, lax.axis_index("x"), lax.axis_index("z"), lax.axis_index("yh")]
     ).astype(jnp.int32)
 
-    out_t = w_out.T
     attn_own = side_by_side(
-        [
-            (OUT_AT, out_t[:, :OUT_CUT]),
-            (QUERY_AT, w_query),
-            (KEYVAL_AT, w_keyval),
-            (REST_AT, out_t[:, OUT_CUT:]),
-        ],
-        ATTN_WIDTH,
+        [(QUERY_AT, w_query), (KEYVAL_AT, w_keyval), (OUT_AT, w_out.T)], ATTN_WIDTH
     )
     attn_pair = pair_rows(attn_own, "yh")
+
     pair_w = 8 * gains_w
     gain_at = (lax.axis_index("yh") * 4 + block) * gains_w
     gain_part = lax.dynamic_update_slice(jnp.zeros((2, pair_w), F32), norm_gains, (0, gain_at))
     for axis in ("core", "yl", "yh"):
         gain_part = gain_part + other(gain_part, axis)
     mlp_own, gain_part = after((w_gateup[:, 0], w_gateup[:, 1], w_down.T), gain_part)
-    mlp_own = [(i * hidden_w, part) for i, part in enumerate(mlp_own)]
-    mlp_pair = pair_rows(side_by_side(mlp_own, 3 * hidden_w), "yh")
     gain_part = gain_part.T
     gain_high = lax.reduce_precision(gain_part, 8, 7)
     gain_low = (gain_part - gain_high).astype(BF16)
     gain_high = gain_high.astype(BF16)
-    first, second = attn_pair[:, :HALF_WIDTH], attn_pair[:, HALF_WIDTH:]
-    first += side_by_side([(0, gain_high), (2, gain_low)], HALF_WIDTH)
-
-    along_z, along_x, _ = from_both([first] * 4, "z", [second] * 4, "x", False)
-    along_z, along_x, mlp_pair, tokens = lax.optimization_barrier(
-        (jnp.stack(along_z), jnp.stack(along_x), mlp_pair, tokens)
-    )
-    mlp_w = lax.all_gather(mlp_pair, ("x", "z"), axis=0, tiled=True)
+    attn_pair += side_by_side([(0, gain_high), (2, gain_low)], ATTN_WIDTH)
+    attn_w = lax.all_gather(attn_pair, ("x", "z"), axis=0, tiled=True)
+
+    mlp_own = [(i * hidden_w, part) for i, part in enumerate(mlp_own)]
+    mlp_pair = pair_rows(side_by_side(mlp_own, 3 * hidden_w), "yh")
+    half = 3 * hidden_w // 2
+    along_z, along_x, _ = from_both(
+        [mlp_pair[:, :half]] * 4, "z", [mlp_pair[:, half:]] * 4, "x", False
+    )
+    along_z, along_x, tokens = lax.optimization_barrier(
+        (jnp.stack(along_z), jnp.stack(along_x), tokens)
+    )
     along_x, along_z, far = from_both(
         [along_z] * 4, "x", [along_x] * 4, "z", True, other(tokens, "yl")
     )
@@ -650,12 +646,13 @@
     angles = freqs[:, None] * positions[None, :]
     cosine, sine = jnp.cos(angles), jnp.sin(angles)
 
-    gain_rows, attn_w, h_first, qt, kt, vt, attn, probs, *parts = attend(
-        place, token_pieces, along_x, along_z, cosine, sine
+    gain_rows, h_first, qt, kt, vt, attn, probs, *parts = attend(
+        place, token_pieces, attn_w, cosine, sine
     )
     grad_far, parts = after(grad_far, parts)
     grad_pieces = [cotangent, other(cotangent, "core"), grad_far, other(grad_far, "core")]
-    middle_far = far_sum(parts[2], parts[3])
+    diagonal, (along_x, along_z) = after(other(parts[3], "core"), (along_x, along_z))
+    middle_far = (parts[2].astype(F32) + diagonal.astype(F32)).astype(BF16)
     middle = (
         tokens.astype(F32) + near_sum(parts[0], parts[1]) + other(middle_far, "yl").astype(F32)
     )
@@ -665,12 +662,12 @@
     h_pieces = [h_own, other(h_own, "core")]
     h_far = other(h_own, "yl")
     hidden_a, dgu_a, back_own, back_core, out_own, out_core = feed(
-        place, mlp_w, h_pieces, grad_pieces[:2]
+        place, along_x, along_z, h_pieces, grad_pieces[:2]
     )
     h_far, hidden_a = after(h_far, hidden_a)
     h_pieces += [h_far, other(h_far, "core")]
     hidden_b, dgu_b, back_chip, back_diag, out_chip, out_diag = feed(
-        place, mlp_w, h_pieces[2:], grad_pieces[2:]
+        place, along_x, along_z, h_pieces[2:], grad_pieces[2:]
     )
     back_near = near_sum(back_own, back_core)
     out_near = near_sum(out_own, out_core)

time: 339 us -> 364 us (1.074)
  waiting for transfers between devices: 101 us -> 131 us
  starting transfers between devices: 88.9 us -> 84.3 us
    ppermute x55, waiting for transfers between devices: 101 us -> 131 us  [from_offset(): lax.ppermute(v, axis, [((i + offset) % size, i) for i in range(size)])]
    ppermute x55, starting transfers between devices: 80.7 us -> 76 us  [from_offset(): lax.ppermute(v, axis, [((i + offset) % size, i) for i in range(size)])]
  transfers between devices with their start and end apart: 60 -> 60, of which waited for: 26 -> 31; matrix products, arithmetic and copies ran while one was open for 9% -> 8% of each run, Pallas kernels for 26% -> 25%
where the time goes in v7:
time: 364 us; the launch traced here: 357 us
  waiting for transfers between devices  131 us (36%)
  Pallas kernels  88.3 us (24%)
  starting transfers between devices  84.3 us (23%)
  other arithmetic  28 us (8%)
  between operations  15.1 us (4%)
  local copies, waits for them, and re-layouts  10.3 us (3%)
    ppermute x55, waiting for transfers between devices, from_offset(): lax.ppermute(v, axis, [((i + offset) % size, i) for i in range(size)])  131 us
    pallas_call x6, Pallas kernels, kernel_call(): pl.pallas_call(kernel, out_shape=list(small_outs) + list(outs), in_specs=...  86.5 us
    ppermute x55, starting transfers between devices, from_offset(): lax.ppermute(v, axis, [((i + offset) % size, i) for i in range(size)])  76 us
    ppermute x3, starting transfers between devices, body(): lax.ppermute(gain_sum, ('yl', 'core'), [(i ^ step, i) for i in range(4)])  8.31 us
  transfers between devices with their start and end apart: 60, of which 31 were waited for; matrix products, arithmetic and copies ran while one was open for 8% of the time, Pallas kernels for 25%

profile of v7, /device:TPU:1, one launch (start us, length us, event | category | flops | bytes accessed | tf_op | source)
XLA Modules:
  0.0 356.8 jit_solution(3972956373787302609)
XLA Ops:
  10.5 3.1 collective-permute-start.18
  15.7 2.5 collective-permute-done.1
  25.7 5.5 %collective-permute-done.3 = bf16[48,3072]{1,0:T(8,128)(2,1)S(1)} collective-permute-done((bf16[48,3072]{1,0:T(8,128)(2,1)S(1)}, bf16[48,3072]{1,0:T(8,128)(2,1)S(1)}, u32[]{:S(2)}, u32[]{:S(2)}) %collective-permute-start.3) | collective-permute-done | bytes 294944 | tf_op jit(solution)/shard_map/ppermute | solution.py:544
  31.4 3.8 %collective-permute-start.4 = (bf16[96,1536]{1,0:T(8,128)(2,1)S(1)}, bf16[96,1536]{1,0:T(8,128)(2,1)S(1)}, u32[]{:S(2)}, u32[]{:S(2)}) collective-permute-start(bf16[96,1536]{1,0:T(8,128)(2,1)S(1)} %get-tuple-element.307), channel_id=1, source_target_pairs={{8,0},{16,8},{24,16},{0,24},{9,1},{17,9},{25,17},{1,25},{10,2},{18... | collective-permute-start | bytes 884744 | tf_op jit(solution)/shard_map/ppermute | solution.py:544
  35.3 2.5 collective-permute-start.5
  40.7 2.7 collective-permute-start.9
  43.4 3.9 %collective-permute-done.6 = bf16[96,1536]{1,0:T(8,128)(2,1)S(1)} collective-permute-done((bf16[96,1536]{1,0:T(8,128)(2,1)S(1)}, bf16[96,1536]{1,0:T(8,128)(2,1)S(1)}, u32[]{:S(2)}, u32[]{:S(2)}) %collective-permute-start.6) | collective-permute-done | bytes 294944 | tf_op jit(solution)/shard_map/ppermute | solution.py:544
  47.3 3.3 collective-permute-done.8
  50.6 3.6 collective-permute-done.9
  54.6 2.4 collective-permute-start.11
  59.8 9.8 %collective-permute-done.14.t2 = bf16[256,1536]{1,0:T(8,128)(2,1)} collective-permute-done((bf16[256,1536]{1,0:T(8,128)(2,1)S(1)}, bf16[256,1536]{1,0:T(8,128)(2,1)}, u32[]{:S(2)}, u32[]{:S(2)}) %collective-permute-start.14) | collective-permute-done | bytes 786464 | tf_op jit(solution)/shard_map/ppermute | solution.py:544
  69.6 15.2 %collective-permute-start.16 = (bf16[256,1536]{1,0:T(8,128)(2,1)S(1)}, bf16[256,1536]{1,0:T(8,128)(2,1)}, u32[]{:S(2)}, u32[]{:S(2)}) collective-permute-start(bf16[256,1536]{1,0:T(8,128)(2,1)S(1)} %copy-done.3), channel_id=1, source_target_pairs={{1,0},{0,1},{3,2},{2,3},{5,4},{4,5},{7,6},{6,7},{9,8},{8,9},{11,10... | collective-permute-start | bytes 2359304 | tf_op jit(solution)/shard_map/ppermute | solution.py:544
  84.8 11.9 %collective-permute-done.10.a1 = bf16[4,96,1536]{2,1,0:T(8,128)(2,1)S(1)} collective-permute-done((bf16[4,96,1536]{2,1,0:T(8,128)(2,1)S(1)}, bf16[4,96,1536]{2,1,0:T(8,128)(2,1)S(1)}, u32[]{:S(2)}, u32[]{:S(2)}) %collective-permute-start.10) | collective-permute-done | bytes 1179680 | tf_op jit(solution)/shard_map/ppermute | solution.py:544
  97.8 6.0 %collective-permute-start.17 = (bf16[256,1536]{1,0:T(8,128)(2,1)}, bf16[256,1536]{1,0:T(8,128)(2,1)}, u32[]{:S(2)}, u32[]{:S(2)}) collective-permute-start(bf16[256,1536]{1,0:T(8,128)(2,1)} %collective-permute-done.14.t2), channel_id=1, source_target_pairs={{1,0},{0,1},{3,2},{2,3},{5,4},{4,5},{7,6},{6,7},{9,8},{8,9},{11,10... | collective-permute-start | bytes 2359304 | tf_op jit(solution)/shard_map/ppermute | solution.py:544
  109.4 17.1 %attend.1 = (f32[2,1536]{1,0:T(2,128)}, bf16[1024,1536]{1,0:T(8,128)(2,1)}, bf16[4,96,1024]{2,1,0:T(8,128)(2,1)}, bf16[2,96,1024]{2,1,0:T(8,128)(2,1)}, bf16[2,9...) custom-call(s32[4]{0:T(128)} %pad_add_fusion.2.place, ...), custom_call_target="tpu_custom_call" | custom-call | flops 1 | bytes 1 | tf_op jit(solution)/shard_map/attend/pallas_call | solution.py:88
  128.5 4.7 %collective-permute-done.21.a2 = bf16[4,96,1536]{2,1,0:T(8,128)(2,1)} collective-permute-done((bf16[4,96,1536]{2,1,0:T(8,128)(2,1)S(1)}, bf16[4,96,1536]{2,1,0:T(8,128)(2,1)}, u32[]{:S(2)}, u32[]{:S(2)}) %collective-permute-start.21) | collective-permute-done | bytes 1179680 | tf_op jit(solution)/shard_map/ppermute | solution.py:544
  134.4 2.8 collective-permute-start.19
  139.3 18.7 %collective-permute-done.23 = bf16[256,1536]{1,0:T(8,128)(2,1)S(1)} collective-permute-done((bf16[256,1536]{1,0:T(8,128)(2,1)S(1)}, bf16[256,1536]{1,0:T(8,128)(2,1)S(1)}, u32[]{:S(2)}, u32[]{:S(2)}) %collective-permute-start.23) | collective-permute-done | bytes 786464 | tf_op jit(solution)/shard_map/ppermute | solution.py:544
  161.7 15.2 %feed.2 = (bf16[512,1024]{1,0:T(8,128)(2,1)}, bf16[512,2048]{1,0:T(8,128)(2,1)}, bf16[256,1536]{1,0:T(8,128)(2,1)}, bf16[256,1536]{1,0:T(8,128)(2,1)}, bf16[256,...) custom-call(s32[4]{0:T(128)} %pad_add_fusion.2.place, bf16[256,1536]{1,0:T(8,128)(2,1)} %copy-done.8, ...), custom_call_target="tpu_custom_call" | custom-call | flops 1 | bytes 1 | tf_op jit(solution)/shard_map/feed/pallas_call | solution.py:88
  182.8 15.3 %feed.3 = (bf16[512,1024]{1,0:T(8,128)(2,1)}, bf16[512,2048]{1,0:T(8,128)(2,1)}, bf16[256,1536]{1,0:T(8,128)(2,1)}, bf16[256,1536]{1,0:T(8,128)(2,1)}, bf16[256,...) custom-call(s32[4]{0:T(128)} %pad_add_fusion.2.place, bf16[256,1536]{1,0:T(8,128)(2,1)} %collective-permute-done.24.h0.h2, ...), custom_call_target="tpu_custom_call" | custom-call | flops 1 | bytes 1 | tf_op jit(solution)/shard_map/feed/pallas_call | solution.py:88
  202.4 15.4 %feed_grads.1 = bf16[1536,3072]{1,0:T(8,128)(2,1)} custom-call(s32[4]{0:T(128)} %pad_add_fusion.2.place, bf16[256,1536]{1,0:T(8,128)(2,1)} %copy-done.8, bf16[256,1536]{1,0:T(8,128)(2,1)} %collective-permute-done.25.h1, bf16[256,1536]{1,0:T(8,128)(2,1)} %collective-permute-done.24.h0.h2, bf16[256,1536]{1,0:T(8,128)(2,1)} %copy-done.16, ...), custom_call_target="tpu_custom_call" | custom-call | flops 1 | bytes 1 | tf_op jit(solution)/shard_map/feed_grads/pallas_call | solution.py:88
  217.8 3.8 %collective-permute-done.32 = bf16[256,1536]{1,0:T(8,128)(2,1)} collective-permute-done((bf16[256,1536]{1,0:T(8,128)(2,1)}, bf16[256,1536]{1,0:T(8,128)(2,1)}, u32[]{:S(2)}, u32[]{:S(2)}) %collective-permute-start.32) | collective-permute-done | bytes 786464 | tf_op jit(solution)/shard_map/ppermute | solution.py:544
  224.3 3.2 fusion.11
  229.5 17.2 %collective-permute-done.34.o2 = bf16[256,1536]{1,0:T(8,128)(2,1)S(1)} collective-permute-done((bf16[256,1536]{1,0:T(8,128)(2,1)S(1)}, bf16[256,1536]{1,0:T(8,128)(2,1)S(1)}, u32[]{:S(2)}, u32[]{:S(2)}) %collective-permute-start.34) | collective-permute-done | bytes 786464 | tf_op jit(solution)/shard_map/ppermute | solution.py:544
  250.5 17.1 %attend_back.1 = (bf16[768,1024]{1,0:T(8,128)(2,1)}, bf16[384,576]{1,0:T(8,128)(2,1)}, bf16[384,576]{1,0:T(8,128)(2,1)}, bf16[384,576]{1,0:T(8,128)(2,1)}, bf16[...) custom-call(s32[4]{0:T(128)} %pad_add_fusion.2.place, ...), custom_call_target="tpu_custom_call" | custom-call | flops 1 | bytes 1 | tf_op jit(solution)/shard_map/attend_back/pallas_call | solution.py:88
  271.0 6.4 %project_back.1 = (bf16[256,1536]{1,0:T(8,128)(2,1)}, bf16[256,1536]{1,0:T(8,128)(2,1)}, bf16[256,1536]{1,0:T(8,128)(2,1)}, bf16[256,1536]{1,0:T(8,128)(2,1)}) custom-call(s32[4]{0:T(128)} %pad_add_fusion.2.place, bf16[768,1024]{1,0:T(8,128)(2,1)} %get-tuple-element.235.dqkv_hbm, bf16[1536,1280]{1,0:T(8,128)(2,1)} %all-gather.2.cloned.1.call-done.w_hbm), custom_call_target="tpu_custom_call" | custom-call | flops 1 | bytes 1 | tf_op jit(solution)/shard_map/project_back/pallas_call | solution.py:88
  277.5 10.2 %collective-permute-done.37.refs_1_ = bf16[384,576]{1,0:T(8,128)(2,1)S(1)} collective-permute-done((bf16[384,576]{1,0:T(8,128)(2,1)}, bf16[384,576]{1,0:T(8,128)(2,1)S(1)}, u32[]{:S(2)}, u32[]{:S(2)}) %collective-permute-start.37) | collective-permute-done | bytes 442400 | tf_op jit(solution)/shard_map/ppermute | solution.py:544
  295.8 2.4 add_convert_fusion.1
  298.2 11.4 %collective-permute-done.42.refs_2_ = bf16[384,576]{1,0:T(8,128)(2,1)S(1)} collective-permute-done((bf16[384,576]{1,0:T(8,128)(2,1)}, bf16[384,576]{1,0:T(8,128)(2,1)S(1)}, u32[]{:S(2)}, u32[]{:S(2)}) %collective-permute-start.42) | collective-permute-done | bytes 442400 | tf_op jit(solution)/shard_map/ppermute | solution.py:544
  309.6 2.7 collective-permute-done.43.refs_6_
  319.1 3.3 collective-permute-done.47.refs_7_
  338.8 6.6 %collective-permute-start.55 = (f32[2,48]{1,0:T(2,128)S(1)}, f32[2,48]{1,0:T(2,128)S(1)}, u32[]{:S(2)}, u32[]{:S(2)}) collective-permute-start(f32[2,48]{1,0:T(2,128)S(1)} %pad_maximum_fusion.2), channel_id=1, source_target_pairs={{1,0},{0,1},{3,2},{2,3},{5,4},{4,5},{7,6},{6,7},{9,8},{8,9},{11,10... | collective-permute-start | bytes 1160 | tf_op jit(solution)/shard_map/ppermute | solution.py:729
  (224 shorter events, 92.2 us)
Async XLA Ops:
  7.2 102.2 %all-gather.2.cloned.1.call-start = ((), (), s32[]{:S(2)}) async-start(), calls=%async_computation.1 | async-start | bytes 4177920 | tf_op jit(solution)/shard_map/all_gather | solution.py:626
  10.5 12.2 %collective-permute-start.18 = (bf16[48,1280]{1,0:T(8,128)(2,1)S(1)}, bf16[48,1280]{1,0:T(8,128)(2,1)S(1)}, u32[]{:S(2)}, u32[]{:S(2)}) collective-permute-start(bf16[48,1280]{1,0:T(8,128)(2,1)S(1)} %pad_add_fusion.1), channel_id=1, source_target_pairs={{4,0},{0,4},{5,1},{1,5},{6,2},{2,6},{7,3},{3,7},{12,8},{8,12},{13,... | collective-permute-start | bytes 368648 | tf_op jit(solution)/shard_map/ppermute | solution.py:544
  23.6 298.8 %reduce-scatter.2.cloned.1.call-start = ((), (), s32[]{:S(2)}) async-start(), calls=%async_computation.2 | async-start | bytes 10027008 | tf_op jit(solution)/shard_map/reduce_scatter | solution.py:680
  35.3 12.0 %collective-permute-start.6 = (bf16[96,1536]{1,0:T(8,128)(2,1)S(1)}, bf16[96,1536]{1,0:T(8,128)(2,1)S(1)}, u32[]{:S(2)}, u32[]{:S(2)}) collective-permute-start(bf16[96,1536]{1,0:T(8,128)(2,1)S(1)} %get-tuple-element.307), channel_id=1, source_target_pairs={{24,0},{0,8},{8,16},{16,24},{25,1},{1,9},{9,17},{17,25},{26,2},{2,... | collective-permute-start | bytes 884744 | tf_op jit(solution)/shard_map/ppermute | solution.py:544
  37.7 12.8 %collective-permute-start.8 = (bf16[96,1536]{1,0:T(8,128)(2,1)S(1)}, bf16[96,1536]{1,0:T(8,128)(2,1)S(1)}, u32[]{:S(2)}, u32[]{:S(2)}) collective-permute-start(bf16[96,1536]{1,0:T(8,128)(2,1)S(1)} %get-tuple-element.307), channel_id=1, source_target_pairs={{16,0},{24,8},{0,16},{8,24},{17,1},{25,9},{1,17},{9,25},{18,2},{26... | collective-permute-start | bytes 884744 | tf_op jit(solution)/shard_map/ppermute | solution.py:544
  40.7 13.5 %collective-permute-start.9 = (bf16[96,1536]{1,0:T(8,128)(2,1)S(1)}, bf16[96,1536]{1,0:T(8,128)(2,1)S(1)}, u32[]{:S(2)}, u32[]{:S(2)}) collective-permute-start(bf16[96,1536]{1,0:T(8,128)(2,1)S(1)} %get-tuple-element.306), channel_id=1, source_target_pairs={{64,0},{96,32},{0,64},{32,96},{65,1},{97,33},{1,65},{33,97},{66,2}... | collective-permute-start | bytes 884744 | tf_op jit(solution)/shard_map/ppermute | solution.py:544
  54.5 42.3 %collective-permute-start.10 = (bf16[4,96,1536]{2,1,0:T(8,128)(2,1)S(1)}, bf16[4,96,1536]{2,1,0:T(8,128)(2,1)S(1)}, u32[]{:S(2)}, u32[]{:S(2)}) collective-permute-start(bf16[4,96,1536]{2,1,0:T(8,128)(2,1)S(1)} %pad_maximum_fusion.a0), channel_id=1, source_target_pairs={{32,0},{64,32},{96,64},{0,96},{33,1},{65,33},{97,65},{1,97},{34,2}... | collective-permute-start | bytes 3538952 | tf_op jit(solution)/shard_map/ppermute | solution.py:544
  54.6 42.2 %collective-permute-start.11 = (bf16[4,96,1536]{2,1,0:T(8,128)(2,1)S(1)}, bf16[4,96,1536]{2,1,0:T(8,128)(2,1)S(1)}, u32[]{:S(2)}, u32[]{:S(2)}) collective-permute-start(bf16[4,96,1536]{2,1,0:T(8,128)(2,1)S(1)} %pad_maximum_fusion.1.b0), channel_id=1, source_target_pairs={{8,0},{16,8},{24,16},{0,24},{9,1},{17,9},{25,17},{1,25},{10,2},{18... | collective-permute-start | bytes 3538952 | tf_op jit(solution)/shard_map/ppermute | solution.py:544
  57.0 39.8 %collective-permute-start.12 = (bf16[4,96,1536]{2,1,0:T(8,128)(2,1)S(1)}, bf16[4,96,1536]{2,1,0:T(8,128)(2,1)S(1)}, u32[]{:S(2)}, u32[]{:S(2)}) collective-permute-start(bf16[4,96,1536]{2,1,0:T(8,128)(2,1)S(1)} %pad_maximum_fusion.a0), channel_id=1, source_target_pairs={{96,0},{0,32},{32,64},{64,96},{97,1},{1,33},{33,65},{65,97},{98,2}... | collective-permute-start | bytes 3538952 | tf_op jit(solution)/shard_map/ppermute | solution.py:544
  58.4 38.4 %collective-permute-start.13 = (bf16[4,96,1536]{2,1,0:T(8,128)(2,1)S(1)}, bf16[4,96,1536]{2,1,0:T(8,128)(2,1)S(1)}, u32[]{:S(2)}, u32[]{:S(2)}) collective-permute-start(bf16[4,96,1536]{2,1,0:T(8,128)(2,1)S(1)} %pad_maximum_fusion.1.b0), channel_id=1, source_target_pairs={{24,0},{0,8},{8,16},{16,24},{25,1},{1,9},{9,17},{17,25},{26,2},{2,... | collective-permute-start | bytes 3538952 | tf_op jit(solution)/shard_map/ppermute | solution.py:544
  69.6 39.7 %collective-permute-start.16 = (bf16[256,1536]{1,0:T(8,128)(2,1)S(1)}, bf16[256,1536]{1,0:T(8,128)(2,1)}, u32[]{:S(2)}, u32[]{:S(2)}) collective-permute-start(bf16[256,1536]{1,0:T(8,128)(2,1)S(1)} %copy-done.3), channel_id=1, source_target_pairs={{1,0},{0,1},{3,2},{2,3},{5,4},{4,5},{7,6},{6,7},{9,8},{8,9},{11,10... | collective-permute-start | bytes 2359304 | tf_op jit(solution)/shard_map/ppermute | solution.py:544
  103.8 22.7 %collective-permute-start.15 = (bf16[256,1536]{1,0:T(8,128)(2,1)}, bf16[256,1536]{1,0:T(8,128)(2,1)}, u32[]{:S(2)}, u32[]{:S(2)}) collective-permute-start(bf16[256,1536]{1,0:T(8,128)(2,1)} %g0.1), channel_id=1, source_target_pairs={{2,0},{0,2},{3,1},{1,3},{6,4},{4,6},{7,5},{5,7},{10,8},{8,10},{11,... | collective-permute-start | bytes 2359304 | tf_op jit(solution)/shard_map/ppermute | solution.py:544
  105.3 27.8 %collective-permute-start.21 = (bf16[4,96,1536]{2,1,0:T(8,128)(2,1)S(1)}, bf16[4,96,1536]{2,1,0:T(8,128)(2,1)}, u32[]{:S(2)}, u32[]{:S(2)}) collective-permute-start(bf16[4,96,1536]{2,1,0:T(8,128)(2,1)S(1)} %pad_maximum_fusion.a0), channel_id=1, source_target_pairs={{64,0},{96,32},{0,64},{32,96},{65,1},{97,33},{1,65},{33,97},{66,2}... | collective-permute-start | bytes 3538952 | tf_op jit(solution)/shard_map/ppermute | solution.py:544
  107.0 27.4 %collective-permute-start.22 = (bf16[4,96,1536]{2,1,0:T(8,128)(2,1)S(1)}, bf16[4,96,1536]{2,1,0:T(8,128)(2,1)}, u32[]{:S(2)}, u32[]{:S(2)}) collective-permute-start(bf16[4,96,1536]{2,1,0:T(8,128)(2,1)S(1)} %pad_maximum_fusion.1.b0), channel_id=1, source_target_pairs={{16,0},{24,8},{0,16},{8,24},{17,1},{25,9},{1,17},{9,25},{18,2},{26... | collective-permute-start | bytes 3538952 | tf_op jit(solution)/shard_map/ppermute | solution.py:544
  138.5 19.5 %collective-permute-start.23 = (bf16[256,1536]{1,0:T(8,128)(2,1)S(1)}, bf16[256,1536]{1,0:T(8,128)(2,1)S(1)}, u32[]{:S(2)}, u32[]{:S(2)}) collective-permute-start(bf16[256,1536]{1,0:T(8,128)(2,1)S(1)} %add_convert_fusion.4), channel_id=1, source_target_pairs={{2,0},{0,2},{3,1},{1,3},{6,4},{4,6},{7,5},{5,7},{10,8},{8,10},{11,... | collective-permute-start | bytes 2359304 | tf_op jit(solution)/shard_map/ppermute | solution.py:544
  138.9 21.3 %collective-permute-start.26 = (bf16[256,1536]{1,0:T(8,128)(2,1)}, bf16[256,1536]{1,0:T(8,128)(2,1)S(1)}, u32[]{:S(2)}, u32[]{:S(2)}) collective-permute-start(bf16[256,1536]{1,0:T(8,128)(2,1)} %g0.1), channel_id=1, source_target_pairs={{1,0},{0,1},{3,2},{2,3},{5,4},{4,5},{7,6},{6,7},{9,8},{8,9},{11,10... | collective-permute-start | bytes 2359304 | tf_op jit(solution)/shard_map/ppermute | solution.py:544
  159.7 19.2 %collective-permute-start.24 = (bf16[256,1536]{1,0:T(8,128)(2,1)S(1)}, bf16[256,1536]{1,0:T(8,128)(2,1)}, u32[]{:S(2)}, u32[]{:S(2)}) collective-permute-start(bf16[256,1536]{1,0:T(8,128)(2,1)S(1)} %multiply_convert_fusion.h0), channel_id=1, source_target_pairs={{2,0},{0,2},{3,1},{1,3},{6,4},{4,6},{7,5},{5,7},{10,8},{8,10},{11,... | collective-permute-start | bytes 2359304 | tf_op jit(solution)/shard_map/ppermute | solution.py:544
  159.8 20.4 %collective-permute-start.28 = (bf16[256,1536]{1,0:T(8,128)(2,1)}, bf16[256,1536]{1,0:T(8,128)(2,1)}, u32[]{:S(2)}, u32[]{:S(2)}) collective-permute-start(bf16[256,1536]{1,0:T(8,128)(2,1)} %collective-permute-done.15.g0.g2), channel_id=1, source_target_pairs={{1,0},{0,1},{3,2},{2,3},{5,4},{4,5},{7,6},{6,7},{9,8},{8,9},{11,10... | collective-permute-start | bytes 2359304 | tf_op jit(solution)/shard_map/ppermute | solution.py:544
  179.8 18.8 %collective-permute-start.31 = (bf16[256,1536]{1,0:T(8,128)(2,1)}, bf16[256,1536]{1,0:T(8,128)(2,1)S(1)}, u32[]{:S(2)}, u32[]{:S(2)}) collective-permute-start(bf16[256,1536]{1,0:T(8,128)(2,1)} %get-tuple-element.205), channel_id=1, source_target_pairs={{1,0},{0,1},{3,2},{2,3},{5,4},{4,5},{7,6},{6,7},{9,8},{8,9},{11,10... | collective-permute-start | bytes 2359304 | tf_op jit(solution)/shard_map/ppermute | solution.py:544
  202.2 19.5 %collective-permute-start.32 = (bf16[256,1536]{1,0:T(8,128)(2,1)}, bf16[256,1536]{1,0:T(8,128)(2,1)}, u32[]{:S(2)}, u32[]{:S(2)}) collective-permute-start(bf16[256,1536]{1,0:T(8,128)(2,1)} %add_convert_fusion.2), channel_id=1, source_target_pairs={{2,0},{0,2},{3,1},{1,3},{6,4},{4,6},{7,5},{5,7},{10,8},{8,10},{11,... | collective-permute-start | bytes 2359304 | tf_op jit(solution)/shard_map/ppermute | solution.py:544
  227.4 19.3 %collective-permute-start.34 = (bf16[256,1536]{1,0:T(8,128)(2,1)S(1)}, bf16[256,1536]{1,0:T(8,128)(2,1)S(1)}, u32[]{:S(2)}, u32[]{:S(2)}) collective-permute-start(bf16[256,1536]{1,0:T(8,128)(2,1)S(1)} %get-tuple-element.216.o0), channel_id=1, source_target_pairs={{2,0},{0,2},{3,1},{1,3},{6,4},{4,6},{7,5},{5,7},{10,8},{8,10},{11,... | collective-permute-start | bytes 2359304 | tf_op jit(solution)/shard_map/ppermute | solution.py:544
  227.5 19.9 %collective-permute-start.29 = (bf16[256,1536]{1,0:T(8,128)(2,1)S(1)}, bf16[256,1536]{1,0:T(8,128)(2,1)S(1)}, u32[]{:S(2)}, u32[]{:S(2)}) collective-permute-start(bf16[256,1536]{1,0:T(8,128)(2,1)S(1)} %copy-done.35), channel_id=1, source_target_pairs={{1,0},{0,1},{3,2},{2,3},{5,4},{4,5},{7,6},{6,7},{9,8},{8,9},{11,10... | collective-permute-start | bytes 2359304 | tf_op jit(solution)/shard_map/ppermute | solution.py:544
  229.3 19.2 %collective-permute-start.33 = (bf16[256,1536]{1,0:T(8,128)(2,1)S(1)}, bf16[256,1536]{1,0:T(8,128)(2,1)S(1)}, u32[]{:S(2)}, u32[]{:S(2)}) collective-permute-start(bf16[256,1536]{1,0:T(8,128)(2,1)S(1)} %get-tuple-element.216.o0), channel_id=1, source_target_pairs={{1,0},{0,1},{3,2},{2,3},{5,4},{4,5},{7,6},{6,7},{9,8},{8,9},{11,10... | collective-permute-start | bytes 2359304 | tf_op jit(solution)/shard_map/ppermute | solution.py:544
  250.2 20.8 %collective-permute-start.41 = (bf16[256,1536]{1,0:T(8,128)(2,1)}, bf16[256,1536]{1,0:T(8,128)(2,1)}, u32[]{:S(2)}, u32[]{:S(2)}) collective-permute-start(bf16[256,1536]{1,0:T(8,128)(2,1)} %add_convert_fusion.3), channel_id=1, source_target_pairs={{2,0},{0,2},{3,1},{1,3},{6,4},{4,6},{7,5},{5,7},{10,8},{8,10},{11,... | collective-permute-start | bytes 2359304 | tf_op jit(solution)/shard_map/ppermute | solution.py:544
  267.6 20.0 %collective-permute-start.37 = (bf16[384,576]{1,0:T(8,128)(2,1)}, bf16[384,576]{1,0:T(8,128)(2,1)S(1)}, u32[]{:S(2)}, u32[]{:S(2)}) collective-permute-start(bf16[384,576]{1,0:T(8,128)(2,1)} %get-tuple-element.229), channel_id=1, source_target_pairs={{32,0},{64,32},{96,64},{0,96},{33,1},{65,33},{97,65},{1,97},{34,2}... | collective-permute-start | bytes 1327112 | tf_op jit(solution)/shard_map/ppermute | solution.py:544
  268.6 19.2 %collective-permute-start.38 = (bf16[4,96,576]{2,1,0:T(8,128)(2,1)}, bf16[4,96,576]{2,1,0:T(8,128)(2,1)S(1)}, u32[]{:S(2)}, u32[]{:S(2)}) collective-permute-start(bf16[4,96,576]{2,1,0:T(8,128)(2,1)} %get-tuple-element.230), channel_id=1, source_target_pairs={{8,0},{16,8},{24,16},{0,24},{9,1},{17,9},{25,17},{1,25},{10,2},{18... | collective-permute-start | bytes 1327112 | tf_op jit(solution)/shard_map/ppermute | solution.py:544
  270.7 18.0 %collective-permute-start.39 = (bf16[384,576]{1,0:T(8,128)(2,1)}, bf16[384,576]{1,0:T(8,128)(2,1)S(1)}, u32[]{:S(2)}, u32[]{:S(2)}) collective-permute-start(bf16[384,576]{1,0:T(8,128)(2,1)} %get-tuple-element.231), channel_id=1, source_target_pairs={{96,0},{0,32},{32,64},{64,96},{97,1},{1,33},{33,65},{65,97},{98,2}... | collective-permute-start | bytes 1327112 | tf_op jit(solution)/shard_map/ppermute | solution.py:544
  270.7 18.4 %collective-permute-start.40 = (bf16[4,96,576]{2,1,0:T(8,128)(2,1)}, bf16[4,96,576]{2,1,0:T(8,128)(2,1)S(1)}, u32[]{:S(2)}, u32[]{:S(2)}) collective-permute-start(bf16[4,96,576]{2,1,0:T(8,128)(2,1)} %get-tuple-element.232), channel_id=1, source_target_pairs={{24,0},{0,8},{8,16},{16,24},{25,1},{1,9},{9,17},{17,25},{26,2},{2,... | collective-permute-start | bytes 1327112 | tf_op jit(solution)/shard_map/ppermute | solution.py:544
  290.0 19.6 %collective-permute-start.42 = (bf16[384,576]{1,0:T(8,128)(2,1)}, bf16[384,576]{1,0:T(8,128)(2,1)S(1)}, u32[]{:S(2)}, u32[]{:S(2)}) collective-permute-start(bf16[384,576]{1,0:T(8,128)(2,1)} %get-tuple-element.244), channel_id=1, source_target_pairs={{64,0},{96,32},{0,64},{32,96},{65,1},{97,33},{1,65},{33,97},{66,2}... | collective-permute-start | bytes 1327112 | tf_op jit(solution)/shard_map/ppermute | solution.py:544
  291.7 20.6 %collective-permute-start.43 = (bf16[4,96,576]{2,1,0:T(8,128)(2,1)}, bf16[4,96,576]{2,1,0:T(8,128)(2,1)S(1)}, u32[]{:S(2)}, u32[]{:S(2)}) collective-permute-start(bf16[4,96,576]{2,1,0:T(8,128)(2,1)} %get-tuple-element.245), channel_id=1, source_target_pairs={{16,0},{24,8},{0,16},{8,24},{17,1},{25,9},{1,17},{9,25},{18,2},{26... | collective-permute-start | bytes 1327112 | tf_op jit(solution)/shard_map/ppermute | solution.py:544
  291.8 35.3 %collective-permute-start.50 = (bf16[256,1536]{1,0:T(8,128)(2,1)}, bf16[256,1536]{1,0:T(8,128)(2,1)}, u32[]{:S(2)}, u32[]{:S(2)}) collective-permute-start(bf16[256,1536]{1,0:T(8,128)(2,1)} %get-tuple-element.278), channel_id=1, source_target_pairs={{1,0},{0,1},{3,2},{2,3},{5,4},{4,5},{7,6},{6,7},{9,8},{8,9},{11,10... | collective-permute-start | bytes 2359304 | tf_op jit(solution)/shard_map/ppermute | solution.py:544
  294.7 32.4 %collective-permute-start.52 = (bf16[256,1536]{1,0:T(8,128)(2,1)}, bf16[256,1536]{1,0:T(8,128)(2,1)}, u32[]{:S(2)}, u32[]{:S(2)}) collective-permute-start(bf16[256,1536]{1,0:T(8,128)(2,1)} %add_convert_fusion), channel_id=1, source_target_pairs={{2,0},{0,2},{3,1},{1,3},{6,4},{4,6},{7,5},{5,7},{10,8},{8,10},{11,... | collective-permute-start | bytes 2359304 | tf_op jit(solution)/shard_map/ppermute | solution.py:544
  (64 other events, 574.8 us)
Sparse Core Ops, SparseCore 0:
  23.8 71.2 all-gather.1
  221.8 95.4 reduce-scatter.1

commit v8 on v6

--- a/solution.py
+++ b/solution.py
@@ -120,31 +120,42 @@
     group_size = heads // kt_ref.shape[0]
     rows = a0.shape[1]
     fetch, store = Moves(in_sem), Moves(out_sem)
-    came = []
+    gains_came, came = [], []
     for far, (along_x, along_z) in enumerate(zip((a0, a1, a2, a3), (b0, b1, b2, b3))):
         for near in range(4):
-            at_a = lax.rem(ix + far, 4) * 4 + lax.rem(iz + near, 4)
-            at_b = lax.rem(ix + near, 4) * 4 + lax.rem(iz + far, 4)
-            came.append(fetch.start(
-                along_x.at[near], w_ref.at[block_at(at_a, rows), pl.ds(0, HALF_WIDTH)]))
-            came.append(fetch.start(
-                along_z.at[near], w_ref.at[block_at(at_b, rows), pl.ds(HALF_WIDTH, HALF_WIDTH)]))
+            at_a = block_at(lax.rem(ix + far, 4) * 4 + lax.rem(iz + near, 4), rows)
+            at_b = block_at(lax.rem(ix + near, 4) * 4 + lax.rem(iz + far, 4), rows)
+            for source, first, width, target, copies in (
+                (along_x, 0, OUT_AT, at_a, gains_came),
+                (along_x, OUT_AT, HALF_WIDTH - OUT_AT, at_a, came),
+                (along_z, HALF_WIDTH, HALF_WIDTH, at_b, came),
+            ):
+                copies.append((
+                    source.at[near, :, pl.ds(first % HALF_WIDTH, width)],
+                    w_ref.at[target, pl.ds(first, width)],
+                ))
+    gains_came = [fetch.start(*copy) for copy in gains_came]
     tokens_came = [
         fetch.start(piece, t_ref.at[i]) for i, piece in enumerate((t0, t1, t2, t3))
     ]
-    for copy in came:
+    came = [fetch.start(*copy) for copy in came]
+    for copy in gains_came:
         copy.wait()
-    store.start(w_ref, w_hbm)
     gains = w_ref[:, GAIN_AT:OUT_AT].astype(F32).T
     gain_row = gains[0:1] + gains[2:3]
     gains_ref[...] = gains[0:2] + gains[2:4]
     for step in range(4):
-        at = block_at(lax.bitwise_xor(block, step), size)
         tokens_came[step].wait()
         value = t_ref[step].astype(F32)
         factor = lax.rsqrt(jnp.mean(value * value, -1, keepdims=True) + norm_eps)
-        normed = (value * factor * gain_row).astype(BF16)
-        h_ref[at, :] = normed
+        h_ref[block_at(lax.bitwise_xor(block, step), size), :] = (
+            value * factor * gain_row).astype(BF16)
+    for copy in came:
+        copy.wait()
+    store.start(w_ref, w_hbm)
+    for step in range(4):
+        at = slice(step * size, (step + 1) * size)
+        normed = h_ref[at, :]
         cosine = cos_ref[:, at]
         sine = sin_ref[:, at]
         every = dot_n(normed, w_ref[:, QUERY_AT:REST_AT]).T
@@ -211,7 +222,7 @@
         attend_kernel, "attend", place, (cosine, sine), (*pieces, *along_x, *along_z),
         [like(s) for s in kept + [(size, width)] * 4], [like((2, width), F32)],
         [vmem(s) for s in [(4, size, width)] + kept + [(4, size, width), (groups, length, HD)]],
-        36, 10, groups)
+        52, 10, groups)
 
 
 def attend_back_kernel(place, cos_ref, sin_ref,
@@ -623,7 +634,8 @@
     gain_part = lax.dynamic_update_slice(jnp.zeros((2, pair_w), F32), norm_gains, (0, gain_at))
     for axis in ("core", "yl", "yh"):
         gain_part = gain_part + other(gain_part, axis)
-    mlp_own, gain_part = after((w_gateup[:, 0], w_gateup[:, 1], w_down.T), gain_part)
+    (gate_up, down, tokens), gain_part = after((w_gateup, w_down, tokens), gain_part)
+    mlp_own = (gate_up[:, 0], gate_up[:, 1], down.T)
     mlp_own = [(i * hidden_w, part) for i, part in enumerate(mlp_own)]
     mlp_pair = pair_rows(side_by_side(mlp_own, 3 * hidden_w), "yh")
     gain_part = gain_part.T
@@ -634,13 +646,12 @@
     first += side_by_side([(0, gain_high), (2, gain_low)], HALF_WIDTH)
 
     along_z, along_x, _ = from_both([first] * 4, "z", [second] * 4, "x", False)
-    along_z, along_x, mlp_pair, tokens = lax.optimization_barrier(
-        (jnp.stack(along_z), jnp.stack(along_x), mlp_pair, tokens)
+    far = other(tokens, "yl")
+    along_z, along_x, mlp_pair, far = lax.optimization_barrier(
+        (jnp.stack(along_z), jnp.stack(along_x), mlp_pair, far)
     )
     mlp_w = lax.all_gather(mlp_pair, ("x", "z"), axis=0, tiled=True)
-    along_x, along_z, far = from_both(
-        [along_z] * 4, "x", [along_x] * 4, "z", True, other(tokens, "yl")
-    )
+    along_x, along_z, _ = from_both([along_z] * 4, "x", [along_x] * 4, "z", False)
     token_pieces = [tokens, other(tokens, "core"), far, other(far, "core")]
     cotangent, far = after(cotangent, far)
     grad_far = other(cotangent, "yl")
@@ -672,14 +683,14 @@
     hidden_b, dgu_b, back_chip, back_diag, out_chip, out_diag = feed(
         place, mlp_w, h_pieces[2:], grad_pieces[2:]
     )
-    back_near = near_sum(back_own, back_core)
+    back_core = other(back_core, "core")
     out_near = near_sum(out_own, out_core)
 
     back_far = far_sum(back_chip, back_diag)
-    hidden_b, (back_far, back_near) = after(hidden_b, (back_far, back_near))
+    hidden_b, (back_far, back_core) = after(hidden_b, (back_far, back_core))
     mlp_grads = feed_grads(place, h_pieces, grad_pieces, dgu_a, dgu_b, hidden_a, hidden_b)
     mlp_grads, back_far = after(mlp_grads, other(back_far, "yl"))
-    d_h2_own = back_near + back_far.astype(F32)
+    d_h2_own = back_own.astype(F32) + back_core.astype(F32) + back_far.astype(F32)
     early = lax.psum_scatter(mlp_grads, ("x", "z"), scatter_dimension=0, tiled=True)
     out_far = far_sum(out_chip, out_diag)
 

time: 339 us -> 339 us (level)
  waiting for transfers between devices: 101 us -> 116 us
  starting transfers between devices: 88.9 us -> 76 us
    ppermute x55, waiting for transfers between devices: 101 us -> 115 us  [from_offset(): lax.ppermute(v, axis, [((i + offset) % size, i) for i in range(size)])]
    ppermute x55, starting transfers between devices: 80.7 us -> 68 us  [from_offset(): lax.ppermute(v, axis, [((i + offset) % size, i) for i in range(size)])]
  transfers between devices with their start and end apart: 60 -> 60, of which waited for: 26 -> 31; matrix products, arithmetic and copies ran while one was open for 9% -> 10% of each run, Pallas kernels for 26% -> 21%
where the time goes in v8:
time: 339 us; the launch traced here: 333 us
  waiting for transfers between devices  116 us (34%)
  Pallas kernels  86.1 us (25%)
  starting transfers between devices  76 us (22%)
  other arithmetic  27.6 us (8%)
  between operations  15 us (4%)
  local copies, waits for them, and re-layouts  11.9 us (4%)
    ppermute x55, waiting for transfers between devices, from_offset(): lax.ppermute(v, axis, [((i + offset) % size, i) for i in range(size)])  115 us
    pallas_call x6, Pallas kernels, kernel_call(): pl.pallas_call(kernel, out_shape=list(small_outs) + list(outs), in_specs=...  84.3 us
    ppermute x55, starting transfers between devices, from_offset(): lax.ppermute(v, axis, [((i + offset) % size, i) for i in range(size)])  68 us
    ppermute x3, starting transfers between devices, body(): lax.ppermute(gain_sum, ('yl', 'core'), [(i ^ step, i) for i in range(4)])  7.89 us
    convert_element_type x4, other arithmetic, far_sum(): return near_sum(chip, diagonal).astype(BF16)  6.91 us
  transfers between devices with their start and end apart: 60, of which 31 were waited for; matrix products, arithmetic and copies ran while one was open for 10% of the time, Pallas kernels for 21%

profile of v8, /device:TPU:1, one launch (start us, length us, event | category | flops | bytes accessed | tf_op | source)
XLA Modules:
  0.0 332.6 jit_solution(13787471668432690241)
XLA Ops:
  13.6 2.7 collective-permute-start.3
  18.0 2.8 collective-permute-done.2
  22.1 3.9 %collective-permute-start.4 = (bf16[96,640]{1,0:T(8,128)(2,1)S(1)}, bf16[96,640]{1,0:T(8,128)(2,1)S(1)}, u32[]{:S(2)}, u32[]{:S(2)}) collective-permute-start(bf16[96,640]{1,0:T(8,128)(2,1)S(1)} %get-tuple-element.278), channel_id=1, source_target_pairs={{8,0},{16,8},{24,16},{0,24},{9,1},{17,9},{25,17},{1,25},{10,2},{18... | collective-permute-start | bytes 368648 | tf_op jit(solution)/shard_map/ppermute | solution.py:555
  26.1 2.5 collective-permute-start.5
  28.6 3.3 collective-permute-start.10
  37.2 2.9 collective-permute-done.9
  40.2 8.0 %collective-permute-done.10 = bf16[48,3072]{1,0:T(8,128)(2,1)S(1)} collective-permute-done((bf16[48,3072]{1,0:T(8,128)(2,1)S(1)}, bf16[48,3072]{1,0:T(8,128)(2,1)S(1)}, u32[]{:S(2)}, u32[]{:S(2)}) %collective-permute-start.10) | collective-permute-done | bytes 294944 | tf_op jit(solution)/shard_map/ppermute | solution.py:555
  49.2 2.5 collective-permute-start.15
  51.8 3.8 %collective-permute-start.16 = (bf16[4,96,640]{2,1,0:T(8,128)(2,1)S(1)}, bf16[4,96,640]{2,1,0:T(8,128)(2,1)S(1)}, u32[]{:S(2)}, u32[]{:S(2)}) collective-permute-start(bf16[4,96,640]{2,1,0:T(8,128)(2,1)S(1)} %get-tuple-element.150.b0), channel_id=1, source_target_pairs={{8,0},{16,8},{24,16},{0,24},{9,1},{17,9},{25,17},{1,25},{10,2},{18... | collective-permute-start | bytes 1474568 | tf_op jit(solution)/shard_map/ppermute | solution.py:555
  55.5 2.7 collective-permute-start.13
  60.3 4.9 %collective-permute-start.14 = (bf16[256,1536]{1,0:T(8,128)(2,1)}, bf16[256,1536]{1,0:T(8,128)(2,1)}, u32[]{:S(2)}, u32[]{:S(2)}) collective-permute-start(bf16[256,1536]{1,0:T(8,128)(2,1)} %collective-permute-done.11.t2), channel_id=1, source_target_pairs={{1,0},{0,1},{3,2},{2,3},{5,4},{4,5},{7,6},{6,7},{9,8},{8,9},{11,10... | collective-permute-start | bytes 2359304 | tf_op jit(solution)/shard_map/ppermute | solution.py:555
  65.3 3.4 %collective-permute-done.17.a3 = bf16[4,96,640]{2,1,0:T(8,128)(2,1)S(1)} collective-permute-done((bf16[4,96,640]{2,1,0:T(8,128)(2,1)S(1)}, bf16[4,96,640]{2,1,0:T(8,128)(2,1)S(1)}, u32[]{:S(2)}, u32[]{:S(2)}) %collective-permute-start.17) | collective-permute-done | bytes 491552 | tf_op jit(solution)/shard_map/ppermute | solution.py:555
  73.9 9.8 %collective-permute-done.19.a2 = bf16[4,96,640]{2,1,0:T(8,128)(2,1)} collective-permute-done((bf16[4,96,640]{2,1,0:T(8,128)(2,1)S(1)}, bf16[4,96,640]{2,1,0:T(8,128)(2,1)}, u32[]{:S(2)}, u32[]{:S(2)}) %collective-permute-start.19) | collective-permute-done | bytes 491552 | tf_op jit(solution)/shard_map/ppermute | solution.py:555
  83.7 15.9 %attend.1 = (f32[2,1536]{1,0:T(2,128)}, bf16[1536,1280]{1,0:T(8,128)(2,1)}, bf16[1024,1536]{1,0:T(8,128)(2,1)}, bf16[4,96,1024]{2,1,0:T(8,128)(2,1)}, bf16[2,96,...) custom-call(s32[4]{0:T(128)} %pad_add_fusion.2.place, ...), custom_call_target="tpu_custom_call" | custom-call | flops 1 | bytes 1 | tf_op jit(solution)/shard_map/attend/pallas_call | solution.py:90
  99.7 9.9 %collective-permute-start.22 = (bf16[256,1536]{1,0:T(8,128)(2,1)}, bf16[256,1536]{1,0:T(8,128)(2,1)S(1)}, u32[]{:S(2)}, u32[]{:S(2)}) collective-permute-start(bf16[256,1536]{1,0:T(8,128)(2,1)} %get-tuple-element.164), channel_id=1, source_target_pairs={{1,0},{0,1},{3,2},{2,3},{5,4},{4,5},{7,6},{6,7},{9,8},{8,9},{11,10... | collective-permute-start | bytes 2359304 | tf_op jit(solution)/shard_map/ppermute | solution.py:555
  113.8 18.2 %collective-permute-done.23 = bf16[256,1536]{1,0:T(8,128)(2,1)S(1)} collective-permute-done((bf16[256,1536]{1,0:T(8,128)(2,1)S(1)}, bf16[256,1536]{1,0:T(8,128)(2,1)S(1)}, u32[]{:S(2)}, u32[]{:S(2)}) %collective-permute-start.23) | collective-permute-done | bytes 786464 | tf_op jit(solution)/shard_map/ppermute | solution.py:555
  136.8 14.7 %feed.2 = (bf16[512,1024]{1,0:T(8,128)(2,1)}, bf16[512,2048]{1,0:T(8,128)(2,1)}, bf16[256,1536]{1,0:T(8,128)(2,1)}, bf16[256,1536]{1,0:T(8,128)(2,1)}, bf16[256,...) custom-call(s32[4]{0:T(128)} %pad_add_fusion.2.place, bf16[256,1536]{1,0:T(8,128)(2,1)} %copy-done.8, ...), custom_call_target="tpu_custom_call" | custom-call | flops 1 | bytes 1 | tf_op jit(solution)/shard_map/feed/pallas_call | solution.py:90
  157.5 14.7 %feed.3 = (bf16[512,1024]{1,0:T(8,128)(2,1)}, bf16[512,2048]{1,0:T(8,128)(2,1)}, bf16[256,1536]{1,0:T(8,128)(2,1)}, bf16[256,1536]{1,0:T(8,128)(2,1)}, bf16[256,...) custom-call(s32[4]{0:T(128)} %pad_add_fusion.2.place, bf16[256,1536]{1,0:T(8,128)(2,1)} %collective-permute-done.24.h0.h2, ...), custom_call_target="tpu_custom_call" | custom-call | flops 1 | bytes 1 | tf_op jit(solution)/shard_map/feed/pallas_call | solution.py:90
  177.2 15.3 %feed_grads.1 = bf16[1536,3072]{1,0:T(8,128)(2,1)} custom-call(s32[4]{0:T(128)} %pad_add_fusion.2.place, bf16[256,1536]{1,0:T(8,128)(2,1)} %copy-done.8, bf16[256,1536]{1,0:T(8,128)(2,1)} %collective-permute-done.25.h1, bf16[256,1536]{1,0:T(8,128)(2,1)} %collective-permute-done.24.h0.h2, bf16[256,1536]{1,0:T(8,128)(2,1)} %copy-done.12, ...), custom_call_target="tpu_custom_call" | custom-call | flops 1 | bytes 1 | tf_op jit(solution)/shard_map/feed_grads/pallas_call | solution.py:90
  192.5 3.7 %collective-permute-done.32 = bf16[256,1536]{1,0:T(8,128)(2,1)} collective-permute-done((bf16[256,1536]{1,0:T(8,128)(2,1)}, bf16[256,1536]{1,0:T(8,128)(2,1)}, u32[]{:S(2)}, u32[]{:S(2)}) %collective-permute-start.32) | collective-permute-done | bytes 786464 | tf_op jit(solution)/shard_map/ppermute | solution.py:555
  199.3 3.1 fusion.10
  204.5 17.2 %collective-permute-done.34.o2 = bf16[256,1536]{1,0:T(8,128)(2,1)S(1)} collective-permute-done((bf16[256,1536]{1,0:T(8,128)(2,1)S(1)}, bf16[256,1536]{1,0:T(8,128)(2,1)S(1)}, u32[]{:S(2)}, u32[]{:S(2)}) %collective-permute-start.34) | collective-permute-done | bytes 786464 | tf_op jit(solution)/shard_map/ppermute | solution.py:555
  225.3 17.3 %attend_back.1 = (bf16[768,1024]{1,0:T(8,128)(2,1)}, bf16[384,576]{1,0:T(8,128)(2,1)}, bf16[384,576]{1,0:T(8,128)(2,1)}, bf16[384,576]{1,0:T(8,128)(2,1)}, bf16[...) custom-call(s32[4]{0:T(128)} %pad_add_fusion.2.place, ...), custom_call_target="tpu_custom_call" | custom-call | flops 1 | bytes 1 | tf_op jit(solution)/shard_map/attend_back/pallas_call | solution.py:90
  246.0 6.5 %project_back.1 = (bf16[256,1536]{1,0:T(8,128)(2,1)}, bf16[256,1536]{1,0:T(8,128)(2,1)}, bf16[256,1536]{1,0:T(8,128)(2,1)}, bf16[256,1536]{1,0:T(8,128)(2,1)}) custom-call(s32[4]{0:T(128)} %pad_add_fusion.2.place, bf16[768,1024]{1,0:T(8,128)(2,1)} %get-tuple-element.207.dqkv_hbm, bf16[1536,1280]{1,0:T(8,128)(2,1)} %get-tuple-element.191.w_hbm), custom_call_target="tpu_custom_call" | custom-call | flops 1 | bytes 1 | tf_op jit(solution)/shard_map/project_back/pallas_call | solution.py:90
  252.5 9.6 %collective-permute-done.37.refs_1_ = bf16[384,576]{1,0:T(8,128)(2,1)S(1)} collective-permute-done((bf16[384,576]{1,0:T(8,128)(2,1)}, bf16[384,576]{1,0:T(8,128)(2,1)S(1)}, u32[]{:S(2)}, u32[]{:S(2)}) %collective-permute-start.37) | collective-permute-done | bytes 442400 | tf_op jit(solution)/shard_map/ppermute | solution.py:555
  271.2 2.4 add_convert_fusion.1
  273.7 11.6 %collective-permute-done.42.refs_2_ = bf16[384,576]{1,0:T(8,128)(2,1)S(1)} collective-permute-done((bf16[384,576]{1,0:T(8,128)(2,1)}, bf16[384,576]{1,0:T(8,128)(2,1)S(1)}, u32[]{:S(2)}, u32[]{:S(2)}) %collective-permute-start.42) | collective-permute-done | bytes 442400 | tf_op jit(solution)/shard_map/ppermute | solution.py:555
  289.8 2.3 collective-permute-done.44.refs_1_
  292.2 2.3 collective-permute-done.46.refs_3_
  294.5 2.8 collective-permute-done.47.refs_7_
  298.3 2.8 collective-permute-start.53
  314.6 6.2 %collective-permute-start.55 = (f32[2,48]{1,0:T(2,128)S(1)}, f32[2,48]{1,0:T(2,128)S(1)}, u32[]{:S(2)}, u32[]{:S(2)}) collective-permute-start(f32[2,48]{1,0:T(2,128)S(1)} %pad_maximum_fusion.2), channel_id=1, source_target_pairs={{1,0},{0,1},{3,2},{2,3},{5,4},{4,5},{7,6},{6,7},{9,8},{8,9},{11,10... | collective-permute-start | bytes 1160 | tf_op jit(solution)/shard_map/ppermute | solution.py:743
  (228 shorter events, 88.1 us)
Async XLA Ops:
  7.2 129.6 %all-gather.2.cloned.1.call-start = ((), (), s32[]{:S(2)}) async-start(), calls=%async_computation.1 | async-start | bytes 10027008 | tf_op jit(solution)/shard_map/all_gather | solution.py:653
  21.8 27.3 %collective-permute-start.11 = (bf16[256,1536]{1,0:T(8,128)(2,1)}, bf16[256,1536]{1,0:T(8,128)(2,1)}, u32[]{:S(2)}, u32[]{:S(2)}) collective-permute-start(bf16[256,1536]{1,0:T(8,128)(2,1)} %t0), channel_id=1, source_target_pairs={{2,0},{0,2},{3,1},{1,3},{6,4},{4,6},{7,5},{5,7},{10,8},{8,10},{11,... | collective-permute-start | bytes 2359304 | tf_op jit(solution)/shard_map/ppermute | solution.py:555
  22.1 9.7 %collective-permute-start.4 = (bf16[96,640]{1,0:T(8,128)(2,1)S(1)}, bf16[96,640]{1,0:T(8,128)(2,1)S(1)}, u32[]{:S(2)}, u32[]{:S(2)}) collective-permute-start(bf16[96,640]{1,0:T(8,128)(2,1)S(1)} %get-tuple-element.278), channel_id=1, source_target_pairs={{8,0},{16,8},{24,16},{0,24},{9,1},{17,9},{25,17},{1,25},{10,2},{18... | collective-permute-start | bytes 368648 | tf_op jit(solution)/shard_map/ppermute | solution.py:555
  28.6 19.6 %collective-permute-start.10 = (bf16[48,3072]{1,0:T(8,128)(2,1)S(1)}, bf16[48,3072]{1,0:T(8,128)(2,1)S(1)}, u32[]{:S(2)}, u32[]{:S(2)}) collective-permute-start(bf16[48,3072]{1,0:T(8,128)(2,1)S(1)} %pad_add_fusion), channel_id=1, source_target_pairs={{4,0},{0,4},{5,1},{1,5},{6,2},{2,6},{7,3},{3,7},{12,8},{8,12},{13,... | collective-permute-start | bytes 884744 | tf_op jit(solution)/shard_map/ppermute | solution.py:555
  49.2 248.1 %reduce-scatter.2.cloned.1.call-start = ((), (), s32[]{:S(2)}) async-start(), calls=%async_computation.2 | async-start | bytes 10027008 | tf_op jit(solution)/shard_map/reduce_scatter | solution.py:694
  49.2 11.0 %collective-permute-start.15 = (bf16[4,96,640]{2,1,0:T(8,128)(2,1)S(1)}, bf16[4,96,640]{2,1,0:T(8,128)(2,1)S(1)}, u32[]{:S(2)}, u32[]{:S(2)}) collective-permute-start(bf16[4,96,640]{2,1,0:T(8,128)(2,1)S(1)} %get-tuple-element.149.a0), channel_id=1, source_target_pairs={{32,0},{64,32},{96,64},{0,96},{33,1},{65,33},{97,65},{1,97},{34,2}... | collective-permute-start | bytes 1474568 | tf_op jit(solution)/shard_map/ppermute | solution.py:555
  51.8 13.5 %collective-permute-start.16 = (bf16[4,96,640]{2,1,0:T(8,128)(2,1)S(1)}, bf16[4,96,640]{2,1,0:T(8,128)(2,1)S(1)}, u32[]{:S(2)}, u32[]{:S(2)}) collective-permute-start(bf16[4,96,640]{2,1,0:T(8,128)(2,1)S(1)} %get-tuple-element.150.b0), channel_id=1, source_target_pairs={{8,0},{16,8},{24,16},{0,24},{9,1},{17,9},{25,17},{1,25},{10,2},{18... | collective-permute-start | bytes 1474568 | tf_op jit(solution)/shard_map/ppermute | solution.py:555
  55.5 13.2 %collective-permute-start.17 = (bf16[4,96,640]{2,1,0:T(8,128)(2,1)S(1)}, bf16[4,96,640]{2,1,0:T(8,128)(2,1)S(1)}, u32[]{:S(2)}, u32[]{:S(2)}) collective-permute-start(bf16[4,96,640]{2,1,0:T(8,128)(2,1)S(1)} %get-tuple-element.149.a0), channel_id=1, source_target_pairs={{96,0},{0,32},{32,64},{64,96},{97,1},{1,33},{33,65},{65,97},{98,2}... | collective-permute-start | bytes 1474568 | tf_op jit(solution)/shard_map/ppermute | solution.py:555
  55.5 13.2 %collective-permute-start.18 = (bf16[4,96,640]{2,1,0:T(8,128)(2,1)S(1)}, bf16[4,96,640]{2,1,0:T(8,128)(2,1)S(1)}, u32[]{:S(2)}, u32[]{:S(2)}) collective-permute-start(bf16[4,96,640]{2,1,0:T(8,128)(2,1)S(1)} %get-tuple-element.150.b0), channel_id=1, source_target_pairs={{24,0},{0,8},{8,16},{16,24},{25,1},{1,9},{9,17},{17,25},{26,2},{2,... | collective-permute-start | bytes 1474568 | tf_op jit(solution)/shard_map/ppermute | solution.py:555
  55.5 28.1 %collective-permute-start.13 = (bf16[256,1536]{1,0:T(8,128)(2,1)S(1)}, bf16[256,1536]{1,0:T(8,128)(2,1)}, u32[]{:S(2)}, u32[]{:S(2)}) collective-permute-start(bf16[256,1536]{1,0:T(8,128)(2,1)S(1)} %copy-done.3), channel_id=1, source_target_pairs={{1,0},{0,1},{3,2},{2,3},{5,4},{4,5},{7,6},{6,7},{9,8},{8,9},{11,10... | collective-permute-start | bytes 2359304 | tf_op jit(solution)/shard_map/ppermute | solution.py:555
  60.3 23.4 %collective-permute-start.14 = (bf16[256,1536]{1,0:T(8,128)(2,1)}, bf16[256,1536]{1,0:T(8,128)(2,1)}, u32[]{:S(2)}, u32[]{:S(2)}) collective-permute-start(bf16[256,1536]{1,0:T(8,128)(2,1)} %collective-permute-done.11.t2), channel_id=1, source_target_pairs={{1,0},{0,1},{3,2},{2,3},{5,4},{4,5},{7,6},{6,7},{9,8},{8,9},{11,10... | collective-permute-start | bytes 2359304 | tf_op jit(solution)/shard_map/ppermute | solution.py:555
  65.3 34.3 %collective-permute-start.12 = (bf16[256,1536]{1,0:T(8,128)(2,1)S(1)}, bf16[256,1536]{1,0:T(8,128)(2,1)}, u32[]{:S(2)}, u32[]{:S(2)}) collective-permute-start(bf16[256,1536]{1,0:T(8,128)(2,1)S(1)} %copy-done.6), channel_id=1, source_target_pairs={{2,0},{0,2},{3,1},{1,3},{6,4},{4,6},{7,5},{5,7},{10,8},{8,10},{11,... | collective-permute-start | bytes 2359304 | tf_op jit(solution)/shard_map/ppermute | solution.py:555
  68.8 14.9 %collective-permute-start.19 = (bf16[4,96,640]{2,1,0:T(8,128)(2,1)S(1)}, bf16[4,96,640]{2,1,0:T(8,128)(2,1)}, u32[]{:S(2)}, u32[]{:S(2)}) collective-permute-start(bf16[4,96,640]{2,1,0:T(8,128)(2,1)S(1)} %get-tuple-element.149.a0), channel_id=1, source_target_pairs={{64,0},{96,32},{0,64},{32,96},{65,1},{97,33},{1,65},{33,97},{66,2}... | collective-permute-start | bytes 1474568 | tf_op jit(solution)/shard_map/ppermute | solution.py:555
  70.4 13.3 %collective-permute-start.20 = (bf16[4,96,640]{2,1,0:T(8,128)(2,1)S(1)}, bf16[4,96,640]{2,1,0:T(8,128)(2,1)}, u32[]{:S(2)}, u32[]{:S(2)}) collective-permute-start(bf16[4,96,640]{2,1,0:T(8,128)(2,1)S(1)} %get-tuple-element.150.b0), channel_id=1, source_target_pairs={{16,0},{24,8},{0,16},{8,24},{17,1},{25,9},{1,17},{9,25},{18,2},{26... | collective-permute-start | bytes 1474568 | tf_op jit(solution)/shard_map/ppermute | solution.py:555
  99.7 12.0 %collective-permute-start.22 = (bf16[256,1536]{1,0:T(8,128)(2,1)}, bf16[256,1536]{1,0:T(8,128)(2,1)S(1)}, u32[]{:S(2)}, u32[]{:S(2)}) collective-permute-start(bf16[256,1536]{1,0:T(8,128)(2,1)} %get-tuple-element.164), channel_id=1, source_target_pairs={{1,0},{0,1},{3,2},{2,3},{5,4},{4,5},{7,6},{6,7},{9,8},{8,9},{11,10... | collective-permute-start | bytes 2359304 | tf_op jit(solution)/shard_map/ppermute | solution.py:555
  113.0 19.0 %collective-permute-start.23 = (bf16[256,1536]{1,0:T(8,128)(2,1)S(1)}, bf16[256,1536]{1,0:T(8,128)(2,1)S(1)}, u32[]{:S(2)}, u32[]{:S(2)}) collective-permute-start(bf16[256,1536]{1,0:T(8,128)(2,1)S(1)} %add_convert_fusion.4), channel_id=1, source_target_pairs={{2,0},{0,2},{3,1},{1,3},{6,4},{4,6},{7,5},{5,7},{10,8},{8,10},{11,... | collective-permute-start | bytes 2359304 | tf_op jit(solution)/shard_map/ppermute | solution.py:555
  113.1 21.3 %collective-permute-start.26 = (bf16[256,1536]{1,0:T(8,128)(2,1)S(1)}, bf16[256,1536]{1,0:T(8,128)(2,1)S(1)}, u32[]{:S(2)}, u32[]{:S(2)}) collective-permute-start(bf16[256,1536]{1,0:T(8,128)(2,1)S(1)} %copy-done.6), channel_id=1, source_target_pairs={{1,0},{0,1},{3,2},{2,3},{5,4},{4,5},{7,6},{6,7},{9,8},{8,9},{11,10... | collective-permute-start | bytes 2359304 | tf_op jit(solution)/shard_map/ppermute | solution.py:555
  134.0 19.2 %collective-permute-start.24 = (bf16[256,1536]{1,0:T(8,128)(2,1)S(1)}, bf16[256,1536]{1,0:T(8,128)(2,1)}, u32[]{:S(2)}, u32[]{:S(2)}) collective-permute-start(bf16[256,1536]{1,0:T(8,128)(2,1)S(1)} %multiply_convert_fusion.h0), channel_id=1, source_target_pairs={{2,0},{0,2},{3,1},{1,3},{6,4},{4,6},{7,5},{5,7},{10,8},{8,10},{11,... | collective-permute-start | bytes 2359304 | tf_op jit(solution)/shard_map/ppermute | solution.py:555
  134.0 20.4 %collective-permute-start.28 = (bf16[256,1536]{1,0:T(8,128)(2,1)}, bf16[256,1536]{1,0:T(8,128)(2,1)}, u32[]{:S(2)}, u32[]{:S(2)}) collective-permute-start(bf16[256,1536]{1,0:T(8,128)(2,1)} %collective-permute-done.12.g0.g2), channel_id=1, source_target_pairs={{1,0},{0,1},{3,2},{2,3},{5,4},{4,5},{7,6},{6,7},{9,8},{8,9},{11,10... | collective-permute-start | bytes 2359304 | tf_op jit(solution)/shard_map/ppermute | solution.py:555
  177.0 19.2 %collective-permute-start.32 = (bf16[256,1536]{1,0:T(8,128)(2,1)}, bf16[256,1536]{1,0:T(8,128)(2,1)}, u32[]{:S(2)}, u32[]{:S(2)}) collective-permute-start(bf16[256,1536]{1,0:T(8,128)(2,1)} %add_convert_fusion.2), channel_id=1, source_target_pairs={{2,0},{0,2},{3,1},{1,3},{6,4},{4,6},{7,5},{5,7},{10,8},{8,10},{11,... | collective-permute-start | bytes 2359304 | tf_op jit(solution)/shard_map/ppermute | solution.py:555
  202.4 19.2 %collective-permute-start.34 = (bf16[256,1536]{1,0:T(8,128)(2,1)S(1)}, bf16[256,1536]{1,0:T(8,128)(2,1)S(1)}, u32[]{:S(2)}, u32[]{:S(2)}) collective-permute-start(bf16[256,1536]{1,0:T(8,128)(2,1)S(1)} %get-tuple-element.187.o0), channel_id=1, source_target_pairs={{2,0},{0,2},{3,1},{1,3},{6,4},{4,6},{7,5},{5,7},{10,8},{8,10},{11,... | collective-permute-start | bytes 2359304 | tf_op jit(solution)/shard_map/ppermute | solution.py:555
  202.4 20.1 %collective-permute-start.29 = (bf16[256,1536]{1,0:T(8,128)(2,1)S(1)}, bf16[256,1536]{1,0:T(8,128)(2,1)S(1)}, u32[]{:S(2)}, u32[]{:S(2)}) collective-permute-start(bf16[256,1536]{1,0:T(8,128)(2,1)S(1)} %copy-done.36), channel_id=1, source_target_pairs={{1,0},{0,1},{3,2},{2,3},{5,4},{4,5},{7,6},{6,7},{9,8},{8,9},{11,10... | collective-permute-start | bytes 2359304 | tf_op jit(solution)/shard_map/ppermute | solution.py:555
  204.2 19.5 %collective-permute-start.33 = (bf16[256,1536]{1,0:T(8,128)(2,1)S(1)}, bf16[256,1536]{1,0:T(8,128)(2,1)S(1)}, u32[]{:S(2)}, u32[]{:S(2)}) collective-permute-start(bf16[256,1536]{1,0:T(8,128)(2,1)S(1)} %get-tuple-element.187.o0), channel_id=1, source_target_pairs={{1,0},{0,1},{3,2},{2,3},{5,4},{4,5},{7,6},{6,7},{9,8},{8,9},{11,10... | collective-permute-start | bytes 2359304 | tf_op jit(solution)/shard_map/ppermute | solution.py:555
  225.3 20.7 %collective-permute-start.41 = (bf16[256,1536]{1,0:T(8,128)(2,1)}, bf16[256,1536]{1,0:T(8,128)(2,1)}, u32[]{:S(2)}, u32[]{:S(2)}) collective-permute-start(bf16[256,1536]{1,0:T(8,128)(2,1)} %add_convert_fusion.3), channel_id=1, source_target_pairs={{2,0},{0,2},{3,1},{1,3},{6,4},{4,6},{7,5},{5,7},{10,8},{8,10},{11,... | collective-permute-start | bytes 2359304 | tf_op jit(solution)/shard_map/ppermute | solution.py:555
  242.6 19.5 %collective-permute-start.37 = (bf16[384,576]{1,0:T(8,128)(2,1)}, bf16[384,576]{1,0:T(8,128)(2,1)S(1)}, u32[]{:S(2)}, u32[]{:S(2)}) collective-permute-start(bf16[384,576]{1,0:T(8,128)(2,1)} %get-tuple-element.201), channel_id=1, source_target_pairs={{32,0},{64,32},{96,64},{0,96},{33,1},{65,33},{97,65},{1,97},{34,2}... | collective-permute-start | bytes 1327112 | tf_op jit(solution)/shard_map/ppermute | solution.py:555
  244.3 18.7 %collective-permute-start.38 = (bf16[4,96,576]{2,1,0:T(8,128)(2,1)}, bf16[4,96,576]{2,1,0:T(8,128)(2,1)S(1)}, u32[]{:S(2)}, u32[]{:S(2)}) collective-permute-start(bf16[4,96,576]{2,1,0:T(8,128)(2,1)} %get-tuple-element.202), channel_id=1, source_target_pairs={{8,0},{16,8},{24,16},{0,24},{9,1},{17,9},{25,17},{1,25},{10,2},{18... | collective-permute-start | bytes 1327112 | tf_op jit(solution)/shard_map/ppermute | solution.py:555
  244.9 19.4 %collective-permute-start.39 = (bf16[384,576]{1,0:T(8,128)(2,1)}, bf16[384,576]{1,0:T(8,128)(2,1)S(1)}, u32[]{:S(2)}, u32[]{:S(2)}) collective-permute-start(bf16[384,576]{1,0:T(8,128)(2,1)} %get-tuple-element.203), channel_id=1, source_target_pairs={{96,0},{0,32},{32,64},{64,96},{97,1},{1,33},{33,65},{65,97},{98,2}... | collective-permute-start | bytes 1327112 | tf_op jit(solution)/shard_map/ppermute | solution.py:555
  245.8 18.5 %collective-permute-start.40 = (bf16[4,96,576]{2,1,0:T(8,128)(2,1)}, bf16[4,96,576]{2,1,0:T(8,128)(2,1)S(1)}, u32[]{:S(2)}, u32[]{:S(2)}) collective-permute-start(bf16[4,96,576]{2,1,0:T(8,128)(2,1)} %get-tuple-element.204), channel_id=1, source_target_pairs={{24,0},{0,8},{8,16},{16,24},{25,1},{1,9},{9,17},{17,25},{26,2},{2,... | collective-permute-start | bytes 1327112 | tf_op jit(solution)/shard_map/ppermute | solution.py:555
  265.3 20.0 %collective-permute-start.42 = (bf16[384,576]{1,0:T(8,128)(2,1)}, bf16[384,576]{1,0:T(8,128)(2,1)S(1)}, u32[]{:S(2)}, u32[]{:S(2)}) collective-permute-start(bf16[384,576]{1,0:T(8,128)(2,1)} %get-tuple-element.216), channel_id=1, source_target_pairs={{64,0},{96,32},{0,64},{32,96},{65,1},{97,33},{1,65},{33,97},{66,2}... | collective-permute-start | bytes 1327112 | tf_op jit(solution)/shard_map/ppermute | solution.py:555
  266.6 20.6 %collective-permute-start.43 = (bf16[4,96,576]{2,1,0:T(8,128)(2,1)}, bf16[4,96,576]{2,1,0:T(8,128)(2,1)S(1)}, u32[]{:S(2)}, u32[]{:S(2)}) collective-permute-start(bf16[4,96,576]{2,1,0:T(8,128)(2,1)} %get-tuple-element.217), channel_id=1, source_target_pairs={{16,0},{24,8},{0,16},{8,24},{17,1},{25,9},{1,17},{9,25},{18,2},{26... | collective-permute-start | bytes 1327112 | tf_op jit(solution)/shard_map/ppermute | solution.py:555
  266.9 35.6 %collective-permute-start.50 = (bf16[256,1536]{1,0:T(8,128)(2,1)}, bf16[256,1536]{1,0:T(8,128)(2,1)}, u32[]{:S(2)}, u32[]{:S(2)}) collective-permute-start(bf16[256,1536]{1,0:T(8,128)(2,1)} %get-tuple-element.250), channel_id=1, source_target_pairs={{1,0},{0,1},{3,2},{2,3},{5,4},{4,5},{7,6},{6,7},{9,8},{8,9},{11,10... | collective-permute-start | bytes 2359304 | tf_op jit(solution)/shard_map/ppermute | solution.py:555
  269.7 32.8 %collective-permute-start.52 = (bf16[256,1536]{1,0:T(8,128)(2,1)}, bf16[256,1536]{1,0:T(8,128)(2,1)}, u32[]{:S(2)}, u32[]{:S(2)}) collective-permute-start(bf16[256,1536]{1,0:T(8,128)(2,1)} %add_convert_fusion), channel_id=1, source_target_pairs={{2,0},{0,2},{3,1},{1,3},{6,4},{4,6},{7,5},{5,7},{10,8},{8,10},{11,... | collective-permute-start | bytes 2359304 | tf_op jit(solution)/shard_map/ppermute | solution.py:555
  (66 other events, 566.8 us)
Sparse Core Ops, SparseCore 0:
  49.3 87.4 all-gather.1
  196.4 95.7 reduce-scatter.1

commit v9 on v8

--- a/solution.py
+++ b/solution.py
@@ -227,11 +227,11 @@
 
 def attend_back_kernel(place, cos_ref, sin_ref,
                        o0, o1, o2, o3, w_hbm, h_hbm, qt_hbm, kt_hbm, vt_hbm, attn_hbm, probs_hbm,
-                       dqkv_hbm, x0, x1, x2, x3, y0, y1, y2, y3,
+                       keep_hbm, send_hbm, y0, y1, y2, y3, c0, c1, c2, c3,
                        o_ref, w_ref, h_ref, qt_ref, kt_ref, vt_ref, attn_ref, probs_ref,
-                       do_ref, dqkv_ref, first_ref, second_ref, v_ref, delta_ref, dk_ref, dv_ref,
+                       do_ref, dqkv_ref, first_ref, second_ref, v_ref, proj_ref, part_ref, delta_ref, dk_ref, dv_ref,
                        in_sem, out_sem, probs_sem):
-    block, ix, iz = place[0], place[1], place[2]
+    block, iz, mine = place[0], place[2], place[3]
     heads, _, length = qt_ref.shape
     groups = kt_ref.shape[0]
     group_size = heads // groups
@@ -262,6 +262,7 @@
     for group in range(groups):
         probs_copy(group).start()
     h_came = fetch.start(h_hbm, h_ref)
+    proj_came = fetch.start(w_hbm.at[:, pl.ds(QUERY_AT, REST_AT - QUERY_AT)], proj_ref)
     for copy in early:
         copy.wait()
     do_ref[...] = dot_tt(w_ref[...], o_ref[...]).astype(BF16)
@@ -304,22 +305,26 @@
         dqkv_ref[head_rows(heads + 2 * group), :] = turned_back(
             dk_ref[group] * SCALE, cos_ref[...], sin_ref[...])
         dqkv_ref[head_rows(heads + 2 * group + 1), :] = dv_ref[group].astype(BF16)
-    store.start(dqkv_ref, dqkv_hbm)
     h_came.wait()
 
     rows = width // 16
     part = dot_tt(h_ref[...], dqkv_ref[...]).astype(BF16)
     first_ref[:, :heads_w] = part[:, :heads_w]
-    second_ref[:, LATE_WIDTH - heads_w :] = part[:, heads_w:]
-    part = dot_tt(o_ref[...], attn_ref[...]).astype(BF16)
-    first_ref[:, heads_w:] = part[:, :LATE_OUT]
-    second_ref[:, : heads_w - LATE_OUT] = part[:, LATE_OUT:]
-    for offset, (x_out, y_out) in enumerate(((x0, y0), (x1, y1), (x2, y2), (x3, y3))):
-        to_x = lax.rem(ix + 4 - offset, 4)
+    second_ref[...] = part[:, heads_w:]
+    first_ref[:, heads_w:] = dot_tt(o_ref[...], attn_ref[...]).astype(BF16)
+    for i in range(16):
+        for half, out in ((mine, keep_hbm), (1 - mine, send_hbm)):
+            store.start(first_ref.at[block_at(2 * i + half, rows // 2), :], out.at[i])
+    for offset, out in enumerate((y0, y1, y2, y3)):
         to_z = lax.rem(iz + 4 - offset, 4)
-        store.start(first_ref.at[block_at(to_x, 4 * rows), :], x_out)
         for i in range(4):
-            store.start(second_ref.at[block_at(i * 4 + to_z, rows), :], y_out.at[i])
+            store.start(second_ref.at[block_at(i * 4 + to_z, rows), :], out.at[i])
+
+    proj_came.wait()
+    for step, out in ((1, c1), (3, c3), (2, c2), (0, c0)):
+        at = block_at(lax.bitwise_xor(block, step), size)
+        part_ref[step] = dot_tt(dqkv_ref[:, at], proj_ref[...]).astype(BF16)
+        store.start(part_ref.at[step], out)
     store.wait()
 
 
@@ -329,44 +334,21 @@
     groups = kt.shape[0]
     every_w = (heads + 2 * groups) * HD
     rows = width // 16
-    outs = [(every_w, length)] + [(4 * rows, LATE_WIDTH)] * 4 + [(4, rows, LATE_WIDTH)] * 4
+    heads_w = heads * HD
+    outs = [(16, rows // 2, 2 * heads_w)] * 2 + [(4, rows, every_w - heads_w)] * 4
+    outs += [pieces[0].shape] * 4
     scratch = [
         (length, width), (width, heads * HD), (length, width),
         qt.shape, kt.shape, vt.shape, attn.shape, probs.shape,
-        attn.shape, (every_w, length), (width, LATE_WIDTH), (width, LATE_WIDTH),
-        (groups, length, HD),
+        attn.shape, (every_w, length), (width, 2 * heads_w), (width, every_w - heads_w),
+        (groups, length, HD), (width, every_w), (4, *pieces[0].shape),
     ]
     wide = [(heads, 1, length), kt.shape, kt.shape]
     return kernel_call(
         attend_back_kernel, "attend_back", place, (cosine, sine),
         (*pieces, weights, h_first, qt, kt, vt, attn, probs),
         [like(s) for s in outs], [],
-        [vmem(s) for s in scratch] + [vmem(s, F32) for s in wide], 11, 21, groups)
-
-
-def project_back_kernel(place, dqkv_hbm, w_hbm, c0, c1, c2, c3,
-                        dqkv_ref, w_ref, part_ref, in_sem, out_sem):
-    block = place[0]
-    size = part_ref.shape[1]
-    fetch, store = Moves(in_sem), Moves(out_sem)
-    fetch.start(w_hbm.at[:, pl.ds(QUERY_AT, REST_AT - QUERY_AT)], w_ref)
-    fetch.start(dqkv_hbm, dqkv_ref)
-    fetch.wait()
-    for step, out in ((3, c3), (2, c2), (1, c1), (0, c0)):
-        at = block_at(lax.bitwise_xor(block, step), size)
-        part_ref[step] = dot_tt(dqkv_ref[:, at], w_ref[...]).astype(BF16)
-        store.start(part_ref.at[step], out)
-    store.wait()
-
-
-def project_back(place, d_qkv, weights):
-    every_w, length = d_qkv.shape
-    width = weights.shape[0]
-    size = length // 4
-    return kernel_call(
-        project_back_kernel, "project_back", place, (), (d_qkv, weights),
-        [like((size, width))] * 4, [],
-        [vmem(s) for s in (d_qkv.shape, (width, every_w), (4, size, width))], 2, 4)
+        [vmem(s) for s in scratch] + [vmem(s, F32) for s in wide], 12, 52, groups)
 
 
 def feed_kernel(place, h0, h1, g0, g1, w_hbm, hidden_hbm, dgu_hbm, b0, b1, r0, r1,
@@ -478,66 +460,64 @@
         [like((width, 3 * hidden_w))], [], [vmem(s) for s in scratch], 20, 6)[0]
 
 
-LATE_OUT, LATE_WIDTH = 192, 576
-
-
-def late_middle_kernel(place, *refs):
-    x_in, y_in, outs = refs[0:4], refs[4:8], refs[8:]
-    ix, iz = place[1], place[2]
-    rows = outs[0].shape[0]
-    for offset in range(4):
-        at = block_at(lax.rem(iz + 4 - offset, 4), rows)
-        total = x_in[0][at, :].astype(F32)
-        for ref in x_in[1:]:
-            total += ref[at, :].astype(F32)
-        outs[offset][...] = total.astype(BF16)
+def late_middle_kernel(place, keep_ref, came_ref, y0, y1, y2, y3, *outs):
+    ix = place[1]
+    _, rows, width = keep_ref.shape
+    for offset, out in enumerate(outs):
         to = lax.rem(ix + 4 - offset, 4)
-        total = y_in[0][to].astype(F32)
-        for ref in y_in[1:]:
+        at = pl.ds(to * 4, 4)
+        total = keep_ref[at].astype(F32) + came_ref[at].astype(F32)
+        out[: 4 * rows, :] = total.reshape(4 * rows, width).astype(BF16)
+        total = y0[to].astype(F32)
+        for ref in (y1, y2, y3):
             total += ref[to].astype(F32)
-        outs[4 + offset][...] = total.astype(BF16)
-
-
-def late_middle(place, along_x, along_z):
-    _, rows, width = along_z[0].shape
+        for half in range(2):
+            out[4 * rows :, half * width // 2 : (half + 1) * width // 2] = (
+                total[half * rows : (half + 1) * rows].astype(BF16))
+
+
+def late_middle(place, keep, came, along_z):
+    _, rows, width = keep.shape
     return pl.pallas_call(
         late_middle_kernel,
-        out_shape=[like((rows, width))] * 8,
-        in_specs=[scalars()] + [whole()] * 8,
-        out_specs=[whole()] * 8,
+        out_shape=[like((5 * rows, width))] * 4,
+        in_specs=[scalars()] + [whole()] * 6,
+        out_specs=[whole()] * 4,
         compiler_params=pltpu.CompilerParams(vmem_limit_bytes=16 * MIB),
         cost_estimate=SMALL,
         name="late_middle",
-    )(place, *along_x, *along_z)
+    )(place, keep, came, *along_z)
 
 
 def late_last_kernel(place, *refs):
-    x_in, y_in, keep_ref, send_ref = refs[0:4], refs[4:8], refs[8], refs[9]
-    mine = place[3]
-    rows = keep_ref.shape[0]
-    for inputs, columns in ((x_in, slice(0, LATE_WIDTH)), (y_in, slice(LATE_WIDTH, 2 * LATE_WIDTH))):
-        for ref, half in ((keep_ref, mine), (send_ref, 1 - mine)):
-            at = block_at(half, rows)
-            total = inputs[0][at, :].astype(F32)
-            for other_ref in inputs[1:]:
-                total += other_ref[at, :].astype(F32)
-            ref[:, columns] = total.astype(ref.dtype)
-
-
-def late_last(place, along_z, along_x):
-    rows, width = along_x[0].shape
+    inputs, outs, (keep_ref, send_ref) = refs[0:4], refs[4:8], refs[8:10]
+    iz, mine = place[2], place[3]
+    rows, width = keep_ref.shape
+
+    def total(row_at, column_at):
+        return sum(ref[row_at, column_at].astype(F32) for ref in inputs)
+
+    for offset, out in enumerate(outs):
+        to = lax.rem(iz + 4 - offset, 4)
+        out[...] = total(block_at(to, rows), slice(None)).astype(out.dtype)
+    last = slice(4 * rows, 5 * rows)
+    keep_ref[...] = total(last, block_at(mine, width))
+    send_ref[...] = total(last, block_at(1 - mine, width)).astype(BF16)
+
+
+def late_last(place, along_x):
+    rows, width = along_x[0].shape[0] // 5, along_x[0].shape[1]
+    outs = [like((rows, width), F32)] + [like((rows, width))] * 3
+    outs += [like((rows, width // 2), F32), like((rows, width // 2))]
     return pl.pallas_call(
         late_last_kernel,
-        out_shape=[
-            jax.ShapeDtypeStruct((rows // 2, 2 * width), F32),
-            jax.ShapeDtypeStruct((rows // 2, 2 * width), BF16),
-        ],
-        in_specs=[scalars()] + [whole()] * 8,
-        out_specs=[whole()] * 2,
+        out_shape=outs,
+        in_specs=[scalars()] + [whole()] * 4,
+        out_specs=[whole()] * 6,
         compiler_params=pltpu.CompilerParams(vmem_limit_bytes=16 * MIB),
         cost_estimate=SMALL,
         name="late_last",
-    )(place, *along_z, *along_x)
+    )(place, *along_x)
 
 
 def norm_rows(values_in):
@@ -634,10 +614,11 @@
     gain_part = lax.dynamic_update_slice(jnp.zeros((2, pair_w), F32), norm_gains, (0, gain_at))
     for axis in ("core", "yl", "yh"):
         gain_part = gain_part + other(gain_part, axis)
-    (gate_up, down, tokens), gain_part = after((w_gateup, w_down, tokens), gain_part)
+    (gate_up, down), gain_part = after((w_gateup, w_down), gain_part)
     mlp_own = (gate_up[:, 0], gate_up[:, 1], down.T)
     mlp_own = [(i * hidden_w, part) for i, part in enumerate(mlp_own)]
     mlp_pair = pair_rows(side_by_side(mlp_own, 3 * hidden_w), "yh")
+    tokens, mlp_pair = after(tokens, mlp_pair)
     gain_part = gain_part.T
     gain_high = lax.reduce_precision(gain_part, 8, 7)
     gain_low = (gain_part - gain_high).astype(BF16)
@@ -706,31 +687,32 @@
     back = attend_back(
         place, cosine, sine, out_pieces, attn_w, h_first, qt, kt, vt, attn, probs
     )
-    d_qkv, *late_parts = back
-    d_qkv, out_far = after(d_qkv, out_far)
-    along_x, along_z, parts = from_both(
-        late_parts[:4], "x", late_parts[4:], "z", True, project_back(place, d_qkv, attn_w)
-    )
-    d_far = other(far_sum(parts[2], parts[3]), "yl")
+    back, out_far = after(back, out_far)
+    late_parts, parts = back[:6], back[6:]
+    keep, send, *along_z = late_parts
+    came = other(send, "yh")
+    along_z[1:] = [from_offset(along_z[i], "z", i, 4) for i in (1, 2, 3)]
+    (came, along_z), d_far = after((came, along_z), far_sum(parts[2], parts[3]))
+    along_x = list(late_middle(place, keep, came, along_z))
+    along_x[1:] = [from_offset(along_x[i], "x", i, 4) for i in (1, 2, 3)]
+    (along_x[1], along_x[3]), early = after((along_x[1], along_x[3]), early)
+    early = pair_sum(early, "yh")
+    d_far = other(d_far, "yl")
     result = (middle + out_near + out_far.astype(F32)).astype(BF16)
-    along_x, result = after(along_x, result)
-    middle_parts = late_middle(place, along_x, along_z)
-    along_z, along_x, early = from_both(
-        middle_parts[:4], "z", middle_parts[4:], "x", True, early
-    )
-    early = pair_sum(early, "yh")
     d_h1_own = near_sum(parts[0], parts[1]) + d_far.astype(F32)
-    along_z, (d_h1_own, early) = after(along_z, (d_h1_own, early))
-    late_keep, late_send = late_last(place, along_z, along_x)
-    late = late_keep + other(late_send, "yh").astype(F32)
+    along_x, (early, d_h1_own) = after(along_x, (early, d_h1_own))
+    late, *send_z, late_keyval, send_pair = late_last(place, along_x)
+    send_z = [from_offset(v, "z", i + 1, 4) for i, v in enumerate(send_z)]
+    send_z, send_pair = after(send_z, other(send_pair, "yh"))
+    late = late + sum(v.astype(F32) for v in send_z)
+    grad_keyval = late_keyval + send_pair.astype(F32)
 
     normed1, factor1 = norm_rows(tokens.astype(F32))
     d_norm1 = norm_back(d_h1_own, normed1, factor1, gain_rows[0])
     input_grad = (d_middle + d_norm1).astype(BF16)
 
     grad_query = late[:, :heads_w]
-    grad_keyval = late[:, 2 * LATE_WIDTH - heads_w :]
-    grad_out = late[:, heads_w : 2 * LATE_WIDTH - heads_w].T
+    grad_out = late[:, heads_w:].T
     grad_gateup = early[:, : 2 * hidden_w].reshape(-1, 2, hidden_w)
 
     gain_sum = jnp.stack(

time: 339 us -> 351 us (1.035)
  starting transfers between devices: 76 us -> 93.5 us
  waiting for transfers between devices: 116 us -> 112 us
    ppermute x55 -> x53, starting transfers between devices: 68 us -> 82.3 us  [from_offset(): lax.ppermute(v, axis, [((i + offset) % size, i) for i in range(size)])]
    ppermute x55 -> x53, waiting for transfers between devices: 115 us -> 105 us  [from_offset(): lax.ppermute(v, axis, [((i + offset) % size, i) for i in range(size)])]
    all_gather x1, waiting for transfers between devices: 0.73 us -> 6.94 us  [body(): mlp_w = lax.all_gather(mlp_pair, ('x', 'z'), axis=0, tiled=True)]
    pallas_call x6 -> x5, Pallas kernels: 84.3 us -> 81.7 us  [kernel_call(): pl.pallas_call(kernel, out_shape=list(small_outs) + list(outs), in_specs=...]
  transfers between devices with their start and end apart: 60 -> 58, of which waited for: 31 -> 27; matrix products, arithmetic and copies ran while one was open for 10% -> 10% of each run, Pallas kernels for 21% -> 20%
where the time goes in v9:
time: 351 us; the launch traced here: 345 us
  waiting for transfers between devices  112 us (32%)
  starting transfers between devices  93.5 us (27%)
  Pallas kernels  83.4 us (24%)
  other arithmetic  28.5 us (8%)
  between operations  15.1 us (4%)
  local copies, waits for them, and re-layouts  12.8 us (4%)
    ppermute x53, waiting for transfers between devices, from_offset(): lax.ppermute(v, axis, [((i + offset) % size, i) for i in range(size)])  105 us
    ppermute x53, starting transfers between devices, from_offset(): lax.ppermute(v, axis, [((i + offset) % size, i) for i in range(size)])  82.3 us
    pallas_call x5, Pallas kernels, kernel_call(): pl.pallas_call(kernel, out_shape=list(small_outs) + list(outs), in_specs=...  81.7 us
    ppermute x3, starting transfers between devices, body(): lax.ppermute(gain_sum, ('yl', 'core'), [(i ^ step, i) for i in range(4)])  11 us
  transfers between devices with their start and end apart: 58, of which 27 were waited for; matrix products, arithmetic and copies ran while one was open for 10% of the time, Pallas kernels for 20%

profile of v9, /device:TPU:1, one launch (start us, length us, event | category | flops | bytes accessed | tf_op | source)
XLA Modules:
  0.0 344.8 jit_solution(13734404303543823721)
XLA Ops:
  13.8 3.1 collective-permute-start.2
  20.3 3.0 collective-permute-start.3
  23.6 3.8 %collective-permute-done.3 = bf16[48,3072]{1,0:T(8,128)(2,1)S(1)} collective-permute-done((bf16[48,3072]{1,0:T(8,128)(2,1)S(1)}, bf16[48,3072]{1,0:T(8,128)(2,1)S(1)}, u32[]{:S(2)}, u32[]{:S(2)}) %collective-permute-start.3) | collective-permute-done | bytes 294944 | tf_op jit(solution)/shard_map/ppermute | solution.py:535
  30.6 2.8 collective-permute-start.10
  33.4 3.8 %collective-permute-start.5 = (bf16[96,640]{1,0:T(8,128)(2,1)S(1)}, bf16[96,640]{1,0:T(8,128)(2,1)S(1)}, u32[]{:S(2)}, u32[]{:S(2)}) collective-permute-start(bf16[96,640]{1,0:T(8,128)(2,1)S(1)} %get-tuple-element.250), channel_id=1, source_target_pairs={{8,0},{16,8},{24,16},{0,24},{9,1},{17,9},{25,17},{1,25},{10,2},{18... | collective-permute-start | bytes 368648 | tf_op jit(solution)/shard_map/ppermute | solution.py:535
  44.5 2.9 collective-permute-done.11.t2
  50.0 3.8 %collective-permute-start.16 = (bf16[4,96,640]{2,1,0:T(8,128)(2,1)S(1)}, bf16[4,96,640]{2,1,0:T(8,128)(2,1)S(1)}, u32[]{:S(2)}, u32[]{:S(2)}) collective-permute-start(bf16[4,96,640]{2,1,0:T(8,128)(2,1)S(1)} %get-tuple-element.137.b0), channel_id=1, source_target_pairs={{8,0},{16,8},{24,16},{0,24},{9,1},{17,9},{25,17},{1,25},{10,2},{18... | collective-permute-start | bytes 1474568 | tf_op jit(solution)/shard_map/ppermute | solution.py:535
  53.8 5.0 %collective-permute-start.13 = (bf16[256,1536]{1,0:T(8,128)(2,1)S(1)}, bf16[256,1536]{1,0:T(8,128)(2,1)}, u32[]{:S(2)}, u32[]{:S(2)}) collective-permute-start(bf16[256,1536]{1,0:T(8,128)(2,1)S(1)} %copy-done.6), channel_id=1, source_target_pairs={{1,0},{0,1},{3,2},{2,3},{5,4},{4,5},{7,6},{6,7},{9,8},{8,9},{11,10... | collective-permute-start | bytes 2359304 | tf_op jit(solution)/shard_map/ppermute | solution.py:535
  58.8 2.7 collective-permute-start.14
  66.1 3.7 %collective-permute-start.20 = (bf16[4,96,640]{2,1,0:T(8,128)(2,1)S(1)}, bf16[4,96,640]{2,1,0:T(8,128)(2,1)}, u32[]{:S(2)}, u32[]{:S(2)}) collective-permute-start(bf16[4,96,640]{2,1,0:T(8,128)(2,1)S(1)} %get-tuple-element.137.b0), channel_id=1, source_target_pairs={{16,0},{24,8},{0,16},{8,24},{17,1},{25,9},{1,17},{9,25},{18,2},{26... | collective-permute-start | bytes 1474568 | tf_op jit(solution)/shard_map/ppermute | solution.py:535
  71.9 7.9 %collective-permute-done.19.a2 = bf16[4,96,640]{2,1,0:T(8,128)(2,1)} collective-permute-done((bf16[4,96,640]{2,1,0:T(8,128)(2,1)S(1)}, bf16[4,96,640]{2,1,0:T(8,128)(2,1)}, u32[]{:S(2)}, u32[]{:S(2)}) %collective-permute-start.19) | collective-permute-done | bytes 491552 | tf_op jit(solution)/shard_map/ppermute | solution.py:535
  79.8 3.8 %collective-permute-done.20.b2 = bf16[4,96,640]{2,1,0:T(8,128)(2,1)} collective-permute-done((bf16[4,96,640]{2,1,0:T(8,128)(2,1)S(1)}, bf16[4,96,640]{2,1,0:T(8,128)(2,1)}, u32[]{:S(2)}, u32[]{:S(2)}) %collective-permute-start.20) | collective-permute-done | bytes 491552 | tf_op jit(solution)/shard_map/ppermute | solution.py:535
  83.7 15.9 %attend.1 = (f32[2,1536]{1,0:T(2,128)}, bf16[1536,1280]{1,0:T(8,128)(2,1)}, bf16[1024,1536]{1,0:T(8,128)(2,1)}, bf16[4,96,1024]{2,1,0:T(8,128)(2,1)}, bf16[2,96,...) custom-call(s32[4]{0:T(128)} %pad_add_fusion.2.place, ...), custom_call_target="tpu_custom_call" | custom-call | flops 1 | bytes 1 | tf_op jit(solution)/shard_map/attend/pallas_call | solution.py:90
  99.7 6.1 %collective-permute-start.22 = (bf16[256,1536]{1,0:T(8,128)(2,1)}, bf16[256,1536]{1,0:T(8,128)(2,1)S(1)}, u32[]{:S(2)}, u32[]{:S(2)}) collective-permute-start(bf16[256,1536]{1,0:T(8,128)(2,1)} %get-tuple-element.151), channel_id=1, source_target_pairs={{1,0},{0,1},{3,2},{2,3},{5,4},{4,5},{7,6},{6,7},{9,8},{8,9},{11,10... | collective-permute-start | bytes 2359304 | tf_op jit(solution)/shard_map/ppermute | solution.py:535
  111.4 16.8 %collective-permute-done.23 = bf16[256,1536]{1,0:T(8,128)(2,1)S(1)} collective-permute-done((bf16[256,1536]{1,0:T(8,128)(2,1)S(1)}, bf16[256,1536]{1,0:T(8,128)(2,1)S(1)}, u32[]{:S(2)}, u32[]{:S(2)}) %collective-permute-start.23) | collective-permute-done | bytes 786464 | tf_op jit(solution)/shard_map/ppermute | solution.py:535
  132.7 6.9 %all-gather.2.cloned.1.call-done.w_hbm = bf16[1536,3072]{1,0:T(8,128)(2,1)} async-done(((bf16[96,3072]{1,0:T(8,128)(2,1)}), bf16[1536,3072]{1,0:T(8,128)(2,1)}) %all-gather.2.cloned.1.call-update) | async-done | bytes 9437200 | tf_op jit(solution)/shard_map/all_gather | solution.py:634
  139.7 14.7 %feed.2 = (bf16[512,1024]{1,0:T(8,128)(2,1)}, bf16[512,2048]{1,0:T(8,128)(2,1)}, bf16[256,1536]{1,0:T(8,128)(2,1)}, bf16[256,1536]{1,0:T(8,128)(2,1)}, bf16[256,...) custom-call(s32[4]{0:T(128)} %pad_add_fusion.2.place, bf16[256,1536]{1,0:T(8,128)(2,1)} %copy-done.11, ...), custom_call_target="tpu_custom_call" | custom-call | flops 1 | bytes 1 | tf_op jit(solution)/shard_map/feed/pallas_call | solution.py:90
  158.6 14.8 %feed.3 = (bf16[512,1024]{1,0:T(8,128)(2,1)}, bf16[512,2048]{1,0:T(8,128)(2,1)}, bf16[256,1536]{1,0:T(8,128)(2,1)}, bf16[256,1536]{1,0:T(8,128)(2,1)}, bf16[256,...) custom-call(s32[4]{0:T(128)} %pad_add_fusion.2.place, bf16[256,1536]{1,0:T(8,128)(2,1)} %collective-permute-done.26.h0.h2, ...), custom_call_target="tpu_custom_call" | custom-call | flops 1 | bytes 1 | tf_op jit(solution)/shard_map/feed/pallas_call | solution.py:90
  179.6 15.4 %feed_grads.1 = bf16[1536,3072]{1,0:T(8,128)(2,1)} custom-call(s32[4]{0:T(128)} %pad_add_fusion.2.place, bf16[256,1536]{1,0:T(8,128)(2,1)} %copy-done.11, bf16[256,1536]{1,0:T(8,128)(2,1)} %collective-permute-done.24.h1, bf16[256,1536]{1,0:T(8,128)(2,1)} %collective-permute-done.26.h0.h2, bf16[256,1536]{1,0:T(8,128)(2,1)} %copy-done.14, ...), custom_call_target="tpu_custom_call" | custom-call | flops 1 | bytes 1 | tf_op jit(solution)/shard_map/feed_grads/pallas_call | solution.py:90
  200.5 3.1 fusion.10
  206.8 15.9 %collective-permute-done.32.o2 = bf16[256,1536]{1,0:T(8,128)(2,1)S(1)} collective-permute-done((bf16[256,1536]{1,0:T(8,128)(2,1)S(1)}, bf16[256,1536]{1,0:T(8,128)(2,1)S(1)}, u32[]{:S(2)}, u32[]{:S(2)}) %collective-permute-start.32) | collective-permute-done | bytes 786464 | tf_op jit(solution)/shard_map/ppermute | solution.py:535
  227.0 20.9 %attend_back.1 = (bf16[16,48,768]{2,1,0:T(8,128)(2,1)}, bf16[16,48,768]{2,1,0:T(8,128)(2,1)}, bf16[4,96,384]{2,1,0:T(8,128)(2,1)}, bf16[4,96,384]{2,1,0:T(8,128)...) custom-call(s32[4]{0:T(128)} %pad_add_fusion.2.place, ...), custom_call_target="tpu_custom_call" | custom-call | flops 1 | bytes 1 | tf_op jit(solution)/shard_map/attend_back/pallas_call | solution.py:90
  258.7 4.5 %collective-permute-done.39.y1 = bf16[4,96,384]{2,1,0:T(8,128)(2,1)S(1)} collective-permute-done((bf16[4,96,384]{2,1,0:T(8,128)(2,1)}, bf16[4,96,384]{2,1,0:T(8,128)(2,1)S(1)}, u32[]{:S(2)}, u32[]{:S(2)}) %collective-permute-start.39) | collective-permute-done | bytes 294944 | tf_op jit(solution)/shard_map/ppermute | solution.py:535
  265.4 7.0 %collective-permute-done.41.y3 = bf16[4,96,384]{2,1,0:T(8,128)(2,1)S(1)} collective-permute-done((bf16[4,96,384]{2,1,0:T(8,128)(2,1)}, bf16[4,96,384]{2,1,0:T(8,128)(2,1)S(1)}, u32[]{:S(2)}, u32[]{:S(2)}) %collective-permute-start.41) | collective-permute-done | bytes 294944 | tf_op jit(solution)/shard_map/ppermute | solution.py:535
  272.4 6.4 %collective-permute-done.38.came_ref = bf16[16,48,768]{2,1,0:T(8,128)(2,1)S(1)} collective-permute-done((bf16[16,48,768]{2,1,0:T(8,128)(2,1)}, bf16[16,48,768]{2,1,0:T(8,128)(2,1)S(1)}, u32[]{:S(2)}, u32[]{:S(2)}) %collective-permute-start.38) | collective-permute-done | bytes 1179680 | tf_op jit(solution)/shard_map/ppermute | solution.py:535
  285.5 11.3 %collective-permute-done.43.refs_1_ = bf16[240,768]{1,0:T(8,128)(2,1)S(1)} collective-permute-done((bf16[240,768]{1,0:T(8,128)(2,1)S(1)}, bf16[240,768]{1,0:T(8,128)(2,1)S(1)}, u32[]{:S(2)}, u32[]{:S(2)}) %collective-permute-start.43) | collective-permute-done | bytes 368672 | tf_op jit(solution)/shard_map/ppermute | solution.py:535
  296.8 3.3 collective-permute-done.44.refs_3_
  301.2 2.9 collective-permute-start.46
  304.1 2.8 convert_add_fusion.1
  312.2 2.8 collective-permute-start.52
  320.0 2.8 fusion.6
  324.1 9.3 %collective-permute-start.53 = (f32[2,48]{1,0:T(2,128)S(1)}, f32[2,48]{1,0:T(2,128)S(1)}, u32[]{:S(2)}, u32[]{:S(2)}) collective-permute-start(f32[2,48]{1,0:T(2,128)S(1)} %pad_maximum_fusion.2), channel_id=1, source_target_pairs={{1,0},{0,1},{3,2},{2,3},{5,4},{4,5},{7,6},{6,7},{9,8},{8,9},{11,10... | collective-permute-start | bytes 1160 | tf_op jit(solution)/shard_map/ppermute | solution.py:725
  (229 shorter events, 99.6 us)
Async XLA Ops:
  7.2 132.5 %all-gather.2.cloned.1.call-start = ((), (), s32[]{:S(2)}) async-start(), calls=%async_computation.1 | async-start | bytes 10027008 | tf_op jit(solution)/shard_map/all_gather | solution.py:634
  28.4 19.0 %collective-permute-start.11 = (bf16[256,1536]{1,0:T(8,128)(2,1)S(1)}, bf16[256,1536]{1,0:T(8,128)(2,1)S(1)}, u32[]{:S(2)}, u32[]{:S(2)}) collective-permute-start(bf16[256,1536]{1,0:T(8,128)(2,1)S(1)} %copy-done.6), channel_id=1, source_target_pairs={{2,0},{0,2},{3,1},{1,3},{6,4},{4,6},{7,5},{5,7},{10,8},{8,10},{11,... | collective-permute-start | bytes 2359304 | tf_op jit(solution)/shard_map/ppermute | solution.py:535
  47.4 252.7 %reduce-scatter.2.cloned.1.call-start = ((), (), s32[]{:S(2)}) async-start(), calls=%async_computation.2 | async-start | bytes 10027008 | tf_op jit(solution)/shard_map/reduce_scatter | solution.py:675
  47.5 11.3 %collective-permute-start.15 = (bf16[4,96,640]{2,1,0:T(8,128)(2,1)S(1)}, bf16[4,96,640]{2,1,0:T(8,128)(2,1)S(1)}, u32[]{:S(2)}, u32[]{:S(2)}) collective-permute-start(bf16[4,96,640]{2,1,0:T(8,128)(2,1)S(1)} %get-tuple-element.136.a0), channel_id=1, source_target_pairs={{32,0},{64,32},{96,64},{0,96},{33,1},{65,33},{97,65},{1,97},{34,2}... | collective-permute-start | bytes 1474568 | tf_op jit(solution)/shard_map/ppermute | solution.py:535
  50.0 11.5 %collective-permute-start.16 = (bf16[4,96,640]{2,1,0:T(8,128)(2,1)S(1)}, bf16[4,96,640]{2,1,0:T(8,128)(2,1)S(1)}, u32[]{:S(2)}, u32[]{:S(2)}) collective-permute-start(bf16[4,96,640]{2,1,0:T(8,128)(2,1)S(1)} %get-tuple-element.137.b0), channel_id=1, source_target_pairs={{8,0},{16,8},{24,16},{0,24},{9,1},{17,9},{25,17},{1,25},{10,2},{18... | collective-permute-start | bytes 1474568 | tf_op jit(solution)/shard_map/ppermute | solution.py:535
  53.8 11.5 %collective-permute-start.18 = (bf16[4,96,640]{2,1,0:T(8,128)(2,1)S(1)}, bf16[4,96,640]{2,1,0:T(8,128)(2,1)S(1)}, u32[]{:S(2)}, u32[]{:S(2)}) collective-permute-start(bf16[4,96,640]{2,1,0:T(8,128)(2,1)S(1)} %get-tuple-element.137.b0), channel_id=1, source_target_pairs={{24,0},{0,8},{8,16},{16,24},{25,1},{1,9},{9,17},{17,25},{26,2},{2,... | collective-permute-start | bytes 1474568 | tf_op jit(solution)/shard_map/ppermute | solution.py:535
  53.8 29.9 %collective-permute-start.13 = (bf16[256,1536]{1,0:T(8,128)(2,1)S(1)}, bf16[256,1536]{1,0:T(8,128)(2,1)}, u32[]{:S(2)}, u32[]{:S(2)}) collective-permute-start(bf16[256,1536]{1,0:T(8,128)(2,1)S(1)} %copy-done.6), channel_id=1, source_target_pairs={{1,0},{0,1},{3,2},{2,3},{5,4},{4,5},{7,6},{6,7},{9,8},{8,9},{11,10... | collective-permute-start | bytes 2359304 | tf_op jit(solution)/shard_map/ppermute | solution.py:535
  58.8 24.9 %collective-permute-start.14 = (bf16[256,1536]{1,0:T(8,128)(2,1)S(1)}, bf16[256,1536]{1,0:T(8,128)(2,1)}, u32[]{:S(2)}, u32[]{:S(2)}) collective-permute-start(bf16[256,1536]{1,0:T(8,128)(2,1)S(1)} %collective-permute-done.11.t2), channel_id=1, source_target_pairs={{1,0},{0,1},{3,2},{2,3},{5,4},{4,5},{7,6},{6,7},{9,8},{8,9},{11,10... | collective-permute-start | bytes 2359304 | tf_op jit(solution)/shard_map/ppermute | solution.py:535
  61.5 38.2 %collective-permute-start.12 = (bf16[256,1536]{1,0:T(8,128)(2,1)S(1)}, bf16[256,1536]{1,0:T(8,128)(2,1)}, u32[]{:S(2)}, u32[]{:S(2)}) collective-permute-start(bf16[256,1536]{1,0:T(8,128)(2,1)S(1)} %copy-done.9), channel_id=1, source_target_pairs={{2,0},{0,2},{3,1},{1,3},{6,4},{4,6},{7,5},{5,7},{10,8},{8,10},{11,... | collective-permute-start | bytes 2359304 | tf_op jit(solution)/shard_map/ppermute | solution.py:535
  62.9 16.9 %collective-permute-start.19 = (bf16[4,96,640]{2,1,0:T(8,128)(2,1)S(1)}, bf16[4,96,640]{2,1,0:T(8,128)(2,1)}, u32[]{:S(2)}, u32[]{:S(2)}) collective-permute-start(bf16[4,96,640]{2,1,0:T(8,128)(2,1)S(1)} %get-tuple-element.136.a0), channel_id=1, source_target_pairs={{64,0},{96,32},{0,64},{32,96},{65,1},{97,33},{1,65},{33,97},{66,2}... | collective-permute-start | bytes 1474568 | tf_op jit(solution)/shard_map/ppermute | solution.py:535
  66.1 17.6 %collective-permute-start.20 = (bf16[4,96,640]{2,1,0:T(8,128)(2,1)S(1)}, bf16[4,96,640]{2,1,0:T(8,128)(2,1)}, u32[]{:S(2)}, u32[]{:S(2)}) collective-permute-start(bf16[4,96,640]{2,1,0:T(8,128)(2,1)S(1)} %get-tuple-element.137.b0), channel_id=1, source_target_pairs={{16,0},{24,8},{0,16},{8,24},{17,1},{25,9},{1,17},{9,25},{18,2},{26... | collective-permute-start | bytes 1474568 | tf_op jit(solution)/shard_map/ppermute | solution.py:535
  109.3 19.0 %collective-permute-start.23 = (bf16[256,1536]{1,0:T(8,128)(2,1)S(1)}, bf16[256,1536]{1,0:T(8,128)(2,1)S(1)}, u32[]{:S(2)}, u32[]{:S(2)}) collective-permute-start(bf16[256,1536]{1,0:T(8,128)(2,1)S(1)} %add_convert_fusion.4), channel_id=1, source_target_pairs={{2,0},{0,2},{3,1},{1,3},{6,4},{4,6},{7,5},{5,7},{10,8},{8,10},{11,... | collective-permute-start | bytes 2359304 | tf_op jit(solution)/shard_map/ppermute | solution.py:535
  110.6 21.3 %collective-permute-start.25 = (bf16[256,1536]{1,0:T(8,128)(2,1)S(1)}, bf16[256,1536]{1,0:T(8,128)(2,1)S(1)}, u32[]{:S(2)}, u32[]{:S(2)}) collective-permute-start(bf16[256,1536]{1,0:T(8,128)(2,1)S(1)} %copy-done.9), channel_id=1, source_target_pairs={{1,0},{0,1},{3,2},{2,3},{5,4},{4,5},{7,6},{6,7},{9,8},{8,9},{11,10... | collective-permute-start | bytes 2359304 | tf_op jit(solution)/shard_map/ppermute | solution.py:535
  130.3 24.1 %collective-permute-start.26 = (bf16[256,1536]{1,0:T(8,128)(2,1)S(1)}, bf16[256,1536]{1,0:T(8,128)(2,1)}, u32[]{:S(2)}, u32[]{:S(2)}) collective-permute-start(bf16[256,1536]{1,0:T(8,128)(2,1)S(1)} %multiply_convert_fusion.h0), channel_id=1, source_target_pairs={{2,0},{0,2},{3,1},{1,3},{6,4},{4,6},{7,5},{5,7},{10,8},{8,10},{11,... | collective-permute-start | bytes 2359304 | tf_op jit(solution)/shard_map/ppermute | solution.py:535
  131.5 24.1 %collective-permute-start.28 = (bf16[256,1536]{1,0:T(8,128)(2,1)}, bf16[256,1536]{1,0:T(8,128)(2,1)}, u32[]{:S(2)}, u32[]{:S(2)}) collective-permute-start(bf16[256,1536]{1,0:T(8,128)(2,1)} %collective-permute-done.12.g0.g2), channel_id=1, source_target_pairs={{1,0},{0,1},{3,2},{2,3},{5,4},{4,5},{7,6},{6,7},{9,8},{8,9},{11,10... | collective-permute-start | bytes 2359304 | tf_op jit(solution)/shard_map/ppermute | solution.py:535
  178.2 19.2 %collective-permute-start.31 = (bf16[256,1536]{1,0:T(8,128)(2,1)}, bf16[256,1536]{1,0:T(8,128)(2,1)}, u32[]{:S(2)}, u32[]{:S(2)}) collective-permute-start(bf16[256,1536]{1,0:T(8,128)(2,1)} %add_convert_fusion.3), channel_id=1, source_target_pairs={{2,0},{0,2},{3,1},{1,3},{6,4},{4,6},{7,5},{5,7},{10,8},{8,10},{11,... | collective-permute-start | bytes 2359304 | tf_op jit(solution)/shard_map/ppermute | solution.py:535
  203.6 19.1 %collective-permute-start.32 = (bf16[256,1536]{1,0:T(8,128)(2,1)S(1)}, bf16[256,1536]{1,0:T(8,128)(2,1)S(1)}, u32[]{:S(2)}, u32[]{:S(2)}) collective-permute-start(bf16[256,1536]{1,0:T(8,128)(2,1)S(1)} %get-tuple-element.175.o0), channel_id=1, source_target_pairs={{2,0},{0,2},{3,1},{1,3},{6,4},{4,6},{7,5},{5,7},{10,8},{8,10},{11,... | collective-permute-start | bytes 2359304 | tf_op jit(solution)/shard_map/ppermute | solution.py:535
  204.8 18.7 %collective-permute-start.34 = (bf16[256,1536]{1,0:T(8,128)(2,1)S(1)}, bf16[256,1536]{1,0:T(8,128)(2,1)S(1)}, u32[]{:S(2)}, u32[]{:S(2)}) collective-permute-start(bf16[256,1536]{1,0:T(8,128)(2,1)S(1)} %copy-done.40), channel_id=1, source_target_pairs={{1,0},{0,1},{3,2},{2,3},{5,4},{4,5},{7,6},{6,7},{9,8},{8,9},{11,10... | collective-permute-start | bytes 2359304 | tf_op jit(solution)/shard_map/ppermute | solution.py:535
  206.6 17.2 %collective-permute-start.35 = (bf16[256,1536]{1,0:T(8,128)(2,1)S(1)}, bf16[256,1536]{1,0:T(8,128)(2,1)S(1)}, u32[]{:S(2)}, u32[]{:S(2)}) collective-permute-start(bf16[256,1536]{1,0:T(8,128)(2,1)S(1)} %get-tuple-element.175.o0), channel_id=1, source_target_pairs={{1,0},{0,1},{3,2},{2,3},{5,4},{4,5},{7,6},{6,7},{9,8},{8,9},{11,10... | collective-permute-start | bytes 2359304 | tf_op jit(solution)/shard_map/ppermute | solution.py:535
  225.6 22.3 %collective-permute-start.37 = (bf16[256,1536]{1,0:T(8,128)(2,1)S(1)}, bf16[256,1536]{1,0:T(8,128)(2,1)S(1)}, u32[]{:S(2)}, u32[]{:S(2)}) collective-permute-start(bf16[256,1536]{1,0:T(8,128)(2,1)S(1)} %add_convert_fusion.2), channel_id=1, source_target_pairs={{2,0},{0,2},{3,1},{1,3},{6,4},{4,6},{7,5},{5,7},{10,8},{8,10},{11,... | collective-permute-start | bytes 2359304 | tf_op jit(solution)/shard_map/ppermute | solution.py:535
  249.5 29.3 %collective-permute-start.38 = (bf16[16,48,768]{2,1,0:T(8,128)(2,1)}, bf16[16,48,768]{2,1,0:T(8,128)(2,1)S(1)}, u32[]{:S(2)}, u32[]{:S(2)}) collective-permute-start(bf16[16,48,768]{2,1,0:T(8,128)(2,1)} %get-tuple-element.199), channel_id=1, source_target_pairs={{4,0},{0,4},{5,1},{1,5},{6,2},{2,6},{7,3},{3,7},{12,8},{8,12},{13,... | collective-permute-start | bytes 3538952 | tf_op jit(solution)/shard_map/ppermute | solution.py:535
  251.9 11.3 %collective-permute-start.39 = (bf16[4,96,384]{2,1,0:T(8,128)(2,1)}, bf16[4,96,384]{2,1,0:T(8,128)(2,1)S(1)}, u32[]{:S(2)}, u32[]{:S(2)}) collective-permute-start(bf16[4,96,384]{2,1,0:T(8,128)(2,1)} %get-tuple-element.201), channel_id=1, source_target_pairs={{8,0},{16,8},{24,16},{0,24},{9,1},{17,9},{25,17},{1,25},{10,2},{18... | collective-permute-start | bytes 884744 | tf_op jit(solution)/shard_map/ppermute | solution.py:535
  254.6 17.7 %collective-permute-start.41 = (bf16[4,96,384]{2,1,0:T(8,128)(2,1)}, bf16[4,96,384]{2,1,0:T(8,128)(2,1)S(1)}, u32[]{:S(2)}, u32[]{:S(2)}) collective-permute-start(bf16[4,96,384]{2,1,0:T(8,128)(2,1)} %get-tuple-element.203), channel_id=1, source_target_pairs={{24,0},{0,8},{8,16},{16,24},{25,1},{1,9},{9,17},{17,25},{26,2},{2,... | collective-permute-start | bytes 884744 | tf_op jit(solution)/shard_map/ppermute | solution.py:535
  255.3 48.8 %collective-permute-start.47 = (bf16[256,1536]{1,0:T(8,128)(2,1)}, bf16[256,1536]{1,0:T(8,128)(2,1)}, u32[]{:S(2)}, u32[]{:S(2)}) collective-permute-start(bf16[256,1536]{1,0:T(8,128)(2,1)} %get-tuple-element.220), channel_id=1, source_target_pairs={{1,0},{0,1},{3,2},{2,3},{5,4},{4,5},{7,6},{6,7},{9,8},{8,9},{11,10... | collective-permute-start | bytes 2359304 | tf_op jit(solution)/shard_map/ppermute | solution.py:535
  278.8 25.3 %collective-permute-start.48 = (bf16[256,1536]{1,0:T(8,128)(2,1)}, bf16[256,1536]{1,0:T(8,128)(2,1)}, u32[]{:S(2)}, u32[]{:S(2)}) collective-permute-start(bf16[256,1536]{1,0:T(8,128)(2,1)} %add_convert_fusion), channel_id=1, source_target_pairs={{2,0},{0,2},{3,1},{1,3},{6,4},{4,6},{7,5},{5,7},{10,8},{8,10},{11,... | collective-permute-start | bytes 2359304 | tf_op jit(solution)/shard_map/ppermute | solution.py:535
  280.0 16.8 %collective-permute-start.43 = (bf16[240,768]{1,0:T(8,128)(2,1)S(1)}, bf16[240,768]{1,0:T(8,128)(2,1)S(1)}, u32[]{:S(2)}, u32[]{:S(2)}) collective-permute-start(bf16[240,768]{1,0:T(8,128)(2,1)S(1)} %get-tuple-element.212), channel_id=1, source_target_pairs={{32,0},{64,32},{96,64},{0,96},{33,1},{65,33},{97,65},{1,97},{34,2}... | collective-permute-start | bytes 1105928 | tf_op jit(solution)/shard_map/ppermute | solution.py:535
  282.4 17.7 %collective-permute-start.44 = (bf16[240,768]{1,0:T(8,128)(2,1)S(1)}, bf16[240,768]{1,0:T(8,128)(2,1)S(1)}, u32[]{:S(2)}, u32[]{:S(2)}) collective-permute-start(bf16[240,768]{1,0:T(8,128)(2,1)S(1)} %get-tuple-element.213), channel_id=1, source_target_pairs={{96,0},{0,32},{32,64},{64,96},{97,1},{1,33},{33,65},{65,97},{98,2}... | collective-permute-start | bytes 1105928 | tf_op jit(solution)/shard_map/ppermute | solution.py:535
  283.7 24.7 %collective-permute-start.45 = (bf16[240,768]{1,0:T(8,128)(2,1)S(1)}, bf16[240,768]{1,0:T(8,128)(2,1)S(1)}, u32[]{:S(2)}, u32[]{:S(2)}) collective-permute-start(bf16[240,768]{1,0:T(8,128)(2,1)S(1)} %get-tuple-element.216), channel_id=1, source_target_pairs={{64,0},{96,32},{0,64},{32,96},{65,1},{97,33},{1,65},{33,97},{66,2}... | collective-permute-start | bytes 1105928 | tf_op jit(solution)/shard_map/ppermute | solution.py:535
  309.1 14.1 %collective-permute-start.49 = (bf16[48,768]{1,0:T(8,128)(2,1)S(1)}, bf16[48,768]{1,0:T(8,128)(2,1)S(1)}, u32[]{:S(2)}, u32[]{:S(2)}) collective-permute-start(bf16[48,768]{1,0:T(8,128)(2,1)S(1)} %get-tuple-element.228), channel_id=1, source_target_pairs={{8,0},{16,8},{24,16},{0,24},{9,1},{17,9},{25,17},{1,25},{10,2},{18... | collective-permute-start | bytes 221192 | tf_op jit(solution)/shard_map/ppermute | solution.py:535
  311.4 11.8 %collective-permute-start.50 = (bf16[48,768]{1,0:T(8,128)(2,1)S(1)}, bf16[48,768]{1,0:T(8,128)(2,1)S(1)}, u32[]{:S(2)}, u32[]{:S(2)}) collective-permute-start(bf16[48,768]{1,0:T(8,128)(2,1)S(1)} %get-tuple-element.229), channel_id=1, source_target_pairs={{16,0},{24,8},{0,16},{8,24},{17,1},{25,9},{1,17},{9,25},{18,2},{26... | collective-permute-start | bytes 221192 | tf_op jit(solution)/shard_map/ppermute | solution.py:535
  311.4 11.8 %collective-permute-start.51 = (bf16[48,768]{1,0:T(8,128)(2,1)S(1)}, bf16[48,768]{1,0:T(8,128)(2,1)S(1)}, u32[]{:S(2)}, u32[]{:S(2)}) collective-permute-start(bf16[48,768]{1,0:T(8,128)(2,1)S(1)} %get-tuple-element.230), channel_id=1, source_target_pairs={{24,0},{0,8},{8,16},{16,24},{25,1},{1,9},{9,17},{17,25},{26,2},{2,... | collective-permute-start | bytes 221192 | tf_op jit(solution)/shard_map/ppermute | solution.py:535
  324.1 12.7 %collective-permute-start.53 = (f32[2,48]{1,0:T(2,128)S(1)}, f32[2,48]{1,0:T(2,128)S(1)}, u32[]{:S(2)}, u32[]{:S(2)}) collective-permute-start(f32[2,48]{1,0:T(2,128)S(1)} %pad_maximum_fusion.2), channel_id=1, source_target_pairs={{1,0},{0,1},{3,2},{2,3},{5,4},{4,5},{7,6},{6,7},{9,8},{8,9},{11,10... | collective-permute-start | bytes 1160 | tf_op jit(solution)/shard_map/ppermute | solution.py:725
  (67 other events, 783.9 us)
Sparse Core Ops, SparseCore 0:
  47.6 92.0 all-gather.1
  197.6 101.0 reduce-scatter.1

commit v10 on v8

--- a/solution.py
+++ b/solution.py
@@ -18,7 +18,7 @@
 GAIN_AT, OUT_AT, QUERY_AT, KEYVAL_AT, REST_AT, ATTN_WIDTH = 0, 128, 256, 640, 1024, 1280
 HALF_WIDTH = ATTN_WIDTH // 2
 OUT_CUT = QUERY_AT - OUT_AT
-LIMIT = 60
+LIMIT = 56
 
 
 def dot_n(left, right):
@@ -634,7 +634,7 @@
     gain_part = lax.dynamic_update_slice(jnp.zeros((2, pair_w), F32), norm_gains, (0, gain_at))
     for axis in ("core", "yl", "yh"):
         gain_part = gain_part + other(gain_part, axis)
-    (gate_up, down, tokens), gain_part = after((w_gateup, w_down, tokens), gain_part)
+    (gate_up, down), gain_part = after((w_gateup, w_down), gain_part)
     mlp_own = (gate_up[:, 0], gate_up[:, 1], down.T)
     mlp_own = [(i * hidden_w, part) for i, part in enumerate(mlp_own)]
     mlp_pair = pair_rows(side_by_side(mlp_own, 3 * hidden_w), "yh")
@@ -646,12 +646,13 @@
     first += side_by_side([(0, gain_high), (2, gain_low)], HALF_WIDTH)
 
     along_z, along_x, _ = from_both([first] * 4, "z", [second] * 4, "x", False)
-    far = other(tokens, "yl")
-    along_z, along_x, mlp_pair, far = lax.optimization_barrier(
-        (jnp.stack(along_z), jnp.stack(along_x), mlp_pair, far)
+    along_z, along_x, mlp_pair, tokens = lax.optimization_barrier(
+        (jnp.stack(along_z), jnp.stack(along_x), mlp_pair, tokens)
     )
     mlp_w = lax.all_gather(mlp_pair, ("x", "z"), axis=0, tiled=True)
-    along_x, along_z, _ = from_both([along_z] * 4, "x", [along_x] * 4, "z", False)
+    along_x, along_z, far = from_both(
+        [along_z] * 4, "x", [along_x] * 4, "z", True, other(tokens, "yl")
+    )
     token_pieces = [tokens, other(tokens, "core"), far, other(far, "core")]
     cotangent, far = after(cotangent, far)
     grad_far = other(cotangent, "yl")

time: 339 us -> 330 us (0.973)
  waiting for transfers between devices: 116 us -> 109 us
    ppermute x55, waiting for transfers between devices: 115 us -> 105 us  [from_offset(): lax.ppermute(v, axis, [((i + offset) % size, i) for i in range(size)])]
  transfers between devices with their start and end apart: 60 -> 60, of which waited for: 31 -> 27; matrix products, arithmetic and copies ran while one was open for 10% -> 9% of each run, Pallas kernels for 21% -> 22%
where the time goes in v10:
time: 330 us; the launch traced here: 323 us
  waiting for transfers between devices  109 us (33%)
  Pallas kernels  86.1 us (26%)
  starting transfers between devices  74.7 us (23%)
  other arithmetic  25.9 us (8%)
  between operations  15 us (5%)
  local copies, waits for them, and re-layouts  11.9 us (4%)
    ppermute x55, waiting for transfers between devices, from_offset(): lax.ppermute(v, axis, [((i + offset) % size, i) for i in range(size)])  105 us
    pallas_call x6, Pallas kernels, kernel_call(): pl.pallas_call(kernel, out_shape=list(small_outs) + list(outs), in_specs=...  84.4 us
    ppermute x55, starting transfers between devices, from_offset(): lax.ppermute(v, axis, [((i + offset) % size, i) for i in range(size)])  66.3 us
    ppermute x3, starting transfers between devices, body(): lax.ppermute(gain_sum, ('yl', 'core'), [(i ^ step, i) for i in range(4)])  8.35 us
    convert_element_type x4, other arithmetic, far_sum(): return near_sum(chip, diagonal).astype(BF16)  6.82 us
  transfers between devices with their start and end apart: 60, of which 27 were waited for; matrix products, arithmetic and copies ran while one was open for 9% of the time, Pallas kernels for 22%

profile of v10, /device:TPU:1, one launch (start us, length us, event | category | flops | bytes accessed | tf_op | source)
XLA Modules:
  0.0 323.1 jit_solution(8395620036674141364)
XLA Ops:
  13.6 2.7 collective-permute-start
  18.0 2.8 collective-permute-done.3
  22.0 3.8 %collective-permute-start.4 = (bf16[96,640]{1,0:T(8,128)(2,1)S(1)}, bf16[96,640]{1,0:T(8,128)(2,1)S(1)}, u32[]{:S(2)}, u32[]{:S(2)}) collective-permute-start(bf16[96,640]{1,0:T(8,128)(2,1)S(1)} %get-tuple-element.290), channel_id=1, source_target_pairs={{8,0},{16,8},{24,16},{0,24},{9,1},{17,9},{25,17},{1,25},{10,2},{18... | collective-permute-start | bytes 368648 | tf_op jit(solution)/shard_map/ppermute | solution.py:555
  25.9 2.5 collective-permute-start.5
  28.4 2.7 collective-permute-start.10
  34.1 3.6 %collective-permute-done.6 = bf16[96,640]{1,0:T(8,128)(2,1)S(1)} collective-permute-done((bf16[96,640]{1,0:T(8,128)(2,1)S(1)}, bf16[96,640]{1,0:T(8,128)(2,1)S(1)}, u32[]{:S(2)}, u32[]{:S(2)}) %collective-permute-start.6) | collective-permute-done | bytes 122912 | tf_op jit(solution)/shard_map/ppermute | solution.py:555
  43.6 7.0 %collective-permute-done.11.a1 = bf16[4,96,640]{2,1,0:T(8,128)(2,1)S(1)} collective-permute-done((bf16[4,96,640]{2,1,0:T(8,128)(2,1)S(1)}, bf16[4,96,640]{2,1,0:T(8,128)(2,1)S(1)}, u32[]{:S(2)}, u32[]{:S(2)}) %collective-permute-start.11) | collective-permute-done | bytes 491552 | tf_op jit(solution)/shard_map/ppermute | solution.py:555
  50.7 4.1 %collective-permute-start.17 = (bf16[256,1536]{1,0:T(8,128)(2,1)S(1)}, bf16[256,1536]{1,0:T(8,128)(2,1)}, u32[]{:S(2)}, u32[]{:S(2)}) collective-permute-start(bf16[256,1536]{1,0:T(8,128)(2,1)S(1)} %copy-done.3), channel_id=1, source_target_pairs={{1,0},{0,1},{3,2},{2,3},{5,4},{4,5},{7,6},{6,7},{9,8},{8,9},{11,10... | collective-permute-start | bytes 2359304 | tf_op jit(solution)/shard_map/ppermute | solution.py:555
  54.9 2.5 collective-permute-done.15.t2
  57.3 5.7 %collective-permute-start.18 = (bf16[256,1536]{1,0:T(8,128)(2,1)S(1)}, bf16[256,1536]{1,0:T(8,128)(2,1)}, u32[]{:S(2)}, u32[]{:S(2)}) collective-permute-start(bf16[256,1536]{1,0:T(8,128)(2,1)S(1)} %collective-permute-done.15.t2), channel_id=1, source_target_pairs={{1,0},{0,1},{3,2},{2,3},{5,4},{4,5},{7,6},{6,7},{9,8},{8,9},{11,10... | collective-permute-start | bytes 2359304 | tf_op jit(solution)/shard_map/ppermute | solution.py:555
  68.4 10.4 %collective-permute-done.19.a2 = bf16[4,96,640]{2,1,0:T(8,128)(2,1)} collective-permute-done((bf16[4,96,640]{2,1,0:T(8,128)(2,1)S(1)}, bf16[4,96,640]{2,1,0:T(8,128)(2,1)}, u32[]{:S(2)}, u32[]{:S(2)}) %collective-permute-start.19) | collective-permute-done | bytes 491552 | tf_op jit(solution)/shard_map/ppermute | solution.py:555
  79.1 15.9 %attend.1 = (f32[2,1536]{1,0:T(2,128)}, bf16[1536,1280]{1,0:T(8,128)(2,1)}, bf16[1024,1536]{1,0:T(8,128)(2,1)}, bf16[4,96,1024]{2,1,0:T(8,128)(2,1)}, bf16[2,96,...) custom-call(s32[4]{0:T(128)} %pad_add_fusion.2.place, ...), custom_call_target="tpu_custom_call" | custom-call | flops 1 | bytes 1 | tf_op jit(solution)/shard_map/attend/pallas_call | solution.py:90
  102.3 16.5 %collective-permute-done.23 = bf16[256,1536]{1,0:T(8,128)(2,1)S(1)} collective-permute-done((bf16[256,1536]{1,0:T(8,128)(2,1)S(1)}, bf16[256,1536]{1,0:T(8,128)(2,1)S(1)}, u32[]{:S(2)}, u32[]{:S(2)}) %collective-permute-start.23) | collective-permute-done | bytes 786464 | tf_op jit(solution)/shard_map/ppermute | solution.py:555
  123.9 2.9 all-gather.2.cloned.1.call-done.w_hbm
  126.8 14.7 %feed.2 = (bf16[512,1024]{1,0:T(8,128)(2,1)}, bf16[512,2048]{1,0:T(8,128)(2,1)}, bf16[256,1536]{1,0:T(8,128)(2,1)}, bf16[256,1536]{1,0:T(8,128)(2,1)}, bf16[256,...) custom-call(s32[4]{0:T(128)} %pad_add_fusion.2.place, bf16[256,1536]{1,0:T(8,128)(2,1)} %multiply_convert_fusion.h0, ...), custom_call_target="tpu_custom_call" | custom-call | flops 1 | bytes 1 | tf_op jit(solution)/shard_map/feed/pallas_call | solution.py:90
  142.7 2.1 collective-permute-done.27.h1.h3
  145.7 14.7 %feed.3 = (bf16[512,1024]{1,0:T(8,128)(2,1)}, bf16[512,2048]{1,0:T(8,128)(2,1)}, bf16[256,1536]{1,0:T(8,128)(2,1)}, bf16[256,1536]{1,0:T(8,128)(2,1)}, bf16[256,...) custom-call(s32[4]{0:T(128)} %pad_add_fusion.2.place, bf16[256,1536]{1,0:T(8,128)(2,1)} %collective-permute-done.24.h0.h2, ...), custom_call_target="tpu_custom_call" | custom-call | flops 1 | bytes 1 | tf_op jit(solution)/shard_map/feed/pallas_call | solution.py:90
  163.0 2.2 add_convert_fusion.2
  166.5 15.4 %feed_grads.1 = bf16[1536,3072]{1,0:T(8,128)(2,1)} custom-call(s32[4]{0:T(128)} %pad_add_fusion.2.place, bf16[256,1536]{1,0:T(8,128)(2,1)} %multiply_convert_fusion.h0, bf16[256,1536]{1,0:T(8,128)(2,1)} %collective-permute-done.25.h1, bf16[256,1536]{1,0:T(8,128)(2,1)} %collective-permute-done.24.h0.h2, bf16[256,1536]{1,0:T(8,128)(2,1)} %copy-done.9, ...), custom_call_target="tpu_custom_call" | custom-call | flops 1 | bytes 1 | tf_op jit(solution)/shard_map/feed_grads/pallas_call | solution.py:90
  181.9 2.5 collective-permute-done.32
  187.8 3.3 %fusion.10 = (bf16[256,1536]{1,0:T(8,128)(2,1)S(1)}, f32[256,1536]{1,0:T(8,128)}) fusion(f32[256]{0:T(256)S(1)} %broadcast_multiply_fusion.1, f32[256,1536]{1,0:T(8,128)S(1)} %get-tuple-element.286, f32[1536]{0:T(1024)S(1)} %get-tuple-element.279, bf16[256,1536]{1,0:T(8,128)(2,1)} %collective-permute-done.32, bf16[256,1536]{1,0:T(8,128)(2,1)} %collective-permute-done.31, ...), kind=kLoop, calls=%fused_computation.60 | loop fusion | flops 5111808 | bytes 7086080 | tf_op jit(solution)/shard_map/convert_element_type | solution.py:700
  193.2 17.1 %collective-permute-done.34.o2 = bf16[256,1536]{1,0:T(8,128)(2,1)S(1)} collective-permute-done((bf16[256,1536]{1,0:T(8,128)(2,1)S(1)}, bf16[256,1536]{1,0:T(8,128)(2,1)S(1)}, u32[]{:S(2)}, u32[]{:S(2)}) %collective-permute-start.34) | collective-permute-done | bytes 786464 | tf_op jit(solution)/shard_map/ppermute | solution.py:555
  215.3 17.2 %attend_back.1 = (bf16[768,1024]{1,0:T(8,128)(2,1)}, bf16[384,576]{1,0:T(8,128)(2,1)}, bf16[384,576]{1,0:T(8,128)(2,1)}, bf16[384,576]{1,0:T(8,128)(2,1)}, bf16[...) custom-call(s32[4]{0:T(128)} %pad_add_fusion.2.place, ...), custom_call_target="tpu_custom_call" | custom-call | flops 1 | bytes 1 | tf_op jit(solution)/shard_map/attend_back/pallas_call | solution.py:90
  232.5 2.4 collective-permute-start.37
  236.6 6.5 %project_back.1 = (bf16[256,1536]{1,0:T(8,128)(2,1)}, bf16[256,1536]{1,0:T(8,128)(2,1)}, bf16[256,1536]{1,0:T(8,128)(2,1)}, bf16[256,1536]{1,0:T(8,128)(2,1)}) custom-call(s32[4]{0:T(128)} %pad_add_fusion.2.place, bf16[768,1024]{1,0:T(8,128)(2,1)} %get-tuple-element.219.dqkv_hbm, bf16[1536,1280]{1,0:T(8,128)(2,1)} %get-tuple-element.203.w_hbm), custom_call_target="tpu_custom_call" | custom-call | flops 1 | bytes 1 | tf_op jit(solution)/shard_map/project_back/pallas_call | solution.py:90
  243.2 9.1 %collective-permute-done.37.refs_1_ = bf16[384,576]{1,0:T(8,128)(2,1)S(1)} collective-permute-done((bf16[384,576]{1,0:T(8,128)(2,1)}, bf16[384,576]{1,0:T(8,128)(2,1)S(1)}, u32[]{:S(2)}, u32[]{:S(2)}) %collective-permute-start.37) | collective-permute-done | bytes 442400 | tf_op jit(solution)/shard_map/ppermute | solution.py:555
  258.0 2.2 add_convert_fusion
  263.1 12.5 %collective-permute-done.42.refs_2_ = bf16[384,576]{1,0:T(8,128)(2,1)S(1)} collective-permute-done((bf16[384,576]{1,0:T(8,128)(2,1)}, bf16[384,576]{1,0:T(8,128)(2,1)S(1)}, u32[]{:S(2)}, u32[]{:S(2)}) %collective-permute-start.42) | collective-permute-done | bytes 442400 | tf_op jit(solution)/shard_map/ppermute | solution.py:555
  279.8 2.3 collective-permute-done.44.refs_1_
  284.6 2.4 collective-permute-done.47.refs_7_
  288.0 3.2 collective-permute-start.53
  304.3 6.6 %collective-permute-start.55 = (f32[2,48]{1,0:T(2,128)S(1)}, f32[2,48]{1,0:T(2,128)S(1)}, u32[]{:S(2)}, u32[]{:S(2)}) collective-permute-start(f32[2,48]{1,0:T(2,128)S(1)} %pad_maximum_fusion.2), channel_id=1, source_target_pairs={{1,0},{0,1},{3,2},{2,3},{5,4},{4,5},{7,6},{6,7},{9,8},{8,9},{11,10... | collective-permute-start | bytes 1160 | tf_op jit(solution)/shard_map/ppermute | solution.py:744
  (230 shorter events, 88.6 us)
Async XLA Ops:
  7.2 119.7 %all-gather.2.cloned.1.call-start = ((), (), s32[]{:S(2)}) async-start(), calls=%async_computation.1 | async-start | bytes 10027008 | tf_op jit(solution)/shard_map/all_gather | solution.py:652
  22.0 9.0 %collective-permute-start.4 = (bf16[96,640]{1,0:T(8,128)(2,1)S(1)}, bf16[96,640]{1,0:T(8,128)(2,1)S(1)}, u32[]{:S(2)}, u32[]{:S(2)}) collective-permute-start(bf16[96,640]{1,0:T(8,128)(2,1)S(1)} %get-tuple-element.290), channel_id=1, source_target_pairs={{8,0},{16,8},{24,16},{0,24},{9,1},{17,9},{25,17},{1,25},{10,2},{18... | collective-permute-start | bytes 368648 | tf_op jit(solution)/shard_map/ppermute | solution.py:555
  28.4 10.9 %collective-permute-start.10 = (bf16[48,3072]{1,0:T(8,128)(2,1)S(1)}, bf16[48,3072]{1,0:T(8,128)(2,1)S(1)}, u32[]{:S(2)}, u32[]{:S(2)}) collective-permute-start(bf16[48,3072]{1,0:T(8,128)(2,1)S(1)} %pad_add_fusion), channel_id=1, source_target_pairs={{4,0},{0,4},{5,1},{1,5},{6,2},{2,6},{7,3},{3,7},{12,8},{8,12},{13,... | collective-permute-start | bytes 884744 | tf_op jit(solution)/shard_map/ppermute | solution.py:555
  40.3 246.7 %reduce-scatter.2.cloned.1.call-start = ((), (), s32[]{:S(2)}) async-start(), calls=%async_computation.2 | async-start | bytes 10027008 | tf_op jit(solution)/shard_map/reduce_scatter | solution.py:695
  40.4 16.9 %collective-permute-start.15 = (bf16[256,1536]{1,0:T(8,128)(2,1)S(1)}, bf16[256,1536]{1,0:T(8,128)(2,1)S(1)}, u32[]{:S(2)}, u32[]{:S(2)}) collective-permute-start(bf16[256,1536]{1,0:T(8,128)(2,1)S(1)} %copy-done.3), channel_id=1, source_target_pairs={{2,0},{0,2},{3,1},{1,3},{6,4},{4,6},{7,5},{5,7},{10,8},{8,10},{11,... | collective-permute-start | bytes 2359304 | tf_op jit(solution)/shard_map/ppermute | solution.py:555
  40.5 10.2 %collective-permute-start.11 = (bf16[4,96,640]{2,1,0:T(8,128)(2,1)S(1)}, bf16[4,96,640]{2,1,0:T(8,128)(2,1)S(1)}, u32[]{:S(2)}, u32[]{:S(2)}) collective-permute-start(bf16[4,96,640]{2,1,0:T(8,128)(2,1)S(1)} %get-tuple-element.161.a0), channel_id=1, source_target_pairs={{32,0},{64,32},{96,64},{0,96},{33,1},{65,33},{97,65},{1,97},{34,2}... | collective-permute-start | bytes 1474568 | tf_op jit(solution)/shard_map/ppermute | solution.py:555
  41.7 13.1 %collective-permute-start.12 = (bf16[4,96,640]{2,1,0:T(8,128)(2,1)S(1)}, bf16[4,96,640]{2,1,0:T(8,128)(2,1)S(1)}, u32[]{:S(2)}, u32[]{:S(2)}) collective-permute-start(bf16[4,96,640]{2,1,0:T(8,128)(2,1)S(1)} %get-tuple-element.162.b0), channel_id=1, source_target_pairs={{8,0},{16,8},{24,16},{0,24},{9,1},{17,9},{25,17},{1,25},{10,2},{18... | collective-permute-start | bytes 1474568 | tf_op jit(solution)/shard_map/ppermute | solution.py:555
  43.1 11.7 %collective-permute-start.13 = (bf16[4,96,640]{2,1,0:T(8,128)(2,1)S(1)}, bf16[4,96,640]{2,1,0:T(8,128)(2,1)S(1)}, u32[]{:S(2)}, u32[]{:S(2)}) collective-permute-start(bf16[4,96,640]{2,1,0:T(8,128)(2,1)S(1)} %get-tuple-element.161.a0), channel_id=1, source_target_pairs={{96,0},{0,32},{32,64},{64,96},{97,1},{1,33},{33,65},{65,97},{98,2}... | collective-permute-start | bytes 1474568 | tf_op jit(solution)/shard_map/ppermute | solution.py:555
  43.2 11.7 %collective-permute-start.14 = (bf16[4,96,640]{2,1,0:T(8,128)(2,1)S(1)}, bf16[4,96,640]{2,1,0:T(8,128)(2,1)S(1)}, u32[]{:S(2)}, u32[]{:S(2)}) collective-permute-start(bf16[4,96,640]{2,1,0:T(8,128)(2,1)S(1)} %get-tuple-element.162.b0), channel_id=1, source_target_pairs={{24,0},{0,8},{8,16},{16,24},{25,1},{1,9},{9,17},{17,25},{26,2},{2,... | collective-permute-start | bytes 1474568 | tf_op jit(solution)/shard_map/ppermute | solution.py:555
  50.7 28.4 %collective-permute-start.17 = (bf16[256,1536]{1,0:T(8,128)(2,1)S(1)}, bf16[256,1536]{1,0:T(8,128)(2,1)}, u32[]{:S(2)}, u32[]{:S(2)}) collective-permute-start(bf16[256,1536]{1,0:T(8,128)(2,1)S(1)} %copy-done.3), channel_id=1, source_target_pairs={{1,0},{0,1},{3,2},{2,3},{5,4},{4,5},{7,6},{6,7},{9,8},{8,9},{11,10... | collective-permute-start | bytes 2359304 | tf_op jit(solution)/shard_map/ppermute | solution.py:555
  57.3 21.8 %collective-permute-start.18 = (bf16[256,1536]{1,0:T(8,128)(2,1)S(1)}, bf16[256,1536]{1,0:T(8,128)(2,1)}, u32[]{:S(2)}, u32[]{:S(2)}) collective-permute-start(bf16[256,1536]{1,0:T(8,128)(2,1)S(1)} %collective-permute-done.15.t2), channel_id=1, source_target_pairs={{1,0},{0,1},{3,2},{2,3},{5,4},{4,5},{7,6},{6,7},{9,8},{8,9},{11,10... | collective-permute-start | bytes 2359304 | tf_op jit(solution)/shard_map/ppermute | solution.py:555
  63.0 32.1 %collective-permute-start.16 = (bf16[256,1536]{1,0:T(8,128)(2,1)S(1)}, bf16[256,1536]{1,0:T(8,128)(2,1)}, u32[]{:S(2)}, u32[]{:S(2)}) collective-permute-start(bf16[256,1536]{1,0:T(8,128)(2,1)S(1)} %copy-done.5), channel_id=1, source_target_pairs={{2,0},{0,2},{3,1},{1,3},{6,4},{4,6},{7,5},{5,7},{10,8},{8,10},{11,... | collective-permute-start | bytes 2359304 | tf_op jit(solution)/shard_map/ppermute | solution.py:555
  64.8 14.1 %collective-permute-start.19 = (bf16[4,96,640]{2,1,0:T(8,128)(2,1)S(1)}, bf16[4,96,640]{2,1,0:T(8,128)(2,1)}, u32[]{:S(2)}, u32[]{:S(2)}) collective-permute-start(bf16[4,96,640]{2,1,0:T(8,128)(2,1)S(1)} %get-tuple-element.161.a0), channel_id=1, source_target_pairs={{64,0},{96,32},{0,64},{32,96},{65,1},{97,33},{1,65},{33,97},{66,2}... | collective-permute-start | bytes 1474568 | tf_op jit(solution)/shard_map/ppermute | solution.py:555
  64.8 14.3 %collective-permute-start.20 = (bf16[4,96,640]{2,1,0:T(8,128)(2,1)S(1)}, bf16[4,96,640]{2,1,0:T(8,128)(2,1)}, u32[]{:S(2)}, u32[]{:S(2)}) collective-permute-start(bf16[4,96,640]{2,1,0:T(8,128)(2,1)S(1)} %get-tuple-element.162.b0), channel_id=1, source_target_pairs={{16,0},{24,8},{0,16},{8,24},{17,1},{25,9},{1,17},{9,25},{18,2},{26... | collective-permute-start | bytes 1474568 | tf_op jit(solution)/shard_map/ppermute | solution.py:555
  99.9 19.0 %collective-permute-start.23 = (bf16[256,1536]{1,0:T(8,128)(2,1)S(1)}, bf16[256,1536]{1,0:T(8,128)(2,1)S(1)}, u32[]{:S(2)}, u32[]{:S(2)}) collective-permute-start(bf16[256,1536]{1,0:T(8,128)(2,1)S(1)} %add_convert_fusion.4), channel_id=1, source_target_pairs={{2,0},{0,2},{3,1},{1,3},{6,4},{4,6},{7,5},{5,7},{10,8},{8,10},{11,... | collective-permute-start | bytes 2359304 | tf_op jit(solution)/shard_map/ppermute | solution.py:555
  100.8 22.0 %collective-permute-start.26 = (bf16[256,1536]{1,0:T(8,128)(2,1)S(1)}, bf16[256,1536]{1,0:T(8,128)(2,1)S(1)}, u32[]{:S(2)}, u32[]{:S(2)}) collective-permute-start(bf16[256,1536]{1,0:T(8,128)(2,1)S(1)} %copy-done.5), channel_id=1, source_target_pairs={{1,0},{0,1},{3,2},{2,3},{5,4},{4,5},{7,6},{6,7},{9,8},{8,9},{11,10... | collective-permute-start | bytes 2359304 | tf_op jit(solution)/shard_map/ppermute | solution.py:555
  121.6 19.9 %collective-permute-start.24 = (bf16[256,1536]{1,0:T(8,128)(2,1)}, bf16[256,1536]{1,0:T(8,128)(2,1)}, u32[]{:S(2)}, u32[]{:S(2)}) collective-permute-start(bf16[256,1536]{1,0:T(8,128)(2,1)} %multiply_convert_fusion.h0), channel_id=1, source_target_pairs={{2,0},{0,2},{3,1},{1,3},{6,4},{4,6},{7,5},{5,7},{10,8},{8,10},{11,... | collective-permute-start | bytes 2359304 | tf_op jit(solution)/shard_map/ppermute | solution.py:555
  122.5 20.1 %collective-permute-start.28 = (bf16[256,1536]{1,0:T(8,128)(2,1)}, bf16[256,1536]{1,0:T(8,128)(2,1)}, u32[]{:S(2)}, u32[]{:S(2)}) collective-permute-start(bf16[256,1536]{1,0:T(8,128)(2,1)} %collective-permute-done.16.g0.g2), channel_id=1, source_target_pairs={{1,0},{0,1},{3,2},{2,3},{5,4},{4,5},{7,6},{6,7},{9,8},{8,9},{11,10... | collective-permute-start | bytes 2359304 | tf_op jit(solution)/shard_map/ppermute | solution.py:555
  165.2 19.2 %collective-permute-start.32 = (bf16[256,1536]{1,0:T(8,128)(2,1)}, bf16[256,1536]{1,0:T(8,128)(2,1)}, u32[]{:S(2)}, u32[]{:S(2)}) collective-permute-start(bf16[256,1536]{1,0:T(8,128)(2,1)} %add_convert_fusion.2), channel_id=1, source_target_pairs={{2,0},{0,2},{3,1},{1,3},{6,4},{4,6},{7,5},{5,7},{10,8},{8,10},{11,... | collective-permute-start | bytes 2359304 | tf_op jit(solution)/shard_map/ppermute | solution.py:555
  191.1 19.1 %collective-permute-start.34 = (bf16[256,1536]{1,0:T(8,128)(2,1)S(1)}, bf16[256,1536]{1,0:T(8,128)(2,1)S(1)}, u32[]{:S(2)}, u32[]{:S(2)}) collective-permute-start(bf16[256,1536]{1,0:T(8,128)(2,1)S(1)} %get-tuple-element.199.o0), channel_id=1, source_target_pairs={{2,0},{0,2},{3,1},{1,3},{6,4},{4,6},{7,5},{5,7},{10,8},{8,10},{11,... | collective-permute-start | bytes 2359304 | tf_op jit(solution)/shard_map/ppermute | solution.py:555
  192.3 18.9 %collective-permute-start.29 = (bf16[256,1536]{1,0:T(8,128)(2,1)S(1)}, bf16[256,1536]{1,0:T(8,128)(2,1)S(1)}, u32[]{:S(2)}, u32[]{:S(2)}) collective-permute-start(bf16[256,1536]{1,0:T(8,128)(2,1)S(1)} %copy-done.36), channel_id=1, source_target_pairs={{1,0},{0,1},{3,2},{2,3},{5,4},{4,5},{7,6},{6,7},{9,8},{8,9},{11,10... | collective-permute-start | bytes 2359304 | tf_op jit(solution)/shard_map/ppermute | solution.py:555
  192.9 19.5 %collective-permute-start.33 = (bf16[256,1536]{1,0:T(8,128)(2,1)S(1)}, bf16[256,1536]{1,0:T(8,128)(2,1)S(1)}, u32[]{:S(2)}, u32[]{:S(2)}) collective-permute-start(bf16[256,1536]{1,0:T(8,128)(2,1)S(1)} %get-tuple-element.199.o0), channel_id=1, source_target_pairs={{1,0},{0,1},{3,2},{2,3},{5,4},{4,5},{7,6},{6,7},{9,8},{8,9},{11,10... | collective-permute-start | bytes 2359304 | tf_op jit(solution)/shard_map/ppermute | solution.py:555
  214.1 22.5 %collective-permute-start.41 = (bf16[256,1536]{1,0:T(8,128)(2,1)}, bf16[256,1536]{1,0:T(8,128)(2,1)S(1)}, u32[]{:S(2)}, u32[]{:S(2)}) collective-permute-start(bf16[256,1536]{1,0:T(8,128)(2,1)} %add_convert_fusion.3), channel_id=1, source_target_pairs={{2,0},{0,2},{3,1},{1,3},{6,4},{4,6},{7,5},{5,7},{10,8},{8,10},{11,... | collective-permute-start | bytes 2359304 | tf_op jit(solution)/shard_map/ppermute | solution.py:555
  232.5 19.8 %collective-permute-start.37 = (bf16[384,576]{1,0:T(8,128)(2,1)}, bf16[384,576]{1,0:T(8,128)(2,1)S(1)}, u32[]{:S(2)}, u32[]{:S(2)}) collective-permute-start(bf16[384,576]{1,0:T(8,128)(2,1)} %get-tuple-element.213), channel_id=1, source_target_pairs={{32,0},{64,32},{96,64},{0,96},{33,1},{65,33},{97,65},{1,97},{34,2}... | collective-permute-start | bytes 1327112 | tf_op jit(solution)/shard_map/ppermute | solution.py:555
  234.9 18.3 %collective-permute-start.38 = (bf16[4,96,576]{2,1,0:T(8,128)(2,1)}, bf16[4,96,576]{2,1,0:T(8,128)(2,1)S(1)}, u32[]{:S(2)}, u32[]{:S(2)}) collective-permute-start(bf16[4,96,576]{2,1,0:T(8,128)(2,1)} %get-tuple-element.214), channel_id=1, source_target_pairs={{8,0},{16,8},{24,16},{0,24},{9,1},{17,9},{25,17},{1,25},{10,2},{18... | collective-permute-start | bytes 1327112 | tf_op jit(solution)/shard_map/ppermute | solution.py:555
  235.6 18.7 %collective-permute-start.39 = (bf16[384,576]{1,0:T(8,128)(2,1)}, bf16[384,576]{1,0:T(8,128)(2,1)S(1)}, u32[]{:S(2)}, u32[]{:S(2)}) collective-permute-start(bf16[384,576]{1,0:T(8,128)(2,1)} %get-tuple-element.215), channel_id=1, source_target_pairs={{96,0},{0,32},{32,64},{64,96},{97,1},{1,33},{33,65},{65,97},{98,2}... | collective-permute-start | bytes 1327112 | tf_op jit(solution)/shard_map/ppermute | solution.py:555
  236.4 18.0 %collective-permute-start.40 = (bf16[4,96,576]{2,1,0:T(8,128)(2,1)}, bf16[4,96,576]{2,1,0:T(8,128)(2,1)S(1)}, u32[]{:S(2)}, u32[]{:S(2)}) collective-permute-start(bf16[4,96,576]{2,1,0:T(8,128)(2,1)} %get-tuple-element.216), channel_id=1, source_target_pairs={{24,0},{0,8},{8,16},{16,24},{25,1},{1,9},{9,17},{17,25},{26,2},{2,... | collective-permute-start | bytes 1327112 | tf_op jit(solution)/shard_map/ppermute | solution.py:555
  255.3 20.3 %collective-permute-start.42 = (bf16[384,576]{1,0:T(8,128)(2,1)}, bf16[384,576]{1,0:T(8,128)(2,1)S(1)}, u32[]{:S(2)}, u32[]{:S(2)}) collective-permute-start(bf16[384,576]{1,0:T(8,128)(2,1)} %get-tuple-element.228), channel_id=1, source_target_pairs={{64,0},{96,32},{0,64},{32,96},{65,1},{97,33},{1,65},{33,97},{66,2}... | collective-permute-start | bytes 1327112 | tf_op jit(solution)/shard_map/ppermute | solution.py:555
  256.7 20.5 %collective-permute-start.43 = (bf16[4,96,576]{2,1,0:T(8,128)(2,1)S(1)}, bf16[4,96,576]{2,1,0:T(8,128)(2,1)S(1)}, u32[]{:S(2)}, u32[]{:S(2)}) collective-permute-start(bf16[4,96,576]{2,1,0:T(8,128)(2,1)S(1)} %copy-done.38), channel_id=1, source_target_pairs={{16,0},{24,8},{0,16},{8,24},{17,1},{25,9},{1,17},{9,25},{18,2},{26... | collective-permute-start | bytes 1327112 | tf_op jit(solution)/shard_map/ppermute | solution.py:555
  257.4 35.0 %collective-permute-start.50 = (bf16[256,1536]{1,0:T(8,128)(2,1)}, bf16[256,1536]{1,0:T(8,128)(2,1)}, u32[]{:S(2)}, u32[]{:S(2)}) collective-permute-start(bf16[256,1536]{1,0:T(8,128)(2,1)} %get-tuple-element.262), channel_id=1, source_target_pairs={{1,0},{0,1},{3,2},{2,3},{5,4},{4,5},{7,6},{6,7},{9,8},{8,9},{11,10... | collective-permute-start | bytes 2359304 | tf_op jit(solution)/shard_map/ppermute | solution.py:555
  260.2 32.1 %collective-permute-start.52 = (bf16[256,1536]{1,0:T(8,128)(2,1)}, bf16[256,1536]{1,0:T(8,128)(2,1)}, u32[]{:S(2)}, u32[]{:S(2)}) collective-permute-start(bf16[256,1536]{1,0:T(8,128)(2,1)} %add_convert_fusion), channel_id=1, source_target_pairs={{2,0},{0,2},{3,1},{1,3},{6,4},{4,6},{7,5},{5,7},{10,8},{8,10},{11,... | collective-permute-start | bytes 2359304 | tf_op jit(solution)/shard_map/ppermute | solution.py:555
  304.3 10.0 %collective-permute-start.55 = (f32[2,48]{1,0:T(2,128)S(1)}, f32[2,48]{1,0:T(2,128)S(1)}, u32[]{:S(2)}, u32[]{:S(2)}) collective-permute-start(f32[2,48]{1,0:T(2,128)S(1)} %pad_maximum_fusion.2), channel_id=1, source_target_pairs={{1,0},{0,1},{3,2},{2,3},{5,4},{4,5},{7,6},{6,7},{9,8},{8,9},{11,10... | collective-permute-start | bytes 1160 | tf_op jit(solution)/shard_map/ppermute | solution.py:744
  (67 other events, 561.2 us)
Sparse Core Ops, SparseCore 0:
  40.4 86.3 all-gather.1
  184.5 97.4 reduce-scatter.1
